TPU v7x, 32 devices: a whole 2x2x4 slice. The times are simulated.
32 devices in a mesh: groups: 2 (over y), seq: 4 (over z), chan: 2 (over x), sub: 2 (over core).
Axes of the slice: x: 2, y: 2, z: 4, core: 2. Of those that a mesh axis runs over, the one named last changes fastest.
Arguments:
- x_in: bfloat16 [1024, 8192], P(('groups', 'seq'), ('chan', 'sub')), parts along dimension 0, may hold values from -36 to 36
- b_in: bfloat16 [1024, 4, 256], P(('groups', 'seq'), 'chan'), parts along dimension 0, may hold values from -6 to 6
- c_in: bfloat16 [1024, 4, 256], P(('groups', 'seq'), 'chan'), parts along dimension 0, may hold values from -0.375 to 0.375
- step_size: float32 [1024, 128], P(('groups', 'seq'), ('chan', 'sub')), parts along dimension 0, may hold values from 0.02 to 0.2
- log_decay: float32 [1024, 128], P(('groups', 'seq'), ('chan', 'sub')), parts along dimension 0, may hold values from -1 to 0, as said below
- skip: float32 [128], P(('chan', 'sub')), may hold values from 0.5 to 1.5
- gate_in: bfloat16 [1024, 8192], P(('groups', 'seq'), ('chan', 'sub')), parts along dimension 0, may hold values from -6 to 6
- norm_gain: float32 [8192], P(('chan', 'sub')), may hold values from 0.1 to 1.9
- walsh_sign: int32 [8192], P(('chan', 'sub')), may hold values from 0 to 1
- channel_shift_power: int32 [8192], P(('chan', 'sub')), may hold values from -1 to 3
- out_weight: bfloat16 [8192, 4096], P(('chan', 'sub'), 'seq'), may hold values from -0.0625 to 0.0625
Outputs:
- projected: bfloat16 [1024, 4096], P(('groups', 'seq', 'chan', 'sub')), parts along dimension 0
There are 2 independent parts, one for each index of `groups`. A program takes and returns all parts, laid end to end along the dimension named above; an argument that names none is the same for every part. Nothing has to cross between parts.
Inputs may be any that keep to these rules, and one draw needn't show every extreme that they name: `log_decay`: every entry is negative.
All inputs are finite; a program needn't handle non-finite values.
Results may differ from a plain program's by a relative error of at most 0.024.
Values may be sent and summed in bfloat16 or wider, within the bound.
No kernel may reach another device: no remote copies, remote signals or barrier semaphores. Data moves between devices by JAX's collectives and lax.ppermute only.
A program may use at most 128 MiB of HBM per device.

v0:
```python
import functools
import math

import jax
import jax.numpy as jnp
import numpy as np
from jax import lax
from jax.experimental import pallas as pl
from jax.experimental.pallas import tpu as pltpu
from jax.sharding import PartitionSpec as P

LOCAL_HEADS = 128
P_SIZE = 64
G = 4
NORM_HEADS = 16


norm_eps = 1e-05
clip_level = 4.0
expo_levels = (-1, 0, 1, 2, 3)
LANES = 128
H_BLOCK = 256
f32 = jnp.float32
bf16 = jnp.bfloat16
PARAMS = pltpu.CompilerParams(vmem_limit_bytes=40 * 2**20)


def power_two(expo, sign_flip):
    result = jnp.zeros(expo.shape, jnp.float32)
    for level in expo_levels:
        result = result + jnp.where(
            expo == level, jnp.float32(2.0 ** (sign_flip * level)), jnp.float32(0.0)
        )
    return result


def dot(a, b):
    return jnp.dot(a, b, preferred_element_type=f32)


def dot_nt(a, b):
    return lax.dot_general(a, b, (((1,), (1,)), ((), ())), preferred_element_type=f32)


def parts_of(value, count):
    terms = []
    for _ in range(count):
        term = value.astype(bf16)
        terms.append(term)
        value = value - term.astype(f32)
    return terms


def exact_dot(exact, value, count=3):
    return sum(dot(exact, term) for term in parts_of(value, count))


def spread(value, expand, count=2):
    return sum(dot(term, expand) for term in parts_of(value, count))


def causal_mask(size):
    row = lax.broadcasted_iota(jnp.int32, (size, size), 0)
    col = lax.broadcasted_iota(jnp.int32, (size, size), 1)
    return row >= col


def message_kernel(x_ref, b_ref, step_ref, decay_ref, expand_ref, msg_ref, cumul_ref):
    tokens, width = x_ref.shape
    heads = step_ref.shape[1]
    states = b_ref.shape[1]
    expand = expand_ref[...]
    triangle = causal_mask(tokens).astype(f32).astype(bf16)
    cumul = exact_dot(triangle, decay_ref[...])
    cumul_ref[...] = cumul
    total = cumul[tokens - 1 : tokens, :]
    scale = spread(jnp.exp(total - cumul) * step_ref[...], expand)
    msg_ref[:, :width] = (x_ref[...].astype(f32) * scale).astype(bf16)
    msg_ref[:, width : width + states] = b_ref[...]
    high, low = parts_of(jnp.exp(total), 2)
    base = width + states
    msg_ref[:, base:] = jnp.zeros((tokens, msg_ref.shape[1] - base), bf16)
    msg_ref[:, base : base + heads] = jnp.broadcast_to(high, (tokens, heads))
    msg_ref[:, base + heads : base + 2 * heads] = jnp.broadcast_to(low, (tokens, heads))


def local_kernel(
    x_ref, b_ref, c_ref, step_ref, cumul_ref, gate_ref, skip_ref, expand_ref, own_ref, far_ref
):
    tokens, width = x_ref.shape
    heads = step_ref.shape[1]
    causal = causal_mask(tokens)
    inner = dot_nt(c_ref[...], b_ref[...])
    cumul = cumul_ref[...]
    cumul_t = cumul.T
    step_t = step_ref[...].T
    first = lax.broadcasted_iota(jnp.int32, (tokens, 2 * P_SIZE), 1) < P_SIZE
    for pair in range(heads // 2):
        mixings = []
        for head in (2 * pair, 2 * pair + 1):
            differ = cumul[:, head : head + 1] - cumul_t[head : head + 1, :]
            ratio = jnp.exp(jnp.where(causal, differ, -jnp.inf))
            mixings.append((ratio * (inner * step_t[head : head + 1, :])).astype(bf16))
        at = slice(pair * 2 * P_SIZE, (pair + 1) * 2 * P_SIZE)
        x_pair = x_ref[:, at]
        zero = jnp.zeros_like(x_pair)
        blocks = jnp.concatenate(
            [jnp.where(first, x_pair, zero), jnp.where(first, zero, x_pair)], axis=0
        )
        own = dot(jnp.concatenate(mixings, axis=1), blocks)
        own = own + x_pair.astype(f32) * skip_ref[:, at]
        gate = gate_ref[:, at].astype(f32)
        own_ref[:, at] = own * (gate / (1.0 + jnp.exp(-gate)))
    reach = jnp.exp(cumul)
    tile = min(width, 512)
    for start in range(0, width, tile):
        at = slice(start, start + tile)
        gate = gate_ref[:, at].astype(f32)
        far_ref[:, at] = spread(reach, expand_ref[:, at]) * (gate / (1.0 + jnp.exp(-gate)))


def mix_kernel(count, *refs):
    messages = refs[:count]
    c_ref, own_ref, far_ref, gain_ref, table_ref, expand_ref, out_ref = refs[count:]
    tokens, width = own_ref.shape
    states = c_ref.shape[1]
    heads = expand_ref.shape[0]
    base = width + states
    c_group = c_ref[...]
    inners = []
    decays = []
    for msg_ref in messages:
        inners.append(dot_nt(c_group, msg_ref[:, width:base]).astype(bf16))
        decay = dot(msg_ref[:16, base : base + heads], expand_ref[...]) + dot(
            msg_ref[:16, base + heads : base + 2 * heads], expand_ref[...]
        )
        decays.append(decay[:1, :])
    norm_width = NORM_HEADS * P_SIZE
    table = table_ref[...]
    parts = []
    for start in range(0, width, norm_width):
        pres = []
        square = jnp.zeros((tokens, 1), f32)
        for begin in range(start, start + norm_width, H_BLOCK):
            at = slice(begin, begin + H_BLOCK)
            carried = None
            for k in reversed(range(count)):
                term = dot(inners[k], messages[k][:, at])
                carried = term if carried is None else term + decays[k][:, at] * carried
            pre = own_ref[:, at]
            if carried is not None:
                pre = pre + far_ref[:, at] * carried
            square = square + jnp.sum(pre * pre, axis=1, keepdims=True)
            pres.append(pre)
        inverse = lax.rsqrt(square * (1.0 / norm_width) + norm_eps)
        for index, pre in enumerate(pres):
            at = slice(start + index * H_BLOCK, start + (index + 1) * H_BLOCK)
            signed = (pre * inverse * gain_ref[:, at]).astype(bf16)
            parts.append(dot(signed, table))
    span = 1
    while span < len(parts):
        for low in range(len(parts)):
            if low & span == 0:
                a, b = parts[low], parts[low + span]
                parts[low], parts[low + span] = a + b, a - b
        span *= 2
    for index, part in enumerate(parts):
        out_ref[:, index * H_BLOCK : (index + 1) * H_BLOCK] = part.astype(bf16)


def sylvester(order):
    table = np.ones((1, 1), np.float32)
    while table.shape[0] < order:
        table = np.block([[table, table], [table, -table]])
    return table


def shift_up(value, axis, distance):
    count = lax.axis_size(axis)
    return lax.ppermute(value, axis, [(k, k + distance) for k in range(count - distance)])


def turn(value, axis, distance):
    count = lax.axis_size(axis)
    return lax.ppermute(value, axis, [(k, (k + distance) % count) for k in range(count)])


def swap(value, axis, bit):
    count = lax.axis_size(axis)
    return lax.ppermute(value, axis, [(k, k ^ (1 << bit)) for k in range(count)])


def bits_of(axis):
    return range(lax.axis_size(axis).bit_length() - 1)


def halve(value, axis):
    here = lax.axis_index(axis)
    for bit in reversed(bits_of(axis)):
        pair = value.reshape((2, value.shape[0] // 2) + value.shape[1:])
        mine = here // 2**bit % 2
        keep = lax.dynamic_index_in_dim(pair, mine, 0, keepdims=False)
        give = lax.dynamic_index_in_dim(pair, 1 - mine, 0, keepdims=False)
        value = (keep.astype(f32) + swap(give, axis, bit).astype(f32)).astype(bf16)
    return value[0]


def body(
    x_in,
    b_in,
    c_in,
    step_size,
    log_decay,
    skip,
    gate_in,
    norm_gain,
    walsh_sign,
    channel_shift_power,
    out_weight,
):
    tokens, width = x_in.shape
    heads = step_size.shape[1]
    states = b_in.shape[2]
    seq_count = lax.axis_size("seq")
    sub_index = lax.axis_index("sub")
    group_local = sub_index * heads // (LOCAL_HEADS // G)
    b_group = lax.dynamic_slice_in_dim(b_in, group_local, 1, 1)[:, 0, :]
    c_group = lax.dynamic_slice_in_dim(c_in, group_local, 1, 1)[:, 0, :]
    expand = jnp.asarray(np.kron(np.eye(heads), np.ones((1, P_SIZE))), bf16)
    table = jnp.asarray(sylvester(H_BLOCK), bf16)

    tail = pl.cdiv(2 * heads, LANES) * LANES
    message, cumul = pl.pallas_call(
        message_kernel,
        out_shape=(
            jax.ShapeDtypeStruct((tokens, width + states + tail), bf16),
            jax.ShapeDtypeStruct((tokens, heads), f32),
        ),
        compiler_params=PARAMS,
        name="message",
    )(x_in, b_group, step_size, log_decay, expand)
    arrived = [shift_up(message, "seq", k) for k in range(1, seq_count)]

    wide_skip = jnp.repeat(skip, P_SIZE)[None, :]
    own, far = pl.pallas_call(
        local_kernel,
        out_shape=(
            jax.ShapeDtypeStruct((tokens, width), f32),
            jax.ShapeDtypeStruct((tokens, width), f32),
        ),
        compiler_params=PARAMS,
        name="local",
    )(x_in, b_group, c_group, step_size, cumul, gate_in, wide_skip, expand)

    signed_gain = (jnp.where(walsh_sign == 1, 1.0, -1.0) * norm_gain)[None, :]
    mixed = pl.pallas_call(
        functools.partial(mix_kernel, len(arrived)),
        out_shape=jax.ShapeDtypeStruct((tokens, width), bf16),
        compiler_params=PARAMS,
        name="mix",
    )(*arrived, c_group, own, far, signed_gain, table, expand)

    for axis in ("sub", "chan"):
        here = lax.axis_index(axis)
        for bit in bits_of(axis):
            other = swap(mixed.astype(bf16), axis, bit).astype(f32)
            sign = 1.0 - 2.0 * (here // 2**bit % 2).astype(f32)
            mixed = mixed.astype(f32) * sign + other
    rotated = mixed * (1.0 / math.sqrt(LOCAL_HEADS * P_SIZE))
    quant = jnp.clip(
        rotated * power_two(channel_shift_power, 1)[None, :], -clip_level, clip_level
    ).astype(bf16)
    scaled = (quant.astype(f32) * power_two(channel_shift_power, -1)[None, :]).astype(bf16)

    chan_count, sub_count = lax.axis_size("chan"), lax.axis_size("sub")
    rows = tokens // (chan_count * sub_count)
    order = sorted(range(1, seq_count), key=lambda k: -min(k, seq_count - k))
    blocks = {0: scaled}
    for k in order:
        blocks[k] = turn(scaled, "seq", k)
    sums = []
    for k in [0] + order:
        partial = dot(blocks[k], out_weight).astype(bf16)
        partial = partial.reshape(chan_count, sub_count, rows, -1)
        partial = halve(jnp.swapaxes(partial, 0, 1), "sub")
        done = halve(partial, "chan")
        sums.append((k, turn(done, "seq", -k % seq_count) if k else done))
    pieces = [value for _, value in sorted(sums, key=lambda item: item[0])]
    stacked = jnp.stack(pieces + pieces, axis=0)
    here = lax.axis_index("seq")
    placed = lax.dynamic_slice_in_dim(
        stacked, (seq_count - here) % seq_count, seq_count, 0
    )
    return jnp.swapaxes(placed, 0, 1).reshape(rows, -1)


def solution(mesh):
    return jax.shard_map(
        body,
        mesh=mesh,
        in_specs=(
            P(("groups", "seq"), ("chan", "sub")),
            P(("groups", "seq"), "chan", None),
            P(("groups", "seq"), "chan", None),
            P(("groups", "seq"), ("chan", "sub")),
            P(("groups", "seq"), ("chan", "sub")),
            P(("chan", "sub")),
            P(("groups", "seq"), ("chan", "sub")),
            P(("chan", "sub")),
            P(("chan", "sub")),
            P(("chan", "sub")),
            P(("chan", "sub"), "seq"),
        ),
        out_specs=P(("groups", "seq", "chan", "sub"), None),
        check_vma=False,
    )
```

profile of v0, /device:TPU:0, one launch (start us, length us, event | category | flops | bytes accessed | tf_op | source)
XLA Modules:
  0.0 151.8 jit_solution(5445918408211509996)
XLA Ops:
  0.0 0.9 copy-done
  0.9 0.1 constant_dynamic-slice_fusion.1
  1.1 0.8 copy.22.step_ref
  1.9 0.8 copy.23.decay_ref
  2.7 1.0 copy-done.1
  3.7 0.9 copy-done.3
  4.7 0.6 message.1
  5.3 5.0 %collective-permute-start = (bf16[128,2432]{1,0:T(8,128)(2,1)S(1)}, bf16[128,2432]{1,0:T(8,128)(2,1)S(1)}, u32[]{:S(2)}, u32[]{:S(2)}) collective-permute-start(bf16[128,2432]{1,0:T(8,128)(2,1)S(1)} %get-tuple-element.9), channel_id=1, source_target_pairs={{0,4},{4,8},{8,12},{1,5},{5,9},{9,13},{2,6},{6,10},{10,14},{3,7},{... | collective-permute-start | bytes 1867784 | tf_op jit(solution)/shard_map/ppermute | solution.py:180
  10.3 4.5 %collective-permute-start.1 = (bf16[128,2432]{1,0:T(8,128)(2,1)S(1)}, bf16[128,2432]{1,0:T(8,128)(2,1)S(1)}, u32[]{:S(2)}, u32[]{:S(2)}) collective-permute-start(bf16[128,2432]{1,0:T(8,128)(2,1)S(1)} %get-tuple-element.9), channel_id=1, source_target_pairs={{0,8},{4,12},{1,9},{5,13},{2,10},{6,14},{3,11},{7,15},{16,24},{20,... | collective-permute-start | bytes 1867784 | tf_op jit(solution)/shard_map/ppermute | solution.py:180
  14.8 1.3 collective-permute-start.2
  16.1 1.0 constant_dynamic-slice_fusion
  17.2 0.7 broadcast_in_dim.52
  18.0 1.0 copy-done.2
  19.0 0.9 copy-done.4
  20.0 1.0 copy-done.6
  21.0 1.5 local.1
  22.5 0.7 select_multiply_fusion
  23.2 1.5 collective-permute-done.refs_0_
  24.7 13.4 %collective-permute-done.1.refs_1_ = bf16[128,2432]{1,0:T(8,128)(2,1)S(1)} collective-permute-done((bf16[128,2432]{1,0:T(8,128)(2,1)S(1)}, bf16[128,2432]{1,0:T(8,128)(2,1)S(1)}, u32[]{:S(2)}, u32[]{:S(2)}) %collective-permute-start.1) | collective-permute-done | bytes 622624 | tf_op jit(solution)/shard_map/ppermute | solution.py:180
  38.0 12.2 %collective-permute-done.2.refs_2_ = bf16[128,2432]{1,0:T(8,128)(2,1)S(1)} collective-permute-done((bf16[128,2432]{1,0:T(8,128)(2,1)S(1)}, bf16[128,2432]{1,0:T(8,128)(2,1)S(1)}, u32[]{:S(2)}, u32[]{:S(2)}) %collective-permute-start.2) | collective-permute-done | bytes 622624 | tf_op jit(solution)/shard_map/ppermute | solution.py:180
  50.2 0.9 copy-done.5
  51.1 0.9 copy-done.7
  52.0 1.4 mix.1
  53.6 1.9 %collective-permute-done.3 = bf16[128,2048]{1,0:T(8,128)(2,1)S(1)} collective-permute-done((bf16[128,2048]{1,0:T(8,128)(2,1)S(1)}, bf16[128,2048]{1,0:T(8,128)(2,1)S(1)}, u32[]{:S(2)}, u32[]{:S(2)}) %collective-permute-start.3) | collective-permute-done | bytes 524320 | tf_op jit(solution)/shard_map/ppermute | solution.py:190
  55.5 0.2 fusion
  55.6 1.6 %collective-permute-start.4 = (bf16[128,2048]{1,0:T(8,128)(2,1)S(1)}, bf16[128,2048]{1,0:T(8,128)(2,1)S(1)}, u32[]{:S(2)}, u32[]{:S(2)}) collective-permute-start(bf16[128,2048]{1,0:T(8,128)(2,1)S(1)} %fusion), channel_id=1, source_target_pairs={{0,2},{2,0},{1,3},{3,1},{4,6},{6,4},{5,7},{7,5},{8,10},{10,8},{9,1... | collective-permute-start | bytes 1572872 | tf_op jit(solution)/shard_map/ppermute | solution.py:190
  57.2 12.4 %collective-permute-done.4 = bf16[128,2048]{1,0:T(8,128)(2,1)S(1)} collective-permute-done((bf16[128,2048]{1,0:T(8,128)(2,1)S(1)}, bf16[128,2048]{1,0:T(8,128)(2,1)S(1)}, u32[]{:S(2)}, u32[]{:S(2)}) %collective-permute-start.4) | collective-permute-done | bytes 524320 | tf_op jit(solution)/shard_map/ppermute | solution.py:190
  69.7 0.4 multiply_convert_fusion
  70.0 2.9 %convolution_convert_fusion.3 = bf16[128,1024]{1,0:T(8,128)(2,1)S(1)} fusion(bf16[128,2048]{1,0:T(8,128)(2,1)S(1)} %multiply_convert_fusion, bf16[2048,1024]{1,0:T(8,128)(2,1)} %param.23), kind=kOutput, calls=%fused_computation.3 | convolution fusion | flops 537001984 | bytes 4980736 | tf_op jit(solution)/shard_map/dot_general | solution.py:38
  73.1 14.9 %collective-permute-start.7 = (bf16[128,2048]{1,0:T(8,128)(2,1)S(1)}, bf16[128,2048]{1,0:T(8,128)(2,1)S(1)}, u32[]{:S(2)}, u32[]{:S(2)}) collective-permute-start(bf16[128,2048]{1,0:T(8,128)(2,1)S(1)} %multiply_convert_fusion), channel_id=1, source_target_pairs={{0,4},{4,8},{8,12},{12,0},{1,5},{5,9},{9,13},{13,1},{2,6},{6,10},{... | collective-permute-start | bytes 1572872 | tf_op jit(solution)/shard_map/ppermute | solution.py:185
  88.0 1.6 %collective-permute-start.6 = (bf16[1,32,1024]{2,1,0:T(8,128)(2,1)S(1)}, bf16[1,32,1024]{2,1,0:T(8,128)(2,1)S(1)}, u32[]{:S(2)}, u32[]{:S(2)}) collective-permute-start(bf16[1,32,1024]{2,1,0:T(8,128)(2,1)S(1)} %dynamic-slice_bitcast_fusion.8), channel_id=1, source_target_pairs={{0,2},{2,0},{1,3},{3,1},{4,6},{6,4},{5,7},{7,5},{8,10},{10,8},{9,1... | collective-permute-start | bytes 196616 | tf_op jit(solution)/shard_map/ppermute | solution.py:190
  89.6 3.4 %collective-permute-start.11 = (bf16[128,2048]{1,0:T(8,128)(2,1)S(1)}, bf16[128,2048]{1,0:T(8,128)(2,1)S(1)}, u32[]{:S(2)}, u32[]{:S(2)}) collective-permute-start(bf16[128,2048]{1,0:T(8,128)(2,1)S(1)} %multiply_convert_fusion), channel_id=1, source_target_pairs={{0,8},{4,12},{8,0},{12,4},{1,9},{5,13},{9,1},{13,5},{2,10},{6,14},... | collective-permute-start | bytes 1572872 | tf_op jit(solution)/shard_map/ppermute | solution.py:185
  93.0 0.7 collective-permute-start.15
  93.7 10.0 %collective-permute-done.7 = bf16[128,2048]{1,0:T(8,128)(2,1)S(1)} collective-permute-done((bf16[128,2048]{1,0:T(8,128)(2,1)S(1)}, bf16[128,2048]{1,0:T(8,128)(2,1)S(1)}, u32[]{:S(2)}, u32[]{:S(2)}) %collective-permute-start.7) | collective-permute-done | bytes 524320 | tf_op jit(solution)/shard_map/ppermute | solution.py:185
  103.7 2.9 %convolution_convert_fusion.2 = bf16[128,1024]{1,0:T(8,128)(2,1)S(1)} fusion(bf16[128,2048]{1,0:T(8,128)(2,1)S(1)} %collective-permute-done.7, bf16[2048,1024]{1,0:T(8,128)(2,1)} %param.23), kind=kOutput, calls=%fused_computation.2 | convolution fusion | flops 537001984 | bytes 4980736 | tf_op jit(solution)/shard_map/dot_general | solution.py:38
  106.7 19.2 %collective-permute-done.11 = bf16[128,2048]{1,0:T(8,128)(2,1)S(1)} collective-permute-done((bf16[128,2048]{1,0:T(8,128)(2,1)S(1)}, bf16[128,2048]{1,0:T(8,128)(2,1)S(1)}, u32[]{:S(2)}, u32[]{:S(2)}) %collective-permute-start.11) | collective-permute-done | bytes 524320 | tf_op jit(solution)/shard_map/ppermute | solution.py:185
  125.9 0.7 convolution_convert_fusion.1
  126.8 0.7 convolution_convert_fusion
  127.5 0.6 collective-permute-start.16
  128.1 1.6 %collective-permute-start.9 = (bf16[1,32,1024]{2,1,0:T(8,128)(2,1)S(1)}, bf16[1,32,1024]{2,1,0:T(8,128)(2,1)S(1)}, u32[]{:S(2)}, u32[]{:S(2)}) collective-permute-start(bf16[1,32,1024]{2,1,0:T(8,128)(2,1)S(1)} %dynamic-slice_bitcast_fusion.7), channel_id=1, source_target_pairs={{0,2},{2,0},{1,3},{3,1},{4,6},{6,4},{5,7},{7,5},{8,10},{10,8},{9,1... | collective-permute-start | bytes 196616 | tf_op jit(solution)/shard_map/ppermute | solution.py:190
  129.8 0.6 collective-permute-start.13
  130.4 1.6 %collective-permute-start.17 = (bf16[1,32,1024]{2,1,0:T(8,128)(2,1)S(1)}, bf16[1,32,1024]{2,1,0:T(8,128)(2,1)S(1)}, u32[]{:S(2)}, u32[]{:S(2)}) collective-permute-start(bf16[1,32,1024]{2,1,0:T(8,128)(2,1)S(1)} %dynamic-slice_bitcast_fusion.5), channel_id=1, source_target_pairs={{0,2},{2,0},{1,3},{3,1},{4,6},{6,4},{5,7},{7,5},{8,10},{10,8},{9,1... | collective-permute-start | bytes 196616 | tf_op jit(solution)/shard_map/ppermute | solution.py:190
  132.0 0.9 collective-permute-done.9
  132.9 10.7 %collective-permute-start.10 = (bf16[32,1024]{1,0:T(8,128)(2,1)S(1)}, bf16[32,1024]{1,0:T(8,128)(2,1)S(1)}, u32[]{:S(2)}, u32[]{:S(2)}) collective-permute-start(bf16[32,1024]{1,0:T(8,128)(2,1)S(1)} %fusion.9), channel_id=1, source_target_pairs={{0,12},{4,0},{8,4},{12,8},{1,13},{5,1},{9,5},{13,9},{2,14},{6,2},{... | collective-permute-start | bytes 196616 | tf_op jit(solution)/shard_map/ppermute | solution.py:185
  143.6 1.2 collective-permute-start.14
  144.8 1.1 collective-permute-start.18
  146.0 5.0 %collective-permute-done.14 = bf16[32,1024]{1,0:T(8,128)(2,1)S(1)} collective-permute-done((bf16[32,1024]{1,0:T(8,128)(2,1)S(1)}, bf16[32,1024]{1,0:T(8,128)(2,1)S(1)}, u32[]{:S(2)}, u32[]{:S(2)}) %collective-permute-start.14) | collective-permute-done | bytes 65568 | tf_op jit(solution)/shard_map/ppermute | solution.py:185
  151.1 0.7 copy.35
  (55 shorter events, 0.9 us)
Async XLA Ops:
  0.0 0.9 copy-start
  2.7 1.0 copy-start.1
  3.7 0.9 copy-start.3
  5.3 51.9 %copy-start.9 = (s32[2048]{0:T(1024)S(1)}, s32[2048]{0:T(1024)}, u32[]{:S(2)}) copy-start(s32[2048]{0:T(1024)} %param.22) | copy-start | bytes 24580
  5.3 19.4 %collective-permute-start = (bf16[128,2432]{1,0:T(8,128)(2,1)S(1)}, bf16[128,2432]{1,0:T(8,128)(2,1)S(1)}, u32[]{:S(2)}, u32[]{:S(2)}) collective-permute-start(bf16[128,2432]{1,0:T(8,128)(2,1)S(1)} %get-tuple-element.9), channel_id=1, source_target_pairs={{0,4},{4,8},{8,12},{1,5},{5,9},{9,13},{2,6},{6,10},{10,14},{3,7},{... | collective-permute-start | bytes 1867784 | tf_op jit(solution)/shard_map/ppermute | solution.py:180
  10.3 27.8 %collective-permute-start.1 = (bf16[128,2432]{1,0:T(8,128)(2,1)S(1)}, bf16[128,2432]{1,0:T(8,128)(2,1)S(1)}, u32[]{:S(2)}, u32[]{:S(2)}) collective-permute-start(bf16[128,2432]{1,0:T(8,128)(2,1)S(1)} %get-tuple-element.9), channel_id=1, source_target_pairs={{0,8},{4,12},{1,9},{5,13},{2,10},{6,14},{3,11},{7,15},{16,24},{20,... | collective-permute-start | bytes 1867784 | tf_op jit(solution)/shard_map/ppermute | solution.py:180
  14.8 35.5 %collective-permute-start.2 = (bf16[128,2432]{1,0:T(8,128)(2,1)S(1)}, bf16[128,2432]{1,0:T(8,128)(2,1)S(1)}, u32[]{:S(2)}, u32[]{:S(2)}) collective-permute-start(bf16[128,2432]{1,0:T(8,128)(2,1)S(1)} %get-tuple-element.9), channel_id=1, source_target_pairs={{0,12},{1,13},{2,14},{3,15},{16,28},{17,29},{18,30},{19,31}} | collective-permute-start | bytes 1867784 | tf_op jit(solution)/shard_map/ppermute | solution.py:180
  18.0 1.0 copy-start.2
  19.0 0.9 copy-start.4
  20.0 1.0 copy-start.6
  50.2 0.9 copy-start.5
  51.1 0.9 copy-start.7
  53.5 2.0 %collective-permute-start.3 = (bf16[128,2048]{1,0:T(8,128)(2,1)S(1)}, bf16[128,2048]{1,0:T(8,128)(2,1)S(1)}, u32[]{:S(2)}, u32[]{:S(2)}) collective-permute-start(bf16[128,2048]{1,0:T(8,128)(2,1)S(1)} %mix.1), channel_id=1, source_target_pairs={{0,1},{1,0},{2,3},{3,2},{4,5},{5,4},{6,7},{7,6},{8,9},{9,8},{10,11... | collective-permute-start | bytes 1572872 | tf_op jit(solution)/shard_map/ppermute | solution.py:190
  55.6 14.0 %collective-permute-start.4 = (bf16[128,2048]{1,0:T(8,128)(2,1)S(1)}, bf16[128,2048]{1,0:T(8,128)(2,1)S(1)}, u32[]{:S(2)}, u32[]{:S(2)}) collective-permute-start(bf16[128,2048]{1,0:T(8,128)(2,1)S(1)} %fusion), channel_id=1, source_target_pairs={{0,2},{2,0},{1,3},{3,1},{4,6},{6,4},{5,7},{7,5},{8,10},{10,8},{9,1... | collective-permute-start | bytes 1572872 | tf_op jit(solution)/shard_map/ppermute | solution.py:190
  73.0 15.0 %collective-permute-start.5 = (bf16[1,2,32,1024]{3,2,1,0:T(8,128)(2,1)S(1)}, bf16[1,2,32,1024]{3,2,1,0:T(8,128)(2,1)S(1)}, u32[]{:S(2)}, u32[]{:S(2)}) collective-permute-start(bf16[1,2,32,1024]{3,2,1,0:T(8,128)(2,1)S(1)} %dynamic-slice_bitcast_fusion.4), channel_id=1, source_target_pairs={{0,1},{1,0},{2,3},{3,2},{4,5},{5,4},{6,7},{7,6},{8,9},{9,8},{10,11... | collective-permute-start | bytes 393224 | tf_op jit(solution)/shard_map/ppermute | solution.py:190
  73.1 30.7 %collective-permute-start.7 = (bf16[128,2048]{1,0:T(8,128)(2,1)S(1)}, bf16[128,2048]{1,0:T(8,128)(2,1)S(1)}, u32[]{:S(2)}, u32[]{:S(2)}) collective-permute-start(bf16[128,2048]{1,0:T(8,128)(2,1)S(1)} %multiply_convert_fusion), channel_id=1, source_target_pairs={{0,4},{4,8},{8,12},{12,0},{1,5},{5,9},{9,13},{13,1},{2,6},{6,10},{... | collective-permute-start | bytes 1572872 | tf_op jit(solution)/shard_map/ppermute | solution.py:185
  88.0 5.6 %collective-permute-start.6 = (bf16[1,32,1024]{2,1,0:T(8,128)(2,1)S(1)}, bf16[1,32,1024]{2,1,0:T(8,128)(2,1)S(1)}, u32[]{:S(2)}, u32[]{:S(2)}) collective-permute-start(bf16[1,32,1024]{2,1,0:T(8,128)(2,1)S(1)} %dynamic-slice_bitcast_fusion.8), channel_id=1, source_target_pairs={{0,2},{2,0},{1,3},{3,1},{4,6},{6,4},{5,7},{7,5},{8,10},{10,8},{9,1... | collective-permute-start | bytes 196616 | tf_op jit(solution)/shard_map/ppermute | solution.py:190
  89.6 36.3 %copy-start.8 = (bf16[2048,1024]{1,0:T(8,128)(2,1)S(1)}, bf16[2048,1024]{1,0:T(8,128)(2,1)}, u32[]{:S(2)}) copy-start(bf16[2048,1024]{1,0:T(8,128)(2,1)} %param.23) | copy-start | bytes 12582916
  89.6 36.3 %collective-permute-start.11 = (bf16[128,2048]{1,0:T(8,128)(2,1)S(1)}, bf16[128,2048]{1,0:T(8,128)(2,1)S(1)}, u32[]{:S(2)}, u32[]{:S(2)}) collective-permute-start(bf16[128,2048]{1,0:T(8,128)(2,1)S(1)} %multiply_convert_fusion), channel_id=1, source_target_pairs={{0,8},{4,12},{8,0},{12,4},{1,9},{5,13},{9,1},{13,5},{2,10},{6,14},... | collective-permute-start | bytes 1572872 | tf_op jit(solution)/shard_map/ppermute | solution.py:185
  93.0 33.8 %collective-permute-start.15 = (bf16[128,2048]{1,0:T(8,128)(2,1)S(1)}, bf16[128,2048]{1,0:T(8,128)(2,1)S(1)}, u32[]{:S(2)}, u32[]{:S(2)}) collective-permute-start(bf16[128,2048]{1,0:T(8,128)(2,1)S(1)} %multiply_convert_fusion), channel_id=1, source_target_pairs={{0,12},{4,0},{8,4},{12,8},{1,13},{5,1},{9,5},{13,9},{2,14},{6,2},{... | collective-permute-start | bytes 1572872 | tf_op jit(solution)/shard_map/ppermute | solution.py:185
  106.7 21.4 %collective-permute-start.8 = (bf16[1,2,32,1024]{3,2,1,0:T(8,128)(2,1)S(1)}, bf16[1,2,32,1024]{3,2,1,0:T(8,128)(2,1)S(1)}, u32[]{:S(2)}, u32[]{:S(2)}) collective-permute-start(bf16[1,2,32,1024]{3,2,1,0:T(8,128)(2,1)S(1)} %dynamic-slice_bitcast_fusion.3), channel_id=1, source_target_pairs={{0,1},{1,0},{2,3},{3,2},{4,5},{5,4},{6,7},{7,6},{8,9},{9,8},{10,11... | collective-permute-start | bytes 393224 | tf_op jit(solution)/shard_map/ppermute | solution.py:190
  126.7 3.0 %collective-permute-start.12 = (bf16[1,2,32,1024]{3,2,1,0:T(8,128)(2,1)S(1)}, bf16[1,2,32,1024]{3,2,1,0:T(8,128)(2,1)S(1)}, u32[]{:S(2)}, u32[]{:S(2)}) collective-permute-start(bf16[1,2,32,1024]{3,2,1,0:T(8,128)(2,1)S(1)} %dynamic-slice_bitcast_fusion.2), channel_id=1, source_target_pairs={{0,1},{1,0},{2,3},{3,2},{4,5},{5,4},{6,7},{7,6},{8,9},{9,8},{10,11... | collective-permute-start | bytes 393224 | tf_op jit(solution)/shard_map/ppermute | solution.py:190
  127.5 2.8 %collective-permute-start.16 = (bf16[1,2,32,1024]{3,2,1,0:T(8,128)(2,1)S(1)}, bf16[1,2,32,1024]{3,2,1,0:T(8,128)(2,1)S(1)}, u32[]{:S(2)}, u32[]{:S(2)}) collective-permute-start(bf16[1,2,32,1024]{3,2,1,0:T(8,128)(2,1)S(1)} %dynamic-slice_bitcast_fusion.1), channel_id=1, source_target_pairs={{0,1},{1,0},{2,3},{3,2},{4,5},{5,4},{6,7},{7,6},{8,9},{9,8},{10,11... | collective-permute-start | bytes 393224 | tf_op jit(solution)/shard_map/ppermute | solution.py:190
  128.1 4.7 %collective-permute-start.9 = (bf16[1,32,1024]{2,1,0:T(8,128)(2,1)S(1)}, bf16[1,32,1024]{2,1,0:T(8,128)(2,1)S(1)}, u32[]{:S(2)}, u32[]{:S(2)}) collective-permute-start(bf16[1,32,1024]{2,1,0:T(8,128)(2,1)S(1)} %dynamic-slice_bitcast_fusion.7), channel_id=1, source_target_pairs={{0,2},{2,0},{1,3},{3,1},{4,6},{6,4},{5,7},{7,5},{8,10},{10,8},{9,1... | collective-permute-start | bytes 196616 | tf_op jit(solution)/shard_map/ppermute | solution.py:190
  129.8 13.8 %collective-permute-start.13 = (bf16[1,32,1024]{2,1,0:T(8,128)(2,1)S(1)}, bf16[1,32,1024]{2,1,0:T(8,128)(2,1)S(1)}, u32[]{:S(2)}, u32[]{:S(2)}) collective-permute-start(bf16[1,32,1024]{2,1,0:T(8,128)(2,1)S(1)} %dynamic-slice_bitcast_fusion.6), channel_id=1, source_target_pairs={{0,2},{2,0},{1,3},{3,1},{4,6},{6,4},{5,7},{7,5},{8,10},{10,8},{9,1... | collective-permute-start | bytes 196616 | tf_op jit(solution)/shard_map/ppermute | solution.py:190
  130.4 14.4 %collective-permute-start.17 = (bf16[1,32,1024]{2,1,0:T(8,128)(2,1)S(1)}, bf16[1,32,1024]{2,1,0:T(8,128)(2,1)S(1)}, u32[]{:S(2)}, u32[]{:S(2)}) collective-permute-start(bf16[1,32,1024]{2,1,0:T(8,128)(2,1)S(1)} %dynamic-slice_bitcast_fusion.5), channel_id=1, source_target_pairs={{0,2},{2,0},{1,3},{3,1},{4,6},{6,4},{5,7},{7,5},{8,10},{10,8},{9,1... | collective-permute-start | bytes 196616 | tf_op jit(solution)/shard_map/ppermute | solution.py:190
  132.9 13.1 %collective-permute-start.10 = (bf16[32,1024]{1,0:T(8,128)(2,1)S(1)}, bf16[32,1024]{1,0:T(8,128)(2,1)S(1)}, u32[]{:S(2)}, u32[]{:S(2)}) collective-permute-start(bf16[32,1024]{1,0:T(8,128)(2,1)S(1)} %fusion.9), channel_id=1, source_target_pairs={{0,12},{4,0},{8,4},{12,8},{1,13},{5,1},{9,5},{13,9},{2,14},{6,2},{... | collective-permute-start | bytes 196616 | tf_op jit(solution)/shard_map/ppermute | solution.py:185
  143.6 7.3 %collective-permute-start.14 = (bf16[32,1024]{1,0:T(8,128)(2,1)S(1)}, bf16[32,1024]{1,0:T(8,128)(2,1)S(1)}, u32[]{:S(2)}, u32[]{:S(2)}) collective-permute-start(bf16[32,1024]{1,0:T(8,128)(2,1)S(1)} %fusion.10), channel_id=1, source_target_pairs={{0,8},{4,12},{8,0},{12,4},{1,9},{5,13},{9,1},{13,5},{2,10},{6,14},... | collective-permute-start | bytes 196616 | tf_op jit(solution)/shard_map/ppermute | solution.py:185
  144.8 6.1 %collective-permute-start.18 = (bf16[32,1024]{1,0:T(8,128)(2,1)S(1)}, bf16[32,1024]{1,0:T(8,128)(2,1)S(1)}, u32[]{:S(2)}, u32[]{:S(2)}) collective-permute-start(bf16[32,1024]{1,0:T(8,128)(2,1)S(1)} %fusion.11), channel_id=1, source_target_pairs={{0,4},{4,8},{8,12},{12,0},{1,5},{5,9},{9,13},{13,1},{2,6},{6,10},{... | collective-permute-start | bytes 196616 | tf_op jit(solution)/shard_map/ppermute | solution.py:185
where the time goes:
time: 152 us
  waiting for transfers between devices  76.4 us (50%)
  starting transfers between devices  50.5 us (33%)
  local copies, waits for them, and re-layouts  12.2 us (8%)
  matrix products  7.26 us (5%)
  Pallas kernels  3.53 us (2%)
    ppermute x6, waiting for transfers between devices, turn(): lax.ppermute(value, axis, [(k, (k + distance) % count) for k in range(cou...  34.1 us
    ppermute x6, starting transfers between devices, turn(): lax.ppermute(value, axis, [(k, (k + distance) % count) for k in range(cou...  32.1 us
    ppermute x3, waiting for transfers between devices, shift_up(): lax.ppermute(value, axis, [(k, k + distance) for k in range(count - dista...  27.1 us
    ppermute x10, waiting for transfers between devices, swap(): return lax.ppermute(value, axis, [(k, k ^ 1 << bit) for k in range(count)])  15.2 us
    ppermute x3, starting transfers between devices, shift_up(): lax.ppermute(value, axis, [(k, k + distance) for k in range(count - dista...  10.8 us
    unnamed x30, local copies, waits for them, and re-layouts  9.36 us
    ppermute x10, starting transfers between devices, swap(): return lax.ppermute(value, axis, [(k, k ^ 1 << bit) for k in range(count)])  7.69 us
    dot_general x4, matrix products, dot(): return jnp.dot(a, b, preferred_element_type=f32)  7.26 us
  transfers between devices with their start and end apart: 19, of which 9 were waited for; matrix products, arithmetic and copies ran while one was open for 5% of the time, Pallas kernels for 1%

commit v1 on v0

--- a/solution.py
+++ b/solution.py
@@ -157,6 +157,213 @@
             at = slice(start + index * H_BLOCK, start + (index + 1) * H_BLOCK)
             signed = (pre * inverse * gain_ref[:, at]).astype(bf16)
             parts.append(dot(signed, table))
+    butterflies(parts)
+    for index, part in enumerate(parts):
+        out_ref[:, index * H_BLOCK : (index + 1) * H_BLOCK] = part.astype(bf16)
+
+
+def half_at(which, size):
+    return pl.ds(pl.multiple_of(which * size, size), size)
+
+
+def pack_kernel(
+    where_ref,
+    x_ref,
+    gate_ref,
+    b_ref,
+    c_ref,
+    step_ref,
+    decay_ref,
+    expand_ref,
+    pair_ref,
+    straight_ref,
+    cross_ref,
+):
+    tokens, width = x_ref.shape
+    half, heads, states = width // 2, step_ref.shape[1] // 2, b_ref.shape[1]
+    member = where_ref[0]
+    step = step_ref[...]
+    decay = decay_ref[...]
+    triangle = causal_mask(tokens).astype(f32).astype(bf16)
+    cumul = exact_dot(triangle, decay)
+    total = cumul[tokens - 1 : tokens, :]
+    scale = jnp.exp(total - cumul) * step
+    kept = jnp.exp(total)
+
+    def pick(value, which):
+        return jnp.where(which == 0, value[:, :heads], value[:, heads:])
+
+    other = 1 - member
+    pair_ref[:, :half] = x_ref[:, half_at(other, half)]
+    pair_ref[:, half : 2 * half] = gate_ref[:, half_at(other, half)]
+    pair_ref[:, 2 * half : 2 * half + states] = b_ref[...]
+    base = 2 * half + 2 * states
+    pair_ref[:, 2 * half + states : base] = c_ref[...]
+    pair_ref[:, base:] = jnp.zeros((tokens, pair_ref.shape[1] - base), bf16)
+    terms = parts_of(pick(step, other), 3) + parts_of(pick(decay, other), 3)
+    for index, term in enumerate(terms):
+        pair_ref[:, base + index * heads : base + (index + 1) * heads] = term
+
+    base = half + states
+    for out_ref, which in ((straight_ref, member), (cross_ref, other)):
+        wide = spread(pick(scale, which), expand_ref[...])
+        out_ref[:, :half] = (x_ref[:, half_at(which, half)].astype(f32) * wide).astype(bf16)
+        out_ref[:, half:base] = b_ref[...]
+        out_ref[:, base:] = jnp.zeros((tokens, out_ref.shape[1] - base), bf16)
+        for index, term in enumerate(parts_of(pick(kept, which), 2)):
+            out_ref[:, base + index * heads : base + (index + 1) * heads] = jnp.broadcast_to(
+                term, (tokens, heads)
+            )
+
+
+def pair_kernel(
+    where_ref,
+    x_ref,
+    gate_ref,
+    b_ref,
+    c_ref,
+    step_ref,
+    decay_ref,
+    msg_ref,
+    skip_ref,
+    expand_ref,
+    own_ref,
+    far_ref,
+    c_pair_ref,
+    x_both,
+    gate_both,
+    b_both,
+    step_both,
+    decay_both,
+):
+    tokens, width = x_ref.shape
+    half, heads, states = width // 2, step_ref.shape[1] // 2, b_ref.shape[1]
+    member = where_ref[0]
+    mine, theirs = half_at(member, tokens), half_at(1 - member, tokens)
+
+    def pick(value):
+        return jnp.where(member == 0, value[:, :heads], value[:, heads:])
+
+    x_both[mine, :] = x_ref[:, half_at(member, half)]
+    x_both[theirs, :] = msg_ref[:, :half]
+    gate_both[mine, :] = gate_ref[:, half_at(member, half)]
+    gate_both[theirs, :] = msg_ref[:, half : 2 * half]
+    b_both[mine, :] = b_ref[...]
+    b_both[theirs, :] = msg_ref[:, 2 * half : 2 * half + states]
+    base = 2 * half + 2 * states
+    c_pair_ref[mine, :] = c_ref[...]
+    c_pair_ref[theirs, :] = msg_ref[:, 2 * half + states : base]
+
+    def received(first):
+        terms = [
+            msg_ref[:, base + index * heads : base + (index + 1) * heads].astype(f32)
+            for index in range(first, first + 3)
+        ]
+        return (terms[2] + terms[1]) + terms[0]
+
+    step_both[mine, :] = pick(step_ref[...])
+    step_both[theirs, :] = received(0)
+    decay_both[mine, :] = pick(decay_ref[...])
+    decay_both[theirs, :] = received(3)
+
+    span = 2 * tokens
+    causal = causal_mask(span)
+    inner = jnp.where(causal, dot_nt(c_pair_ref[...], b_both[...]), 0.0)
+    cumul = exact_dot(causal.astype(f32).astype(bf16), decay_both[...])
+    cumul_t = cumul.T
+    step_t = step_both[...].T
+    skip = skip_ref[:, half_at(member, half)]
+    reach = parts_of(jnp.exp(cumul), 2)
+    first = lax.broadcasted_iota(jnp.int32, (tokens, 2 * P_SIZE), 1) < P_SIZE
+    for pair in range(heads // 2):
+        at = slice(pair * 2 * P_SIZE, (pair + 1) * 2 * P_SIZE)
+        spans = []
+        for block in range(2):
+            x_block = x_both[block * tokens : (block + 1) * tokens, at]
+            zero = jnp.zeros_like(x_block)
+            spans.append((jnp.where(first, x_block, zero), jnp.where(first, zero, x_block)))
+        for block in range(2):
+            rows = slice(block * tokens, (block + 1) * tokens)
+            mixings, values = [], []
+            for place, head in enumerate((2 * pair, 2 * pair + 1)):
+                for earlier in range(block + 1):
+                    cols = slice(earlier * tokens, (earlier + 1) * tokens)
+                    differ = cumul[rows, head : head + 1] - cumul_t[head : head + 1, cols]
+                    if earlier == block:
+                        differ = jnp.where(causal[:tokens, :tokens], differ, 0.0)
+                    ratio = jnp.exp(differ)
+                    mixings.append(
+                        (ratio * (inner[rows, cols] * step_t[head : head + 1, cols])).astype(bf16)
+                    )
+                    values.append(spans[earlier][place])
+            own = dot(jnp.concatenate(mixings, axis=1), jnp.concatenate(values, axis=0))
+            own = own + x_both[rows, at].astype(f32) * skip[:, at]
+            gate = gate_both[rows, at].astype(f32)
+            gate = gate / (1.0 + jnp.exp(-gate))
+            own_ref[rows, at] = own * gate
+            wide = sum(dot(term[rows, :], expand_ref[:, at]) for term in reach)
+            far_ref[rows, at] = wide * gate
+
+
+def gate_mix_kernel(count, pieces, *refs):
+    straight, cross = refs[:count], refs[count : 2 * count]
+    where_ref, c_ref, own_ref, far_ref, gain_ref, table_ref, expand_ref = refs[2 * count : -2]
+    out_refs = refs[-2:]
+    span, half = own_ref.shape
+    states = c_ref.shape[1]
+    heads = expand_ref.shape[0]
+    base = half + states
+    member = where_ref[0]
+    c_pair = c_ref[...]
+
+    def kept(msg_ref):
+        return (
+            dot(msg_ref[:16, base : base + heads], expand_ref[...])
+            + dot(msg_ref[:16, base + heads : base + 2 * heads], expand_ref[...])
+        )[:1, :]
+
+    inners, factors, pair_kept = [], [], []
+    for straight_ref, cross_ref in zip(straight, cross):
+        inners.append(
+            [dot_nt(c_pair, ref[:, half:base]).astype(bf16) for ref in (straight_ref, cross_ref)]
+        )
+        one, two = kept(straight_ref), kept(cross_ref)
+        pair_kept.append(one * two)
+        factors.append((jnp.where(member == 0, two, 1.0), jnp.where(member == 0, 1.0, one)))
+    gain = gain_ref[:, half_at(member, half)]
+    table = table_ref[...]
+    parts = []
+    norm_width = NORM_HEADS * P_SIZE
+    for start in range(0, half, norm_width):
+        pres = []
+        square = jnp.zeros((span, 1), f32)
+        for begin in range(start, start + norm_width, H_BLOCK):
+            at = slice(begin, begin + H_BLOCK)
+            pre = own_ref[:, at]
+            carried = None
+            for k in reversed(range(count)):
+                term = factors[k][0][:, at] * dot(inners[k][0], straight[k][:, at])
+                term = term + factors[k][1][:, at] * dot(inners[k][1], cross[k][:, at])
+                carried = term if carried is None else term + pair_kept[k][:, at] * carried
+            if carried is not None:
+                pre = pre + far_ref[:, at] * carried
+            square = square + jnp.sum(pre * pre, axis=1, keepdims=True)
+            pres.append(pre)
+        inverse = lax.rsqrt(square * (1.0 / norm_width) + norm_eps)
+        for index, pre in enumerate(pres):
+            at = slice(start + index * H_BLOCK, start + (index + 1) * H_BLOCK)
+            parts.append(dot((pre * inverse * gain[:, at]).astype(bf16), table))
+    butterflies(parts)
+    size = span // pieces
+    for index, part in enumerate(parts):
+        at = slice(index * H_BLOCK, (index + 1) * H_BLOCK)
+        part = part.astype(bf16)
+        for piece in range(pieces):
+            to = slice(piece // 2 * size, (piece // 2 + 1) * size)
+            out_refs[piece % 2][to, at] = part[piece * size : (piece + 1) * size, :]
+
+
+def butterflies(parts):
     span = 1
     while span < len(parts):
         for low in range(len(parts)):
@@ -164,8 +371,40 @@
                 a, b = parts[low], parts[low + span]
                 parts[low], parts[low + span] = a + b, a - b
         span *= 2
-    for index, part in enumerate(parts):
-        out_ref[:, index * H_BLOCK : (index + 1) * H_BLOCK] = part.astype(bf16)
+
+
+def project_kernel(pairs, where_ref, *refs):
+    pieces = refs[: 2 * pairs]
+    up_ref, down_ref, weight_ref, out_ref = refs[2 * pairs :]
+    half = pieces[0].shape[1]
+    sign = (1 - 2 * where_ref[0]).astype(f32)
+    sub_count, chan_count, _, blocks, size, features = out_ref.shape
+    for pair in range(pairs):
+        one = pieces[2 * pair][...].astype(f32)
+        two = pieces[2 * pair + 1][...].astype(f32)
+        total = None
+        for side, mixed in enumerate((one + two, (one - two) * sign)):
+            at = slice(side * half, (side + 1) * half)
+            quant = jnp.clip(mixed * up_ref[:, at], -clip_level, clip_level).astype(bf16)
+            scaled = (quant.astype(f32) * down_ref[:, at]).astype(bf16)
+            term = dot(scaled, weight_ref[at, :])
+            total = term if total is None else total + term
+        total = total.astype(bf16)
+        row = 0
+        for block in range(blocks):
+            for chan in range(chan_count):
+                for sub in range(sub_count):
+                    out_ref[sub, chan, pair, block] = total[row : row + size, :]
+                    row += size
+
+
+def place_kernel(count, where_ref, *refs):
+    out_ref = refs[-1]
+    size, features = refs[0].shape
+    for index, ref in enumerate(refs[:-1]):
+        group, distance = index // count, index % count
+        at = half_at(where_ref[0] ^ distance, features)
+        out_ref[group * size : (group + 1) * size, at] = ref[...]
 
 
 def sylvester(order):
@@ -205,7 +444,159 @@
     return value[0]
 
 
-def body(
+def call(kernel, out_shape, name, args, scalars=0, scratch=()):
+    specs = [pl.BlockSpec(memory_space=pltpu.SMEM)] * scalars
+    specs += [pl.BlockSpec(memory_space=pltpu.VMEM)] * (len(args) - scalars)
+    return pl.pallas_call(
+        kernel,
+        out_shape=out_shape,
+        in_specs=specs,
+        scratch_shapes=scratch,
+        compiler_params=PARAMS,
+        name=name,
+    )(*args)
+
+
+def swap_seq(value, distance):
+    count = lax.axis_size("seq")
+    return lax.ppermute(value, "seq", [(k, k ^ distance) for k in range(count)])
+
+
+def paired_body(
+    x_in,
+    b_in,
+    c_in,
+    step_size,
+    log_decay,
+    skip,
+    gate_in,
+    norm_gain,
+    walsh_sign,
+    channel_shift_power,
+    out_weight,
+):
+    tokens, width = x_in.shape
+    heads = step_size.shape[1]
+    states = b_in.shape[2]
+    half, half_heads = width // 2, heads // 2
+    seq_count, chan_count, sub_count = (lax.axis_size(a) for a in ("seq", "chan", "sub"))
+    pairs = seq_count // 2
+    here = lax.axis_index("seq")
+    member = here % 2
+    where = jnp.full((1,), member, jnp.int32)
+    group_local = lax.axis_index("sub") * heads // (LOCAL_HEADS // G)
+    b_group = lax.dynamic_slice_in_dim(b_in, group_local, 1, 1)[:, 0, :]
+    c_group = lax.dynamic_slice_in_dim(c_in, group_local, 1, 1)[:, 0, :]
+    expand = jnp.asarray(np.kron(np.eye(half_heads), np.ones((1, P_SIZE))), bf16)
+    table = jnp.asarray(sylvester(H_BLOCK), bf16)
+
+    def shape(rows, columns, kind):
+        return jax.ShapeDtypeStruct((rows, columns), kind)
+
+    def padded(columns):
+        return pl.cdiv(columns, LANES) * LANES
+
+    local = (x_in, gate_in, b_group, c_group, step_size, log_decay)
+    later = shape(tokens, half + states + padded(2 * half_heads), bf16)
+    to_pair, straight, cross = call(
+        pack_kernel,
+        (shape(tokens, 2 * half + 2 * states + padded(6 * half_heads), bf16), later, later),
+        "pack",
+        (where, *local, expand),
+        1,
+    )
+    to_pair = swap_seq(to_pair, 1)
+    straights, crosses = [], []
+    for ahead in range(1, pairs):
+        firsts = range(seq_count - 2 * ahead)
+        straights.append(lax.ppermute(straight, "seq", [(k, k + 2 * ahead) for k in firsts]))
+        crosses.append(lax.ppermute(cross, "seq", [(k, (k ^ 1) + 2 * ahead) for k in firsts]))
+
+    span = 2 * tokens
+    own, far, c_pair = call(
+        pair_kernel,
+        (shape(span, half, f32), shape(span, half, f32), shape(span, states, bf16)),
+        "pair",
+        (where, *local, to_pair, jnp.repeat(skip, P_SIZE)[None, :], expand),
+        1,
+        (
+            pltpu.VMEM((span, half), bf16),
+            pltpu.VMEM((span, half), bf16),
+            pltpu.VMEM((span, states), bf16),
+            pltpu.VMEM((span, half_heads), f32),
+            pltpu.VMEM((span, half_heads), f32),
+        ),
+    )
+    signed_gain = (jnp.where(walsh_sign == 1, 1.0, -1.0) * norm_gain)[None, :]
+    owners = chan_count * sub_count
+    size = tokens // (2 * owners)
+    count = len(straights)
+    chunks = pl.pallas_call(
+        functools.partial(gate_mix_kernel, count, span // size),
+        out_shape=(shape(tokens, half, bf16),) * 2,
+        in_specs=[pl.BlockSpec(memory_space=pltpu.VMEM)] * (2 * count)
+        + [pl.BlockSpec(memory_space=pltpu.SMEM)]
+        + [pl.BlockSpec(memory_space=pltpu.VMEM)] * 6,
+        compiler_params=PARAMS,
+        name="mix",
+    )(*straights, *crosses, where, c_pair, own, far, signed_gain, table, expand)
+
+    def across(mixed):
+        for axis in ("sub", "chan"):
+            place = lax.axis_index(axis)
+            for bit in bits_of(axis):
+                sign = 1.0 - 2.0 * (place // 2**bit % 2).astype(f32)
+                mixed = (mixed.astype(f32) * sign + swap(mixed, axis, bit).astype(f32)).astype(bf16)
+        return mixed
+
+    first, second = across(chunks[0]), across(chunks[1])
+    gathered = [first, swap_seq(first, 1)]
+    for ahead in range(1, pairs):
+        gathered.append(swap_seq(first, 2 * ahead))
+        gathered.append(swap_seq(gathered[-1], 1))
+    gathered = [gathered, [second] + [swap_seq(second, k) for k in range(1, seq_count)]]
+
+    up = (power_two(channel_shift_power, 1) * (1.0 / math.sqrt(LOCAL_HEADS * P_SIZE)))[None, :]
+    down = power_two(channel_shift_power, -1)[None, :]
+    features = out_weight.shape[1]
+    placed = []
+    for pieces in gathered:
+        partial = call(
+            functools.partial(project_kernel, pairs),
+            jax.ShapeDtypeStruct((sub_count, chan_count, pairs, 2, size, features), bf16),
+            "project",
+            (where, *pieces, up, down, out_weight),
+            1,
+        )
+        summed = halve(halve(partial, "sub"), "chan")
+        for distance in range(seq_count):
+            block = (member + distance) % 2
+            value = lax.dynamic_index_in_dim(summed[distance // 2], block, 0, keepdims=False)
+            placed.append(swap_seq(value, distance) if distance else value)
+    return call(
+        functools.partial(place_kernel, seq_count),
+        shape(2 * size, seq_count * features, bf16),
+        "place",
+        (jnp.full((1,), here, jnp.int32), *placed),
+        1,
+    )
+
+
+def body(x_in, b_in, c_in, step_size, *rest):
+    tokens, heads = step_size.shape
+    seq_count = lax.axis_size("seq")
+    pieces = 2 * lax.axis_size("chan") * lax.axis_size("sub")
+    if (
+        heads % (2 * NORM_HEADS) == 0
+        and seq_count % 2 == 0
+        and seq_count & (seq_count - 1) == 0
+        and tokens % (16 * pieces) == 0
+    ):
+        return paired_body(x_in, b_in, c_in, step_size, *rest)
+    return plain_body(x_in, b_in, c_in, step_size, *rest)
+
+
+def plain_body(
     x_in,
     b_in,
     c_in,

time: 152 us -> 129 us (0.85)
  waiting for transfers between devices: 76.4 us -> 63.8 us
  starting transfers between devices: 50.5 us -> 42 us
  matrix products: 7.26 us -> 0 us
  Pallas kernels: 3.53 us -> 7.45 us
  local copies, waits for them, and re-layouts: 12.2 us -> 13.9 us
    dot_general x4 -> x0, matrix products: 7.26 us -> none  [dot(): return jnp.dot(a, b, preferred_element_type=f32)]
    ppermute x9 -> x15, waiting for transfers between devices: 61.2 us -> 54.3 us  [the longest x13 44.9 us: swap_seq(): return lax.ppermute(value, 'seq', [(k, k ^ distance) for k in range(count)])]
    ppermute x9 -> x15, starting transfers between devices: 42.8 us -> 36 us  [the longest x13 30.2 us: swap_seq(): return lax.ppermute(value, 'seq', [(k, k ^ distance) for k in range(count)])]
    ppermute x10 -> x8, waiting for transfers between devices: 15.2 us -> 9.4 us  [swap(): return lax.ppermute(value, axis, [(k, k ^ 1 << bit) for k in range(count)])]
    pallas_call x3 -> x6, Pallas kernels: 3.53 us -> 7.45 us  [the longest x5 6.53 us: call(): pl.pallas_call(kernel, out_shape=out_shape, in_specs=specs, scratch_shape...]
    unnamed x30 -> x24, local copies, waits for them, and re-layouts: 9.36 us -> 11.7 us
    ppermute x10 -> x8, starting transfers between devices: 7.69 us -> 5.96 us  [swap(): return lax.ppermute(value, axis, [(k, k ^ 1 << bit) for k in range(count)])]
  transfers between devices with their start and end apart: 19 -> 23, of which waited for: 9 -> 12; matrix products, arithmetic and copies ran while one was open for 5% -> 2% of each run, Pallas kernels for 1% -> 4%
where the time goes in v1:
time: 129 us
  waiting for transfers between devices  63.8 us (49%)
  starting transfers between devices  42 us (33%)
  local copies, waits for them, and re-layouts  13.9 us (11%)
  Pallas kernels  7.45 us (6%)
  other arithmetic  1.29 us (1%)
    ppermute x13, waiting for transfers between devices, swap_seq(): return lax.ppermute(value, 'seq', [(k, k ^ distance) for k in range(count)])  44.9 us
    ppermute x13, starting transfers between devices, swap_seq(): return lax.ppermute(value, 'seq', [(k, k ^ distance) for k in range(count)])  30.2 us
    unnamed x24, local copies, waits for them, and re-layouts  11.7 us
    ppermute x8, waiting for transfers between devices, swap(): return lax.ppermute(value, axis, [(k, k ^ 1 << bit) for k in range(count)])  9.4 us
    ppermute x1, waiting for transfers between devices, paired_body(): lax.ppermute(cross, 'seq', [(k, (k ^ 1) + 2 * ahead) for k in firsts])  6.62 us
    pallas_call x5, Pallas kernels, call(): pl.pallas_call(kernel, out_shape=out_shape, in_specs=specs, scratch_shape...  6.53 us
    ppermute x8, starting transfers between devices, swap(): return lax.ppermute(value, axis, [(k, k ^ 1 << bit) for k in range(count)])  5.96 us
    ppermute x1, starting transfers between devices, paired_body(): lax.ppermute(straight, 'seq', [(k, k + 2 * ahead) for k in firsts])  4.51 us
  transfers between devices with their start and end apart: 23, of which 12 were waited for; matrix products, arithmetic and copies ran while one was open for 2% of the time, Pallas kernels for 4%

profile of v1, /device:TPU:0, one launch (start us, length us, event | category | flops | bytes accessed | tf_op | source)
XLA Modules:
  0.0 128.8 jit_solution(8143198452081563367)
XLA Ops:
  0.0 1.3 constant_dynamic-slice_fusion.2
  1.3 0.8 copy.20.step_ref
  2.1 0.8 copy.21.decay_ref
  3.0 1.0 copy-done.2
  4.0 1.0 copy-done.4
  5.0 0.8 copy-done.6
  5.8 0.7 pack.1
  6.5 3.1 %collective-permute-start.2 = (bf16[128,2688]{1,0:T(8,128)(2,1)S(1)}, bf16[128,2688]{1,0:T(8,128)(2,1)S(1)}, u32[]{:S(2)}, u32[]{:S(2)}) collective-permute-start(bf16[128,2688]{1,0:T(8,128)(2,1)S(1)} %get-tuple-element.15), channel_id=1, source_target_pairs={{0,4},{4,0},{8,12},{12,8},{1,5},{5,1},{9,13},{13,9},{2,6},{6,2},{1... | collective-permute-start | bytes 2064392 | tf_op jit(solution)/shard_map/ppermute | solution.py:462
  9.6 4.5 %collective-permute-start = (bf16[128,1408]{1,0:T(8,128)(2,1)S(1)}, bf16[128,1408]{1,0:T(8,128)(2,1)S(1)}, u32[]{:S(2)}, u32[]{:S(2)}) collective-permute-start(bf16[128,1408]{1,0:T(8,128)(2,1)S(1)} %get-tuple-element.13), channel_id=1, source_target_pairs={{0,8},{4,12},{1,9},{5,13},{2,10},{6,14},{3,11},{7,15},{16,24},{20,... | collective-permute-start | bytes 1081352 | tf_op jit(solution)/shard_map/ppermute | solution.py:512
  14.1 1.3 %collective-permute-start.1 = (bf16[128,1408]{1,0:T(8,128)(2,1)S(1)}, bf16[128,1408]{1,0:T(8,128)(2,1)S(1)}, u32[]{:S(2)}, u32[]{:S(2)}) collective-permute-start(bf16[128,1408]{1,0:T(8,128)(2,1)S(1)} %get-tuple-element.14), channel_id=1, source_target_pairs={{0,12},{4,8},{1,13},{5,9},{2,14},{6,10},{3,15},{7,11},{16,28},{20,... | collective-permute-start | bytes 1081352 | tf_op jit(solution)/shard_map/ppermute | solution.py:513
  15.5 0.7 broadcast_in_dim.64
  16.3 0.7 select_multiply_fusion
  17.0 8.5 %collective-permute-done.2.msg_ref = bf16[128,2688]{1,0:T(8,128)(2,1)S(1)} collective-permute-done((bf16[128,2688]{1,0:T(8,128)(2,1)S(1)}, bf16[128,2688]{1,0:T(8,128)(2,1)S(1)}, u32[]{:S(2)}, u32[]{:S(2)}) %collective-permute-start.2) | collective-permute-done | bytes 688160 | tf_op jit(solution)/shard_map/ppermute | solution.py:462
  25.5 1.0 copy-done.3
  26.5 1.0 copy-done.5
  27.6 0.8 copy-done.7
  28.3 2.0 %pair.1 = (f32[256,1024]{1,0:T(8,128)S(1)}, f32[256,1024]{1,0:T(8,128)S(1)}, bf16[256,256]{1,0:T(8,128)(2,1)S(1)}) custom-call(s32[1]{0:T(128)} %bitcast.1.where_ref.refs_2_, bf16[128,2048]{1,0:T(8,128)(2,1)S(1)} %copy-done.3, bf16[128,2048]{1,0:T(8,128)(2,1)S(1)} %copy-done.5, bf16[128,256]{1,0:T(8,128)(2,1)S(1)} %bitcast.38, ...), custom_call_target="tpu_custom_call" | custom-call | tf_op jit(solution)/shard_map/pair/pallas_call | solution.py:450
  30.4 2.9 %collective-permute-done.refs_0_ = bf16[128,1408]{1,0:T(8,128)(2,1)S(1)} collective-permute-done((bf16[128,1408]{1,0:T(8,128)(2,1)S(1)}, bf16[128,1408]{1,0:T(8,128)(2,1)S(1)}, u32[]{:S(2)}, u32[]{:S(2)}) %collective-permute-start) | collective-permute-done | bytes 360480 | tf_op jit(solution)/shard_map/ppermute | solution.py:512
  33.2 6.6 %collective-permute-done.1.refs_1_ = bf16[128,1408]{1,0:T(8,128)(2,1)S(1)} collective-permute-done((bf16[128,1408]{1,0:T(8,128)(2,1)S(1)}, bf16[128,1408]{1,0:T(8,128)(2,1)S(1)}, u32[]{:S(2)}, u32[]{:S(2)}) %collective-permute-start.1) | collective-permute-done | bytes 360480 | tf_op jit(solution)/shard_map/ppermute | solution.py:513
  39.9 0.9 mix.1
  41.4 1.0 collective-permute-done.13
  42.5 1.5 %collective-permute-start.14 = (bf16[128,1024]{1,0:T(8,128)(2,1)S(1)}, bf16[128,1024]{1,0:T(8,128)(2,1)S(1)}, u32[]{:S(2)}, u32[]{:S(2)}) collective-permute-start(bf16[128,1024]{1,0:T(8,128)(2,1)S(1)} %add_convert_fusion.2), channel_id=1, source_target_pairs={{0,2},{2,0},{1,3},{3,1},{4,6},{6,4},{5,7},{7,5},{8,10},{10,8},{9,1... | collective-permute-start | bytes 786440 | tf_op jit(solution)/shard_map/ppermute | solution.py:429
  44.2 0.6 collective-permute-start.4
  44.8 6.9 %collective-permute-done.14 = bf16[128,1024]{1,0:T(8,128)(2,1)S(1)} collective-permute-done((bf16[128,1024]{1,0:T(8,128)(2,1)S(1)}, bf16[128,1024]{1,0:T(8,128)(2,1)S(1)}, u32[]{:S(2)}, u32[]{:S(2)}) %collective-permute-start.14) | collective-permute-done | bytes 262176 | tf_op jit(solution)/shard_map/ppermute | solution.py:429
  51.8 5.4 %collective-permute-start.15 = (bf16[128,1024]{1,0:T(8,128)(2,1)S(1)}, bf16[128,1024]{1,0:T(8,128)(2,1)S(1)}, u32[]{:S(2)}, u32[]{:S(2)}) collective-permute-start(bf16[128,1024]{1,0:T(8,128)(2,1)S(1)} %add_convert_fusion.1.refs_0_), channel_id=1, source_target_pairs={{0,4},{4,0},{8,12},{12,8},{1,5},{5,1},{9,13},{13,9},{2,6},{6,2},{1... | collective-permute-start | bytes 786440 | tf_op jit(solution)/shard_map/ppermute | solution.py:462
  57.1 4.6 %collective-permute-start.16 = (bf16[128,1024]{1,0:T(8,128)(2,1)S(1)}, bf16[128,1024]{1,0:T(8,128)(2,1)S(1)}, u32[]{:S(2)}, u32[]{:S(2)}) collective-permute-start(bf16[128,1024]{1,0:T(8,128)(2,1)S(1)} %add_convert_fusion.1.refs_0_), channel_id=1, source_target_pairs={{0,8},{4,12},{8,0},{12,4},{1,9},{5,13},{9,1},{13,5},{2,10},{6,14},... | collective-permute-start | bytes 786440 | tf_op jit(solution)/shard_map/ppermute | solution.py:462
  61.9 2.0 %collective-permute-start.6 = (bf16[128,1024]{1,0:T(8,128)(2,1)S(1)}, bf16[128,1024]{1,0:T(8,128)(2,1)S(1)}, u32[]{:S(2)}, u32[]{:S(2)}) collective-permute-start(bf16[128,1024]{1,0:T(8,128)(2,1)S(1)} %add_convert_fusion.4.refs_0_), channel_id=1, source_target_pairs={{0,8},{4,12},{8,0},{12,4},{1,9},{5,13},{9,1},{13,5},{2,10},{6,14},... | collective-permute-start | bytes 786440 | tf_op jit(solution)/shard_map/ppermute | solution.py:462
  63.9 1.8 %collective-permute-done.15.refs_1_ = bf16[128,1024]{1,0:T(8,128)(2,1)S(1)} collective-permute-done((bf16[128,1024]{1,0:T(8,128)(2,1)S(1)}, bf16[128,1024]{1,0:T(8,128)(2,1)S(1)}, u32[]{:S(2)}, u32[]{:S(2)}) %collective-permute-start.15) | collective-permute-done | bytes 262176 | tf_op jit(solution)/shard_map/ppermute | solution.py:462
  65.6 20.2 %collective-permute-done.16.refs_2_ = bf16[128,1024]{1,0:T(8,128)(2,1)S(1)} collective-permute-done((bf16[128,1024]{1,0:T(8,128)(2,1)S(1)}, bf16[128,1024]{1,0:T(8,128)(2,1)S(1)}, u32[]{:S(2)}, u32[]{:S(2)}) %collective-permute-start.16) | collective-permute-done | bytes 262176 | tf_op jit(solution)/shard_map/ppermute | solution.py:462
  85.8 2.2 %copy-done = bf16[2048,1024]{1,0:T(8,128)(2,1)S(1)} copy-done((bf16[2048,1024]{1,0:T(8,128)(2,1)S(1)}, bf16[2048,1024]{1,0:T(8,128)(2,1)}, u32[]{:S(2)}) %copy-start) | copy-done | bytes 4194328
  88.0 1.5 %project.3 = bf16[2,2,2,2,16,1024]{5,4,3,2,1,0:T(8,128)(2,1)S(1)} custom-call(s32[1]{0:T(128)} %bitcast.1.where_ref.refs_2_, bf16[128,1024]{1,0:T(8,128)(2,1)S(1)} %add_convert_fusion.1.refs_0_, bf16[128,1024]{1,0:T(8,128)(2,1)S(1)} %collective-permute-done.15.refs_1_, bf16[128,1024]{1,0:T(8,128)(2,1)S(1)} %collective-permute-done.16.refs_2_, ...), custom_call_target="tpu_custom_call" | custom-call | tf_op jit(solution)/shard_map/project/pallas_call | solution.py:450
  89.7 6.2 %collective-permute-start.5 = (bf16[128,1024]{1,0:T(8,128)(2,1)S(1)}, bf16[128,1024]{1,0:T(8,128)(2,1)S(1)}, u32[]{:S(2)}, u32[]{:S(2)}) collective-permute-start(bf16[128,1024]{1,0:T(8,128)(2,1)S(1)} %add_convert_fusion.4.refs_0_), channel_id=1, source_target_pairs={{0,4},{4,0},{8,12},{12,8},{1,5},{5,1},{9,13},{13,9},{2,6},{6,2},{1... | collective-permute-start | bytes 786440 | tf_op jit(solution)/shard_map/ppermute | solution.py:462
  96.1 1.6 %collective-permute-start.19 = (bf16[1,2,2,16,1024]{4,3,2,1,0:T(8,128)(2,1)S(1)}, bf16[1,2,2,16,1024]{4,3,2,1,0:T(8,128)(2,1)S(1)}, u32[]{:S(2)}, u32[]{:S(2)}) collective-permute-start(bf16[1,2,2,16,1024]{4,3,2,1,0:T(8,128)(2,1)S(1)} %dynamic-slice_bitcast_fusion), channel_id=1, source_target_pairs={{0,2},{2,0},{1,3},{3,1},{4,6},{6,4},{5,7},{7,5},{8,10},{10,8},{9,1... | collective-permute-start | bytes 393224 | tf_op jit(solution)/shard_map/ppermute | solution.py:429
  97.7 5.4 %collective-permute-done.5.refs_1_ = bf16[128,1024]{1,0:T(8,128)(2,1)S(1)} collective-permute-done((bf16[128,1024]{1,0:T(8,128)(2,1)S(1)}, bf16[128,1024]{1,0:T(8,128)(2,1)S(1)}, u32[]{:S(2)}, u32[]{:S(2)}) %collective-permute-start.5) | collective-permute-done | bytes 262176 | tf_op jit(solution)/shard_map/ppermute | solution.py:462
  103.1 5.3 %collective-permute-done.7.refs_3_ = bf16[128,1024]{1,0:T(8,128)(2,1)S(1)} collective-permute-done((bf16[128,1024]{1,0:T(8,128)(2,1)S(1)}, bf16[128,1024]{1,0:T(8,128)(2,1)S(1)}, u32[]{:S(2)}, u32[]{:S(2)}) %collective-permute-start.7) | collective-permute-done | bytes 262176 | tf_op jit(solution)/shard_map/ppermute | solution.py:462
  108.4 2.2 %copy-done.1 = bf16[2048,1024]{1,0:T(8,128)(2,1)S(1)} copy-done((bf16[2048,1024]{1,0:T(8,128)(2,1)S(1)}, bf16[2048,1024]{1,0:T(8,128)(2,1)}, u32[]{:S(2)}) %copy-start.1) | copy-done | bytes 4194328
  110.6 1.5 %project.2 = bf16[2,2,2,2,16,1024]{5,4,3,2,1,0:T(8,128)(2,1)S(1)} custom-call(s32[1]{0:T(128)} %bitcast.1.where_ref.refs_2_, bf16[128,1024]{1,0:T(8,128)(2,1)S(1)} %add_convert_fusion.4.refs_0_, bf16[128,1024]{1,0:T(8,128)(2,1)S(1)} %collective-permute-done.5.refs_1_, bf16[128,1024]{1,0:T(8,128)(2,1)S(1)} %collective-permute-done.6.refs_2_, ...), custom_call_target="tpu_custom_call" | custom-call | tf_op jit(solution)/shard_map/project/pallas_call | solution.py:450
  112.3 1.4 %collective-permute-done.8 = bf16[1,2,2,2,16,1024]{5,4,3,2,1,0:T(8,128)(2,1)S(1)} collective-permute-done((bf16[1,2,2,2,16,1024]{5,4,3,2,1,0:T(8,128)(2,1)S(1)}, bf16[1,2,2,2,16,1024]{5,4,3,2,1,0:T(8,128)(2,1)S(1)}, u32[]{:S(2)}, u32[]{:S(2)}) %collective-permute-start.8) | collective-permute-done | bytes 262176 | tf_op jit(solution)/shard_map/ppermute | solution.py:429
  113.9 1.6 %collective-permute-start.9 = (bf16[1,2,2,16,1024]{4,3,2,1,0:T(8,128)(2,1)S(1)}, bf16[1,2,2,16,1024]{4,3,2,1,0:T(8,128)(2,1)S(1)}, u32[]{:S(2)}, u32[]{:S(2)}) collective-permute-start(bf16[1,2,2,16,1024]{4,3,2,1,0:T(8,128)(2,1)S(1)} %dynamic-slice_bitcast_fusion.1), channel_id=1, source_target_pairs={{0,2},{2,0},{1,3},{3,1},{4,6},{6,4},{5,7},{7,5},{8,10},{10,8},{9,1... | collective-permute-start | bytes 393224 | tf_op jit(solution)/shard_map/ppermute | solution.py:429
  115.4 1.8 %collective-permute-start.20 = (bf16[16,1024]{1,0:T(8,128)(2,1)S(1)}, bf16[16,1024]{1,0:T(8,128)(2,1)S(1)}, u32[]{:S(2)}, u32[]{:S(2)}) collective-permute-start(bf16[16,1024]{1,0:T(8,128)(2,1)S(1)} %get-tuple-element.33), channel_id=1, source_target_pairs={{0,4},{4,0},{8,12},{12,8},{1,5},{5,1},{9,13},{13,9},{2,6},{6,2},{1... | collective-permute-start | bytes 98312 | tf_op jit(solution)/shard_map/ppermute | solution.py:462
  117.2 0.6 collective-permute-start.21
  117.8 2.0 %collective-permute-start.22 = (bf16[16,1024]{1,0:T(8,128)(2,1)S(1)}, bf16[16,1024]{1,0:T(8,128)(2,1)S(1)}, u32[]{:S(2)}, u32[]{:S(2)}) collective-permute-start(bf16[16,1024]{1,0:T(8,128)(2,1)S(1)} %get-tuple-element.31), channel_id=1, source_target_pairs={{0,12},{4,8},{8,4},{12,0},{1,13},{5,9},{9,5},{13,1},{2,14},{6,10},... | collective-permute-start | bytes 98312 | tf_op jit(solution)/shard_map/ppermute | solution.py:462
  119.9 1.5 %collective-permute-start.10 = (bf16[16,1024]{1,0:T(8,128)(2,1)S(1)}, bf16[16,1024]{1,0:T(8,128)(2,1)S(1)}, u32[]{:S(2)}, u32[]{:S(2)}) collective-permute-start(bf16[16,1024]{1,0:T(8,128)(2,1)S(1)} %get-tuple-element.37), channel_id=1, source_target_pairs={{0,4},{4,0},{8,12},{12,8},{1,5},{5,1},{9,13},{13,9},{2,6},{6,2},{1... | collective-permute-start | bytes 98312 | tf_op jit(solution)/shard_map/ppermute | solution.py:462
  121.4 0.9 collective-permute-start.11
  122.3 2.0 %collective-permute-start.12 = (bf16[16,1024]{1,0:T(8,128)(2,1)S(1)}, bf16[16,1024]{1,0:T(8,128)(2,1)S(1)}, u32[]{:S(2)}, u32[]{:S(2)}) collective-permute-start(bf16[16,1024]{1,0:T(8,128)(2,1)S(1)} %get-tuple-element.35), channel_id=1, source_target_pairs={{0,12},{4,8},{8,4},{12,0},{1,13},{5,9},{9,5},{13,1},{2,14},{6,10},... | collective-permute-start | bytes 98312 | tf_op jit(solution)/shard_map/ppermute | solution.py:462
  124.4 2.2 %collective-permute-done.11.refs_2_ = bf16[16,1024]{1,0:T(8,128)(2,1)S(1)} collective-permute-done((bf16[16,1024]{1,0:T(8,128)(2,1)S(1)}, bf16[16,1024]{1,0:T(8,128)(2,1)S(1)}, u32[]{:S(2)}, u32[]{:S(2)}) %collective-permute-start.11) | collective-permute-done | bytes 32800 | tf_op jit(solution)/shard_map/ppermute | solution.py:462
  126.5 1.5 %collective-permute-done.12.refs_3_ = bf16[16,1024]{1,0:T(8,128)(2,1)S(1)} collective-permute-done((bf16[16,1024]{1,0:T(8,128)(2,1)S(1)}, bf16[16,1024]{1,0:T(8,128)(2,1)S(1)}, u32[]{:S(2)}, u32[]{:S(2)}) %collective-permute-start.12) | collective-permute-done | bytes 32800 | tf_op jit(solution)/shard_map/ppermute | solution.py:462
  128.0 0.7 place.1
  (52 shorter events, 1.7 us)
Async XLA Ops:
  0.0 39.9 %copy-start.8 = (bf16[256,256]{1,0:T(8,128)(2,1)S(1)}, bf16[256,256]{1,0:T(8,128)(2,1)}, u32[]{:S(2)}) copy-start(bf16[256,256]{1,0:T(8,128)(2,1)} %constant.196.clone.refs_7_) | copy-start | bytes 393220
  0.0 44.0 %copy-start.9 = (s32[2048]{0:T(1024)S(1)}, s32[2048]{0:T(1024)}, u32[]{:S(2)}) copy-start(s32[2048]{0:T(1024)} %param.22) | copy-start | bytes 24580
  3.0 1.0 copy-start.2
  4.0 1.0 copy-start.4
  5.0 0.8 copy-start.6
  6.5 18.9 %collective-permute-start.2 = (bf16[128,2688]{1,0:T(8,128)(2,1)S(1)}, bf16[128,2688]{1,0:T(8,128)(2,1)S(1)}, u32[]{:S(2)}, u32[]{:S(2)}) collective-permute-start(bf16[128,2688]{1,0:T(8,128)(2,1)S(1)} %get-tuple-element.15), channel_id=1, source_target_pairs={{0,4},{4,0},{8,12},{12,8},{1,5},{5,1},{9,13},{13,9},{2,6},{6,2},{1... | collective-permute-start | bytes 2064392 | tf_op jit(solution)/shard_map/ppermute | solution.py:462
  9.6 23.6 %collective-permute-start = (bf16[128,1408]{1,0:T(8,128)(2,1)S(1)}, bf16[128,1408]{1,0:T(8,128)(2,1)S(1)}, u32[]{:S(2)}, u32[]{:S(2)}) collective-permute-start(bf16[128,1408]{1,0:T(8,128)(2,1)S(1)} %get-tuple-element.13), channel_id=1, source_target_pairs={{0,8},{4,12},{1,9},{5,13},{2,10},{6,14},{3,11},{7,15},{16,24},{20,... | collective-permute-start | bytes 1081352 | tf_op jit(solution)/shard_map/ppermute | solution.py:512
  14.1 25.7 %collective-permute-start.1 = (bf16[128,1408]{1,0:T(8,128)(2,1)S(1)}, bf16[128,1408]{1,0:T(8,128)(2,1)S(1)}, u32[]{:S(2)}, u32[]{:S(2)}) collective-permute-start(bf16[128,1408]{1,0:T(8,128)(2,1)S(1)} %get-tuple-element.14), channel_id=1, source_target_pairs={{0,12},{4,8},{1,13},{5,9},{2,14},{6,10},{3,15},{7,11},{16,28},{20,... | collective-permute-start | bytes 1081352 | tf_op jit(solution)/shard_map/ppermute | solution.py:513
  25.5 1.0 copy-start.3
  26.5 1.0 copy-start.5
  27.5 0.8 copy-start.7
  40.8 1.6 %collective-permute-start.13 = (bf16[128,1024]{1,0:T(8,128)(2,1)S(1)}, bf16[128,1024]{1,0:T(8,128)(2,1)S(1)}, u32[]{:S(2)}, u32[]{:S(2)}) collective-permute-start(bf16[128,1024]{1,0:T(8,128)(2,1)S(1)} %get-tuple-element.20), channel_id=1, source_target_pairs={{0,1},{1,0},{2,3},{3,2},{4,5},{5,4},{6,7},{7,6},{8,9},{9,8},{10,11... | collective-permute-start | bytes 786440 | tf_op jit(solution)/shard_map/ppermute | solution.py:429
  40.9 3.2 %collective-permute-start.3 = (bf16[128,1024]{1,0:T(8,128)(2,1)S(1)}, bf16[128,1024]{1,0:T(8,128)(2,1)S(1)}, u32[]{:S(2)}, u32[]{:S(2)}) collective-permute-start(bf16[128,1024]{1,0:T(8,128)(2,1)S(1)} %get-tuple-element.19), channel_id=1, source_target_pairs={{0,1},{1,0},{2,3},{3,2},{4,5},{5,4},{6,7},{7,6},{8,9},{9,8},{10,11... | collective-permute-start | bytes 786440 | tf_op jit(solution)/shard_map/ppermute | solution.py:429
  42.5 9.2 %collective-permute-start.14 = (bf16[128,1024]{1,0:T(8,128)(2,1)S(1)}, bf16[128,1024]{1,0:T(8,128)(2,1)S(1)}, u32[]{:S(2)}, u32[]{:S(2)}) collective-permute-start(bf16[128,1024]{1,0:T(8,128)(2,1)S(1)} %add_convert_fusion.2), channel_id=1, source_target_pairs={{0,2},{2,0},{1,3},{3,1},{4,6},{6,4},{5,7},{7,5},{8,10},{10,8},{9,1... | collective-permute-start | bytes 786440 | tf_op jit(solution)/shard_map/ppermute | solution.py:429
  44.2 17.6 %collective-permute-start.4 = (bf16[128,1024]{1,0:T(8,128)(2,1)S(1)}, bf16[128,1024]{1,0:T(8,128)(2,1)S(1)}, u32[]{:S(2)}, u32[]{:S(2)}) collective-permute-start(bf16[128,1024]{1,0:T(8,128)(2,1)S(1)} %add_convert_fusion.5), channel_id=1, source_target_pairs={{0,2},{2,0},{1,3},{3,1},{4,6},{6,4},{5,7},{7,5},{8,10},{10,8},{9,1... | collective-permute-start | bytes 786440 | tf_op jit(solution)/shard_map/ppermute | solution.py:429
  51.8 13.9 %collective-permute-start.15 = (bf16[128,1024]{1,0:T(8,128)(2,1)S(1)}, bf16[128,1024]{1,0:T(8,128)(2,1)S(1)}, u32[]{:S(2)}, u32[]{:S(2)}) collective-permute-start(bf16[128,1024]{1,0:T(8,128)(2,1)S(1)} %add_convert_fusion.1.refs_0_), channel_id=1, source_target_pairs={{0,4},{4,0},{8,12},{12,8},{1,5},{5,1},{9,13},{13,9},{2,6},{6,2},{1... | collective-permute-start | bytes 786440 | tf_op jit(solution)/shard_map/ppermute | solution.py:462
  57.1 28.7 %collective-permute-start.16 = (bf16[128,1024]{1,0:T(8,128)(2,1)S(1)}, bf16[128,1024]{1,0:T(8,128)(2,1)S(1)}, u32[]{:S(2)}, u32[]{:S(2)}) collective-permute-start(bf16[128,1024]{1,0:T(8,128)(2,1)S(1)} %add_convert_fusion.1.refs_0_), channel_id=1, source_target_pairs={{0,8},{4,12},{8,0},{12,4},{1,9},{5,13},{9,1},{13,5},{2,10},{6,14},... | collective-permute-start | bytes 786440 | tf_op jit(solution)/shard_map/ppermute | solution.py:462
  61.7 24.1 %collective-permute-start.17 = (bf16[128,1024]{1,0:T(8,128)(2,1)S(1)}, bf16[128,1024]{1,0:T(8,128)(2,1)S(1)}, u32[]{:S(2)}, u32[]{:S(2)}) collective-permute-start(bf16[128,1024]{1,0:T(8,128)(2,1)S(1)} %add_convert_fusion.1.refs_0_), channel_id=1, source_target_pairs={{0,12},{4,8},{8,4},{12,0},{1,13},{5,9},{9,5},{13,1},{2,14},{6,10},... | collective-permute-start | bytes 786440 | tf_op jit(solution)/shard_map/ppermute | solution.py:462
  61.9 34.0 %collective-permute-start.6 = (bf16[128,1024]{1,0:T(8,128)(2,1)S(1)}, bf16[128,1024]{1,0:T(8,128)(2,1)S(1)}, u32[]{:S(2)}, u32[]{:S(2)}) collective-permute-start(bf16[128,1024]{1,0:T(8,128)(2,1)S(1)} %add_convert_fusion.4.refs_0_), channel_id=1, source_target_pairs={{0,8},{4,12},{8,0},{12,4},{1,9},{5,13},{9,1},{13,5},{2,10},{6,14},... | collective-permute-start | bytes 786440 | tf_op jit(solution)/shard_map/ppermute | solution.py:462
  85.8 2.2 %copy-start = (bf16[2048,1024]{1,0:T(8,128)(2,1)S(1)}, bf16[2048,1024]{1,0:T(8,128)(2,1)}, u32[]{:S(2)}) copy-start(bf16[2048,1024]{1,0:T(8,128)(2,1)} %refs_6_.3) | copy-start | bytes 12582916
  89.6 6.4 %collective-permute-start.18 = (bf16[1,2,2,2,16,1024]{5,4,3,2,1,0:T(8,128)(2,1)S(1)}, bf16[1,2,2,2,16,1024]{5,4,3,2,1,0:T(8,128)(2,1)S(1)}, u32[]{:S(2)}, u32[]{:S(2)}) collective-permute-start(bf16[1,2,2,2,16,1024]{5,4,3,2,1,0:T(8,128)(2,1)S(1)} %constant_dynamic-slice_fusion), channel_id=1, source_target_pairs={{0,1},{1,0},{2,3},{3,2},{4,5},{5,4},{6,7},{7,6},{8,9},{9,8},{10,11... | collective-permute-start | bytes 786440 | tf_op jit(solution)/shard_map/ppermute | solution.py:429
  89.7 13.4 %collective-permute-start.5 = (bf16[128,1024]{1,0:T(8,128)(2,1)S(1)}, bf16[128,1024]{1,0:T(8,128)(2,1)S(1)}, u32[]{:S(2)}, u32[]{:S(2)}) collective-permute-start(bf16[128,1024]{1,0:T(8,128)(2,1)S(1)} %add_convert_fusion.4.refs_0_), channel_id=1, source_target_pairs={{0,4},{4,0},{8,12},{12,8},{1,5},{5,1},{9,13},{13,9},{2,6},{6,2},{1... | collective-permute-start | bytes 786440 | tf_op jit(solution)/shard_map/ppermute | solution.py:462
  95.9 12.5 %collective-permute-start.7 = (bf16[128,1024]{1,0:T(8,128)(2,1)S(1)}, bf16[128,1024]{1,0:T(8,128)(2,1)S(1)}, u32[]{:S(2)}, u32[]{:S(2)}) collective-permute-start(bf16[128,1024]{1,0:T(8,128)(2,1)S(1)} %collective-permute-done.6.refs_2_), channel_id=1, source_target_pairs={{0,4},{4,0},{8,12},{12,8},{1,5},{5,1},{9,13},{13,9},{2,6},{6,2},{1... | collective-permute-start | bytes 786440 | tf_op jit(solution)/shard_map/ppermute | solution.py:462
  96.1 16.1 %collective-permute-start.19 = (bf16[1,2,2,16,1024]{4,3,2,1,0:T(8,128)(2,1)S(1)}, bf16[1,2,2,16,1024]{4,3,2,1,0:T(8,128)(2,1)S(1)}, u32[]{:S(2)}, u32[]{:S(2)}) collective-permute-start(bf16[1,2,2,16,1024]{4,3,2,1,0:T(8,128)(2,1)S(1)} %dynamic-slice_bitcast_fusion), channel_id=1, source_target_pairs={{0,2},{2,0},{1,3},{3,1},{4,6},{6,4},{5,7},{7,5},{8,10},{10,8},{9,1... | collective-permute-start | bytes 393224 | tf_op jit(solution)/shard_map/ppermute | solution.py:429
  108.4 2.2 %copy-start.1 = (bf16[2048,1024]{1,0:T(8,128)(2,1)S(1)}, bf16[2048,1024]{1,0:T(8,128)(2,1)}, u32[]{:S(2)}) copy-start(bf16[2048,1024]{1,0:T(8,128)(2,1)} %refs_6_.3) | copy-start | bytes 12582916
  112.2 1.6 %collective-permute-start.8 = (bf16[1,2,2,2,16,1024]{5,4,3,2,1,0:T(8,128)(2,1)S(1)}, bf16[1,2,2,2,16,1024]{5,4,3,2,1,0:T(8,128)(2,1)S(1)}, u32[]{:S(2)}, u32[]{:S(2)}) collective-permute-start(bf16[1,2,2,2,16,1024]{5,4,3,2,1,0:T(8,128)(2,1)S(1)} %constant_dynamic-slice_fusion.1), channel_id=1, source_target_pairs={{0,1},{1,0},{2,3},{3,2},{4,5},{5,4},{6,7},{7,6},{8,9},{9,8},{10,11... | collective-permute-start | bytes 786440 | tf_op jit(solution)/shard_map/ppermute | solution.py:429
  113.9 6.0 %collective-permute-start.9 = (bf16[1,2,2,16,1024]{4,3,2,1,0:T(8,128)(2,1)S(1)}, bf16[1,2,2,16,1024]{4,3,2,1,0:T(8,128)(2,1)S(1)}, u32[]{:S(2)}, u32[]{:S(2)}) collective-permute-start(bf16[1,2,2,16,1024]{4,3,2,1,0:T(8,128)(2,1)S(1)} %dynamic-slice_bitcast_fusion.1), channel_id=1, source_target_pairs={{0,2},{2,0},{1,3},{3,1},{4,6},{6,4},{5,7},{7,5},{8,10},{10,8},{9,1... | collective-permute-start | bytes 393224 | tf_op jit(solution)/shard_map/ppermute | solution.py:429
  115.4 6.9 %collective-permute-start.20 = (bf16[16,1024]{1,0:T(8,128)(2,1)S(1)}, bf16[16,1024]{1,0:T(8,128)(2,1)S(1)}, u32[]{:S(2)}, u32[]{:S(2)}) collective-permute-start(bf16[16,1024]{1,0:T(8,128)(2,1)S(1)} %get-tuple-element.33), channel_id=1, source_target_pairs={{0,4},{4,0},{8,12},{12,8},{1,5},{5,1},{9,13},{13,9},{2,6},{6,2},{1... | collective-permute-start | bytes 98312 | tf_op jit(solution)/shard_map/ppermute | solution.py:462
  117.2 7.2 %collective-permute-start.21 = (bf16[16,1024]{1,0:T(8,128)(2,1)S(1)}, bf16[16,1024]{1,0:T(8,128)(2,1)S(1)}, u32[]{:S(2)}, u32[]{:S(2)}) collective-permute-start(bf16[16,1024]{1,0:T(8,128)(2,1)S(1)} %get-tuple-element.32), channel_id=1, source_target_pairs={{0,8},{4,12},{8,0},{12,4},{1,9},{5,13},{9,1},{13,5},{2,10},{6,14},... | collective-permute-start | bytes 98312 | tf_op jit(solution)/shard_map/ppermute | solution.py:462
  117.8 6.6 %collective-permute-start.22 = (bf16[16,1024]{1,0:T(8,128)(2,1)S(1)}, bf16[16,1024]{1,0:T(8,128)(2,1)S(1)}, u32[]{:S(2)}, u32[]{:S(2)}) collective-permute-start(bf16[16,1024]{1,0:T(8,128)(2,1)S(1)} %get-tuple-element.31), channel_id=1, source_target_pairs={{0,12},{4,8},{8,4},{12,0},{1,13},{5,9},{9,5},{13,1},{2,14},{6,10},... | collective-permute-start | bytes 98312 | tf_op jit(solution)/shard_map/ppermute | solution.py:462
  119.9 4.5 %collective-permute-start.10 = (bf16[16,1024]{1,0:T(8,128)(2,1)S(1)}, bf16[16,1024]{1,0:T(8,128)(2,1)S(1)}, u32[]{:S(2)}, u32[]{:S(2)}) collective-permute-start(bf16[16,1024]{1,0:T(8,128)(2,1)S(1)} %get-tuple-element.37), channel_id=1, source_target_pairs={{0,4},{4,0},{8,12},{12,8},{1,5},{5,1},{9,13},{13,9},{2,6},{6,2},{1... | collective-permute-start | bytes 98312 | tf_op jit(solution)/shard_map/ppermute | solution.py:462
  121.4 5.2 %collective-permute-start.11 = (bf16[16,1024]{1,0:T(8,128)(2,1)S(1)}, bf16[16,1024]{1,0:T(8,128)(2,1)S(1)}, u32[]{:S(2)}, u32[]{:S(2)}) collective-permute-start(bf16[16,1024]{1,0:T(8,128)(2,1)S(1)} %get-tuple-element.36), channel_id=1, source_target_pairs={{0,8},{4,12},{8,0},{12,4},{1,9},{5,13},{9,1},{13,5},{2,10},{6,14},... | collective-permute-start | bytes 98312 | tf_op jit(solution)/shard_map/ppermute | solution.py:462
  122.3 5.7 %collective-permute-start.12 = (bf16[16,1024]{1,0:T(8,128)(2,1)S(1)}, bf16[16,1024]{1,0:T(8,128)(2,1)S(1)}, u32[]{:S(2)}, u32[]{:S(2)}) collective-permute-start(bf16[16,1024]{1,0:T(8,128)(2,1)S(1)} %get-tuple-element.35), channel_id=1, source_target_pairs={{0,12},{4,8},{8,4},{12,0},{1,13},{5,9},{9,5},{13,1},{2,14},{6,10},... | collective-permute-start | bytes 98312 | tf_op jit(solution)/shard_map/ppermute | solution.py:462

commit v2 on v1

--- a/solution.py
+++ b/solution.py
@@ -20,9 +20,11 @@
 expo_levels = (-1, 0, 1, 2, 3)
 LANES = 128
 H_BLOCK = 256
+COST = pl.CostEstimate(flops=1, transcendentals=0, bytes_accessed=30_000_000)
 f32 = jnp.float32
 bf16 = jnp.bfloat16
-PARAMS = pltpu.CompilerParams(vmem_limit_bytes=40 * 2**20)
+PARAMS = pltpu.CompilerParams(vmem_limit_bytes=16 * 2**20)
+WIDE_PARAMS = pltpu.CompilerParams(vmem_limit_bytes=16 * 2**20)
 
 
 def power_two(expo, sign_flip):
@@ -166,6 +168,72 @@
     return pl.ds(pl.multiple_of(which * size, size), size)
 
 
+def start_all(copies):
+    for copy in copies:
+        copy.start()
+    return copies
+
+
+def wait_all(copies):
+    for copy in copies:
+        copy.wait()
+
+
+def later_kernel(
+    where_ref,
+    x_ref,
+    b_ref,
+    step_ref,
+    decay_ref,
+    straight_ref,
+    cross_ref,
+    x_own,
+    b_own,
+    step_own,
+    decay_own,
+    sems,
+):
+    copies = start_all(
+        [
+            pltpu.make_async_copy(ref, own, sems.at[index])
+            for index, (ref, own) in enumerate(
+                (
+                    (decay_ref, decay_own),
+                    (step_ref, step_own),
+                    (b_ref, b_own),
+                    (x_ref, x_own),
+                )
+            )
+        ]
+    )
+    tokens, width = x_ref.shape
+    half, heads, states = width // 2, step_ref.shape[0] // 2, b_ref.shape[1]
+    member = where_ref[0]
+    expand = expansion(heads)
+    triangle = causal_mask(tokens).astype(f32).astype(bf16)
+    wait_all(copies[:2])
+    cumul = exact_dot(triangle, decay_own[...].T)
+    total = cumul[tokens - 1 : tokens, :]
+    scale = jnp.exp(total - cumul) * step_own[...].T
+    kept = jnp.exp(total)
+
+    def pick(value, which):
+        return jnp.where(which == 0, value[:, :heads], value[:, heads:])
+
+    base = half + states
+    copies[2].wait()
+    copies[3].wait()
+    for out_ref, which in ((straight_ref, member), (cross_ref, 1 - member)):
+        wide = spread(pick(scale, which), expand)
+        out_ref[:, :half] = (x_own[:, half_at(which, half)].astype(f32) * wide).astype(bf16)
+        out_ref[:, half:base] = b_own[...]
+        out_ref[:, base:] = jnp.zeros((tokens, out_ref.shape[1] - base), bf16)
+        for index, term in enumerate(parts_of(pick(kept, which), 2)):
+            out_ref[:, base + index * heads : base + (index + 1) * heads] = jnp.broadcast_to(
+                term, (tokens, heads)
+            )
+
+
 def pack_kernel(
     where_ref,
     x_ref,
@@ -174,46 +242,48 @@
     c_ref,
     step_ref,
     decay_ref,
-    expand_ref,
+    after_ref,
     pair_ref,
-    straight_ref,
-    cross_ref,
+    step_own,
+    decay_own,
+    sems,
 ):
     tokens, width = x_ref.shape
-    half, heads, states = width // 2, step_ref.shape[1] // 2, b_ref.shape[1]
-    member = where_ref[0]
-    step = step_ref[...]
-    decay = decay_ref[...]
-    triangle = causal_mask(tokens).astype(f32).astype(bf16)
-    cumul = exact_dot(triangle, decay)
-    total = cumul[tokens - 1 : tokens, :]
-    scale = jnp.exp(total - cumul) * step
-    kept = jnp.exp(total)
-
-    def pick(value, which):
-        return jnp.where(which == 0, value[:, :heads], value[:, heads:])
-
-    other = 1 - member
-    pair_ref[:, :half] = x_ref[:, half_at(other, half)]
-    pair_ref[:, half : 2 * half] = gate_ref[:, half_at(other, half)]
-    pair_ref[:, 2 * half : 2 * half + states] = b_ref[...]
+    half, heads, states = width // 2, step_ref.shape[0] // 2, b_ref.shape[1]
+    other = 1 - where_ref[0]
     base = 2 * half + 2 * states
-    pair_ref[:, 2 * half + states : base] = c_ref[...]
+    copies = start_all(
+        [
+            pltpu.make_async_copy(ref, own, sems.at[index])
+            for index, (ref, own) in enumerate(
+                (
+                    (decay_ref, decay_own),
+                    (step_ref, step_own),
+                    (x_ref.at[:, half_at(other, half)], pair_ref.at[:, :half]),
+                    (gate_ref.at[:, half_at(other, half)], pair_ref.at[:, half : 2 * half]),
+                    (b_ref, pair_ref.at[:, 2 * half : 2 * half + states]),
+                    (c_ref, pair_ref.at[:, 2 * half + states : base]),
+                )
+            )
+        ]
+    )
+
+    def pick(value):
+        return jnp.where(other == 0, value[:heads, :], value[heads:, :]).T
+
+    wait_all(copies[:2])
     pair_ref[:, base:] = jnp.zeros((tokens, pair_ref.shape[1] - base), bf16)
-    terms = parts_of(pick(step, other), 3) + parts_of(pick(decay, other), 3)
+    terms = parts_of(pick(step_own[...]), 3) + parts_of(pick(decay_own[...]), 3)
     for index, term in enumerate(terms):
         pair_ref[:, base + index * heads : base + (index + 1) * heads] = term
-
-    base = half + states
-    for out_ref, which in ((straight_ref, member), (cross_ref, other)):
-        wide = spread(pick(scale, which), expand_ref[...])
-        out_ref[:, :half] = (x_ref[:, half_at(which, half)].astype(f32) * wide).astype(bf16)
-        out_ref[:, half:base] = b_ref[...]
-        out_ref[:, base:] = jnp.zeros((tokens, out_ref.shape[1] - base), bf16)
-        for index, term in enumerate(parts_of(pick(kept, which), 2)):
-            out_ref[:, base + index * heads : base + (index + 1) * heads] = jnp.broadcast_to(
-                term, (tokens, heads)
-            )
+    wait_all(copies[2:])
+
+
+def expansion(heads):
+    shape = (heads, heads * P_SIZE)
+    row = lax.broadcasted_iota(jnp.int32, shape, 0)
+    col = lax.broadcasted_iota(jnp.int32, shape, 1)
+    return ((col >= row * P_SIZE) & (col < (row + 1) * P_SIZE)).astype(f32).astype(bf16)
 
 
 def pair_kernel(
@@ -226,7 +296,6 @@
     decay_ref,
     msg_ref,
     skip_ref,
-    expand_ref,
     own_ref,
     far_ref,
     c_pair_ref,
@@ -235,23 +304,37 @@
     b_both,
     step_both,
     decay_both,
+    step_own,
+    decay_own,
+    sems,
 ):
     tokens, width = x_ref.shape
-    half, heads, states = width // 2, step_ref.shape[1] // 2, b_ref.shape[1]
+    half, heads, states = width // 2, step_ref.shape[0] // 2, b_ref.shape[1]
     member = where_ref[0]
     mine, theirs = half_at(member, tokens), half_at(1 - member, tokens)
+    copies = start_all(
+        [
+            pltpu.make_async_copy(ref, own, sems.at[index])
+            for index, (ref, own) in enumerate(
+                (
+                    (decay_ref, decay_own),
+                    (step_ref, step_own),
+                    (b_ref, b_both.at[mine, :]),
+                    (c_ref, c_pair_ref.at[mine, :]),
+                    (x_ref.at[:, half_at(member, half)], x_both.at[mine, :]),
+                    (gate_ref.at[:, half_at(member, half)], gate_both.at[mine, :]),
+                )
+            )
+        ]
+    )
 
     def pick(value):
-        return jnp.where(member == 0, value[:, :heads], value[:, heads:])
-
-    x_both[mine, :] = x_ref[:, half_at(member, half)]
+        return jnp.where(member == 0, value[:heads, :], value[heads:, :]).T
+
     x_both[theirs, :] = msg_ref[:, :half]
-    gate_both[mine, :] = gate_ref[:, half_at(member, half)]
     gate_both[theirs, :] = msg_ref[:, half : 2 * half]
-    b_both[mine, :] = b_ref[...]
     b_both[theirs, :] = msg_ref[:, 2 * half : 2 * half + states]
     base = 2 * half + 2 * states
-    c_pair_ref[mine, :] = c_ref[...]
     c_pair_ref[theirs, :] = msg_ref[:, 2 * half + states : base]
 
     def received(first):
@@ -261,10 +344,11 @@
         ]
         return (terms[2] + terms[1]) + terms[0]
 
-    step_both[mine, :] = pick(step_ref[...])
     step_both[theirs, :] = received(0)
-    decay_both[mine, :] = pick(decay_ref[...])
     decay_both[theirs, :] = received(3)
+    wait_all(copies)
+    step_both[mine, :] = pick(step_own[...])
+    decay_both[mine, :] = pick(decay_own[...])
 
     span = 2 * tokens
     causal = causal_mask(span)
@@ -273,6 +357,7 @@
     cumul_t = cumul.T
     step_t = step_both[...].T
     skip = skip_ref[:, half_at(member, half)]
+    expand = expansion(heads)
     reach = parts_of(jnp.exp(cumul), 2)
     first = lax.broadcasted_iota(jnp.int32, (tokens, 2 * P_SIZE), 1) < P_SIZE
     for pair in range(heads // 2):
@@ -301,25 +386,26 @@
             gate = gate_both[rows, at].astype(f32)
             gate = gate / (1.0 + jnp.exp(-gate))
             own_ref[rows, at] = own * gate
-            wide = sum(dot(term[rows, :], expand_ref[:, at]) for term in reach)
+            wide = sum(dot(term[rows, :], expand[:, at]) for term in reach)
             far_ref[rows, at] = wide * gate
 
 
 def gate_mix_kernel(count, pieces, *refs):
     straight, cross = refs[:count], refs[count : 2 * count]
-    where_ref, c_ref, own_ref, far_ref, gain_ref, table_ref, expand_ref = refs[2 * count : -2]
+    where_ref, c_ref, own_ref, far_ref, gain_ref, table_ref = refs[2 * count : -2]
     out_refs = refs[-2:]
     span, half = own_ref.shape
     states = c_ref.shape[1]
-    heads = expand_ref.shape[0]
+    heads = half // P_SIZE
     base = half + states
     member = where_ref[0]
     c_pair = c_ref[...]
+    expand = expansion(heads)
 
     def kept(msg_ref):
         return (
-            dot(msg_ref[:16, base : base + heads], expand_ref[...])
-            + dot(msg_ref[:16, base + heads : base + 2 * heads], expand_ref[...])
+            dot(msg_ref[:16, base : base + heads], expand)
+            + dot(msg_ref[:16, base + heads : base + 2 * heads], expand)
         )[:1, :]
 
     inners, factors, pair_kept = [], [], []
@@ -373,24 +459,48 @@
         span *= 2
 
 
-def project_kernel(pairs, where_ref, *refs):
+def add_kernel(sign_ref, mixed_ref, received_ref, out_ref):
+    sign = sign_ref[0].astype(f32)
+    out_ref[...] = (mixed_ref[...].astype(f32) * sign + received_ref[...].astype(f32)).astype(bf16)
+
+
+def project_kernel(pairs, where_ref, weight_ref, *refs):
     pieces = refs[: 2 * pairs]
-    up_ref, down_ref, weight_ref, out_ref = refs[2 * pairs :]
-    half = pieces[0].shape[1]
+    up_ref, down_ref, out_ref, weight_own, sums, sems = refs[2 * pairs :]
+    rows, half = pieces[0].shape
     sign = (1 - 2 * where_ref[0]).astype(f32)
     sub_count, chan_count, _, blocks, size, features = out_ref.shape
+    tile = half // 2
+    copies = start_all(
+        [
+            pltpu.make_async_copy(
+                weight_ref.at[start : start + tile, :],
+                weight_own.at[start : start + tile, :],
+                sems.at[start // tile],
+            )
+            for start in range(0, 2 * half, tile)
+        ]
+    )
+    for step, copy in enumerate(copies):
+        at = slice(step * tile, (step + 1) * tile)
+        inner = slice(step * tile % half, step * tile % half + tile)
+        scaled = []
+        for pair in range(pairs):
+            one = pieces[2 * pair][:, inner].astype(f32)
+            two = pieces[2 * pair + 1][:, inner].astype(f32)
+            mixed = (one - two) * sign if step * tile >= half else one + two
+            quant = jnp.clip(mixed * up_ref[:, at], -clip_level, clip_level).astype(bf16)
+            scaled.append((quant.astype(f32) * down_ref[:, at]).astype(bf16))
+        copy.wait()
+        term = dot(jnp.concatenate(scaled, axis=0), weight_own[at, :])
+        if step == 0:
+            sums[...] = term
+        elif step < len(copies) - 1:
+            sums[...] += term
+        else:
+            total = (sums[...] + term).astype(bf16)
+    row = 0
     for pair in range(pairs):
-        one = pieces[2 * pair][...].astype(f32)
-        two = pieces[2 * pair + 1][...].astype(f32)
-        total = None
-        for side, mixed in enumerate((one + two, (one - two) * sign)):
-            at = slice(side * half, (side + 1) * half)
-            quant = jnp.clip(mixed * up_ref[:, at], -clip_level, clip_level).astype(bf16)
-            scaled = (quant.astype(f32) * down_ref[:, at]).astype(bf16)
-            term = dot(scaled, weight_ref[at, :])
-            total = term if total is None else total + term
-        total = total.astype(bf16)
-        row = 0
         for block in range(blocks):
             for chan in range(chan_count):
                 for sub in range(sub_count):
@@ -398,13 +508,11 @@
                     row += size
 
 
-def place_kernel(count, where_ref, *refs):
+def place_kernel(where_ref, *refs):
     out_ref = refs[-1]
-    size, features = refs[0].shape
-    for index, ref in enumerate(refs[:-1]):
-        group, distance = index // count, index % count
-        at = half_at(where_ref[0] ^ distance, features)
-        out_ref[group * size : (group + 1) * size, at] = ref[...]
+    features = refs[0].shape[1]
+    for distance, ref in enumerate(refs[:-1]):
+        out_ref[:, half_at(where_ref[0] ^ distance, features)] = ref[...]
 
 
 def sylvester(order):
@@ -444,15 +552,17 @@
     return value[0]
 
 
-def call(kernel, out_shape, name, args, scalars=0, scratch=()):
+def call(kernel, out_shape, name, args, scalars=0, anywhere=0, scratch=(), params=PARAMS):
     specs = [pl.BlockSpec(memory_space=pltpu.SMEM)] * scalars
-    specs += [pl.BlockSpec(memory_space=pltpu.VMEM)] * (len(args) - scalars)
+    specs += [pl.BlockSpec(memory_space=pltpu.HBM)] * anywhere
+    specs += [pl.BlockSpec(memory_space=pltpu.VMEM)] * (len(args) - scalars - anywhere)
     return pl.pallas_call(
         kernel,
         out_shape=out_shape,
         in_specs=specs,
         scratch_shapes=scratch,
-        compiler_params=PARAMS,
+        compiler_params=params,
+        cost_estimate=COST,
         name=name,
     )(*args)
 
@@ -483,11 +593,10 @@
     pairs = seq_count // 2
     here = lax.axis_index("seq")
     member = here % 2
+    group_local = lax.axis_index("sub") * heads // (LOCAL_HEADS // G)
     where = jnp.full((1,), member, jnp.int32)
-    group_local = lax.axis_index("sub") * heads // (LOCAL_HEADS // G)
-    b_group = lax.dynamic_slice_in_dim(b_in, group_local, 1, 1)[:, 0, :]
-    c_group = lax.dynamic_slice_in_dim(c_in, group_local, 1, 1)[:, 0, :]
-    expand = jnp.asarray(np.kron(np.eye(half_heads), np.ones((1, P_SIZE))), bf16)
+    b_group = lax.dynamic_index_in_dim(b_in, group_local, 1, keepdims=False)
+    c_group = lax.dynamic_index_in_dim(c_in, group_local, 1, keepdims=False)
     table = jnp.asarray(sylvester(H_BLOCK), bf16)
 
     def shape(rows, columns, kind):
@@ -496,14 +605,37 @@
     def padded(columns):
         return pl.cdiv(columns, LANES) * LANES
 
-    local = (x_in, gate_in, b_group, c_group, step_size, log_decay)
+    step, decay = step_size.T, log_decay.T
     later = shape(tokens, half + states + padded(2 * half_heads), bf16)
-    to_pair, straight, cross = call(
+    head_buffer = pltpu.VMEM(step.shape, f32)
+    straight, cross = call(
+        later_kernel,
+        (later, later),
+        "later",
+        (where, x_in, b_group, step, decay),
+        1,
+        4,
+        (
+            pltpu.VMEM((tokens, width), bf16),
+            pltpu.VMEM((tokens, states), bf16),
+            head_buffer,
+            head_buffer,
+            pltpu.SemaphoreType.DMA((4,)),
+        ),
+    )
+    local = (x_in, gate_in, b_group, c_group, step, decay)
+    to_pair = call(
         pack_kernel,
-        (shape(tokens, 2 * half + 2 * states + padded(6 * half_heads), bf16), later, later),
+        shape(tokens, 2 * half + 2 * states + padded(6 * half_heads), bf16),
         "pack",
-        (where, *local, expand),
+        (where, *local, straight),
         1,
+        7,
+        (
+            head_buffer,
+            head_buffer,
+            pltpu.SemaphoreType.DMA((6,)),
+        ),
     )
     to_pair = swap_seq(to_pair, 1)
     straights, crosses = [], []
@@ -515,16 +647,24 @@
     span = 2 * tokens
     own, far, c_pair = call(
         pair_kernel,
-        (shape(span, half, f32), shape(span, half, f32), shape(span, states, bf16)),
+        (
+            shape(span, half, f32),
+            shape(span, half, f32),
+            shape(span, states, bf16),
+        ),
         "pair",
-        (where, *local, to_pair, jnp.repeat(skip, P_SIZE)[None, :], expand),
+        (where, *local, to_pair, jnp.repeat(skip, P_SIZE)[None, :]),
         1,
+        6,
         (
             pltpu.VMEM((span, half), bf16),
             pltpu.VMEM((span, half), bf16),
             pltpu.VMEM((span, states), bf16),
             pltpu.VMEM((span, half_heads), f32),
             pltpu.VMEM((span, half_heads), f32),
+            head_buffer,
+            head_buffer,
+            pltpu.SemaphoreType.DMA((6,)),
         ),
     )
     signed_gain = (jnp.where(walsh_sign == 1, 1.0, -1.0) * norm_gain)[None, :]
@@ -536,48 +676,96 @@
         out_shape=(shape(tokens, half, bf16),) * 2,
         in_specs=[pl.BlockSpec(memory_space=pltpu.VMEM)] * (2 * count)
         + [pl.BlockSpec(memory_space=pltpu.SMEM)]
-        + [pl.BlockSpec(memory_space=pltpu.VMEM)] * 6,
+        + [pl.BlockSpec(memory_space=pltpu.VMEM)] * 5,
         compiler_params=PARAMS,
+        cost_estimate=COST,
         name="mix",
-    )(*straights, *crosses, where, c_pair, own, far, signed_gain, table, expand)
-
-    def across(mixed):
-        for axis in ("sub", "chan"):
-            place = lax.axis_index(axis)
-            for bit in bits_of(axis):
-                sign = 1.0 - 2.0 * (place // 2**bit % 2).astype(f32)
-                mixed = (mixed.astype(f32) * sign + swap(mixed, axis, bit).astype(f32)).astype(bf16)
+    )(*straights, *crosses, where, c_pair, own, far, signed_gain, table)
+
+    def add_across(mixed, axis, bit, received):
+        place = lax.axis_index(axis)
+        sign = 1.0 - 2.0 * (place // 2**bit % 2).astype(f32)
+        return (mixed.astype(f32) * sign + received.astype(f32)).astype(bf16)
+
+    def across(mixed, axis):
+        for bit in bits_of(axis):
+            mixed = add_across(mixed, axis, bit, swap(mixed, axis, bit))
         return mixed
 
-    first, second = across(chunks[0]), across(chunks[1])
-    gathered = [first, swap_seq(first, 1)]
-    for ahead in range(1, pairs):
-        gathered.append(swap_seq(first, 2 * ahead))
-        gathered.append(swap_seq(gathered[-1], 1))
-    gathered = [gathered, [second] + [swap_seq(second, k) for k in range(1, seq_count)]]
+    first, second = (across(chunk, "sub") for chunk in chunks)
+    first = across(first, "chan")
+    first, second = lax.optimization_barrier((first, second))
+    bits = bits_of("chan")
+    for bit in bits[:-1]:
+        second = add_across(second, "chan", bit, swap(second, "chan", bit))
+    received = swap(second, "chan", bits[-1]) if bits else None
+    ahead = range(1, pairs)
+    far_first = [swap_seq(first, 2 * k) for k in ahead]
+    near_first = swap_seq(first, 1)
+    first, second, received, far_first, near_first = lax.optimization_barrier(
+        (first, second, received, far_first, near_first)
+    )
+    if bits:
+        sign = 1 - 2 * (lax.axis_index("chan") // 2 ** bits[-1] % 2)
+        second = call(
+            add_kernel,
+            shape(tokens, half, bf16),
+            "add",
+            (jnp.full((1,), sign, jnp.int32), second, received),
+            1,
+        )
+    passed_first = [swap_seq(value, 1) for value in far_first]
+    all_first = [first, near_first]
+    for far, passed in zip(far_first, passed_first):
+        all_first += [far, passed]
+    second_late = lax.optimization_barrier((second, passed_first))[0] if pairs > 1 else second
+    all_second = [second, swap_seq(second_late, 1)]
+    all_second += [swap_seq(second, k) for k in range(2, seq_count)]
 
     up = (power_two(channel_shift_power, 1) * (1.0 / math.sqrt(LOCAL_HEADS * P_SIZE)))[None, :]
     down = power_two(channel_shift_power, -1)[None, :]
     features = out_weight.shape[1]
-    placed = []
-    for pieces in gathered:
-        partial = call(
+
+    def project(pieces):
+        return call(
             functools.partial(project_kernel, pairs),
             jax.ShapeDtypeStruct((sub_count, chan_count, pairs, 2, size, features), bf16),
             "project",
-            (where, *pieces, up, down, out_weight),
+            (where, out_weight, *pieces, up, down),
             1,
+            1,
+            (
+                pltpu.VMEM(out_weight.shape, bf16),
+                pltpu.VMEM((pairs * tokens, features), f32),
+                pltpu.SemaphoreType.DMA((4,)),
+            ),
+            WIDE_PARAMS,
         )
-        summed = halve(halve(partial, "sub"), "chan")
-        for distance in range(seq_count):
-            block = (member + distance) % 2
-            value = lax.dynamic_index_in_dim(summed[distance // 2], block, 0, keepdims=False)
-            placed.append(swap_seq(value, distance) if distance else value)
+
+    def reduce(partial):
+        return halve(halve(partial, "sub"), "chan")
+
+    done = lax.optimization_barrier(jnp.bool_(True))
+    done_first = lax.cond(
+        done,
+        lambda *pieces: reduce(project(pieces)),
+        lambda *pieces: jnp.zeros((pairs, 2, size, features), bf16),
+        *all_first,
+    )
+    done_first, all_second = lax.optimization_barrier((done_first, all_second))
+    done_second = reduce(project(all_second))
+    summed = jnp.stack([done_first, done_second], axis=2)
+    returned = []
+    for distance in range(seq_count):
+        block = (member + distance) % 2
+        value = lax.dynamic_index_in_dim(summed[distance // 2], block, 0, keepdims=False)
+        value = value.reshape(2 * size, features)
+        returned.append(swap_seq(value, distance) if distance else value)
     return call(
-        functools.partial(place_kernel, seq_count),
+        place_kernel,
         shape(2 * size, seq_count * features, bf16),
         "place",
-        (jnp.full((1,), here, jnp.int32), *placed),
+        (jnp.full((1,), here, jnp.int32), *returned),
         1,
     )
 

time: 129 us -> 119 us (0.922)
  starting transfers between devices: 42 us -> 33.4 us
  local copies, waits for them, and re-layouts: 13.9 us -> 8.23 us
  Pallas kernels: 7.45 us -> 12.6 us
  waiting for transfers between devices: 63.8 us -> 62.2 us
    ppermute x13 -> x10, waiting for transfers between devices: 44.9 us -> 31.5 us  [swap_seq(): return lax.ppermute(value, 'seq', [(k, k ^ distance) for k in range(count)])]
    ppermute x8, waiting for transfers between devices: 9.4 us -> 21 us  [swap(): return lax.ppermute(value, axis, [(k, k ^ 1 << bit) for k in range(count)])]
    ppermute x13 -> x10, starting transfers between devices: 30.2 us -> 22.8 us  [swap_seq(): return lax.ppermute(value, 'seq', [(k, k ^ distance) for k in range(count)])]
    unnamed x24 -> x22, local copies, waits for them, and re-layouts: 11.7 us -> 6.02 us
    pallas_call x5 -> x7, Pallas kernels: 6.53 us -> 11.7 us  [call(): pl.pallas_call(kernel, out_shape=out_shape, in_specs=specs, scratch_shape...]
  transfers between devices with their start and end apart: 23 -> 20, of which waited for: 12 -> 17; matrix products, arithmetic and copies ran while one was open for 2% -> 2% of each run, Pallas kernels for 4% -> 5%
where the time goes in v2:
time: 119 us; the launch traced here: 118 us
  waiting for transfers between devices  62.2 us (52%)
  starting transfers between devices  33.4 us (28%)
  Pallas kernels  12.6 us (11%)
  local copies, waits for them, and re-layouts  8.23 us (7%)
  other arithmetic  1.24 us (1%)
    ppermute x10, waiting for transfers between devices, swap_seq(): return lax.ppermute(value, 'seq', [(k, k ^ distance) for k in range(count)])  31.5 us
    ppermute x10, starting transfers between devices, swap_seq(): return lax.ppermute(value, 'seq', [(k, k ^ distance) for k in range(count)])  22.8 us
    ppermute x8, waiting for transfers between devices, swap(): return lax.ppermute(value, axis, [(k, k ^ 1 << bit) for k in range(count)])  21 us
    pallas_call x7, Pallas kernels, call(): pl.pallas_call(kernel, out_shape=out_shape, in_specs=specs, scratch_shape...  11.7 us
    ppermute x1, waiting for transfers between devices, paired_body(): lax.ppermute(cross, 'seq', [(k, (k ^ 1) + 2 * ahead) for k in firsts])  6.72 us
    unnamed x22, local copies, waits for them, and re-layouts  6.02 us
    ppermute x8, starting transfers between devices, swap(): return lax.ppermute(value, axis, [(k, k ^ 1 << bit) for k in range(count)])  4.79 us
    ppermute x1, starting transfers between devices, paired_body(): lax.ppermute(straight, 'seq', [(k, k + 2 * ahead) for k in firsts])  4.5 us
  transfers between devices with their start and end apart: 20, of which 17 were waited for; matrix products, arithmetic and copies ran while one was open for 2% of the time, Pallas kernels for 5%

profile of v2, /device:TPU:0, one launch (start us, length us, event | category | flops | bytes accessed | tf_op | source)
XLA Modules:
  0.0 118.1 jit_solution(5079626299378948873)
XLA Ops:
  0.0 1.3 %constant_dynamic-slice_fusion.4 = (bf16[128,1,256]{2,1,0:T(2,128)(2,1)S(1)}, bf16[128,1,256]{2,1,0:T(2,128)(2,1)S(1)}) fusion(bf16[128,2,256]{2,1,0:T(2,128)(2,1)} %param.16, s32[]{:T(128)S(6)} %select_n.138, bf16[128,2,256]{2,1,0:T(2,128)(2,1)} %param.15), kind=kLoop, calls=%fused_computation.43 | loop fusion | bytes 262148 | tf_op jit(solution)/shard_map/jit(dynamic_index_in_dim)/dynamic_slice | solution.py:599
  1.4 1.0 copy-done
  2.4 0.7 copy-done.4
  3.1 0.7 copy-done.6
  3.8 1.7 %later.1 = (bf16[128,1408]{1,0:T(8,128)(2,1)S(1)}, bf16[128,1408]{1,0:T(8,128)(2,1)}) custom-call(s32[1]{0:T(128)} %bitcast.5.where_ref.refs_2_, bf16[128,2048]{1,0:T(8,128)(2,1)S(1)} %copy-done, bf16[128,256]{1,0:T(8,128)(2,1)S(1)} %bitcast.33, f32[32,128]{1,0:T(8,128)S(1)} %bitcast.39, f32[32,128]{1,0:T(8,128)S(1)} %bitcast.42), custom_call_target="tpu_custom_call" | custom-call | flops 1 | bytes 30000000 | tf_op jit(solution)/shard_map/later/pallas_call | solution.py:559
  5.6 1.0 copy-done.2
  6.6 0.4 pack.1
  7.0 3.1 %collective-permute-start.4 = (bf16[128,2688]{1,0:T(8,128)(2,1)S(1)}, bf16[128,2688]{1,0:T(8,128)(2,1)S(1)}, u32[]{:S(2)}, u32[]{:S(2)}) collective-permute-start(bf16[128,2688]{1,0:T(8,128)(2,1)S(1)} %pack.1), channel_id=1, source_target_pairs={{0,4},{4,0},{8,12},{12,8},{1,5},{5,1},{9,13},{13,9},{2,6},{6,2},{1... | collective-permute-start | bytes 2064392 | tf_op jit(solution)/shard_map/ppermute | solution.py:572
  10.1 4.5 %collective-permute-start.2 = (bf16[128,1408]{1,0:T(8,128)(2,1)S(1)}, bf16[128,1408]{1,0:T(8,128)(2,1)S(1)}, u32[]{:S(2)}, u32[]{:S(2)}) collective-permute-start(bf16[128,1408]{1,0:T(8,128)(2,1)S(1)} %get-tuple-element.52.after_ref), channel_id=1, source_target_pairs={{0,8},{4,12},{1,9},{5,13},{2,10},{6,14},{3,11},{7,15},{16,24},{20,... | collective-permute-start | bytes 1081352 | tf_op jit(solution)/shard_map/ppermute | solution.py:644
  14.6 1.3 %collective-permute-start.3 = (bf16[128,1408]{1,0:T(8,128)(2,1)}, bf16[128,1408]{1,0:T(8,128)(2,1)S(1)}, u32[]{:S(2)}, u32[]{:S(2)}) collective-permute-start(bf16[128,1408]{1,0:T(8,128)(2,1)} %get-tuple-element.53), channel_id=1, source_target_pairs={{0,12},{4,8},{1,13},{5,9},{2,14},{6,10},{3,15},{7,11},{16,28},{20,... | collective-permute-start | bytes 1081352 | tf_op jit(solution)/shard_map/ppermute | solution.py:645
  15.9 0.7 broadcast_in_dim.67
  16.7 0.7 select_multiply_fusion
  17.4 8.5 %collective-permute-done.4.msg_ref = bf16[128,2688]{1,0:T(8,128)(2,1)S(1)} collective-permute-done((bf16[128,2688]{1,0:T(8,128)(2,1)S(1)}, bf16[128,2688]{1,0:T(8,128)(2,1)S(1)}, u32[]{:S(2)}, u32[]{:S(2)}) %collective-permute-start.4) | collective-permute-done | bytes 688160 | tf_op jit(solution)/shard_map/ppermute | solution.py:572
  25.9 1.0 copy-done.3
  27.0 0.7 copy-done.5
  27.7 0.7 copy-done.7
  28.4 2.3 %pair.1 = (f32[256,1024]{1,0:T(8,128)S(1)}, f32[256,1024]{1,0:T(8,128)S(1)}, bf16[256,256]{1,0:T(8,128)(2,1)S(1)}) custom-call(s32[1]{0:T(128)} %bitcast.5.where_ref.refs_2_, bf16[128,2048]{1,0:T(8,128)(2,1)S(1)} %copy-done.1, bf16[128,2048]{1,0:T(8,128)(2,1)S(1)} %copy-done.3, bf16[128,256]{1,0:T(8,128)(2,1)S(1)} %bitcast.35, ...), custom_call_target="tpu_custom_call" | custom-call | flops 1 | bytes 30000000 | tf_op jit(solution)/shard_map/pair/pallas_call | solution.py:559
  30.7 3.0 %collective-permute-done.2.refs_0_ = bf16[128,1408]{1,0:T(8,128)(2,1)S(1)} collective-permute-done((bf16[128,1408]{1,0:T(8,128)(2,1)S(1)}, bf16[128,1408]{1,0:T(8,128)(2,1)S(1)}, u32[]{:S(2)}, u32[]{:S(2)}) %collective-permute-start.2) | collective-permute-done | bytes 360480 | tf_op jit(solution)/shard_map/ppermute | solution.py:644
  33.7 6.7 %collective-permute-done.3.refs_1_ = bf16[128,1408]{1,0:T(8,128)(2,1)S(1)} collective-permute-done((bf16[128,1408]{1,0:T(8,128)(2,1)}, bf16[128,1408]{1,0:T(8,128)(2,1)S(1)}, u32[]{:S(2)}, u32[]{:S(2)}) %collective-permute-start.3) | collective-permute-done | bytes 360480 | tf_op jit(solution)/shard_map/ppermute | solution.py:645
  40.4 0.9 mix.1
  41.4 0.5 collective-permute-start.7
  41.9 1.0 collective-permute-done.5
  43.0 1.6 %collective-permute-start.6 = (bf16[128,1024]{1,0:T(8,128)(2,1)S(1)}, bf16[128,1024]{1,0:T(8,128)(2,1)S(1)}, u32[]{:S(2)}, u32[]{:S(2)}) collective-permute-start(bf16[128,1024]{1,0:T(8,128)(2,1)S(1)} %add_convert_fusion.4), channel_id=1, source_target_pairs={{0,2},{2,0},{1,3},{3,1},{4,6},{6,4},{5,7},{7,5},{8,10},{10,8},{9,1... | collective-permute-start | bytes 786440 | tf_op jit(solution)/shard_map/ppermute | solution.py:537
  44.7 6.8 %collective-permute-done.6 = bf16[128,1024]{1,0:T(8,128)(2,1)S(1)} collective-permute-done((bf16[128,1024]{1,0:T(8,128)(2,1)S(1)}, bf16[128,1024]{1,0:T(8,128)(2,1)S(1)}, u32[]{:S(2)}, u32[]{:S(2)}) %collective-permute-start.6) | collective-permute-done | bytes 262176 | tf_op jit(solution)/shard_map/ppermute | solution.py:537
  51.5 5.4 %collective-permute-start.10 = (bf16[128,1024]{1,0:T(8,128)(2,1)S(1)}, bf16[128,1024]{1,0:T(8,128)(2,1)S(1)}, u32[]{:S(2)}, u32[]{:S(2)}) collective-permute-start(bf16[128,1024]{1,0:T(8,128)(2,1)S(1)} %add_convert_fusion.3), channel_id=1, source_target_pairs={{0,4},{4,0},{8,12},{12,8},{1,5},{5,1},{9,13},{13,9},{2,6},{6,2},{1... | collective-permute-start | bytes 786440 | tf_op jit(solution)/shard_map/ppermute | solution.py:572
  56.9 1.5 %collective-permute-start.8 = (bf16[128,1024]{1,0:T(8,128)(2,1)S(1)}, bf16[128,1024]{1,0:T(8,128)(2,1)S(1)}, u32[]{:S(2)}, u32[]{:S(2)}) collective-permute-start(bf16[128,1024]{1,0:T(8,128)(2,1)S(1)} %add_convert_fusion.2.mixed_ref), channel_id=1, source_target_pairs={{0,2},{2,0},{1,3},{3,1},{4,6},{6,4},{5,7},{7,5},{8,10},{10,8},{9,1... | collective-permute-start | bytes 786440 | tf_op jit(solution)/shard_map/ppermute | solution.py:537
  58.4 4.4 %collective-permute-start.9 = (bf16[128,1024]{1,0:T(8,128)(2,1)S(1)}, bf16[128,1024]{1,0:T(8,128)(2,1)S(1)}, u32[]{:S(2)}, u32[]{:S(2)}) collective-permute-start(bf16[128,1024]{1,0:T(8,128)(2,1)S(1)} %add_convert_fusion.3), channel_id=1, source_target_pairs={{0,8},{4,12},{8,0},{12,4},{1,9},{5,13},{9,1},{13,5},{2,10},{6,14},... | collective-permute-start | bytes 786440 | tf_op jit(solution)/shard_map/ppermute | solution.py:572
  62.8 2.7 %collective-permute-done.10 = bf16[128,1024]{1,0:T(8,128)(2,1)S(1)} collective-permute-done((bf16[128,1024]{1,0:T(8,128)(2,1)S(1)}, bf16[128,1024]{1,0:T(8,128)(2,1)S(1)}, u32[]{:S(2)}, u32[]{:S(2)}) %collective-permute-start.10) | collective-permute-done | bytes 262176 | tf_op jit(solution)/shard_map/ppermute | solution.py:572
  65.5 8.3 %collective-permute-done.9 = bf16[128,1024]{1,0:T(8,128)(2,1)S(1)} collective-permute-done((bf16[128,1024]{1,0:T(8,128)(2,1)S(1)}, bf16[128,1024]{1,0:T(8,128)(2,1)S(1)}, u32[]{:S(2)}, u32[]{:S(2)}) %collective-permute-start.9) | collective-permute-done | bytes 262176 | tf_op jit(solution)/shard_map/ppermute | solution.py:572
  73.9 3.0 %collective-permute-start.13 = (bf16[128,1024]{1,0:T(8,128)(2,1)S(1)}, bf16[128,1024]{1,0:T(8,128)(2,1)S(1)}, u32[]{:S(2)}, u32[]{:S(2)}) collective-permute-start(bf16[128,1024]{1,0:T(8,128)(2,1)S(1)} %add.227.refs_0_), channel_id=1, source_target_pairs={{0,8},{4,12},{8,0},{12,4},{1,9},{5,13},{9,1},{13,5},{2,10},{6,14},... | collective-permute-start | bytes 786440 | tf_op jit(solution)/shard_map/ppermute | solution.py:572
  76.8 1.5 %collective-permute-start.14 = (bf16[128,1024]{1,0:T(8,128)(2,1)S(1)}, bf16[128,1024]{1,0:T(8,128)(2,1)S(1)}, u32[]{:S(2)}, u32[]{:S(2)}) collective-permute-start(bf16[128,1024]{1,0:T(8,128)(2,1)S(1)} %add.227.refs_0_), channel_id=1, source_target_pairs={{0,12},{4,8},{8,4},{12,0},{1,13},{5,9},{9,5},{13,1},{2,14},{6,10},... | collective-permute-start | bytes 786440 | tf_op jit(solution)/shard_map/ppermute | solution.py:572
  78.3 5.7 %collective-permute-done.11 = bf16[128,1024]{1,0:T(8,128)(2,1)S(1)} collective-permute-done((bf16[128,1024]{1,0:T(8,128)(2,1)S(1)}, bf16[128,1024]{1,0:T(8,128)(2,1)S(1)}, u32[]{:S(2)}, u32[]{:S(2)}) %collective-permute-start.11) | collective-permute-done | bytes 262176 | tf_op jit(solution)/shard_map/ppermute | solution.py:572
  84.0 10.7 %conditional.1 = (bf16[2,2,16,1024]{3,2,1,0:T(8,128)(2,1)S(1)}) conditional(s32[]{:T(128)} %convert_element_type.99, () %tuple.15, (s32[1]{0:T(128)}, bf16[2048,1024]{1,0:T(8,128)(2,1)}, bf16[128,1024]{1,0:T(8,128)(2,1)S(1)}, bf16[128,1024]{1,0:T(8,128)(2,1)S(1)}, bf16[128,1024]{1,0:T(8,128)(2,1)S(1)}, /*index=5*/bf16[128,1024]{1,0:T(8,128)(2,1)S(1)}, ...), branch_computations={%region_0.1_spmd, %region_1.2_spmd} | conditional | flops 786474 | bytes 33539460 | solution.py:749
  84.0 3.3 %project.2 = bf16[2,2,2,2,16,1024]{5,4,3,2,1,0:T(8,128)(2,1)S(1)} custom-call(s32[1]{0:T(128)} %get-tuple-element.24.where_ref, bf16[2048,1024]{1,0:T(8,128)(2,1)} %get-tuple-element.25.weight_ref, bf16[128,1024]{1,0:T(8,128)(2,1)S(1)} %get-tuple-element.26.refs_0_, bf16[128,1024]{1,0:T(8,128)(2,1)S(1)} %get-tuple-element.27.refs_1_, ...), custom_call_target="tpu_custom_call" | custom-call | flops 1 | bytes 30000000 | tf_op jit(solution)/shard_map/cond/branch_1_fun/project/pallas_call | solution.py:559
  87.5 1.5 %collective-permute-done = bf16[1,2,2,2,16,1024]{5,4,3,2,1,0:T(8,128)(2,1)S(1)} collective-permute-done((bf16[1,2,2,2,16,1024]{5,4,3,2,1,0:T(8,128)(2,1)S(1)}, bf16[1,2,2,2,16,1024]{5,4,3,2,1,0:T(8,128)(2,1)S(1)}, u32[]{:S(2)}, u32[]{:S(2)}) %collective-permute-start) | collective-permute-done | bytes 262176 | tf_op jit(solution)/shard_map/cond/branch_1_fun/ppermute | solution.py:537
  89.0 0.4 collective-permute-start.1
  89.5 5.2 %collective-permute-done.1 = bf16[1,2,2,16,1024]{4,3,2,1,0:T(8,128)(2,1)S(1)} collective-permute-done((bf16[1,2,2,16,1024]{4,3,2,1,0:T(8,128)(2,1)S(1)}, bf16[1,2,2,16,1024]{4,3,2,1,0:T(8,128)(2,1)S(1)}, u32[]{:S(2)}, u32[]{:S(2)}) %collective-permute-start.1) | collective-permute-done | bytes 131104 | tf_op jit(solution)/shard_map/cond/branch_1_fun/ppermute | solution.py:537
  94.7 0.7 collective-permute-done.13.refs_2_
  95.4 0.8 collective-permute-done.12.refs_1_
  96.2 3.3 %project.3 = bf16[2,2,2,2,16,1024]{5,4,3,2,1,0:T(8,128)(2,1)S(1)} custom-call(s32[1]{0:T(128)} %bitcast.5.where_ref.refs_2_, bf16[2048,1024]{1,0:T(8,128)(2,1)} %weight_ref.1, bf16[128,1024]{1,0:T(8,128)(2,1)S(1)} %add.227.refs_0_, bf16[128,1024]{1,0:T(8,128)(2,1)S(1)} %collective-permute-done.12.refs_1_, ...), custom_call_target="tpu_custom_call" | custom-call | flops 1 | bytes 30000000 | tf_op jit(solution)/shard_map/project/pallas_call | solution.py:559
  99.6 1.5 %collective-permute-done.15 = bf16[1,2,2,2,16,1024]{5,4,3,2,1,0:T(8,128)(2,1)S(1)} collective-permute-done((bf16[1,2,2,2,16,1024]{5,4,3,2,1,0:T(8,128)(2,1)S(1)}, bf16[1,2,2,2,16,1024]{5,4,3,2,1,0:T(8,128)(2,1)S(1)}, u32[]{:S(2)}, u32[]{:S(2)}) %collective-permute-start.15) | collective-permute-done | bytes 262176 | tf_op jit(solution)/shard_map/ppermute | solution.py:537
  101.2 0.6 collective-permute-start.16
  101.7 5.0 %collective-permute-done.16 = bf16[1,2,2,16,1024]{4,3,2,1,0:T(8,128)(2,1)S(1)} collective-permute-done((bf16[1,2,2,16,1024]{4,3,2,1,0:T(8,128)(2,1)S(1)}, bf16[1,2,2,16,1024]{4,3,2,1,0:T(8,128)(2,1)S(1)}, u32[]{:S(2)}, u32[]{:S(2)}) %collective-permute-start.16) | collective-permute-done | bytes 131104 | tf_op jit(solution)/shard_map/ppermute | solution.py:537
  106.9 4.0 %collective-permute-start.18 = (bf16[32,1024]{1,0:T(8,128)(2,1)S(1)}, bf16[32,1024]{1,0:T(8,128)(2,1)S(1)}, u32[]{:S(2)}, u32[]{:S(2)}) collective-permute-start(bf16[32,1024]{1,0:T(8,128)(2,1)S(1)} %bitcast.53), channel_id=1, source_target_pairs={{0,8},{4,12},{8,0},{12,4},{1,9},{5,13},{9,1},{13,5},{2,10},{6,14},... | collective-permute-start | bytes 196616 | tf_op jit(solution)/shard_map/ppermute | solution.py:572
  110.8 1.5 %collective-permute-start.19 = (bf16[32,1024]{1,0:T(8,128)(2,1)S(1)}, bf16[32,1024]{1,0:T(8,128)(2,1)S(1)}, u32[]{:S(2)}, u32[]{:S(2)}) collective-permute-start(bf16[32,1024]{1,0:T(8,128)(2,1)S(1)} %bitcast.52), channel_id=1, source_target_pairs={{0,12},{4,8},{8,4},{12,0},{1,13},{5,9},{9,5},{13,1},{2,14},{6,10},... | collective-permute-start | bytes 196616 | tf_op jit(solution)/shard_map/ppermute | solution.py:572
  112.4 3.3 %collective-permute-done.18.refs_2_ = bf16[32,1024]{1,0:T(8,128)(2,1)S(1)} collective-permute-done((bf16[32,1024]{1,0:T(8,128)(2,1)S(1)}, bf16[32,1024]{1,0:T(8,128)(2,1)S(1)}, u32[]{:S(2)}, u32[]{:S(2)}) %collective-permute-start.18) | collective-permute-done | bytes 65568 | tf_op jit(solution)/shard_map/ppermute | solution.py:572
  115.7 1.4 %collective-permute-done.19.refs_3_ = bf16[32,1024]{1,0:T(8,128)(2,1)S(1)} collective-permute-done((bf16[32,1024]{1,0:T(8,128)(2,1)S(1)}, bf16[32,1024]{1,0:T(8,128)(2,1)S(1)}, u32[]{:S(2)}, u32[]{:S(2)}) %collective-permute-start.19) | collective-permute-done | bytes 65568 | tf_op jit(solution)/shard_map/ppermute | solution.py:572
  117.3 0.7 place.1
  (43 shorter events, 1.4 us)
Async XLA Ops:
  0.0 40.4 %copy-start.8 = (bf16[256,256]{1,0:T(8,128)(2,1)S(1)}, bf16[256,256]{1,0:T(8,128)(2,1)}, u32[]{:S(2)}) copy-start(bf16[256,256]{1,0:T(8,128)(2,1)} %constant.214.clone.refs_7_) | copy-start | bytes 393220
  0.0 25.9 %copy-start.1 = (bf16[128,2048]{1,0:T(8,128)(2,1)S(1)}, bf16[128,2048]{1,0:T(8,128)(2,1)}, u32[]{:S(2)}) copy-start(bf16[128,2048]{1,0:T(8,128)(2,1)} %x_ref.5) | copy-start | bytes 1572868
  1.4 1.0 copy-start
  2.4 0.7 copy-start.4
  3.1 0.7 copy-start.6
  5.6 1.0 copy-start.2
  7.0 77.0 %copy-start.9 = (s32[2048]{0:T(1024)S(1)}, s32[2048]{0:T(1024)}, u32[]{:S(2)}) copy-start(s32[2048]{0:T(1024)} %param.23) | copy-start | bytes 24580
  7.0 18.9 %collective-permute-start.4 = (bf16[128,2688]{1,0:T(8,128)(2,1)S(1)}, bf16[128,2688]{1,0:T(8,128)(2,1)S(1)}, u32[]{:S(2)}, u32[]{:S(2)}) collective-permute-start(bf16[128,2688]{1,0:T(8,128)(2,1)S(1)} %pack.1), channel_id=1, source_target_pairs={{0,4},{4,0},{8,12},{12,8},{1,5},{5,1},{9,13},{13,9},{2,6},{6,2},{1... | collective-permute-start | bytes 2064392 | tf_op jit(solution)/shard_map/ppermute | solution.py:572
  10.1 23.6 %collective-permute-start.2 = (bf16[128,1408]{1,0:T(8,128)(2,1)S(1)}, bf16[128,1408]{1,0:T(8,128)(2,1)S(1)}, u32[]{:S(2)}, u32[]{:S(2)}) collective-permute-start(bf16[128,1408]{1,0:T(8,128)(2,1)S(1)} %get-tuple-element.52.after_ref), channel_id=1, source_target_pairs={{0,8},{4,12},{1,9},{5,13},{2,10},{6,14},{3,11},{7,15},{16,24},{20,... | collective-permute-start | bytes 1081352 | tf_op jit(solution)/shard_map/ppermute | solution.py:644
  14.6 25.8 %collective-permute-start.3 = (bf16[128,1408]{1,0:T(8,128)(2,1)}, bf16[128,1408]{1,0:T(8,128)(2,1)S(1)}, u32[]{:S(2)}, u32[]{:S(2)}) collective-permute-start(bf16[128,1408]{1,0:T(8,128)(2,1)} %get-tuple-element.53), channel_id=1, source_target_pairs={{0,12},{4,8},{1,13},{5,9},{2,14},{6,10},{3,15},{7,11},{16,28},{20,... | collective-permute-start | bytes 1081352 | tf_op jit(solution)/shard_map/ppermute | solution.py:645
  25.9 1.0 copy-start.3
  27.0 0.7 copy-start.5
  27.7 0.7 copy-start.7
  41.3 1.6 %collective-permute-start.5 = (bf16[128,1024]{1,0:T(8,128)(2,1)S(1)}, bf16[128,1024]{1,0:T(8,128)(2,1)S(1)}, u32[]{:S(2)}, u32[]{:S(2)}) collective-permute-start(bf16[128,1024]{1,0:T(8,128)(2,1)S(1)} %get-tuple-element.57), channel_id=1, source_target_pairs={{0,1},{1,0},{2,3},{3,2},{4,5},{5,4},{6,7},{7,6},{8,9},{9,8},{10,11... | collective-permute-start | bytes 786440 | tf_op jit(solution)/shard_map/ppermute | solution.py:537
  41.4 3.2 %collective-permute-start.7 = (bf16[128,1024]{1,0:T(8,128)(2,1)S(1)}, bf16[128,1024]{1,0:T(8,128)(2,1)S(1)}, u32[]{:S(2)}, u32[]{:S(2)}) collective-permute-start(bf16[128,1024]{1,0:T(8,128)(2,1)S(1)} %get-tuple-element.58), channel_id=1, source_target_pairs={{0,1},{1,0},{2,3},{3,2},{4,5},{5,4},{6,7},{7,6},{8,9},{9,8},{10,11... | collective-permute-start | bytes 786440 | tf_op jit(solution)/shard_map/ppermute | solution.py:537
  43.0 8.4 %collective-permute-start.6 = (bf16[128,1024]{1,0:T(8,128)(2,1)S(1)}, bf16[128,1024]{1,0:T(8,128)(2,1)S(1)}, u32[]{:S(2)}, u32[]{:S(2)}) collective-permute-start(bf16[128,1024]{1,0:T(8,128)(2,1)S(1)} %add_convert_fusion.4), channel_id=1, source_target_pairs={{0,2},{2,0},{1,3},{3,1},{4,6},{6,4},{5,7},{7,5},{8,10},{10,8},{9,1... | collective-permute-start | bytes 786440 | tf_op jit(solution)/shard_map/ppermute | solution.py:537
  51.5 14.0 %collective-permute-start.10 = (bf16[128,1024]{1,0:T(8,128)(2,1)S(1)}, bf16[128,1024]{1,0:T(8,128)(2,1)S(1)}, u32[]{:S(2)}, u32[]{:S(2)}) collective-permute-start(bf16[128,1024]{1,0:T(8,128)(2,1)S(1)} %add_convert_fusion.3), channel_id=1, source_target_pairs={{0,4},{4,0},{8,12},{12,8},{1,5},{5,1},{9,13},{13,9},{2,6},{6,2},{1... | collective-permute-start | bytes 786440 | tf_op jit(solution)/shard_map/ppermute | solution.py:572
  56.9 8.6 %collective-permute-start.8 = (bf16[128,1024]{1,0:T(8,128)(2,1)S(1)}, bf16[128,1024]{1,0:T(8,128)(2,1)S(1)}, u32[]{:S(2)}, u32[]{:S(2)}) collective-permute-start(bf16[128,1024]{1,0:T(8,128)(2,1)S(1)} %add_convert_fusion.2.mixed_ref), channel_id=1, source_target_pairs={{0,2},{2,0},{1,3},{3,1},{4,6},{6,4},{5,7},{7,5},{8,10},{10,8},{9,1... | collective-permute-start | bytes 786440 | tf_op jit(solution)/shard_map/ppermute | solution.py:537
  58.4 15.4 %collective-permute-start.9 = (bf16[128,1024]{1,0:T(8,128)(2,1)S(1)}, bf16[128,1024]{1,0:T(8,128)(2,1)S(1)}, u32[]{:S(2)}, u32[]{:S(2)}) collective-permute-start(bf16[128,1024]{1,0:T(8,128)(2,1)S(1)} %add_convert_fusion.3), channel_id=1, source_target_pairs={{0,8},{4,12},{8,0},{12,4},{1,9},{5,13},{9,1},{13,5},{2,10},{6,14},... | collective-permute-start | bytes 786440 | tf_op jit(solution)/shard_map/ppermute | solution.py:572
  73.8 10.2 %collective-permute-start.11 = (bf16[128,1024]{1,0:T(8,128)(2,1)S(1)}, bf16[128,1024]{1,0:T(8,128)(2,1)S(1)}, u32[]{:S(2)}, u32[]{:S(2)}) collective-permute-start(bf16[128,1024]{1,0:T(8,128)(2,1)S(1)} %collective-permute-done.9), channel_id=1, source_target_pairs={{0,4},{4,0},{8,12},{12,8},{1,5},{5,1},{9,13},{13,9},{2,6},{6,2},{1... | collective-permute-start | bytes 786440 | tf_op jit(solution)/shard_map/ppermute | solution.py:572
  73.9 21.5 %collective-permute-start.13 = (bf16[128,1024]{1,0:T(8,128)(2,1)S(1)}, bf16[128,1024]{1,0:T(8,128)(2,1)S(1)}, u32[]{:S(2)}, u32[]{:S(2)}) collective-permute-start(bf16[128,1024]{1,0:T(8,128)(2,1)S(1)} %add.227.refs_0_), channel_id=1, source_target_pairs={{0,8},{4,12},{8,0},{12,4},{1,9},{5,13},{9,1},{13,5},{2,10},{6,14},... | collective-permute-start | bytes 786440 | tf_op jit(solution)/shard_map/ppermute | solution.py:572
  76.8 18.5 %collective-permute-start.14 = (bf16[128,1024]{1,0:T(8,128)(2,1)S(1)}, bf16[128,1024]{1,0:T(8,128)(2,1)S(1)}, u32[]{:S(2)}, u32[]{:S(2)}) collective-permute-start(bf16[128,1024]{1,0:T(8,128)(2,1)S(1)} %add.227.refs_0_), channel_id=1, source_target_pairs={{0,12},{4,8},{8,4},{12,0},{1,13},{5,9},{9,5},{13,1},{2,14},{6,10},... | collective-permute-start | bytes 786440 | tf_op jit(solution)/shard_map/ppermute | solution.py:572
  84.0 12.2 %collective-permute-start.12 = (bf16[128,1024]{1,0:T(8,128)(2,1)S(1)}, bf16[128,1024]{1,0:T(8,128)(2,1)S(1)}, u32[]{:S(2)}, u32[]{:S(2)}) collective-permute-start(bf16[128,1024]{1,0:T(8,128)(2,1)S(1)} %add.227.refs_0_), channel_id=1, source_target_pairs={{0,4},{4,0},{8,12},{12,8},{1,5},{5,1},{9,13},{13,9},{2,6},{6,2},{1... | collective-permute-start | bytes 786440 | tf_op jit(solution)/shard_map/ppermute | solution.py:572
  87.3 1.6 %collective-permute-start = (bf16[1,2,2,2,16,1024]{5,4,3,2,1,0:T(8,128)(2,1)S(1)}, bf16[1,2,2,2,16,1024]{5,4,3,2,1,0:T(8,128)(2,1)S(1)}, u32[]{:S(2)}, u32[]{:S(2)}) collective-permute-start(bf16[1,2,2,2,16,1024]{5,4,3,2,1,0:T(8,128)(2,1)S(1)} %constant_dynamic-slice_fusion), channel_id=1, source_target_pairs={{0,1},{1,0},{2,3},{3,2},{4,5},{5,4},{6,7},{7,6},{8,9},{9,8},{10,11... | collective-permute-start | bytes 786440 | tf_op jit(solution)/shard_map/cond/branch_1_fun/ppermute | solution.py:537
  89.0 5.6 %collective-permute-start.1 = (bf16[1,2,2,16,1024]{4,3,2,1,0:T(8,128)(2,1)S(1)}, bf16[1,2,2,16,1024]{4,3,2,1,0:T(8,128)(2,1)S(1)}, u32[]{:S(2)}, u32[]{:S(2)}) collective-permute-start(bf16[1,2,2,16,1024]{4,3,2,1,0:T(8,128)(2,1)S(1)} %dynamic-slice_bitcast_fusion), channel_id=1, source_target_pairs={{0,2},{2,0},{1,3},{3,1},{4,6},{6,4},{5,7},{7,5},{8,10},{10,8},{9,1... | collective-permute-start | bytes 393224 | tf_op jit(solution)/shard_map/cond/branch_1_fun/ppermute | solution.py:537
  99.5 1.6 %collective-permute-start.15 = (bf16[1,2,2,2,16,1024]{5,4,3,2,1,0:T(8,128)(2,1)S(1)}, bf16[1,2,2,2,16,1024]{5,4,3,2,1,0:T(8,128)(2,1)S(1)}, u32[]{:S(2)}, u32[]{:S(2)}) collective-permute-start(bf16[1,2,2,2,16,1024]{5,4,3,2,1,0:T(8,128)(2,1)S(1)} %constant_dynamic-slice_fusion.3), channel_id=1, source_target_pairs={{0,1},{1,0},{2,3},{3,2},{4,5},{5,4},{6,7},{7,6},{8,9},{9,8},{10,11... | collective-permute-start | bytes 786440 | tf_op jit(solution)/shard_map/ppermute | solution.py:537
  101.2 5.6 %collective-permute-start.16 = (bf16[1,2,2,16,1024]{4,3,2,1,0:T(8,128)(2,1)S(1)}, bf16[1,2,2,16,1024]{4,3,2,1,0:T(8,128)(2,1)S(1)}, u32[]{:S(2)}, u32[]{:S(2)}) collective-permute-start(bf16[1,2,2,16,1024]{4,3,2,1,0:T(8,128)(2,1)S(1)} %dynamic-slice_bitcast_fusion.1), channel_id=1, source_target_pairs={{0,2},{2,0},{1,3},{3,1},{4,6},{6,4},{5,7},{7,5},{8,10},{10,8},{9,1... | collective-permute-start | bytes 393224 | tf_op jit(solution)/shard_map/ppermute | solution.py:537
  106.9 8.8 %collective-permute-start.18 = (bf16[32,1024]{1,0:T(8,128)(2,1)S(1)}, bf16[32,1024]{1,0:T(8,128)(2,1)S(1)}, u32[]{:S(2)}, u32[]{:S(2)}) collective-permute-start(bf16[32,1024]{1,0:T(8,128)(2,1)S(1)} %bitcast.53), channel_id=1, source_target_pairs={{0,8},{4,12},{8,0},{12,4},{1,9},{5,13},{9,1},{13,5},{2,10},{6,14},... | collective-permute-start | bytes 196616 | tf_op jit(solution)/shard_map/ppermute | solution.py:572
  110.8 6.2 %collective-permute-start.19 = (bf16[32,1024]{1,0:T(8,128)(2,1)S(1)}, bf16[32,1024]{1,0:T(8,128)(2,1)S(1)}, u32[]{:S(2)}, u32[]{:S(2)}) collective-permute-start(bf16[32,1024]{1,0:T(8,128)(2,1)S(1)} %bitcast.52), channel_id=1, source_target_pairs={{0,12},{4,8},{8,4},{12,0},{1,13},{5,9},{9,5},{13,1},{2,14},{6,10},... | collective-permute-start | bytes 196616 | tf_op jit(solution)/shard_map/ppermute | solution.py:572
  112.3 5.0 %collective-permute-start.17 = (bf16[32,1024]{1,0:T(8,128)(2,1)S(1)}, bf16[32,1024]{1,0:T(8,128)(2,1)S(1)}, u32[]{:S(2)}, u32[]{:S(2)}) collective-permute-start(bf16[32,1024]{1,0:T(8,128)(2,1)S(1)} %bitcast.54), channel_id=1, source_target_pairs={{0,4},{4,0},{8,12},{12,8},{1,5},{5,1},{9,13},{13,9},{2,6},{6,2},{1... | collective-permute-start | bytes 196616 | tf_op jit(solution)/shard_map/ppermute | solution.py:572

commit v3 on v2

--- a/solution.py
+++ b/solution.py
@@ -21,6 +21,7 @@
 LANES = 128
 H_BLOCK = 256
 COST = pl.CostEstimate(flops=1, transcendentals=0, bytes_accessed=30_000_000)
+SMALL = pl.CostEstimate(flops=1, transcendentals=0, bytes_accessed=1)
 f32 = jnp.float32
 bf16 = jnp.bfloat16
 PARAMS = pltpu.CompilerParams(vmem_limit_bytes=16 * 2**20)
@@ -179,104 +180,65 @@
         copy.wait()
 
 
-def later_kernel(
-    where_ref,
-    x_ref,
-    b_ref,
-    step_ref,
-    decay_ref,
-    straight_ref,
-    cross_ref,
-    x_own,
-    b_own,
-    step_own,
-    decay_own,
-    sems,
-):
-    copies = start_all(
-        [
-            pltpu.make_async_copy(ref, own, sems.at[index])
-            for index, (ref, own) in enumerate(
-                (
-                    (decay_ref, decay_own),
-                    (step_ref, step_own),
-                    (b_ref, b_own),
-                    (x_ref, x_own),
-                )
-            )
-        ]
-    )
-    tokens, width = x_ref.shape
-    half, heads, states = width // 2, step_ref.shape[0] // 2, b_ref.shape[1]
-    member = where_ref[0]
-    expand = expansion(heads)
-    triangle = causal_mask(tokens).astype(f32).astype(bf16)
-    wait_all(copies[:2])
-    cumul = exact_dot(triangle, decay_own[...].T)
-    total = cumul[tokens - 1 : tokens, :]
-    scale = jnp.exp(total - cumul) * step_own[...].T
-    kept = jnp.exp(total)
-
-    def pick(value, which):
-        return jnp.where(which == 0, value[:, :heads], value[:, heads:])
-
-    base = half + states
-    copies[2].wait()
-    copies[3].wait()
-    for out_ref, which in ((straight_ref, member), (cross_ref, 1 - member)):
-        wide = spread(pick(scale, which), expand)
-        out_ref[:, :half] = (x_own[:, half_at(which, half)].astype(f32) * wide).astype(bf16)
-        out_ref[:, half:base] = b_own[...]
-        out_ref[:, base:] = jnp.zeros((tokens, out_ref.shape[1] - base), bf16)
-        for index, term in enumerate(parts_of(pick(kept, which), 2)):
-            out_ref[:, base + index * heads : base + (index + 1) * heads] = jnp.broadcast_to(
-                term, (tokens, heads)
-            )
+def block_rows(index, size):
+    return slice(index * size, (index + 1) * size)
 
 
 def pack_kernel(
     where_ref,
-    x_ref,
-    gate_ref,
+    x_mine_ref,
+    x_other_ref,
     b_ref,
     c_ref,
     step_ref,
     decay_ref,
-    after_ref,
-    pair_ref,
-    step_own,
-    decay_own,
-    sems,
+    mine_ref,
+    other_ref,
+    straight_ref,
+    cross_ref,
 ):
-    tokens, width = x_ref.shape
-    half, heads, states = width // 2, step_ref.shape[0] // 2, b_ref.shape[1]
-    other = 1 - where_ref[0]
-    base = 2 * half + 2 * states
-    copies = start_all(
-        [
-            pltpu.make_async_copy(ref, own, sems.at[index])
-            for index, (ref, own) in enumerate(
-                (
-                    (decay_ref, decay_own),
-                    (step_ref, step_own),
-                    (x_ref.at[:, half_at(other, half)], pair_ref.at[:, :half]),
-                    (gate_ref.at[:, half_at(other, half)], pair_ref.at[:, half : 2 * half]),
-                    (b_ref, pair_ref.at[:, 2 * half : 2 * half + states]),
-                    (c_ref, pair_ref.at[:, 2 * half + states : base]),
-                )
-            )
-        ]
-    )
-
-    def pick(value):
-        return jnp.where(other == 0, value[:heads, :], value[heads:, :]).T
-
-    wait_all(copies[:2])
-    pair_ref[:, base:] = jnp.zeros((tokens, pair_ref.shape[1] - base), bf16)
-    terms = parts_of(pick(step_own[...]), 3) + parts_of(pick(decay_own[...]), 3)
-    for index, term in enumerate(terms):
-        pair_ref[:, base + index * heads : base + (index + 1) * heads] = term
-    wait_all(copies[2:])
+    tokens, states = b_ref.shape
+    half = x_mine_ref.shape[1]
+    heads = step_ref.shape[0] // 2
+    member = where_ref[0]
+    triangle = causal_mask(tokens).astype(f32).astype(bf16)
+    step = step_ref[...].T
+    decay = decay_ref[...].T
+    cumul = exact_dot(triangle, decay)
+    total = cumul[tokens - 1 : tokens, :]
+    scale = jnp.exp(total - cumul) * step
+    kept = jnp.exp(total)
+
+    def pick(value, which):
+        return jnp.where(which == 0, value[:, :heads], value[:, heads:])
+
+    other_ref[:, :half] = x_other_ref[...]
+    for out_ref, base, which in ((mine_ref, 0, member), (other_ref, half, 1 - member)):
+        out_ref[:, base : base + states] = b_ref[...]
+        out_ref[:, base + states : base + 2 * states] = c_ref[...]
+        base += 2 * states
+        out_ref[:, base:] = jnp.zeros((tokens, out_ref.shape[1] - base), bf16)
+        terms = parts_of(pick(step, which), 3) + parts_of(pick(decay, which), 3)
+        for index, term in enumerate(terms):
+            out_ref[:, base + index * heads : base + (index + 1) * heads] = term
+    expand = expansion(heads)
+    for out_ref, x_ref, which in (
+        (straight_ref, x_mine_ref, member),
+        (cross_ref, x_other_ref, 1 - member),
+    ):
+        wide = spread(pick(scale, which), expand)
+        weighted = (x_ref[...].astype(f32) * wide).astype(bf16)
+        for index in range(half // LANES):
+            out_ref[block_rows(index, tokens), :] = weighted[:, block_rows(index, LANES)]
+        for index in range(states // LANES):
+            out_ref[block_rows(half // LANES + index, tokens), :] = b_ref[
+                :, block_rows(index, LANES)
+            ]
+        base = (half + states) // LANES * tokens
+        rows = out_ref.shape[0] - base
+        out_ref[base:, :] = jnp.zeros((rows, LANES), bf16)
+        for index, term in enumerate(parts_of(pick(kept, which), 2)):
+            out_ref[base:, block_rows(index, heads)] = jnp.broadcast_to(term, (rows, heads))
 
 
 def expansion(heads):
@@ -289,66 +251,36 @@
 def pair_kernel(
     where_ref,
     x_ref,
-    gate_ref,
-    b_ref,
-    c_ref,
-    step_ref,
-    decay_ref,
+    meta_ref,
     msg_ref,
     skip_ref,
     own_ref,
     far_ref,
     c_pair_ref,
     x_both,
-    gate_both,
     b_both,
     step_both,
     decay_both,
-    step_own,
-    decay_own,
-    sems,
 ):
-    tokens, width = x_ref.shape
-    half, heads, states = width // 2, step_ref.shape[0] // 2, b_ref.shape[1]
+    tokens, half = x_ref.shape
+    states = c_pair_ref.shape[1]
+    heads = half // P_SIZE
     member = where_ref[0]
-    mine, theirs = half_at(member, tokens), half_at(1 - member, tokens)
-    copies = start_all(
-        [
-            pltpu.make_async_copy(ref, own, sems.at[index])
-            for index, (ref, own) in enumerate(
-                (
-                    (decay_ref, decay_own),
-                    (step_ref, step_own),
-                    (b_ref, b_both.at[mine, :]),
-                    (c_ref, c_pair_ref.at[mine, :]),
-                    (x_ref.at[:, half_at(member, half)], x_both.at[mine, :]),
-                    (gate_ref.at[:, half_at(member, half)], gate_both.at[mine, :]),
-                )
-            )
-        ]
-    )
-
-    def pick(value):
-        return jnp.where(member == 0, value[:heads, :], value[heads:, :]).T
-
-    x_both[theirs, :] = msg_ref[:, :half]
-    gate_both[theirs, :] = msg_ref[:, half : 2 * half]
-    b_both[theirs, :] = msg_ref[:, 2 * half : 2 * half + states]
-    base = 2 * half + 2 * states
-    c_pair_ref[theirs, :] = msg_ref[:, 2 * half + states : base]
-
-    def received(first):
-        terms = [
-            msg_ref[:, base + index * heads : base + (index + 1) * heads].astype(f32)
-            for index in range(first, first + 3)
-        ]
-        return (terms[2] + terms[1]) + terms[0]
-
-    step_both[theirs, :] = received(0)
-    decay_both[theirs, :] = received(3)
-    wait_all(copies)
-    step_both[mine, :] = pick(step_own[...])
-    decay_both[mine, :] = pick(decay_own[...])
+    for which, x, meta in (
+        (member, x_ref, meta_ref),
+        (1 - member, msg_ref.at[:, :half], msg_ref.at[:, half:]),
+    ):
+        rows = half_at(which, tokens)
+        x_both[rows, :] = x[...]
+        b_both[rows, :] = meta[:, :states]
+        c_pair_ref[rows, :] = meta[:, states : 2 * states]
+        for index, both in enumerate((step_both, decay_both)):
+            base = 2 * states + 3 * index * heads
+            terms = [
+                meta[:, base + term * heads : base + (term + 1) * heads].astype(f32)
+                for term in range(3)
+            ]
+            both[rows, :] = (terms[2] + terms[1]) + terms[0]
 
     span = 2 * tokens
     causal = causal_mask(span)
@@ -382,40 +314,42 @@
                     )
                     values.append(spans[earlier][place])
             own = dot(jnp.concatenate(mixings, axis=1), jnp.concatenate(values, axis=0))
-            own = own + x_both[rows, at].astype(f32) * skip[:, at]
-            gate = gate_both[rows, at].astype(f32)
-            gate = gate / (1.0 + jnp.exp(-gate))
-            own_ref[rows, at] = own * gate
-            wide = sum(dot(term[rows, :], expand[:, at]) for term in reach)
-            far_ref[rows, at] = wide * gate
+            own_ref[rows, at] = own + x_both[rows, at].astype(f32) * skip[:, at]
+            far_ref[rows, at] = sum(dot(term[rows, :], expand[:, at]) for term in reach)
 
 
 def gate_mix_kernel(count, pieces, *refs):
-    straight, cross = refs[:count], refs[count : 2 * count]
-    where_ref, c_ref, own_ref, far_ref, gain_ref, table_ref = refs[2 * count : -2]
-    out_refs = refs[-2:]
+    sent = refs[: 2 * count]
+    where_ref, gate_ref, gate_pair_ref, c_ref, own_ref, far_ref, gain_ref, table_ref = refs[
+        2 * count : -3
+    ]
+    out_refs, gate_both = refs[-3:-1], refs[-1]
     span, half = own_ref.shape
+    tokens = span // 2
     states = c_ref.shape[1]
     heads = half // P_SIZE
-    base = half + states
     member = where_ref[0]
     c_pair = c_ref[...]
     expand = expansion(heads)
 
-    def kept(msg_ref):
-        return (
-            dot(msg_ref[:16, base : base + heads], expand)
-            + dot(msg_ref[:16, base + heads : base + 2 * heads], expand)
-        )[:1, :]
-
-    inners, factors, pair_kept = [], [], []
-    for straight_ref, cross_ref in zip(straight, cross):
-        inners.append(
-            [dot_nt(c_pair, ref[:, half:base]).astype(bf16) for ref in (straight_ref, cross_ref)]
-        )
-        one, two = kept(straight_ref), kept(cross_ref)
+    for which, gate in ((member, gate_ref), (1 - member, gate_pair_ref)):
+        gate_both[half_at(which, tokens), :] = gate[...]
+
+    def columns(ref, start, size):
+        blocks = range(start // LANES, (start + size) // LANES)
+        return jnp.concatenate([ref[block_rows(index, tokens), :] for index in blocks], axis=1)
+
+    def kept(ref):
+        base = (half + states) // LANES * tokens
+        high, low = (ref[base:, block_rows(index, heads)] for index in range(2))
+        return (dot(high, expand) + dot(low, expand))[:1, :]
+
+    inners = [dot_nt(c_pair, columns(ref, half, states)).astype(bf16) for ref in sent]
+    factors, pair_kept = [], []
+    for k in range(count):
+        one, two = kept(sent[2 * k]), kept(sent[2 * k + 1])
         pair_kept.append(one * two)
-        factors.append((jnp.where(member == 0, two, 1.0), jnp.where(member == 0, 1.0, one)))
+        factors += [jnp.where(member == 0, two, 1.0), jnp.where(member == 0, 1.0, one)]
     gain = gain_ref[:, half_at(member, half)]
     table = table_ref[...]
     parts = []
@@ -428,11 +362,16 @@
             pre = own_ref[:, at]
             carried = None
             for k in reversed(range(count)):
-                term = factors[k][0][:, at] * dot(inners[k][0], straight[k][:, at])
-                term = term + factors[k][1][:, at] * dot(inners[k][1], cross[k][:, at])
+                term = 0.0
+                for j in (2 * k, 2 * k + 1):
+                    term = term + factors[j][:, at] * dot(
+                        inners[j], columns(sent[j], begin, H_BLOCK)
+                    )
                 carried = term if carried is None else term + pair_kept[k][:, at] * carried
             if carried is not None:
                 pre = pre + far_ref[:, at] * carried
+            gate = gate_both[:, at].astype(f32)
+            pre = pre * (gate / (1.0 + jnp.exp(-gate)))
             square = square + jnp.sum(pre * pre, axis=1, keepdims=True)
             pres.append(pre)
         inverse = lax.rsqrt(square * (1.0 / norm_width) + norm_eps)
@@ -552,7 +491,7 @@
     return value[0]
 
 
-def call(kernel, out_shape, name, args, scalars=0, anywhere=0, scratch=(), params=PARAMS):
+def call(kernel, out_shape, name, args, scalars=0, anywhere=0, scratch=(), params=PARAMS, cost=COST):
     specs = [pl.BlockSpec(memory_space=pltpu.SMEM)] * scalars
     specs += [pl.BlockSpec(memory_space=pltpu.HBM)] * anywhere
     specs += [pl.BlockSpec(memory_space=pltpu.VMEM)] * (len(args) - scalars - anywhere)
@@ -562,7 +501,7 @@
         in_specs=specs,
         scratch_shapes=scratch,
         compiler_params=params,
-        cost_estimate=COST,
+        cost_estimate=cost,
         name=name,
     )(*args)
 
@@ -605,44 +544,26 @@
     def padded(columns):
         return pl.cdiv(columns, LANES) * LANES
 
-    step, decay = step_size.T, log_decay.T
-    later = shape(tokens, half + states + padded(2 * half_heads), bf16)
-    head_buffer = pltpu.VMEM(step.shape, f32)
-    straight, cross = call(
-        later_kernel,
-        (later, later),
-        "later",
-        (where, x_in, b_group, step, decay),
+    def half_of(value, which):
+        return lax.dynamic_slice_in_dim(value, which * half, half, 1)
+
+    x_mine, x_other = half_of(x_in, member), half_of(x_in, 1 - member)
+    gate_mine, gate_other = half_of(gate_in, member), half_of(gate_in, 1 - member)
+    with_pair = shape(tokens, 2 * states + padded(6 * half_heads), bf16)
+    with_later = shape((half + states) // LANES * tokens + 16, LANES, bf16)
+    meta_mine, to_pair, straight, cross = call(
+        pack_kernel,
+        (with_pair, shape(tokens, half + with_pair.shape[1], bf16), with_later, with_later),
+        "pack",
+        (where, x_mine, x_other, b_group, c_group, step_size.T, log_decay.T),
         1,
-        4,
-        (
-            pltpu.VMEM((tokens, width), bf16),
-            pltpu.VMEM((tokens, states), bf16),
-            head_buffer,
-            head_buffer,
-            pltpu.SemaphoreType.DMA((4,)),
-        ),
     )
-    local = (x_in, gate_in, b_group, c_group, step, decay)
-    to_pair = call(
-        pack_kernel,
-        shape(tokens, 2 * half + 2 * states + padded(6 * half_heads), bf16),
-        "pack",
-        (where, *local, straight),
-        1,
-        7,
-        (
-            head_buffer,
-            head_buffer,
-            pltpu.SemaphoreType.DMA((6,)),
-        ),
-    )
-    to_pair = swap_seq(to_pair, 1)
-    straights, crosses = [], []
+    sent = []
     for ahead in range(1, pairs):
         firsts = range(seq_count - 2 * ahead)
-        straights.append(lax.ppermute(straight, "seq", [(k, k + 2 * ahead) for k in firsts]))
-        crosses.append(lax.ppermute(cross, "seq", [(k, (k ^ 1) + 2 * ahead) for k in firsts]))
+        sent.append(lax.ppermute(straight, "seq", [(k, k + 2 * ahead) for k in firsts]))
+        sent.append(lax.ppermute(cross, "seq", [(k, (k ^ 1) + 2 * ahead) for k in firsts]))
+    from_pair, gate_pair = swap_seq(to_pair, 1), swap_seq(gate_other, 1)
 
     span = 2 * tokens
     own, far, c_pair = call(
@@ -653,34 +574,38 @@
             shape(span, states, bf16),
         ),
         "pair",
-        (where, *local, to_pair, jnp.repeat(skip, P_SIZE)[None, :]),
+        (
+            where,
+            x_mine,
+            meta_mine,
+            from_pair,
+            jnp.repeat(skip, P_SIZE)[None, :],
+        ),
         1,
-        6,
+        0,
         (
-            pltpu.VMEM((span, half), bf16),
             pltpu.VMEM((span, half), bf16),
             pltpu.VMEM((span, states), bf16),
             pltpu.VMEM((span, half_heads), f32),
             pltpu.VMEM((span, half_heads), f32),
-            head_buffer,
-            head_buffer,
-            pltpu.SemaphoreType.DMA((6,)),
         ),
+        cost=SMALL,
     )
     signed_gain = (jnp.where(walsh_sign == 1, 1.0, -1.0) * norm_gain)[None, :]
     owners = chan_count * sub_count
     size = tokens // (2 * owners)
-    count = len(straights)
+    count = len(sent) // 2
     chunks = pl.pallas_call(
         functools.partial(gate_mix_kernel, count, span // size),
         out_shape=(shape(tokens, half, bf16),) * 2,
         in_specs=[pl.BlockSpec(memory_space=pltpu.VMEM)] * (2 * count)
         + [pl.BlockSpec(memory_space=pltpu.SMEM)]
-        + [pl.BlockSpec(memory_space=pltpu.VMEM)] * 5,
+        + [pl.BlockSpec(memory_space=pltpu.VMEM)] * 7,
+        scratch_shapes=[pltpu.VMEM((span, half), bf16)],
         compiler_params=PARAMS,
         cost_estimate=COST,
         name="mix",
-    )(*straights, *crosses, where, c_pair, own, far, signed_gain, table)
+    )(*sent, where, gate_mine, gate_pair, c_pair, own, far, signed_gain, table)
 
     def add_across(mixed, axis, bit, received):
         place = lax.axis_index(axis)

time: 119 us -> 111 us (0.933)
  starting transfers between devices: 33.4 us -> 30.9 us
  local copies, waits for them, and re-layouts: 8.23 us -> 6.49 us
  waiting for transfers between devices: 62.2 us -> 60.5 us
  Pallas kernels: 12.6 us -> 11.1 us
    ppermute x10 -> x11, waiting for transfers between devices: 31.5 us -> 41.7 us  [swap_seq(): return lax.ppermute(value, 'seq', [(k, k ^ distance) for k in range(count)])]
    ppermute x1, waiting for transfers between devices: 6.72 us -> 0.01 us  [paired_body(): lax.ppermute(cross, 'seq', [(k, (k ^ 1) + 2 * ahead) for k in firsts])]
    ppermute x10 -> x11, starting transfers between devices: 22.8 us -> 18.2 us  [swap_seq(): return lax.ppermute(value, 'seq', [(k, k ^ distance) for k in range(count)])]
    unnamed x22 -> x10, local copies, waits for them, and re-layouts: 6.02 us -> 1.46 us
    ppermute x1, waiting for transfers between devices: 2.96 us -> 0.01 us  [paired_body(): lax.ppermute(straight, 'seq', [(k, k + 2 * ahead) for k in firsts])]
    dynamic_slice x0 -> x2, local copies, waits for them, and re-layouts: none -> 2.84 us  [half_of(): return lax.dynamic_slice_in_dim(value, which * half, half, 1)]
    ppermute x8, starting transfers between devices: 4.79 us -> 6.93 us  [swap(): return lax.ppermute(value, axis, [(k, k ^ 1 << bit) for k in range(count)])]
    ppermute x8, waiting for transfers between devices: 21 us -> 18.8 us  [swap(): return lax.ppermute(value, axis, [(k, k ^ 1 << bit) for k in range(count)])]
  transfers between devices with their start and end apart: 20 -> 21, of which waited for: 17 -> 15; matrix products, arithmetic and copies ran while one was open for 2% -> 3% of each run, Pallas kernels for 5% -> 5%
where the time goes in v3:
time: 111 us
  waiting for transfers between devices  60.5 us (55%)
  starting transfers between devices  30.9 us (28%)
  Pallas kernels  11.1 us (10%)
  local copies, waits for them, and re-layouts  6.49 us (6%)
  other arithmetic  1.24 us (1%)
    ppermute x11, waiting for transfers between devices, swap_seq(): return lax.ppermute(value, 'seq', [(k, k ^ distance) for k in range(count)])  41.7 us
    ppermute x8, waiting for transfers between devices, swap(): return lax.ppermute(value, axis, [(k, k ^ 1 << bit) for k in range(count)])  18.8 us
    ppermute x11, starting transfers between devices, swap_seq(): return lax.ppermute(value, 'seq', [(k, k ^ distance) for k in range(count)])  18.2 us
    pallas_call x6, Pallas kernels, call(): pl.pallas_call(kernel, out_shape=out_shape, in_specs=specs, scratch_shape...  10 us
    ppermute x8, starting transfers between devices, swap(): return lax.ppermute(value, axis, [(k, k ^ 1 << bit) for k in range(count)])  6.93 us
    ppermute x1, starting transfers between devices, paired_body(): lax.ppermute(straight, 'seq', [(k, k + 2 * ahead) for k in firsts])  4.5 us
    dynamic_slice x2, local copies, waits for them, and re-layouts, half_of(): return lax.dynamic_slice_in_dim(value, which * half, half, 1)  2.84 us
  transfers between devices with their start and end apart: 21, of which 15 were waited for; matrix products, arithmetic and copies ran while one was open for 3% of the time, Pallas kernels for 5%

profile of v3, /device:TPU:0, one launch (start us, length us, event | category | flops | bytes accessed | tf_op | source)
XLA Modules:
  0.0 110.6 jit_solution(11176146408482252877)
XLA Ops:
  0.0 1.3 %constant_dynamic-slice_fusion.6 = (bf16[128,1,256]{2,1,0:T(2,128)(2,1)S(1)}, bf16[128,1,256]{2,1,0:T(2,128)(2,1)S(1)}) fusion(bf16[128,2,256]{2,1,0:T(2,128)(2,1)} %param.16, s32[]{:T(128)S(6)} %select_n.148, bf16[128,2,256]{2,1,0:T(2,128)(2,1)} %param.15), kind=kLoop, calls=%fused_computation.45 | loop fusion | bytes 262148 | tf_op jit(solution)/shard_map/jit(dynamic_index_in_dim)/dynamic_slice | solution.py:538
  1.3 1.1 constant_dynamic-slice_fusion.8
  2.4 0.7 copy-done.1
  3.1 0.7 copy-done.2
  3.8 0.8 pack.1
  4.7 3.1 %collective-permute-start.5 = (bf16[128,1664]{1,0:T(8,128)(2,1)S(1)}, bf16[128,1664]{1,0:T(8,128)(2,1)S(1)}, u32[]{:S(2)}, u32[]{:S(2)}) collective-permute-start(bf16[128,1664]{1,0:T(8,128)(2,1)S(1)} %get-tuple-element.57), channel_id=1, source_target_pairs={{0,4},{4,0},{8,12},{12,8},{1,5},{5,1},{9,13},{13,9},{2,6},{6,2},{1... | collective-permute-start | bytes 1277960 | tf_op jit(solution)/shard_map/ppermute | solution.py:511
  7.8 4.5 %collective-permute-start.2 = (bf16[1296,128]{1,0:T(8,128)(2,1)S(1)}, bf16[1296,128]{1,0:T(8,128)(2,1)S(1)}, u32[]{:S(2)}, u32[]{:S(2)}) collective-permute-start(bf16[1296,128]{1,0:T(8,128)(2,1)S(1)} %get-tuple-element.54), channel_id=1, source_target_pairs={{0,8},{4,12},{1,9},{5,13},{2,10},{6,14},{3,11},{7,15},{16,24},{20,... | collective-permute-start | bytes 995336 | tf_op jit(solution)/shard_map/ppermute | solution.py:564
  12.3 1.3 %collective-permute-start.3 = (bf16[1296,128]{1,0:T(8,128)(2,1)S(1)}, bf16[1296,128]{1,0:T(8,128)(2,1)S(1)}, u32[]{:S(2)}, u32[]{:S(2)}) collective-permute-start(bf16[1296,128]{1,0:T(8,128)(2,1)S(1)} %get-tuple-element.55), channel_id=1, source_target_pairs={{0,12},{4,8},{1,13},{5,9},{2,14},{6,10},{3,15},{7,11},{16,28},{20,... | collective-permute-start | bytes 995336 | tf_op jit(solution)/shard_map/ppermute | solution.py:565
  13.6 1.8 %constant_dynamic-slice_fusion.4 = (bf16[128,1024]{1,0:T(8,128)(2,1)}, bf16[128,1024]{1,0:T(8,128)(2,1)S(1)}) fusion(bf16[128,2048]{1,0:T(8,128)(2,1)} %param.20, s32[]{:T(128)S(6)} %select_n.146, s32[]{:T(128)S(6)} %select_n.145), kind=kLoop, calls=%fused_computation.43 | loop fusion | bytes 1048584 | tf_op jit(solution)/shard_map/dynamic_slice | solution.py:548
  15.4 0.5 collective-permute-start.4
  15.9 0.7 broadcast_in_dim.67
  16.6 0.1 broadcast_in_dim_reshape.3.skip_ref
  16.7 0.7 select_multiply_fusion
  17.4 0.5 collective-permute-done.5.msg_ref
  18.0 1.9 %pair.1 = (f32[256,1024]{1,0:T(8,128)S(1)}, f32[256,1024]{1,0:T(8,128)S(1)}, bf16[256,256]{1,0:T(8,128)(2,1)S(1)}) custom-call(s32[1]{0:T(128)} %bitcast.5.where_ref.refs_2_, bf16[128,1024]{1,0:T(8,128)(2,1)S(1)} %get-tuple-element.85.x_mine_ref.x_ref, bf16[128,640]{1,0:T(8,128)(2,1)S(1)} %get-tuple-element.56.meta_ref, ...), custom_call_target="tpu_custom_call" | custom-call | flops 1 | bytes 1 | tf_op jit(solution)/shard_map/pair/pallas_call | solution.py:498
  19.9 17.0 %collective-permute-done.4.refs_4_ = bf16[128,1024]{1,0:T(8,128)(2,1)S(1)} collective-permute-done((bf16[128,1024]{1,0:T(8,128)(2,1)}, bf16[128,1024]{1,0:T(8,128)(2,1)S(1)}, u32[]{:S(2)}, u32[]{:S(2)}) %collective-permute-start.4) | collective-permute-done | bytes 262176 | tf_op jit(solution)/shard_map/ppermute | solution.py:511
  36.9 1.1 mix.1
  38.1 0.5 collective-permute-start.8
  38.5 1.0 collective-permute-done.6
  39.6 0.1 add_convert_fusion.4
  39.7 1.6 %collective-permute-start.7 = (bf16[128,1024]{1,0:T(8,128)(2,1)S(1)}, bf16[128,1024]{1,0:T(8,128)(2,1)S(1)}, u32[]{:S(2)}, u32[]{:S(2)}) collective-permute-start(bf16[128,1024]{1,0:T(8,128)(2,1)S(1)} %add_convert_fusion.4), channel_id=1, source_target_pairs={{0,2},{2,0},{1,3},{3,1},{4,6},{6,4},{5,7},{7,5},{8,10},{10,8},{9,1... | collective-permute-start | bytes 786440 | tf_op jit(solution)/shard_map/ppermute | solution.py:476
  41.2 0.1 add_convert_fusion.2.mixed_ref
  41.3 6.8 %collective-permute-done.7 = bf16[128,1024]{1,0:T(8,128)(2,1)S(1)} collective-permute-done((bf16[128,1024]{1,0:T(8,128)(2,1)S(1)}, bf16[128,1024]{1,0:T(8,128)(2,1)S(1)}, u32[]{:S(2)}, u32[]{:S(2)}) %collective-permute-start.7) | collective-permute-done | bytes 262176 | tf_op jit(solution)/shard_map/ppermute | solution.py:476
  48.1 0.1 add_convert_fusion.3
  48.2 6.0 %collective-permute-start.10 = (bf16[128,1024]{1,0:T(8,128)(2,1)S(1)}, bf16[128,1024]{1,0:T(8,128)(2,1)S(1)}, u32[]{:S(2)}, u32[]{:S(2)}) collective-permute-start(bf16[128,1024]{1,0:T(8,128)(2,1)S(1)} %add_convert_fusion.3), channel_id=1, source_target_pairs={{0,8},{4,12},{8,0},{12,4},{1,9},{5,13},{9,1},{13,5},{2,10},{6,14},... | collective-permute-start | bytes 786440 | tf_op jit(solution)/shard_map/ppermute | solution.py:511
  54.1 1.5 %collective-permute-start.9 = (bf16[128,1024]{1,0:T(8,128)(2,1)S(1)}, bf16[128,1024]{1,0:T(8,128)(2,1)S(1)}, u32[]{:S(2)}, u32[]{:S(2)}) collective-permute-start(bf16[128,1024]{1,0:T(8,128)(2,1)S(1)} %add_convert_fusion.2.mixed_ref), channel_id=1, source_target_pairs={{0,2},{2,0},{1,3},{3,1},{4,6},{6,4},{5,7},{7,5},{8,10},{10,8},{9,1... | collective-permute-start | bytes 786440 | tf_op jit(solution)/shard_map/ppermute | solution.py:476
  55.6 10.0 %collective-permute-done.10 = bf16[128,1024]{1,0:T(8,128)(2,1)S(1)} collective-permute-done((bf16[128,1024]{1,0:T(8,128)(2,1)S(1)}, bf16[128,1024]{1,0:T(8,128)(2,1)S(1)}, u32[]{:S(2)}, u32[]{:S(2)}) %collective-permute-start.10) | collective-permute-done | bytes 262176 | tf_op jit(solution)/shard_map/ppermute | solution.py:511
  65.6 1.1 collective-permute-done.11
  66.7 0.6 collective-permute-start.12
  67.3 0.1 add.237.refs_0_
  67.5 3.8 %collective-permute-start.15 = (bf16[128,1024]{1,0:T(8,128)(2,1)S(1)}, bf16[128,1024]{1,0:T(8,128)(2,1)S(1)}, u32[]{:S(2)}, u32[]{:S(2)}) collective-permute-start(bf16[128,1024]{1,0:T(8,128)(2,1)S(1)} %add.237.refs_0_), channel_id=1, source_target_pairs={{0,12},{4,8},{8,4},{12,0},{1,13},{5,9},{9,5},{13,1},{2,14},{6,10},... | collective-permute-start | bytes 786440 | tf_op jit(solution)/shard_map/ppermute | solution.py:511
  71.3 7.2 %collective-permute-done.12 = bf16[128,1024]{1,0:T(8,128)(2,1)S(1)} collective-permute-done((bf16[128,1024]{1,0:T(8,128)(2,1)S(1)}, bf16[128,1024]{1,0:T(8,128)(2,1)S(1)}, u32[]{:S(2)}, u32[]{:S(2)}) %collective-permute-start.12) | collective-permute-done | bytes 262176 | tf_op jit(solution)/shard_map/ppermute | solution.py:511
  78.5 10.7 %conditional.1 = (bf16[2,2,16,1024]{3,2,1,0:T(8,128)(2,1)S(1)}) conditional(s32[]{:T(128)} %convert_element_type.99, () %tuple.15, (s32[1]{0:T(128)}, bf16[2048,1024]{1,0:T(8,128)(2,1)}, bf16[128,1024]{1,0:T(8,128)(2,1)S(1)}, bf16[128,1024]{1,0:T(8,128)(2,1)S(1)}, bf16[128,1024]{1,0:T(8,128)(2,1)S(1)}, /*index=5*/bf16[128,1024]{1,0:T(8,128)(2,1)S(1)}, ...), branch_computations={%region_0.1_spmd, %region_1.2_spmd} | conditional | flops 786474 | bytes 33539460 | solution.py:674
  78.5 3.3 %project.2 = bf16[2,2,2,2,16,1024]{5,4,3,2,1,0:T(8,128)(2,1)S(1)} custom-call(s32[1]{0:T(128)} %get-tuple-element.24.where_ref, bf16[2048,1024]{1,0:T(8,128)(2,1)} %get-tuple-element.25.weight_ref, bf16[128,1024]{1,0:T(8,128)(2,1)S(1)} %get-tuple-element.26.refs_0_, bf16[128,1024]{1,0:T(8,128)(2,1)S(1)} %get-tuple-element.27.refs_1_, ...), custom_call_target="tpu_custom_call" | custom-call | flops 1 | bytes 30000000 | tf_op jit(solution)/shard_map/cond/branch_1_fun/project/pallas_call | solution.py:498
  81.9 1.5 %collective-permute-done = bf16[1,2,2,2,16,1024]{5,4,3,2,1,0:T(8,128)(2,1)S(1)} collective-permute-done((bf16[1,2,2,2,16,1024]{5,4,3,2,1,0:T(8,128)(2,1)S(1)}, bf16[1,2,2,2,16,1024]{5,4,3,2,1,0:T(8,128)(2,1)S(1)}, u32[]{:S(2)}, u32[]{:S(2)}) %collective-permute-start) | collective-permute-done | bytes 262176 | tf_op jit(solution)/shard_map/cond/branch_1_fun/ppermute | solution.py:476
  83.5 1.6 %collective-permute-start.1 = (bf16[1,2,2,16,1024]{4,3,2,1,0:T(8,128)(2,1)S(1)}, bf16[1,2,2,16,1024]{4,3,2,1,0:T(8,128)(2,1)S(1)}, u32[]{:S(2)}, u32[]{:S(2)}) collective-permute-start(bf16[1,2,2,16,1024]{4,3,2,1,0:T(8,128)(2,1)S(1)} %dynamic-slice_bitcast_fusion), channel_id=1, source_target_pairs={{0,2},{2,0},{1,3},{3,1},{4,6},{6,4},{5,7},{7,5},{8,10},{10,8},{9,1... | collective-permute-start | bytes 393224 | tf_op jit(solution)/shard_map/cond/branch_1_fun/ppermute | solution.py:476
  85.1 4.0 %collective-permute-done.1 = bf16[1,2,2,16,1024]{4,3,2,1,0:T(8,128)(2,1)S(1)} collective-permute-done((bf16[1,2,2,16,1024]{4,3,2,1,0:T(8,128)(2,1)S(1)}, bf16[1,2,2,16,1024]{4,3,2,1,0:T(8,128)(2,1)S(1)}, u32[]{:S(2)}, u32[]{:S(2)}) %collective-permute-start.1) | collective-permute-done | bytes 131104 | tf_op jit(solution)/shard_map/cond/branch_1_fun/ppermute | solution.py:476
  89.2 1.4 %collective-permute-done.13.refs_1_ = bf16[128,1024]{1,0:T(8,128)(2,1)S(1)} collective-permute-done((bf16[128,1024]{1,0:T(8,128)(2,1)S(1)}, bf16[128,1024]{1,0:T(8,128)(2,1)S(1)}, u32[]{:S(2)}, u32[]{:S(2)}) %collective-permute-start.13) | collective-permute-done | bytes 262176 | tf_op jit(solution)/shard_map/ppermute | solution.py:511
  90.6 3.3 %project.3 = bf16[2,2,2,2,16,1024]{5,4,3,2,1,0:T(8,128)(2,1)S(1)} custom-call(s32[1]{0:T(128)} %bitcast.5.where_ref.refs_2_, bf16[2048,1024]{1,0:T(8,128)(2,1)} %weight_ref.1, bf16[128,1024]{1,0:T(8,128)(2,1)S(1)} %add.237.refs_0_, bf16[128,1024]{1,0:T(8,128)(2,1)S(1)} %collective-permute-done.13.refs_1_, ...), custom_call_target="tpu_custom_call" | custom-call | flops 1 | bytes 30000000 | tf_op jit(solution)/shard_map/project/pallas_call | solution.py:498
  94.0 1.5 %collective-permute-done.16 = bf16[1,2,2,2,16,1024]{5,4,3,2,1,0:T(8,128)(2,1)S(1)} collective-permute-done((bf16[1,2,2,2,16,1024]{5,4,3,2,1,0:T(8,128)(2,1)S(1)}, bf16[1,2,2,2,16,1024]{5,4,3,2,1,0:T(8,128)(2,1)S(1)}, u32[]{:S(2)}, u32[]{:S(2)}) %collective-permute-start.16) | collective-permute-done | bytes 262176 | tf_op jit(solution)/shard_map/ppermute | solution.py:476
  95.6 1.6 %collective-permute-start.17 = (bf16[1,2,2,16,1024]{4,3,2,1,0:T(8,128)(2,1)S(1)}, bf16[1,2,2,16,1024]{4,3,2,1,0:T(8,128)(2,1)S(1)}, u32[]{:S(2)}, u32[]{:S(2)}) collective-permute-start(bf16[1,2,2,16,1024]{4,3,2,1,0:T(8,128)(2,1)S(1)} %dynamic-slice_bitcast_fusion.1), channel_id=1, source_target_pairs={{0,2},{2,0},{1,3},{3,1},{4,6},{6,4},{5,7},{7,5},{8,10},{10,8},{9,1... | collective-permute-start | bytes 393224 | tf_op jit(solution)/shard_map/ppermute | solution.py:476
  97.2 4.0 %collective-permute-done.17 = bf16[1,2,2,16,1024]{4,3,2,1,0:T(8,128)(2,1)S(1)} collective-permute-done((bf16[1,2,2,16,1024]{4,3,2,1,0:T(8,128)(2,1)S(1)}, bf16[1,2,2,16,1024]{4,3,2,1,0:T(8,128)(2,1)S(1)}, u32[]{:S(2)}, u32[]{:S(2)}) %collective-permute-start.17) | collective-permute-done | bytes 131104 | tf_op jit(solution)/shard_map/ppermute | solution.py:476
  101.3 1.6 %collective-permute-start.19 = (bf16[32,1024]{1,0:T(8,128)(2,1)S(1)}, bf16[32,1024]{1,0:T(8,128)(2,1)S(1)}, u32[]{:S(2)}, u32[]{:S(2)}) collective-permute-start(bf16[32,1024]{1,0:T(8,128)(2,1)S(1)} %bitcast.46), channel_id=1, source_target_pairs={{0,8},{4,12},{8,0},{12,4},{1,9},{5,13},{9,1},{13,5},{2,10},{6,14},... | collective-permute-start | bytes 196616 | tf_op jit(solution)/shard_map/ppermute | solution.py:511
  102.9 2.4 %collective-permute-start.20 = (bf16[32,1024]{1,0:T(8,128)(2,1)S(1)}, bf16[32,1024]{1,0:T(8,128)(2,1)S(1)}, u32[]{:S(2)}, u32[]{:S(2)}) collective-permute-start(bf16[32,1024]{1,0:T(8,128)(2,1)S(1)} %bitcast.45), channel_id=1, source_target_pairs={{0,12},{4,8},{8,4},{12,0},{1,13},{5,9},{9,5},{13,1},{2,14},{6,10},... | collective-permute-start | bytes 196616 | tf_op jit(solution)/shard_map/ppermute | solution.py:511
  105.5 3.0 %collective-permute-done.19.refs_2_ = bf16[32,1024]{1,0:T(8,128)(2,1)S(1)} collective-permute-done((bf16[32,1024]{1,0:T(8,128)(2,1)S(1)}, bf16[32,1024]{1,0:T(8,128)(2,1)S(1)}, u32[]{:S(2)}, u32[]{:S(2)}) %collective-permute-start.19) | collective-permute-done | bytes 65568 | tf_op jit(solution)/shard_map/ppermute | solution.py:511
  108.4 0.8 collective-permute-done.20.refs_3_
  109.2 0.7 collective-permute-done.18.refs_1_
  109.9 0.7 place.1
  (34 shorter events, 0.8 us)
Async XLA Ops:
  0.0 36.9 %copy-start = (bf16[256,256]{1,0:T(8,128)(2,1)S(1)}, bf16[256,256]{1,0:T(8,128)(2,1)}, u32[]{:S(2)}) copy-start(bf16[256,256]{1,0:T(8,128)(2,1)} %constant.219.clone.refs_9_) | copy-start | bytes 393220
  2.4 0.7 copy-start.1
  3.1 0.7 copy-start.2
  4.7 13.3 %collective-permute-start.5 = (bf16[128,1664]{1,0:T(8,128)(2,1)S(1)}, bf16[128,1664]{1,0:T(8,128)(2,1)S(1)}, u32[]{:S(2)}, u32[]{:S(2)}) collective-permute-start(bf16[128,1664]{1,0:T(8,128)(2,1)S(1)} %get-tuple-element.57), channel_id=1, source_target_pairs={{0,4},{4,0},{8,12},{12,8},{1,5},{5,1},{9,13},{13,9},{2,6},{6,2},{1... | collective-permute-start | bytes 1277960 | tf_op jit(solution)/shard_map/ppermute | solution.py:511
  7.8 29.1 %collective-permute-start.2 = (bf16[1296,128]{1,0:T(8,128)(2,1)S(1)}, bf16[1296,128]{1,0:T(8,128)(2,1)S(1)}, u32[]{:S(2)}, u32[]{:S(2)}) collective-permute-start(bf16[1296,128]{1,0:T(8,128)(2,1)S(1)} %get-tuple-element.54), channel_id=1, source_target_pairs={{0,8},{4,12},{1,9},{5,13},{2,10},{6,14},{3,11},{7,15},{16,24},{20,... | collective-permute-start | bytes 995336 | tf_op jit(solution)/shard_map/ppermute | solution.py:564
  12.3 66.2 %copy-start.3 = (s32[2048]{0:T(1024)S(1)}, s32[2048]{0:T(1024)}, u32[]{:S(2)}) copy-start(s32[2048]{0:T(1024)} %param.23) | copy-start | bytes 24580
  12.3 24.6 %collective-permute-start.3 = (bf16[1296,128]{1,0:T(8,128)(2,1)S(1)}, bf16[1296,128]{1,0:T(8,128)(2,1)S(1)}, u32[]{:S(2)}, u32[]{:S(2)}) collective-permute-start(bf16[1296,128]{1,0:T(8,128)(2,1)S(1)} %get-tuple-element.55), channel_id=1, source_target_pairs={{0,12},{4,8},{1,13},{5,9},{2,14},{6,10},{3,15},{7,11},{16,28},{20,... | collective-permute-start | bytes 995336 | tf_op jit(solution)/shard_map/ppermute | solution.py:565
  15.4 21.5 %collective-permute-start.4 = (bf16[128,1024]{1,0:T(8,128)(2,1)}, bf16[128,1024]{1,0:T(8,128)(2,1)S(1)}, u32[]{:S(2)}, u32[]{:S(2)}) collective-permute-start(bf16[128,1024]{1,0:T(8,128)(2,1)} %get-tuple-element.82), channel_id=1, source_target_pairs={{0,4},{4,0},{8,12},{12,8},{1,5},{5,1},{9,13},{13,9},{2,6},{6,2},{1... | collective-permute-start | bytes 786440 | tf_op jit(solution)/shard_map/ppermute | solution.py:511
  38.0 1.6 %collective-permute-start.6 = (bf16[128,1024]{1,0:T(8,128)(2,1)S(1)}, bf16[128,1024]{1,0:T(8,128)(2,1)S(1)}, u32[]{:S(2)}, u32[]{:S(2)}) collective-permute-start(bf16[128,1024]{1,0:T(8,128)(2,1)S(1)} %get-tuple-element.61), channel_id=1, source_target_pairs={{0,1},{1,0},{2,3},{3,2},{4,5},{5,4},{6,7},{7,6},{8,9},{9,8},{10,11... | collective-permute-start | bytes 786440 | tf_op jit(solution)/shard_map/ppermute | solution.py:476
  38.1 3.2 %collective-permute-start.8 = (bf16[128,1024]{1,0:T(8,128)(2,1)S(1)}, bf16[128,1024]{1,0:T(8,128)(2,1)S(1)}, u32[]{:S(2)}, u32[]{:S(2)}) collective-permute-start(bf16[128,1024]{1,0:T(8,128)(2,1)S(1)} %get-tuple-element.62), channel_id=1, source_target_pairs={{0,1},{1,0},{2,3},{3,2},{4,5},{5,4},{6,7},{7,6},{8,9},{9,8},{10,11... | collective-permute-start | bytes 786440 | tf_op jit(solution)/shard_map/ppermute | solution.py:476
  39.7 8.4 %collective-permute-start.7 = (bf16[128,1024]{1,0:T(8,128)(2,1)S(1)}, bf16[128,1024]{1,0:T(8,128)(2,1)S(1)}, u32[]{:S(2)}, u32[]{:S(2)}) collective-permute-start(bf16[128,1024]{1,0:T(8,128)(2,1)S(1)} %add_convert_fusion.4), channel_id=1, source_target_pairs={{0,2},{2,0},{1,3},{3,1},{4,6},{6,4},{5,7},{7,5},{8,10},{10,8},{9,1... | collective-permute-start | bytes 786440 | tf_op jit(solution)/shard_map/ppermute | solution.py:476
  48.2 17.5 %collective-permute-start.10 = (bf16[128,1024]{1,0:T(8,128)(2,1)S(1)}, bf16[128,1024]{1,0:T(8,128)(2,1)S(1)}, u32[]{:S(2)}, u32[]{:S(2)}) collective-permute-start(bf16[128,1024]{1,0:T(8,128)(2,1)S(1)} %add_convert_fusion.3), channel_id=1, source_target_pairs={{0,8},{4,12},{8,0},{12,4},{1,9},{5,13},{9,1},{13,5},{2,10},{6,14},... | collective-permute-start | bytes 786440 | tf_op jit(solution)/shard_map/ppermute | solution.py:511
  54.1 12.6 %collective-permute-start.11 = (bf16[128,1024]{1,0:T(8,128)(2,1)S(1)}, bf16[128,1024]{1,0:T(8,128)(2,1)S(1)}, u32[]{:S(2)}, u32[]{:S(2)}) collective-permute-start(bf16[128,1024]{1,0:T(8,128)(2,1)S(1)} %add_convert_fusion.3), channel_id=1, source_target_pairs={{0,4},{4,0},{8,12},{12,8},{1,5},{5,1},{9,13},{13,9},{2,6},{6,2},{1... | collective-permute-start | bytes 786440 | tf_op jit(solution)/shard_map/ppermute | solution.py:511
  54.1 12.6 %collective-permute-start.9 = (bf16[128,1024]{1,0:T(8,128)(2,1)S(1)}, bf16[128,1024]{1,0:T(8,128)(2,1)S(1)}, u32[]{:S(2)}, u32[]{:S(2)}) collective-permute-start(bf16[128,1024]{1,0:T(8,128)(2,1)S(1)} %add_convert_fusion.2.mixed_ref), channel_id=1, source_target_pairs={{0,2},{2,0},{1,3},{3,1},{4,6},{6,4},{5,7},{7,5},{8,10},{10,8},{9,1... | collective-permute-start | bytes 786440 | tf_op jit(solution)/shard_map/ppermute | solution.py:476
  66.7 11.7 %collective-permute-start.12 = (bf16[128,1024]{1,0:T(8,128)(2,1)S(1)}, bf16[128,1024]{1,0:T(8,128)(2,1)S(1)}, u32[]{:S(2)}, u32[]{:S(2)}) collective-permute-start(bf16[128,1024]{1,0:T(8,128)(2,1)S(1)} %collective-permute-done.10), channel_id=1, source_target_pairs={{0,4},{4,0},{8,12},{12,8},{1,5},{5,1},{9,13},{13,9},{2,6},{6,2},{1... | collective-permute-start | bytes 786440 | tf_op jit(solution)/shard_map/ppermute | solution.py:511
  67.4 21.8 %collective-permute-start.14 = (bf16[128,1024]{1,0:T(8,128)(2,1)S(1)}, bf16[128,1024]{1,0:T(8,128)(2,1)S(1)}, u32[]{:S(2)}, u32[]{:S(2)}) collective-permute-start(bf16[128,1024]{1,0:T(8,128)(2,1)S(1)} %add.237.refs_0_), channel_id=1, source_target_pairs={{0,8},{4,12},{8,0},{12,4},{1,9},{5,13},{9,1},{13,5},{2,10},{6,14},... | collective-permute-start | bytes 786440 | tf_op jit(solution)/shard_map/ppermute | solution.py:511
  67.5 21.7 %collective-permute-start.15 = (bf16[128,1024]{1,0:T(8,128)(2,1)S(1)}, bf16[128,1024]{1,0:T(8,128)(2,1)S(1)}, u32[]{:S(2)}, u32[]{:S(2)}) collective-permute-start(bf16[128,1024]{1,0:T(8,128)(2,1)S(1)} %add.237.refs_0_), channel_id=1, source_target_pairs={{0,12},{4,8},{8,4},{12,0},{1,13},{5,9},{9,5},{13,1},{2,14},{6,10},... | collective-permute-start | bytes 786440 | tf_op jit(solution)/shard_map/ppermute | solution.py:511
  78.4 12.2 %collective-permute-start.13 = (bf16[128,1024]{1,0:T(8,128)(2,1)S(1)}, bf16[128,1024]{1,0:T(8,128)(2,1)S(1)}, u32[]{:S(2)}, u32[]{:S(2)}) collective-permute-start(bf16[128,1024]{1,0:T(8,128)(2,1)S(1)} %add.237.refs_0_), channel_id=1, source_target_pairs={{0,4},{4,0},{8,12},{12,8},{1,5},{5,1},{9,13},{13,9},{2,6},{6,2},{1... | collective-permute-start | bytes 786440 | tf_op jit(solution)/shard_map/ppermute | solution.py:511
  81.8 1.6 %collective-permute-start = (bf16[1,2,2,2,16,1024]{5,4,3,2,1,0:T(8,128)(2,1)S(1)}, bf16[1,2,2,2,16,1024]{5,4,3,2,1,0:T(8,128)(2,1)S(1)}, u32[]{:S(2)}, u32[]{:S(2)}) collective-permute-start(bf16[1,2,2,2,16,1024]{5,4,3,2,1,0:T(8,128)(2,1)S(1)} %constant_dynamic-slice_fusion), channel_id=1, source_target_pairs={{0,1},{1,0},{2,3},{3,2},{4,5},{5,4},{6,7},{7,6},{8,9},{9,8},{10,11... | collective-permute-start | bytes 786440 | tf_op jit(solution)/shard_map/cond/branch_1_fun/ppermute | solution.py:476
  83.5 5.6 %collective-permute-start.1 = (bf16[1,2,2,16,1024]{4,3,2,1,0:T(8,128)(2,1)S(1)}, bf16[1,2,2,16,1024]{4,3,2,1,0:T(8,128)(2,1)S(1)}, u32[]{:S(2)}, u32[]{:S(2)}) collective-permute-start(bf16[1,2,2,16,1024]{4,3,2,1,0:T(8,128)(2,1)S(1)} %dynamic-slice_bitcast_fusion), channel_id=1, source_target_pairs={{0,2},{2,0},{1,3},{3,1},{4,6},{6,4},{5,7},{7,5},{8,10},{10,8},{9,1... | collective-permute-start | bytes 393224 | tf_op jit(solution)/shard_map/cond/branch_1_fun/ppermute | solution.py:476
  93.9 1.6 %collective-permute-start.16 = (bf16[1,2,2,2,16,1024]{5,4,3,2,1,0:T(8,128)(2,1)S(1)}, bf16[1,2,2,2,16,1024]{5,4,3,2,1,0:T(8,128)(2,1)S(1)}, u32[]{:S(2)}, u32[]{:S(2)}) collective-permute-start(bf16[1,2,2,2,16,1024]{5,4,3,2,1,0:T(8,128)(2,1)S(1)} %constant_dynamic-slice_fusion.3), channel_id=1, source_target_pairs={{0,1},{1,0},{2,3},{3,2},{4,5},{5,4},{6,7},{7,6},{8,9},{9,8},{10,11... | collective-permute-start | bytes 786440 | tf_op jit(solution)/shard_map/ppermute | solution.py:476
  95.6 5.6 %collective-permute-start.17 = (bf16[1,2,2,16,1024]{4,3,2,1,0:T(8,128)(2,1)S(1)}, bf16[1,2,2,16,1024]{4,3,2,1,0:T(8,128)(2,1)S(1)}, u32[]{:S(2)}, u32[]{:S(2)}) collective-permute-start(bf16[1,2,2,16,1024]{4,3,2,1,0:T(8,128)(2,1)S(1)} %dynamic-slice_bitcast_fusion.1), channel_id=1, source_target_pairs={{0,2},{2,0},{1,3},{3,1},{4,6},{6,4},{5,7},{7,5},{8,10},{10,8},{9,1... | collective-permute-start | bytes 393224 | tf_op jit(solution)/shard_map/ppermute | solution.py:476
  101.3 7.1 %collective-permute-start.19 = (bf16[32,1024]{1,0:T(8,128)(2,1)S(1)}, bf16[32,1024]{1,0:T(8,128)(2,1)S(1)}, u32[]{:S(2)}, u32[]{:S(2)}) collective-permute-start(bf16[32,1024]{1,0:T(8,128)(2,1)S(1)} %bitcast.46), channel_id=1, source_target_pairs={{0,8},{4,12},{8,0},{12,4},{1,9},{5,13},{9,1},{13,5},{2,10},{6,14},... | collective-permute-start | bytes 196616 | tf_op jit(solution)/shard_map/ppermute | solution.py:511
  102.9 6.3 %collective-permute-start.20 = (bf16[32,1024]{1,0:T(8,128)(2,1)S(1)}, bf16[32,1024]{1,0:T(8,128)(2,1)S(1)}, u32[]{:S(2)}, u32[]{:S(2)}) collective-permute-start(bf16[32,1024]{1,0:T(8,128)(2,1)S(1)} %bitcast.45), channel_id=1, source_target_pairs={{0,12},{4,8},{8,4},{12,0},{1,13},{5,9},{9,5},{13,1},{2,14},{6,10},... | collective-permute-start | bytes 196616 | tf_op jit(solution)/shard_map/ppermute | solution.py:511
  105.4 4.5 %collective-permute-start.18 = (bf16[32,1024]{1,0:T(8,128)(2,1)S(1)}, bf16[32,1024]{1,0:T(8,128)(2,1)S(1)}, u32[]{:S(2)}, u32[]{:S(2)}) collective-permute-start(bf16[32,1024]{1,0:T(8,128)(2,1)S(1)} %bitcast.47), channel_id=1, source_target_pairs={{0,4},{4,0},{8,12},{12,8},{1,5},{5,1},{9,13},{13,9},{2,6},{6,2},{1... | collective-permute-start | bytes 196616 | tf_op jit(solution)/shard_map/ppermute | solution.py:511

commit v4 on v3

--- a/solution.py
+++ b/solution.py
@@ -190,8 +190,7 @@
     x_other_ref,
     b_ref,
     c_ref,
-    step_ref,
-    decay_ref,
+    steps_ref,
     mine_ref,
     other_ref,
     straight_ref,
@@ -199,11 +198,11 @@
 ):
     tokens, states = b_ref.shape
     half = x_mine_ref.shape[1]
-    heads = step_ref.shape[0] // 2
+    heads = steps_ref.shape[0] // 4
     member = where_ref[0]
     triangle = causal_mask(tokens).astype(f32).astype(bf16)
-    step = step_ref[...].T
-    decay = decay_ref[...].T
+    step = steps_ref[: 2 * heads, :].T
+    decay = steps_ref[2 * heads :, :].T
     cumul = exact_dot(triangle, decay)
     total = cumul[tokens - 1 : tokens, :]
     scale = jnp.exp(total - cumul) * step
@@ -549,13 +548,14 @@
 
     x_mine, x_other = half_of(x_in, member), half_of(x_in, 1 - member)
     gate_mine, gate_other = half_of(gate_in, member), half_of(gate_in, 1 - member)
+    steps = jnp.concatenate([step_size.T, log_decay.T], axis=0)
     with_pair = shape(tokens, 2 * states + padded(6 * half_heads), bf16)
     with_later = shape((half + states) // LANES * tokens + 16, LANES, bf16)
     meta_mine, to_pair, straight, cross = call(
         pack_kernel,
         (with_pair, shape(tokens, half + with_pair.shape[1], bf16), with_later, with_later),
         "pack",
-        (where, x_mine, x_other, b_group, c_group, step_size.T, log_decay.T),
+        (where, x_mine, x_other, b_group, c_group, steps),
         1,
     )
     sent = []

time: 111 us -> 110 us (level)
  local copies, waits for them, and re-layouts: 6.49 us -> 5.05 us
    unnamed x10 -> x6, local copies, waits for them, and re-layouts: 1.46 us -> 0.03 us
where the time goes in v4:
time: 110 us
  waiting for transfers between devices  60.5 us (55%)
  starting transfers between devices  30.9 us (28%)
  Pallas kernels  11.2 us (10%)
  local copies, waits for them, and re-layouts  5.05 us (5%)
  other arithmetic  1.98 us (2%)
    ppermute x11, waiting for transfers between devices, swap_seq(): return lax.ppermute(value, 'seq', [(k, k ^ distance) for k in range(count)])  41.6 us
    ppermute x8, waiting for transfers between devices, swap(): return lax.ppermute(value, axis, [(k, k ^ 1 << bit) for k in range(count)])  18.8 us
    ppermute x11, starting transfers between devices, swap_seq(): return lax.ppermute(value, 'seq', [(k, k ^ distance) for k in range(count)])  18.2 us
    pallas_call x6, Pallas kernels, call(): pl.pallas_call(kernel, out_shape=out_shape, in_specs=specs, scratch_shape...  10.1 us
    ppermute x8, starting transfers between devices, swap(): return lax.ppermute(value, axis, [(k, k ^ 1 << bit) for k in range(count)])  6.92 us
    ppermute x1, starting transfers between devices, paired_body(): lax.ppermute(straight, 'seq', [(k, k + 2 * ahead) for k in firsts])  4.5 us
    dynamic_slice x2, local copies, waits for them, and re-layouts, half_of(): return lax.dynamic_slice_in_dim(value, which * half, half, 1)  2.84 us
  transfers between devices with their start and end apart: 21, of which 15 were waited for; matrix products, arithmetic and copies ran while one was open for 3% of the time, Pallas kernels for 5%

profile of v4, /device:TPU:0, one launch (start us, length us, event | category | flops | bytes accessed | tf_op | source)
XLA Modules:
  0.0 110.0 jit_solution(2532936238344427430)
XLA Ops:
  0.0 1.3 %constant_dynamic-slice_fusion.6 = (bf16[128,1,256]{2,1,0:T(2,128)(2,1)S(1)}, bf16[128,1,256]{2,1,0:T(2,128)(2,1)S(1)}) fusion(bf16[128,2,256]{2,1,0:T(2,128)(2,1)} %param.16, s32[]{:T(128)S(6)} %select_n.148, bf16[128,2,256]{2,1,0:T(2,128)(2,1)} %param.15), kind=kLoop, calls=%fused_computation.46 | loop fusion | bytes 262148 | tf_op jit(solution)/shard_map/jit(dynamic_index_in_dim)/dynamic_slice | solution.py:537
  1.3 0.7 pad_maximum_fusion.steps_ref
  2.1 1.1 constant_dynamic-slice_fusion.8
  3.1 0.8 pack.1
  4.0 3.1 %collective-permute-start.5 = (bf16[128,1664]{1,0:T(8,128)(2,1)S(1)}, bf16[128,1664]{1,0:T(8,128)(2,1)S(1)}, u32[]{:S(2)}, u32[]{:S(2)}) collective-permute-start(bf16[128,1664]{1,0:T(8,128)(2,1)S(1)} %get-tuple-element.57), channel_id=1, source_target_pairs={{0,4},{4,0},{8,12},{12,8},{1,5},{5,1},{9,13},{13,9},{2,6},{6,2},{1... | collective-permute-start | bytes 1277960 | tf_op jit(solution)/shard_map/ppermute | solution.py:510
  7.1 4.5 %collective-permute-start.2 = (bf16[1296,128]{1,0:T(8,128)(2,1)S(1)}, bf16[1296,128]{1,0:T(8,128)(2,1)S(1)}, u32[]{:S(2)}, u32[]{:S(2)}) collective-permute-start(bf16[1296,128]{1,0:T(8,128)(2,1)S(1)} %get-tuple-element.54), channel_id=1, source_target_pairs={{0,8},{4,12},{1,9},{5,13},{2,10},{6,14},{3,11},{7,15},{16,24},{20,... | collective-permute-start | bytes 995336 | tf_op jit(solution)/shard_map/ppermute | solution.py:564
  11.6 1.3 %collective-permute-start.3 = (bf16[1296,128]{1,0:T(8,128)(2,1)S(1)}, bf16[1296,128]{1,0:T(8,128)(2,1)S(1)}, u32[]{:S(2)}, u32[]{:S(2)}) collective-permute-start(bf16[1296,128]{1,0:T(8,128)(2,1)S(1)} %get-tuple-element.55), channel_id=1, source_target_pairs={{0,12},{4,8},{1,13},{5,9},{2,14},{6,10},{3,15},{7,11},{16,28},{20,... | collective-permute-start | bytes 995336 | tf_op jit(solution)/shard_map/ppermute | solution.py:565
  12.9 1.8 %constant_dynamic-slice_fusion.4 = (bf16[128,1024]{1,0:T(8,128)(2,1)}, bf16[128,1024]{1,0:T(8,128)(2,1)S(1)}) fusion(bf16[128,2048]{1,0:T(8,128)(2,1)} %param.20, s32[]{:T(128)S(6)} %select_n.146, s32[]{:T(128)S(6)} %select_n.145), kind=kLoop, calls=%fused_computation.44 | loop fusion | bytes 1048584 | tf_op jit(solution)/shard_map/dynamic_slice | solution.py:547
  14.7 0.5 collective-permute-start.4
  15.2 0.7 broadcast_in_dim.67
  15.9 0.1 broadcast_in_dim_reshape.3.skip_ref
  16.0 0.7 select_multiply_fusion
  16.8 0.5 collective-permute-done.5.msg_ref
  17.3 1.9 %pair.1 = (f32[256,1024]{1,0:T(8,128)S(1)}, f32[256,1024]{1,0:T(8,128)S(1)}, bf16[256,256]{1,0:T(8,128)(2,1)S(1)}) custom-call(s32[1]{0:T(128)} %bitcast.5.where_ref.refs_2_, bf16[128,1024]{1,0:T(8,128)(2,1)S(1)} %get-tuple-element.85.x_mine_ref.x_ref, bf16[128,640]{1,0:T(8,128)(2,1)S(1)} %get-tuple-element.56.meta_ref, ...), custom_call_target="tpu_custom_call" | custom-call | flops 1 | bytes 1 | tf_op jit(solution)/shard_map/pair/pallas_call | solution.py:497
  19.2 17.0 %collective-permute-done.4.refs_4_ = bf16[128,1024]{1,0:T(8,128)(2,1)S(1)} collective-permute-done((bf16[128,1024]{1,0:T(8,128)(2,1)}, bf16[128,1024]{1,0:T(8,128)(2,1)S(1)}, u32[]{:S(2)}, u32[]{:S(2)}) %collective-permute-start.4) | collective-permute-done | bytes 262176 | tf_op jit(solution)/shard_map/ppermute | solution.py:510
  36.2 1.1 %mix.1 = (bf16[128,1024]{1,0:T(8,128)(2,1)S(1)}, bf16[128,1024]{1,0:T(8,128)(2,1)S(1)}) custom-call(bf16[1296,128]{1,0:T(8,128)(2,1)S(1)} %collective-permute-done.2.refs_0_, bf16[1296,128]{1,0:T(8,128)(2,1)S(1)} %collective-permute-done.3.refs_1_, s32[1]{0:T(128)} %bitcast.5.where_ref.refs_2_, bf16[128,1024]{1,0:T(8,128)(2,1)S(1)} %get-tuple-element.83.refs_3_, ...), custom_call_target="tpu_custom_call" | custom-call | flops 1 | bytes 30000000 | tf_op jit(solution)/shard_map/mix/pallas_call | solution.py:598
  37.4 0.5 collective-permute-start.8
  37.9 1.0 collective-permute-done.6
  38.9 0.1 add_convert_fusion.4
  39.0 1.6 %collective-permute-start.7 = (bf16[128,1024]{1,0:T(8,128)(2,1)S(1)}, bf16[128,1024]{1,0:T(8,128)(2,1)S(1)}, u32[]{:S(2)}, u32[]{:S(2)}) collective-permute-start(bf16[128,1024]{1,0:T(8,128)(2,1)S(1)} %add_convert_fusion.4), channel_id=1, source_target_pairs={{0,2},{2,0},{1,3},{3,1},{4,6},{6,4},{5,7},{7,5},{8,10},{10,8},{9,1... | collective-permute-start | bytes 786440 | tf_op jit(solution)/shard_map/ppermute | solution.py:475
  40.6 0.1 add_convert_fusion.2.mixed_ref
  40.7 6.8 %collective-permute-done.7 = bf16[128,1024]{1,0:T(8,128)(2,1)S(1)} collective-permute-done((bf16[128,1024]{1,0:T(8,128)(2,1)S(1)}, bf16[128,1024]{1,0:T(8,128)(2,1)S(1)}, u32[]{:S(2)}, u32[]{:S(2)}) %collective-permute-start.7) | collective-permute-done | bytes 262176 | tf_op jit(solution)/shard_map/ppermute | solution.py:475
  47.4 0.1 add_convert_fusion.3
  47.5 6.0 %collective-permute-start.10 = (bf16[128,1024]{1,0:T(8,128)(2,1)S(1)}, bf16[128,1024]{1,0:T(8,128)(2,1)S(1)}, u32[]{:S(2)}, u32[]{:S(2)}) collective-permute-start(bf16[128,1024]{1,0:T(8,128)(2,1)S(1)} %add_convert_fusion.3), channel_id=1, source_target_pairs={{0,8},{4,12},{8,0},{12,4},{1,9},{5,13},{9,1},{13,5},{2,10},{6,14},... | collective-permute-start | bytes 786440 | tf_op jit(solution)/shard_map/ppermute | solution.py:510
  53.5 1.5 %collective-permute-start.9 = (bf16[128,1024]{1,0:T(8,128)(2,1)S(1)}, bf16[128,1024]{1,0:T(8,128)(2,1)S(1)}, u32[]{:S(2)}, u32[]{:S(2)}) collective-permute-start(bf16[128,1024]{1,0:T(8,128)(2,1)S(1)} %add_convert_fusion.2.mixed_ref), channel_id=1, source_target_pairs={{0,2},{2,0},{1,3},{3,1},{4,6},{6,4},{5,7},{7,5},{8,10},{10,8},{9,1... | collective-permute-start | bytes 786440 | tf_op jit(solution)/shard_map/ppermute | solution.py:475
  55.0 10.0 %collective-permute-done.10 = bf16[128,1024]{1,0:T(8,128)(2,1)S(1)} collective-permute-done((bf16[128,1024]{1,0:T(8,128)(2,1)S(1)}, bf16[128,1024]{1,0:T(8,128)(2,1)S(1)}, u32[]{:S(2)}, u32[]{:S(2)}) %collective-permute-start.10) | collective-permute-done | bytes 262176 | tf_op jit(solution)/shard_map/ppermute | solution.py:510
  65.0 1.1 collective-permute-done.11
  66.1 0.6 collective-permute-start.12
  66.7 0.1 add.237.refs_0_
  66.8 0.1 collective-permute-start.14
  66.8 3.8 %collective-permute-start.15 = (bf16[128,1024]{1,0:T(8,128)(2,1)S(1)}, bf16[128,1024]{1,0:T(8,128)(2,1)S(1)}, u32[]{:S(2)}, u32[]{:S(2)}) collective-permute-start(bf16[128,1024]{1,0:T(8,128)(2,1)S(1)} %add.237.refs_0_), channel_id=1, source_target_pairs={{0,12},{4,8},{8,4},{12,0},{1,13},{5,9},{9,5},{13,1},{2,14},{6,10},... | collective-permute-start | bytes 786440 | tf_op jit(solution)/shard_map/ppermute | solution.py:510
  70.6 7.2 %collective-permute-done.12 = bf16[128,1024]{1,0:T(8,128)(2,1)S(1)} collective-permute-done((bf16[128,1024]{1,0:T(8,128)(2,1)S(1)}, bf16[128,1024]{1,0:T(8,128)(2,1)S(1)}, u32[]{:S(2)}, u32[]{:S(2)}) %collective-permute-start.12) | collective-permute-done | bytes 262176 | tf_op jit(solution)/shard_map/ppermute | solution.py:510
  77.8 10.7 %conditional.1 = (bf16[2,2,16,1024]{3,2,1,0:T(8,128)(2,1)S(1)}) conditional(s32[]{:T(128)} %convert_element_type.99, () %tuple.15, (s32[1]{0:T(128)}, bf16[2048,1024]{1,0:T(8,128)(2,1)}, bf16[128,1024]{1,0:T(8,128)(2,1)S(1)}, bf16[128,1024]{1,0:T(8,128)(2,1)S(1)}, bf16[128,1024]{1,0:T(8,128)(2,1)S(1)}, /*index=5*/bf16[128,1024]{1,0:T(8,128)(2,1)S(1)}, ...), branch_computations={%region_0.1_spmd, %region_1.2_spmd} | conditional | flops 786474 | bytes 33539460 | solution.py:674
  77.9 3.3 %project.2 = bf16[2,2,2,2,16,1024]{5,4,3,2,1,0:T(8,128)(2,1)S(1)} custom-call(s32[1]{0:T(128)} %get-tuple-element.24.where_ref, bf16[2048,1024]{1,0:T(8,128)(2,1)} %get-tuple-element.25.weight_ref, bf16[128,1024]{1,0:T(8,128)(2,1)S(1)} %get-tuple-element.26.refs_0_, bf16[128,1024]{1,0:T(8,128)(2,1)S(1)} %get-tuple-element.27.refs_1_, ...), custom_call_target="tpu_custom_call" | custom-call | flops 1 | bytes 30000000 | tf_op jit(solution)/shard_map/cond/branch_1_fun/project/pallas_call | solution.py:497
  81.3 1.5 %collective-permute-done = bf16[1,2,2,2,16,1024]{5,4,3,2,1,0:T(8,128)(2,1)S(1)} collective-permute-done((bf16[1,2,2,2,16,1024]{5,4,3,2,1,0:T(8,128)(2,1)S(1)}, bf16[1,2,2,2,16,1024]{5,4,3,2,1,0:T(8,128)(2,1)S(1)}, u32[]{:S(2)}, u32[]{:S(2)}) %collective-permute-start) | collective-permute-done | bytes 262176 | tf_op jit(solution)/shard_map/cond/branch_1_fun/ppermute | solution.py:475
  82.9 1.6 %collective-permute-start.1 = (bf16[1,2,2,16,1024]{4,3,2,1,0:T(8,128)(2,1)S(1)}, bf16[1,2,2,16,1024]{4,3,2,1,0:T(8,128)(2,1)S(1)}, u32[]{:S(2)}, u32[]{:S(2)}) collective-permute-start(bf16[1,2,2,16,1024]{4,3,2,1,0:T(8,128)(2,1)S(1)} %dynamic-slice_bitcast_fusion), channel_id=1, source_target_pairs={{0,2},{2,0},{1,3},{3,1},{4,6},{6,4},{5,7},{7,5},{8,10},{10,8},{9,1... | collective-permute-start | bytes 393224 | tf_op jit(solution)/shard_map/cond/branch_1_fun/ppermute | solution.py:475
  84.4 4.0 %collective-permute-done.1 = bf16[1,2,2,16,1024]{4,3,2,1,0:T(8,128)(2,1)S(1)} collective-permute-done((bf16[1,2,2,16,1024]{4,3,2,1,0:T(8,128)(2,1)S(1)}, bf16[1,2,2,16,1024]{4,3,2,1,0:T(8,128)(2,1)S(1)}, u32[]{:S(2)}, u32[]{:S(2)}) %collective-permute-start.1) | collective-permute-done | bytes 131104 | tf_op jit(solution)/shard_map/cond/branch_1_fun/ppermute | solution.py:475
  88.5 1.4 %collective-permute-done.13.refs_1_ = bf16[128,1024]{1,0:T(8,128)(2,1)S(1)} collective-permute-done((bf16[128,1024]{1,0:T(8,128)(2,1)S(1)}, bf16[128,1024]{1,0:T(8,128)(2,1)S(1)}, u32[]{:S(2)}, u32[]{:S(2)}) %collective-permute-start.13) | collective-permute-done | bytes 262176 | tf_op jit(solution)/shard_map/ppermute | solution.py:510
  90.0 3.3 %project.3 = bf16[2,2,2,2,16,1024]{5,4,3,2,1,0:T(8,128)(2,1)S(1)} custom-call(s32[1]{0:T(128)} %bitcast.5.where_ref.refs_2_, bf16[2048,1024]{1,0:T(8,128)(2,1)} %weight_ref.1, bf16[128,1024]{1,0:T(8,128)(2,1)S(1)} %add.237.refs_0_, bf16[128,1024]{1,0:T(8,128)(2,1)S(1)} %collective-permute-done.13.refs_1_, ...), custom_call_target="tpu_custom_call" | custom-call | flops 1 | bytes 30000000 | tf_op jit(solution)/shard_map/project/pallas_call | solution.py:497
  93.4 1.5 %collective-permute-done.16 = bf16[1,2,2,2,16,1024]{5,4,3,2,1,0:T(8,128)(2,1)S(1)} collective-permute-done((bf16[1,2,2,2,16,1024]{5,4,3,2,1,0:T(8,128)(2,1)S(1)}, bf16[1,2,2,2,16,1024]{5,4,3,2,1,0:T(8,128)(2,1)S(1)}, u32[]{:S(2)}, u32[]{:S(2)}) %collective-permute-start.16) | collective-permute-done | bytes 262176 | tf_op jit(solution)/shard_map/ppermute | solution.py:475
  95.0 1.6 %collective-permute-start.17 = (bf16[1,2,2,16,1024]{4,3,2,1,0:T(8,128)(2,1)S(1)}, bf16[1,2,2,16,1024]{4,3,2,1,0:T(8,128)(2,1)S(1)}, u32[]{:S(2)}, u32[]{:S(2)}) collective-permute-start(bf16[1,2,2,16,1024]{4,3,2,1,0:T(8,128)(2,1)S(1)} %dynamic-slice_bitcast_fusion.1), channel_id=1, source_target_pairs={{0,2},{2,0},{1,3},{3,1},{4,6},{6,4},{5,7},{7,5},{8,10},{10,8},{9,1... | collective-permute-start | bytes 393224 | tf_op jit(solution)/shard_map/ppermute | solution.py:475
  96.5 4.0 %collective-permute-done.17 = bf16[1,2,2,16,1024]{4,3,2,1,0:T(8,128)(2,1)S(1)} collective-permute-done((bf16[1,2,2,16,1024]{4,3,2,1,0:T(8,128)(2,1)S(1)}, bf16[1,2,2,16,1024]{4,3,2,1,0:T(8,128)(2,1)S(1)}, u32[]{:S(2)}, u32[]{:S(2)}) %collective-permute-start.17) | collective-permute-done | bytes 131104 | tf_op jit(solution)/shard_map/ppermute | solution.py:475
  100.7 1.6 %collective-permute-start.19 = (bf16[32,1024]{1,0:T(8,128)(2,1)S(1)}, bf16[32,1024]{1,0:T(8,128)(2,1)S(1)}, u32[]{:S(2)}, u32[]{:S(2)}) collective-permute-start(bf16[32,1024]{1,0:T(8,128)(2,1)S(1)} %bitcast.44), channel_id=1, source_target_pairs={{0,8},{4,12},{8,0},{12,4},{1,9},{5,13},{9,1},{13,5},{2,10},{6,14},... | collective-permute-start | bytes 196616 | tf_op jit(solution)/shard_map/ppermute | solution.py:510
  102.3 2.4 %collective-permute-start.20 = (bf16[32,1024]{1,0:T(8,128)(2,1)S(1)}, bf16[32,1024]{1,0:T(8,128)(2,1)S(1)}, u32[]{:S(2)}, u32[]{:S(2)}) collective-permute-start(bf16[32,1024]{1,0:T(8,128)(2,1)S(1)} %bitcast.43), channel_id=1, source_target_pairs={{0,12},{4,8},{8,4},{12,0},{1,13},{5,9},{9,5},{13,1},{2,14},{6,10},... | collective-permute-start | bytes 196616 | tf_op jit(solution)/shard_map/ppermute | solution.py:510
  104.8 3.0 %collective-permute-done.19.refs_2_ = bf16[32,1024]{1,0:T(8,128)(2,1)S(1)} collective-permute-done((bf16[32,1024]{1,0:T(8,128)(2,1)S(1)}, bf16[32,1024]{1,0:T(8,128)(2,1)S(1)}, u32[]{:S(2)}, u32[]{:S(2)}) %collective-permute-start.19) | collective-permute-done | bytes 65568 | tf_op jit(solution)/shard_map/ppermute | solution.py:510
  107.8 0.8 collective-permute-done.20.refs_3_
  108.6 0.7 collective-permute-done.18.refs_1_
  109.3 0.7 place.1
  (31 shorter events, 0.7 us)
Async XLA Ops:
  0.0 36.2 %copy-start = (bf16[256,256]{1,0:T(8,128)(2,1)S(1)}, bf16[256,256]{1,0:T(8,128)(2,1)}, u32[]{:S(2)}) copy-start(bf16[256,256]{1,0:T(8,128)(2,1)} %constant.219.clone.refs_9_) | copy-start | bytes 393220
  4.0 13.3 %collective-permute-start.5 = (bf16[128,1664]{1,0:T(8,128)(2,1)S(1)}, bf16[128,1664]{1,0:T(8,128)(2,1)S(1)}, u32[]{:S(2)}, u32[]{:S(2)}) collective-permute-start(bf16[128,1664]{1,0:T(8,128)(2,1)S(1)} %get-tuple-element.57), channel_id=1, source_target_pairs={{0,4},{4,0},{8,12},{12,8},{1,5},{5,1},{9,13},{13,9},{2,6},{6,2},{1... | collective-permute-start | bytes 1277960 | tf_op jit(solution)/shard_map/ppermute | solution.py:510
  7.1 29.1 %collective-permute-start.2 = (bf16[1296,128]{1,0:T(8,128)(2,1)S(1)}, bf16[1296,128]{1,0:T(8,128)(2,1)S(1)}, u32[]{:S(2)}, u32[]{:S(2)}) collective-permute-start(bf16[1296,128]{1,0:T(8,128)(2,1)S(1)} %get-tuple-element.54), channel_id=1, source_target_pairs={{0,8},{4,12},{1,9},{5,13},{2,10},{6,14},{3,11},{7,15},{16,24},{20,... | collective-permute-start | bytes 995336 | tf_op jit(solution)/shard_map/ppermute | solution.py:564
  11.6 66.2 %copy-start.1 = (s32[2048]{0:T(1024)S(1)}, s32[2048]{0:T(1024)}, u32[]{:S(2)}) copy-start(s32[2048]{0:T(1024)} %param.23) | copy-start | bytes 24580
  11.6 24.6 %collective-permute-start.3 = (bf16[1296,128]{1,0:T(8,128)(2,1)S(1)}, bf16[1296,128]{1,0:T(8,128)(2,1)S(1)}, u32[]{:S(2)}, u32[]{:S(2)}) collective-permute-start(bf16[1296,128]{1,0:T(8,128)(2,1)S(1)} %get-tuple-element.55), channel_id=1, source_target_pairs={{0,12},{4,8},{1,13},{5,9},{2,14},{6,10},{3,15},{7,11},{16,28},{20,... | collective-permute-start | bytes 995336 | tf_op jit(solution)/shard_map/ppermute | solution.py:565
  14.7 21.5 %collective-permute-start.4 = (bf16[128,1024]{1,0:T(8,128)(2,1)}, bf16[128,1024]{1,0:T(8,128)(2,1)S(1)}, u32[]{:S(2)}, u32[]{:S(2)}) collective-permute-start(bf16[128,1024]{1,0:T(8,128)(2,1)} %get-tuple-element.82), channel_id=1, source_target_pairs={{0,4},{4,0},{8,12},{12,8},{1,5},{5,1},{9,13},{13,9},{2,6},{6,2},{1... | collective-permute-start | bytes 786440 | tf_op jit(solution)/shard_map/ppermute | solution.py:510
  37.3 1.6 %collective-permute-start.6 = (bf16[128,1024]{1,0:T(8,128)(2,1)S(1)}, bf16[128,1024]{1,0:T(8,128)(2,1)S(1)}, u32[]{:S(2)}, u32[]{:S(2)}) collective-permute-start(bf16[128,1024]{1,0:T(8,128)(2,1)S(1)} %get-tuple-element.61), channel_id=1, source_target_pairs={{0,1},{1,0},{2,3},{3,2},{4,5},{5,4},{6,7},{7,6},{8,9},{9,8},{10,11... | collective-permute-start | bytes 786440 | tf_op jit(solution)/shard_map/ppermute | solution.py:475
  37.4 3.2 %collective-permute-start.8 = (bf16[128,1024]{1,0:T(8,128)(2,1)S(1)}, bf16[128,1024]{1,0:T(8,128)(2,1)S(1)}, u32[]{:S(2)}, u32[]{:S(2)}) collective-permute-start(bf16[128,1024]{1,0:T(8,128)(2,1)S(1)} %get-tuple-element.62), channel_id=1, source_target_pairs={{0,1},{1,0},{2,3},{3,2},{4,5},{5,4},{6,7},{7,6},{8,9},{9,8},{10,11... | collective-permute-start | bytes 786440 | tf_op jit(solution)/shard_map/ppermute | solution.py:475
  39.0 8.4 %collective-permute-start.7 = (bf16[128,1024]{1,0:T(8,128)(2,1)S(1)}, bf16[128,1024]{1,0:T(8,128)(2,1)S(1)}, u32[]{:S(2)}, u32[]{:S(2)}) collective-permute-start(bf16[128,1024]{1,0:T(8,128)(2,1)S(1)} %add_convert_fusion.4), channel_id=1, source_target_pairs={{0,2},{2,0},{1,3},{3,1},{4,6},{6,4},{5,7},{7,5},{8,10},{10,8},{9,1... | collective-permute-start | bytes 786440 | tf_op jit(solution)/shard_map/ppermute | solution.py:475
  47.5 17.5 %collective-permute-start.10 = (bf16[128,1024]{1,0:T(8,128)(2,1)S(1)}, bf16[128,1024]{1,0:T(8,128)(2,1)S(1)}, u32[]{:S(2)}, u32[]{:S(2)}) collective-permute-start(bf16[128,1024]{1,0:T(8,128)(2,1)S(1)} %add_convert_fusion.3), channel_id=1, source_target_pairs={{0,8},{4,12},{8,0},{12,4},{1,9},{5,13},{9,1},{13,5},{2,10},{6,14},... | collective-permute-start | bytes 786440 | tf_op jit(solution)/shard_map/ppermute | solution.py:510
  53.5 12.6 %collective-permute-start.11 = (bf16[128,1024]{1,0:T(8,128)(2,1)S(1)}, bf16[128,1024]{1,0:T(8,128)(2,1)S(1)}, u32[]{:S(2)}, u32[]{:S(2)}) collective-permute-start(bf16[128,1024]{1,0:T(8,128)(2,1)S(1)} %add_convert_fusion.3), channel_id=1, source_target_pairs={{0,4},{4,0},{8,12},{12,8},{1,5},{5,1},{9,13},{13,9},{2,6},{6,2},{1... | collective-permute-start | bytes 786440 | tf_op jit(solution)/shard_map/ppermute | solution.py:510
  53.5 12.6 %collective-permute-start.9 = (bf16[128,1024]{1,0:T(8,128)(2,1)S(1)}, bf16[128,1024]{1,0:T(8,128)(2,1)S(1)}, u32[]{:S(2)}, u32[]{:S(2)}) collective-permute-start(bf16[128,1024]{1,0:T(8,128)(2,1)S(1)} %add_convert_fusion.2.mixed_ref), channel_id=1, source_target_pairs={{0,2},{2,0},{1,3},{3,1},{4,6},{6,4},{5,7},{7,5},{8,10},{10,8},{9,1... | collective-permute-start | bytes 786440 | tf_op jit(solution)/shard_map/ppermute | solution.py:475
  66.1 11.7 %collective-permute-start.12 = (bf16[128,1024]{1,0:T(8,128)(2,1)S(1)}, bf16[128,1024]{1,0:T(8,128)(2,1)S(1)}, u32[]{:S(2)}, u32[]{:S(2)}) collective-permute-start(bf16[128,1024]{1,0:T(8,128)(2,1)S(1)} %collective-permute-done.10), channel_id=1, source_target_pairs={{0,4},{4,0},{8,12},{12,8},{1,5},{5,1},{9,13},{13,9},{2,6},{6,2},{1... | collective-permute-start | bytes 786440 | tf_op jit(solution)/shard_map/ppermute | solution.py:510
  66.8 21.8 %collective-permute-start.14 = (bf16[128,1024]{1,0:T(8,128)(2,1)S(1)}, bf16[128,1024]{1,0:T(8,128)(2,1)S(1)}, u32[]{:S(2)}, u32[]{:S(2)}) collective-permute-start(bf16[128,1024]{1,0:T(8,128)(2,1)S(1)} %add.237.refs_0_), channel_id=1, source_target_pairs={{0,8},{4,12},{8,0},{12,4},{1,9},{5,13},{9,1},{13,5},{2,10},{6,14},... | collective-permute-start | bytes 786440 | tf_op jit(solution)/shard_map/ppermute | solution.py:510
  66.8 21.7 %collective-permute-start.15 = (bf16[128,1024]{1,0:T(8,128)(2,1)S(1)}, bf16[128,1024]{1,0:T(8,128)(2,1)S(1)}, u32[]{:S(2)}, u32[]{:S(2)}) collective-permute-start(bf16[128,1024]{1,0:T(8,128)(2,1)S(1)} %add.237.refs_0_), channel_id=1, source_target_pairs={{0,12},{4,8},{8,4},{12,0},{1,13},{5,9},{9,5},{13,1},{2,14},{6,10},... | collective-permute-start | bytes 786440 | tf_op jit(solution)/shard_map/ppermute | solution.py:510
  77.8 12.2 %collective-permute-start.13 = (bf16[128,1024]{1,0:T(8,128)(2,1)S(1)}, bf16[128,1024]{1,0:T(8,128)(2,1)S(1)}, u32[]{:S(2)}, u32[]{:S(2)}) collective-permute-start(bf16[128,1024]{1,0:T(8,128)(2,1)S(1)} %add.237.refs_0_), channel_id=1, source_target_pairs={{0,4},{4,0},{8,12},{12,8},{1,5},{5,1},{9,13},{13,9},{2,6},{6,2},{1... | collective-permute-start | bytes 786440 | tf_op jit(solution)/shard_map/ppermute | solution.py:510
  81.2 1.6 %collective-permute-start = (bf16[1,2,2,2,16,1024]{5,4,3,2,1,0:T(8,128)(2,1)S(1)}, bf16[1,2,2,2,16,1024]{5,4,3,2,1,0:T(8,128)(2,1)S(1)}, u32[]{:S(2)}, u32[]{:S(2)}) collective-permute-start(bf16[1,2,2,2,16,1024]{5,4,3,2,1,0:T(8,128)(2,1)S(1)} %constant_dynamic-slice_fusion), channel_id=1, source_target_pairs={{0,1},{1,0},{2,3},{3,2},{4,5},{5,4},{6,7},{7,6},{8,9},{9,8},{10,11... | collective-permute-start | bytes 786440 | tf_op jit(solution)/shard_map/cond/branch_1_fun/ppermute | solution.py:475
  82.9 5.6 %collective-permute-start.1 = (bf16[1,2,2,16,1024]{4,3,2,1,0:T(8,128)(2,1)S(1)}, bf16[1,2,2,16,1024]{4,3,2,1,0:T(8,128)(2,1)S(1)}, u32[]{:S(2)}, u32[]{:S(2)}) collective-permute-start(bf16[1,2,2,16,1024]{4,3,2,1,0:T(8,128)(2,1)S(1)} %dynamic-slice_bitcast_fusion), channel_id=1, source_target_pairs={{0,2},{2,0},{1,3},{3,1},{4,6},{6,4},{5,7},{7,5},{8,10},{10,8},{9,1... | collective-permute-start | bytes 393224 | tf_op jit(solution)/shard_map/cond/branch_1_fun/ppermute | solution.py:475
  93.3 1.6 %collective-permute-start.16 = (bf16[1,2,2,2,16,1024]{5,4,3,2,1,0:T(8,128)(2,1)S(1)}, bf16[1,2,2,2,16,1024]{5,4,3,2,1,0:T(8,128)(2,1)S(1)}, u32[]{:S(2)}, u32[]{:S(2)}) collective-permute-start(bf16[1,2,2,2,16,1024]{5,4,3,2,1,0:T(8,128)(2,1)S(1)} %constant_dynamic-slice_fusion.3), channel_id=1, source_target_pairs={{0,1},{1,0},{2,3},{3,2},{4,5},{5,4},{6,7},{7,6},{8,9},{9,8},{10,11... | collective-permute-start | bytes 786440 | tf_op jit(solution)/shard_map/ppermute | solution.py:475
  95.0 5.6 %collective-permute-start.17 = (bf16[1,2,2,16,1024]{4,3,2,1,0:T(8,128)(2,1)S(1)}, bf16[1,2,2,16,1024]{4,3,2,1,0:T(8,128)(2,1)S(1)}, u32[]{:S(2)}, u32[]{:S(2)}) collective-permute-start(bf16[1,2,2,16,1024]{4,3,2,1,0:T(8,128)(2,1)S(1)} %dynamic-slice_bitcast_fusion.1), channel_id=1, source_target_pairs={{0,2},{2,0},{1,3},{3,1},{4,6},{6,4},{5,7},{7,5},{8,10},{10,8},{9,1... | collective-permute-start | bytes 393224 | tf_op jit(solution)/shard_map/ppermute | solution.py:475
  100.7 7.1 %collective-permute-start.19 = (bf16[32,1024]{1,0:T(8,128)(2,1)S(1)}, bf16[32,1024]{1,0:T(8,128)(2,1)S(1)}, u32[]{:S(2)}, u32[]{:S(2)}) collective-permute-start(bf16[32,1024]{1,0:T(8,128)(2,1)S(1)} %bitcast.44), channel_id=1, source_target_pairs={{0,8},{4,12},{8,0},{12,4},{1,9},{5,13},{9,1},{13,5},{2,10},{6,14},... | collective-permute-start | bytes 196616 | tf_op jit(solution)/shard_map/ppermute | solution.py:510
  102.3 6.3 %collective-permute-start.20 = (bf16[32,1024]{1,0:T(8,128)(2,1)S(1)}, bf16[32,1024]{1,0:T(8,128)(2,1)S(1)}, u32[]{:S(2)}, u32[]{:S(2)}) collective-permute-start(bf16[32,1024]{1,0:T(8,128)(2,1)S(1)} %bitcast.43), channel_id=1, source_target_pairs={{0,12},{4,8},{8,4},{12,0},{1,13},{5,9},{9,5},{13,1},{2,14},{6,10},... | collective-permute-start | bytes 196616 | tf_op jit(solution)/shard_map/ppermute | solution.py:510
  104.7 4.5 %collective-permute-start.18 = (bf16[32,1024]{1,0:T(8,128)(2,1)S(1)}, bf16[32,1024]{1,0:T(8,128)(2,1)S(1)}, u32[]{:S(2)}, u32[]{:S(2)}) collective-permute-start(bf16[32,1024]{1,0:T(8,128)(2,1)S(1)} %bitcast.45), channel_id=1, source_target_pairs={{0,4},{4,0},{8,12},{12,8},{1,5},{5,1},{9,13},{13,9},{2,6},{6,2},{1... | collective-permute-start | bytes 196616 | tf_op jit(solution)/shard_map/ppermute | solution.py:510

commit v5 on v4

--- a/solution.py
+++ b/solution.py
@@ -618,34 +618,39 @@
         return mixed
 
     first, second = (across(chunk, "sub") for chunk in chunks)
+    ahead = range(1, pairs)
+    near_second = swap_seq(second, 1)
+    far_early = [swap_seq(second[: tokens // 2], 2 * k) for k in ahead]
     first = across(first, "chan")
-    first, second = lax.optimization_barrier((first, second))
+    first, second, near_second, far_early = lax.optimization_barrier(
+        (first, second, near_second, far_early)
+    )
     bits = bits_of("chan")
+    moving = [second[: tokens // 2], second[tokens // 2 :], *far_early]
     for bit in bits[:-1]:
-        second = add_across(second, "chan", bit, swap(second, "chan", bit))
-    received = swap(second, "chan", bits[-1]) if bits else None
-    ahead = range(1, pairs)
+        moving = [add_across(value, "chan", bit, swap(value, "chan", bit)) for value in moving]
+    received = [swap(value, "chan", bits[-1]) for value in moving if bits]
     far_first = [swap_seq(first, 2 * k) for k in ahead]
     near_first = swap_seq(first, 1)
-    first, second, received, far_first, near_first = lax.optimization_barrier(
-        (first, second, received, far_first, near_first)
+    first, near_second, moving, received, far_first, near_first = lax.optimization_barrier(
+        (first, near_second, moving, received, far_first, near_first)
     )
     if bits:
-        sign = 1 - 2 * (lax.axis_index("chan") // 2 ** bits[-1] % 2)
-        second = call(
-            add_kernel,
-            shape(tokens, half, bf16),
-            "add",
-            (jnp.full((1,), sign, jnp.int32), second, received),
-            1,
-        )
+        sign = jnp.full((1,), 1 - 2 * (lax.axis_index("chan") // 2 ** bits[-1] % 2), jnp.int32)
+        moving = [
+            call(add_kernel, shape(*mixed.shape, bf16), "add", (sign, mixed, other), 1)
+            for mixed, other in zip(moving, received)
+        ]
+    early, late, *far_early = moving
     passed_first = [swap_seq(value, 1) for value in far_first]
     all_first = [first, near_first]
     for far, passed in zip(far_first, passed_first):
         all_first += [far, passed]
-    second_late = lax.optimization_barrier((second, passed_first))[0] if pairs > 1 else second
-    all_second = [second, swap_seq(second_late, 1)]
-    all_second += [swap_seq(second, k) for k in range(2, seq_count)]
+    all_first, far_early = lax.optimization_barrier((all_first, far_early))
+    passed_early = [swap_seq(value, 1) for value in far_early]
+    far_late = [swap_seq(late, 2 * k) for k in ahead]
+    cross_late = [swap_seq(late, 2 * k + 1) for k in ahead]
+    near_second = across(near_second, "chan")
 
     up = (power_two(channel_shift_power, 1) * (1.0 / math.sqrt(LOCAL_HEADS * P_SIZE)))[None, :]
     down = power_two(channel_shift_power, -1)[None, :]
@@ -667,18 +672,27 @@
             WIDE_PARAMS,
         )
 
-    def reduce(partial):
-        return halve(halve(partial, "sub"), "chan")
-
-    done = lax.optimization_barrier(jnp.bool_(True))
-    done_first = lax.cond(
-        done,
-        lambda *pieces: reduce(project(pieces)),
-        lambda *pieces: jnp.zeros((pairs, 2, size, features), bf16),
-        *all_first,
-    )
-    done_first, all_second = lax.optimization_barrier((done_first, all_second))
-    done_second = reduce(project(all_second))
+    go = lax.optimization_barrier(jnp.bool_(True))
+
+    def stage(pieces):
+        return lax.cond(
+            go,
+            lambda *pieces: halve(project(pieces), "sub"),
+            lambda *_: jnp.zeros((chan_count, pairs, 2, size, features), bf16),
+            *pieces,
+        )
+
+    done_first = stage(all_first)
+    done_first, near_second, far_late, cross_late, passed_early = lax.optimization_barrier(
+        (done_first, near_second, far_late, cross_late, passed_early)
+    )
+    all_second = [jnp.concatenate([early, late], axis=0), near_second]
+    for parts in zip(far_early, far_late, passed_early, cross_late):
+        all_second += [jnp.concatenate(parts[:2], axis=0), jnp.concatenate(parts[2:], axis=0)]
+    done_first, done_second = lax.optimization_barrier(
+        (halve(done_first, "chan"), stage(all_second))
+    )
+    done_second = halve(done_second, "chan")
     summed = jnp.stack([done_first, done_second], axis=2)
     returned = []
     for distance in range(seq_count):

time: 110 us -> 109 us (level)
  waiting for transfers between devices: 60.5 us -> 53.1 us
  starting transfers between devices: 30.9 us -> 37 us
    ppermute x11 -> x13, waiting for transfers between devices: 41.6 us -> 36.1 us  [swap_seq(): return lax.ppermute(value, 'seq', [(k, k ^ distance) for k in range(count)])]
    ppermute x11 -> x13, starting transfers between devices: 18.2 us -> 23.6 us  [swap_seq(): return lax.ppermute(value, 'seq', [(k, k ^ distance) for k in range(count)])]
    ppermute x8 -> x11, waiting for transfers between devices: 18.8 us -> 16.9 us  [swap(): return lax.ppermute(value, axis, [(k, k ^ 1 << bit) for k in range(count)])]
    ppermute x8 -> x11, starting transfers between devices: 6.92 us -> 7.58 us  [swap(): return lax.ppermute(value, axis, [(k, k ^ 1 << bit) for k in range(count)])]
    pallas_call x6 -> x8, Pallas kernels: 10.1 us -> 10.1 us  [call(): pl.pallas_call(kernel, out_shape=out_shape, in_specs=specs, scratch_shape...]
  transfers between devices with their start and end apart: 21 -> 26, of which waited for: 15 -> 17; matrix products, arithmetic and copies ran while one was open for 3% -> 4% of each run, Pallas kernels for 5% -> 8%
where the time goes in v5:
time: 109 us
  waiting for transfers between devices  53.1 us (49%)
  starting transfers between devices  37 us (34%)
  Pallas kernels  11.2 us (10%)
  local copies, waits for them, and re-layouts  5.07 us (5%)
  other arithmetic  2.13 us (2%)
    ppermute x13, waiting for transfers between devices, swap_seq(): return lax.ppermute(value, 'seq', [(k, k ^ distance) for k in range(count)])  36.1 us
    ppermute x13, starting transfers between devices, swap_seq(): return lax.ppermute(value, 'seq', [(k, k ^ distance) for k in range(count)])  23.6 us
    ppermute x11, waiting for transfers between devices, swap(): return lax.ppermute(value, axis, [(k, k ^ 1 << bit) for k in range(count)])  16.9 us
    pallas_call x8, Pallas kernels, call(): pl.pallas_call(kernel, out_shape=out_shape, in_specs=specs, scratch_shape...  10.1 us
    ppermute x11, starting transfers between devices, swap(): return lax.ppermute(value, axis, [(k, k ^ 1 << bit) for k in range(count)])  7.58 us
    ppermute x1, starting transfers between devices, paired_body(): lax.ppermute(straight, 'seq', [(k, k + 2 * ahead) for k in firsts])  4.5 us
    dynamic_slice x2, local copies, waits for them, and re-layouts, half_of(): return lax.dynamic_slice_in_dim(value, which * half, half, 1)  2.84 us
  transfers between devices with their start and end apart: 26, of which 17 were waited for; matrix products, arithmetic and copies ran while one was open for 4% of the time, Pallas kernels for 8%

profile of v5, /device:TPU:0, one launch (start us, length us, event | category | flops | bytes accessed | tf_op | source)
XLA Modules:
  0.0 108.9 jit_solution(8114585351036064613)
XLA Ops:
  0.0 1.3 %constant_dynamic-slice_fusion.8 = (bf16[128,1,256]{2,1,0:T(2,128)(2,1)S(1)}, bf16[128,1,256]{2,1,0:T(2,128)(2,1)S(1)}) fusion(bf16[128,2,256]{2,1,0:T(2,128)(2,1)} %param.18, s32[]{:T(128)S(6)} %select_n.147, bf16[128,2,256]{2,1,0:T(2,128)(2,1)} %param.17), kind=kLoop, calls=%fused_computation.50 | loop fusion | bytes 262148 | tf_op jit(solution)/shard_map/jit(dynamic_index_in_dim)/dynamic_slice | solution.py:537
  1.3 0.7 pad_maximum_fusion.3.steps_ref
  2.1 1.1 constant_dynamic-slice_fusion.10
  3.1 0.8 pack.1
  4.0 3.1 %collective-permute-start.5 = (bf16[128,1664]{1,0:T(8,128)(2,1)S(1)}, bf16[128,1664]{1,0:T(8,128)(2,1)S(1)}, u32[]{:S(2)}, u32[]{:S(2)}) collective-permute-start(bf16[128,1664]{1,0:T(8,128)(2,1)S(1)} %get-tuple-element.97), channel_id=1, source_target_pairs={{0,4},{4,0},{8,12},{12,8},{1,5},{5,1},{9,13},{13,9},{2,6},{6,2},{1... | collective-permute-start | bytes 1277960 | tf_op jit(solution)/shard_map/ppermute | solution.py:510
  7.1 4.5 %collective-permute-start.2 = (bf16[1296,128]{1,0:T(8,128)(2,1)S(1)}, bf16[1296,128]{1,0:T(8,128)(2,1)S(1)}, u32[]{:S(2)}, u32[]{:S(2)}) collective-permute-start(bf16[1296,128]{1,0:T(8,128)(2,1)S(1)} %get-tuple-element.94), channel_id=1, source_target_pairs={{0,8},{4,12},{1,9},{5,13},{2,10},{6,14},{3,11},{7,15},{16,24},{20,... | collective-permute-start | bytes 995336 | tf_op jit(solution)/shard_map/ppermute | solution.py:564
  11.6 1.3 %collective-permute-start.3 = (bf16[1296,128]{1,0:T(8,128)(2,1)S(1)}, bf16[1296,128]{1,0:T(8,128)(2,1)S(1)}, u32[]{:S(2)}, u32[]{:S(2)}) collective-permute-start(bf16[1296,128]{1,0:T(8,128)(2,1)S(1)} %get-tuple-element.95), channel_id=1, source_target_pairs={{0,12},{4,8},{1,13},{5,9},{2,14},{6,10},{3,15},{7,11},{16,28},{20,... | collective-permute-start | bytes 995336 | tf_op jit(solution)/shard_map/ppermute | solution.py:565
  12.9 1.8 %constant_dynamic-slice_fusion.6 = (bf16[128,1024]{1,0:T(8,128)(2,1)}, bf16[128,1024]{1,0:T(8,128)(2,1)S(1)}) fusion(bf16[128,2048]{1,0:T(8,128)(2,1)} %param.22, s32[]{:T(128)S(6)} %select_n.145, s32[]{:T(128)S(6)} %select_n.144), kind=kLoop, calls=%fused_computation.48 | loop fusion | bytes 1048584 | tf_op jit(solution)/shard_map/dynamic_slice | solution.py:547
  14.7 0.5 collective-permute-start.4
  15.2 0.7 broadcast_in_dim.67
  16.0 0.7 select_multiply_fusion
  16.8 0.5 collective-permute-done.5.msg_ref
  17.3 1.9 %pair.1 = (f32[256,1024]{1,0:T(8,128)S(1)}, f32[256,1024]{1,0:T(8,128)S(1)}, bf16[256,256]{1,0:T(8,128)(2,1)S(1)}) custom-call(s32[1]{0:T(128)} %bitcast.3.where_ref.refs_2_, bf16[128,1024]{1,0:T(8,128)(2,1)S(1)} %get-tuple-element.138.x_mine_ref.x_ref, bf16[128,640]{1,0:T(8,128)(2,1)S(1)} %get-tuple-element.96.meta_ref, ...), custom_call_target="tpu_custom_call" | custom-call | flops 1 | bytes 1 | tf_op jit(solution)/shard_map/pair/pallas_call | solution.py:497
  19.2 17.0 %collective-permute-done.4.refs_4_ = bf16[128,1024]{1,0:T(8,128)(2,1)S(1)} collective-permute-done((bf16[128,1024]{1,0:T(8,128)(2,1)}, bf16[128,1024]{1,0:T(8,128)(2,1)S(1)}, u32[]{:S(2)}, u32[]{:S(2)}) %collective-permute-start.4) | collective-permute-done | bytes 262176 | tf_op jit(solution)/shard_map/ppermute | solution.py:510
  36.2 1.1 %mix.1 = (bf16[128,1024]{1,0:T(8,128)(2,1)S(1)}, bf16[128,1024]{1,0:T(8,128)(2,1)S(1)}) custom-call(bf16[1296,128]{1,0:T(8,128)(2,1)S(1)} %collective-permute-done.2.refs_0_, bf16[1296,128]{1,0:T(8,128)(2,1)S(1)} %collective-permute-done.3.refs_1_, s32[1]{0:T(128)} %bitcast.3.where_ref.refs_2_, bf16[128,1024]{1,0:T(8,128)(2,1)S(1)} %get-tuple-element.136.refs_3_, ...), custom_call_target="tpu_custom_call" | custom-call | flops 1 | bytes 30000000 | tf_op jit(solution)/shard_map/mix/pallas_call | solution.py:598
  37.9 1.0 collective-permute-done.6
  39.0 1.6 %collective-permute-start.7 = (bf16[128,1024]{1,0:T(8,128)(2,1)S(1)}, bf16[128,1024]{1,0:T(8,128)(2,1)S(1)}, u32[]{:S(2)}, u32[]{:S(2)}) collective-permute-start(bf16[128,1024]{1,0:T(8,128)(2,1)S(1)} %add_convert_fusion.5), channel_id=1, source_target_pairs={{0,2},{2,0},{1,3},{3,1},{4,6},{6,4},{5,7},{7,5},{8,10},{10,8},{9,1... | collective-permute-start | bytes 786440 | tf_op jit(solution)/shard_map/ppermute | solution.py:475
  40.7 4.0 %collective-permute-start.9 = (bf16[128,1024]{1,0:T(8,128)(2,1)S(1)}, bf16[128,1024]{1,0:T(8,128)(2,1)S(1)}, u32[]{:S(2)}, u32[]{:S(2)}) collective-permute-start(bf16[128,1024]{1,0:T(8,128)(2,1)S(1)} %add_convert_fusion.3), channel_id=1, source_target_pairs={{0,4},{4,0},{8,12},{12,8},{1,5},{5,1},{9,13},{13,9},{2,6},{6,2},{1... | collective-permute-start | bytes 786440 | tf_op jit(solution)/shard_map/ppermute | solution.py:510
  44.7 2.0 %collective-permute-start.10 = (bf16[64,1024]{1,0:T(8,128)(2,1)S(1)}, bf16[64,1024]{1,0:T(8,128)(2,1)S(1)}, u32[]{:S(2)}, u32[]{:S(2)}) collective-permute-start(bf16[64,1024]{1,0:T(8,128)(2,1)S(1)} %slice.22), channel_id=1, source_target_pairs={{0,8},{4,12},{8,0},{12,4},{1,9},{5,13},{9,1},{13,5},{2,10},{6,14},... | collective-permute-start | bytes 393224 | tf_op jit(solution)/shard_map/ppermute | solution.py:510
  46.8 0.7 collective-permute-done.7
  47.5 5.6 %collective-permute-done.10.mixed_ref = bf16[64,1024]{1,0:T(8,128)(2,1)S(1)} collective-permute-done((bf16[64,1024]{1,0:T(8,128)(2,1)S(1)}, bf16[64,1024]{1,0:T(8,128)(2,1)S(1)}, u32[]{:S(2)}, u32[]{:S(2)}) %collective-permute-start.10) | collective-permute-done | bytes 131104 | tf_op jit(solution)/shard_map/ppermute | solution.py:510
  53.1 0.7 collective-permute-done.9
  53.9 2.6 %collective-permute-start.14 = (bf16[128,1024]{1,0:T(8,128)(2,1)S(1)}, bf16[128,1024]{1,0:T(8,128)(2,1)S(1)}, u32[]{:S(2)}, u32[]{:S(2)}) collective-permute-start(bf16[128,1024]{1,0:T(8,128)(2,1)S(1)} %add_convert_fusion.4), channel_id=1, source_target_pairs={{0,8},{4,12},{8,0},{12,4},{1,9},{5,13},{9,1},{13,5},{2,10},{6,14},... | collective-permute-start | bytes 786440 | tf_op jit(solution)/shard_map/ppermute | solution.py:510
  56.5 1.3 %collective-permute-start.15 = (bf16[128,1024]{1,0:T(8,128)(2,1)S(1)}, bf16[128,1024]{1,0:T(8,128)(2,1)S(1)}, u32[]{:S(2)}, u32[]{:S(2)}) collective-permute-start(bf16[128,1024]{1,0:T(8,128)(2,1)S(1)} %add_convert_fusion.4), channel_id=1, source_target_pairs={{0,4},{4,0},{8,12},{12,8},{1,5},{5,1},{9,13},{13,9},{2,6},{6,2},{1... | collective-permute-start | bytes 786440 | tf_op jit(solution)/shard_map/ppermute | solution.py:510
  57.8 0.6 collective-permute-start.11
  58.4 1.5 %collective-permute-start.12 = (bf16[64,1024]{1,0:T(8,128)(2,1)S(1)}, bf16[64,1024]{1,0:T(8,128)(2,1)S(1)}, u32[]{:S(2)}, u32[]{:S(2)}) collective-permute-start(bf16[64,1024]{1,0:T(8,128)(2,1)S(1)} %get-tuple-element.117.mixed_ref), channel_id=1, source_target_pairs={{0,2},{2,0},{1,3},{3,1},{4,6},{6,4},{5,7},{7,5},{8,10},{10,8},{9,1... | collective-permute-start | bytes 393224 | tf_op jit(solution)/shard_map/ppermute | solution.py:475
  60.5 3.9 %collective-permute-done.11.received_ref = bf16[64,1024]{1,0:T(8,128)(2,1)S(1)} collective-permute-done((bf16[64,1024]{1,0:T(8,128)(2,1)S(1)}, bf16[64,1024]{1,0:T(8,128)(2,1)S(1)}, u32[]{:S(2)}, u32[]{:S(2)}) %collective-permute-start.11) | collective-permute-done | bytes 131104 | tf_op jit(solution)/shard_map/ppermute | solution.py:475
  64.3 1.9 %collective-permute-done.12.received_ref = bf16[64,1024]{1,0:T(8,128)(2,1)S(1)} collective-permute-done((bf16[64,1024]{1,0:T(8,128)(2,1)S(1)}, bf16[64,1024]{1,0:T(8,128)(2,1)S(1)}, u32[]{:S(2)}, u32[]{:S(2)}) %collective-permute-start.12) | collective-permute-done | bytes 131104 | tf_op jit(solution)/shard_map/ppermute | solution.py:475
  66.3 1.4 %collective-permute-done.13.received_ref = bf16[64,1024]{1,0:T(8,128)(2,1)S(1)} collective-permute-done((bf16[64,1024]{1,0:T(8,128)(2,1)S(1)}, bf16[64,1024]{1,0:T(8,128)(2,1)S(1)}, u32[]{:S(2)}, u32[]{:S(2)}) %collective-permute-start.13) | collective-permute-done | bytes 131104 | tf_op jit(solution)/shard_map/ppermute | solution.py:475
  67.7 0.5 collective-permute-done.14
  68.2 0.5 collective-permute-start.17
  68.7 1.2 %collective-permute-start.16 = (bf16[128,1024]{1,0:T(8,128)(2,1)S(1)}, bf16[128,1024]{1,0:T(8,128)(2,1)S(1)}, u32[]{:S(2)}, u32[]{:S(2)}) collective-permute-start(bf16[128,1024]{1,0:T(8,128)(2,1)S(1)} %collective-permute-done.14), channel_id=1, source_target_pairs={{0,4},{4,0},{8,12},{12,8},{1,5},{5,1},{9,13},{13,9},{2,6},{6,2},{1... | collective-permute-start | bytes 786440 | tf_op jit(solution)/shard_map/ppermute | solution.py:510
  70.0 3.6 %collective-permute-start.18 = (bf16[64,1024]{1,0:T(8,128)(2,1)S(1)}, bf16[64,1024]{1,0:T(8,128)(2,1)S(1)}, u32[]{:S(2)}, u32[]{:S(2)}) collective-permute-start(bf16[64,1024]{1,0:T(8,128)(2,1)S(1)} %add.239), channel_id=1, source_target_pairs={{0,8},{4,12},{8,0},{12,4},{1,9},{5,13},{9,1},{13,5},{2,10},{6,14},... | collective-permute-start | bytes 393224 | tf_op jit(solution)/shard_map/ppermute | solution.py:510
  73.7 6.2 %collective-permute-done.16 = bf16[128,1024]{1,0:T(8,128)(2,1)S(1)} collective-permute-done((bf16[128,1024]{1,0:T(8,128)(2,1)S(1)}, bf16[128,1024]{1,0:T(8,128)(2,1)S(1)}, u32[]{:S(2)}, u32[]{:S(2)}) %collective-permute-start.16) | collective-permute-done | bytes 262176 | tf_op jit(solution)/shard_map/ppermute | solution.py:510
  79.9 5.0 %conditional.2 = (bf16[2,2,2,16,1024]{4,3,2,1,0:T(8,128)(2,1)S(1)}) conditional(s32[]{:T(128)} %convert_element_type.92, () %tuple.22, (s32[1]{0:T(128)}, bf16[2048,1024]{1,0:T(8,128)(2,1)}, bf16[128,1024]{1,0:T(8,128)(2,1)S(1)}, bf16[128,1024]{1,0:T(8,128)(2,1)S(1)}, bf16[128,1024]{1,0:T(8,128)(2,1)S(1)}, /*index=5*/bf16[128,1024]{1,0:T(8,128)(2,1)S(1)}, ...), branch_computations={%region_0.1_spmd, %region_1.2_spmd} | conditional | flops 524309 | bytes 32359552 | solution.py:678
  79.9 3.3 %project.2 = bf16[2,2,2,2,16,1024]{5,4,3,2,1,0:T(8,128)(2,1)S(1)} custom-call(s32[1]{0:T(128)} %get-tuple-element.42.where_ref, bf16[2048,1024]{1,0:T(8,128)(2,1)} %get-tuple-element.44.weight_ref, bf16[128,1024]{1,0:T(8,128)(2,1)S(1)} %get-tuple-element.45.refs_0_, bf16[128,1024]{1,0:T(8,128)(2,1)S(1)} %get-tuple-element.46.refs_1_, ...), custom_call_target="tpu_custom_call" | custom-call | flops 1 | bytes 30000000 | tf_op jit(solution)/shard_map/cond/branch_1_fun/project/pallas_call | solution.py:497
  83.3 1.5 %collective-permute-done = bf16[1,2,2,2,16,1024]{5,4,3,2,1,0:T(8,128)(2,1)S(1)} collective-permute-done((bf16[1,2,2,2,16,1024]{5,4,3,2,1,0:T(8,128)(2,1)S(1)}, bf16[1,2,2,2,16,1024]{5,4,3,2,1,0:T(8,128)(2,1)S(1)}, u32[]{:S(2)}, u32[]{:S(2)}) %collective-permute-start) | collective-permute-done | bytes 262176 | tf_op jit(solution)/shard_map/cond/branch_1_fun/ppermute | solution.py:475
  85.2 1.6 %collective-permute-start.21 = (bf16[1,2,2,16,1024]{4,3,2,1,0:T(8,128)(2,1)S(1)}, bf16[1,2,2,16,1024]{4,3,2,1,0:T(8,128)(2,1)S(1)}, u32[]{:S(2)}, u32[]{:S(2)}) collective-permute-start(bf16[1,2,2,16,1024]{4,3,2,1,0:T(8,128)(2,1)S(1)} %constant_dynamic-slice_fusion.5), channel_id=1, source_target_pairs={{0,2},{2,0},{1,3},{3,1},{4,6},{6,4},{5,7},{7,5},{8,10},{10,8},{9,1... | collective-permute-start | bytes 393224 | tf_op jit(solution)/shard_map/ppermute | solution.py:475
  86.8 5.0 %conditional.3 = (bf16[2,2,2,16,1024]{4,3,2,1,0:T(8,128)(2,1)S(1)}) conditional(s32[]{:T(128)} %convert_element_type.92, () %tuple.28, (s32[1]{0:T(128)}, bf16[2048,1024]{1,0:T(8,128)(2,1)}, bf16[128,1024]{1,0:T(8,128)(2,1)S(1)}, bf16[128,1024]{1,0:T(8,128)(2,1)S(1)}, bf16[128,1024]{1,0:T(8,128)(2,1)S(1)}, /*index=5*/bf16[128,1024]{1,0:T(8,128)(2,1)S(1)}, ...), branch_computations={%region_2.3_spmd, %region_3.4_spmd} | conditional | flops 524309 | bytes 32359552 | solution.py:678
  86.8 3.3 %project.3 = bf16[2,2,2,2,16,1024]{5,4,3,2,1,0:T(8,128)(2,1)S(1)} custom-call(s32[1]{0:T(128)} %get-tuple-element.51.where_ref, bf16[2048,1024]{1,0:T(8,128)(2,1)} %get-tuple-element.52.weight_ref, bf16[128,1024]{1,0:T(8,128)(2,1)S(1)} %get-tuple-element.53.refs_0_, bf16[128,1024]{1,0:T(8,128)(2,1)S(1)} %get-tuple-element.54.refs_1_, ...), custom_call_target="tpu_custom_call" | custom-call | flops 1 | bytes 30000000 | tf_op jit(solution)/shard_map/cond/branch_1_fun/project/pallas_call | solution.py:497
  90.2 1.5 %collective-permute-done.1 = bf16[1,2,2,2,16,1024]{5,4,3,2,1,0:T(8,128)(2,1)S(1)} collective-permute-done((bf16[1,2,2,2,16,1024]{5,4,3,2,1,0:T(8,128)(2,1)S(1)}, bf16[1,2,2,2,16,1024]{5,4,3,2,1,0:T(8,128)(2,1)S(1)}, u32[]{:S(2)}, u32[]{:S(2)}) %collective-permute-start.1) | collective-permute-done | bytes 262176 | tf_op jit(solution)/shard_map/cond/branch_1_fun/ppermute | solution.py:475
  91.9 0.6 collective-permute-start.22
  92.4 5.0 %collective-permute-done.22 = bf16[1,2,2,16,1024]{4,3,2,1,0:T(8,128)(2,1)S(1)} collective-permute-done((bf16[1,2,2,16,1024]{4,3,2,1,0:T(8,128)(2,1)S(1)}, bf16[1,2,2,16,1024]{4,3,2,1,0:T(8,128)(2,1)S(1)}, u32[]{:S(2)}, u32[]{:S(2)}) %collective-permute-start.22) | collective-permute-done | bytes 131104 | tf_op jit(solution)/shard_map/ppermute | solution.py:475
  97.6 4.5 %collective-permute-start.24 = (bf16[32,1024]{1,0:T(8,128)(2,1)S(1)}, bf16[32,1024]{1,0:T(8,128)(2,1)S(1)}, u32[]{:S(2)}, u32[]{:S(2)}) collective-permute-start(bf16[32,1024]{1,0:T(8,128)(2,1)S(1)} %bitcast.38), channel_id=1, source_target_pairs={{0,8},{4,12},{8,0},{12,4},{1,9},{5,13},{9,1},{13,5},{2,10},{6,14},... | collective-permute-start | bytes 196616 | tf_op jit(solution)/shard_map/ppermute | solution.py:510
  102.1 0.7 collective-permute-start.23
  102.8 2.5 %collective-permute-done.24.refs_2_ = bf16[32,1024]{1,0:T(8,128)(2,1)S(1)} collective-permute-done((bf16[32,1024]{1,0:T(8,128)(2,1)S(1)}, bf16[32,1024]{1,0:T(8,128)(2,1)S(1)}, u32[]{:S(2)}, u32[]{:S(2)}) %collective-permute-start.24) | collective-permute-done | bytes 65568 | tf_op jit(solution)/shard_map/ppermute | solution.py:510
  105.3 2.9 %collective-permute-done.25.refs_3_ = bf16[32,1024]{1,0:T(8,128)(2,1)S(1)} collective-permute-done((bf16[32,1024]{1,0:T(8,128)(2,1)S(1)}, bf16[32,1024]{1,0:T(8,128)(2,1)S(1)}, u32[]{:S(2)}, u32[]{:S(2)}) %collective-permute-start.25) | collective-permute-done | bytes 65568 | tf_op jit(solution)/shard_map/ppermute | solution.py:510
  108.1 0.7 place.1
  (50 shorter events, 2.5 us)
Async XLA Ops:
  0.0 36.2 %copy-start = (bf16[256,256]{1,0:T(8,128)(2,1)S(1)}, bf16[256,256]{1,0:T(8,128)(2,1)}, u32[]{:S(2)}) copy-start(bf16[256,256]{1,0:T(8,128)(2,1)} %constant.232.clone.refs_9_) | copy-start | bytes 393220
  4.0 13.3 %collective-permute-start.5 = (bf16[128,1664]{1,0:T(8,128)(2,1)S(1)}, bf16[128,1664]{1,0:T(8,128)(2,1)S(1)}, u32[]{:S(2)}, u32[]{:S(2)}) collective-permute-start(bf16[128,1664]{1,0:T(8,128)(2,1)S(1)} %get-tuple-element.97), channel_id=1, source_target_pairs={{0,4},{4,0},{8,12},{12,8},{1,5},{5,1},{9,13},{13,9},{2,6},{6,2},{1... | collective-permute-start | bytes 1277960 | tf_op jit(solution)/shard_map/ppermute | solution.py:510
  7.1 29.1 %collective-permute-start.2 = (bf16[1296,128]{1,0:T(8,128)(2,1)S(1)}, bf16[1296,128]{1,0:T(8,128)(2,1)S(1)}, u32[]{:S(2)}, u32[]{:S(2)}) collective-permute-start(bf16[1296,128]{1,0:T(8,128)(2,1)S(1)} %get-tuple-element.94), channel_id=1, source_target_pairs={{0,8},{4,12},{1,9},{5,13},{2,10},{6,14},{3,11},{7,15},{16,24},{20,... | collective-permute-start | bytes 995336 | tf_op jit(solution)/shard_map/ppermute | solution.py:564
  11.6 48.9 %copy-start.1 = (s32[2048]{0:T(1024)S(1)}, s32[2048]{0:T(1024)}, u32[]{:S(2)}) copy-start(s32[2048]{0:T(1024)} %param.25) | copy-start | bytes 24580
  11.6 24.6 %collective-permute-start.3 = (bf16[1296,128]{1,0:T(8,128)(2,1)S(1)}, bf16[1296,128]{1,0:T(8,128)(2,1)S(1)}, u32[]{:S(2)}, u32[]{:S(2)}) collective-permute-start(bf16[1296,128]{1,0:T(8,128)(2,1)S(1)} %get-tuple-element.95), channel_id=1, source_target_pairs={{0,12},{4,8},{1,13},{5,9},{2,14},{6,10},{3,15},{7,11},{16,28},{20,... | collective-permute-start | bytes 995336 | tf_op jit(solution)/shard_map/ppermute | solution.py:565
  14.7 21.5 %collective-permute-start.4 = (bf16[128,1024]{1,0:T(8,128)(2,1)}, bf16[128,1024]{1,0:T(8,128)(2,1)S(1)}, u32[]{:S(2)}, u32[]{:S(2)}) collective-permute-start(bf16[128,1024]{1,0:T(8,128)(2,1)} %get-tuple-element.135), channel_id=1, source_target_pairs={{0,4},{4,0},{8,12},{12,8},{1,5},{5,1},{9,13},{13,9},{2,6},{6,2},{1... | collective-permute-start | bytes 786440 | tf_op jit(solution)/shard_map/ppermute | solution.py:510
  37.3 1.6 %collective-permute-start.6 = (bf16[128,1024]{1,0:T(8,128)(2,1)S(1)}, bf16[128,1024]{1,0:T(8,128)(2,1)S(1)}, u32[]{:S(2)}, u32[]{:S(2)}) collective-permute-start(bf16[128,1024]{1,0:T(8,128)(2,1)S(1)} %get-tuple-element.101), channel_id=1, source_target_pairs={{0,1},{1,0},{2,3},{3,2},{4,5},{5,4},{6,7},{7,6},{8,9},{9,8},{10,11... | collective-permute-start | bytes 786440 | tf_op jit(solution)/shard_map/ppermute | solution.py:475
  37.4 3.2 %collective-permute-start.8 = (bf16[128,1024]{1,0:T(8,128)(2,1)S(1)}, bf16[128,1024]{1,0:T(8,128)(2,1)S(1)}, u32[]{:S(2)}, u32[]{:S(2)}) collective-permute-start(bf16[128,1024]{1,0:T(8,128)(2,1)S(1)} %get-tuple-element.102), channel_id=1, source_target_pairs={{0,1},{1,0},{2,3},{3,2},{4,5},{5,4},{6,7},{7,6},{8,9},{9,8},{10,11... | collective-permute-start | bytes 786440 | tf_op jit(solution)/shard_map/ppermute | solution.py:475
  39.0 8.4 %collective-permute-start.7 = (bf16[128,1024]{1,0:T(8,128)(2,1)S(1)}, bf16[128,1024]{1,0:T(8,128)(2,1)S(1)}, u32[]{:S(2)}, u32[]{:S(2)}) collective-permute-start(bf16[128,1024]{1,0:T(8,128)(2,1)S(1)} %add_convert_fusion.5), channel_id=1, source_target_pairs={{0,2},{2,0},{1,3},{3,1},{4,6},{6,4},{5,7},{7,5},{8,10},{10,8},{9,1... | collective-permute-start | bytes 786440 | tf_op jit(solution)/shard_map/ppermute | solution.py:475
  40.7 13.2 %collective-permute-start.9 = (bf16[128,1024]{1,0:T(8,128)(2,1)S(1)}, bf16[128,1024]{1,0:T(8,128)(2,1)S(1)}, u32[]{:S(2)}, u32[]{:S(2)}) collective-permute-start(bf16[128,1024]{1,0:T(8,128)(2,1)S(1)} %add_convert_fusion.3), channel_id=1, source_target_pairs={{0,4},{4,0},{8,12},{12,8},{1,5},{5,1},{9,13},{13,9},{2,6},{6,2},{1... | collective-permute-start | bytes 786440 | tf_op jit(solution)/shard_map/ppermute | solution.py:510
  44.7 8.4 %collective-permute-start.10 = (bf16[64,1024]{1,0:T(8,128)(2,1)S(1)}, bf16[64,1024]{1,0:T(8,128)(2,1)S(1)}, u32[]{:S(2)}, u32[]{:S(2)}) collective-permute-start(bf16[64,1024]{1,0:T(8,128)(2,1)S(1)} %slice.22), channel_id=1, source_target_pairs={{0,8},{4,12},{8,0},{12,4},{1,9},{5,13},{9,1},{13,5},{2,10},{6,14},... | collective-permute-start | bytes 393224 | tf_op jit(solution)/shard_map/ppermute | solution.py:510
  53.9 14.4 %collective-permute-start.14 = (bf16[128,1024]{1,0:T(8,128)(2,1)S(1)}, bf16[128,1024]{1,0:T(8,128)(2,1)S(1)}, u32[]{:S(2)}, u32[]{:S(2)}) collective-permute-start(bf16[128,1024]{1,0:T(8,128)(2,1)S(1)} %add_convert_fusion.4), channel_id=1, source_target_pairs={{0,8},{4,12},{8,0},{12,4},{1,9},{5,13},{9,1},{13,5},{2,10},{6,14},... | collective-permute-start | bytes 786440 | tf_op jit(solution)/shard_map/ppermute | solution.py:510
  56.5 11.7 %collective-permute-start.15 = (bf16[128,1024]{1,0:T(8,128)(2,1)S(1)}, bf16[128,1024]{1,0:T(8,128)(2,1)S(1)}, u32[]{:S(2)}, u32[]{:S(2)}) collective-permute-start(bf16[128,1024]{1,0:T(8,128)(2,1)S(1)} %add_convert_fusion.4), channel_id=1, source_target_pairs={{0,4},{4,0},{8,12},{12,8},{1,5},{5,1},{9,13},{13,9},{2,6},{6,2},{1... | collective-permute-start | bytes 786440 | tf_op jit(solution)/shard_map/ppermute | solution.py:510
  57.8 6.5 %collective-permute-start.11 = (bf16[64,1024]{1,0:T(8,128)(2,1)S(1)}, bf16[64,1024]{1,0:T(8,128)(2,1)S(1)}, u32[]{:S(2)}, u32[]{:S(2)}) collective-permute-start(bf16[64,1024]{1,0:T(8,128)(2,1)S(1)} %get-tuple-element.121.mixed_ref), channel_id=1, source_target_pairs={{0,2},{2,0},{1,3},{3,1},{4,6},{6,4},{5,7},{7,5},{8,10},{10,8},{9,1... | collective-permute-start | bytes 393224 | tf_op jit(solution)/shard_map/ppermute | solution.py:475
  58.4 7.8 %collective-permute-start.12 = (bf16[64,1024]{1,0:T(8,128)(2,1)S(1)}, bf16[64,1024]{1,0:T(8,128)(2,1)S(1)}, u32[]{:S(2)}, u32[]{:S(2)}) collective-permute-start(bf16[64,1024]{1,0:T(8,128)(2,1)S(1)} %get-tuple-element.117.mixed_ref), channel_id=1, source_target_pairs={{0,2},{2,0},{1,3},{3,1},{4,6},{6,4},{5,7},{7,5},{8,10},{10,8},{9,1... | collective-permute-start | bytes 393224 | tf_op jit(solution)/shard_map/ppermute | solution.py:475
  59.9 7.7 %collective-permute-start.13 = (bf16[64,1024]{1,0:T(8,128)(2,1)S(1)}, bf16[64,1024]{1,0:T(8,128)(2,1)S(1)}, u32[]{:S(2)}, u32[]{:S(2)}) collective-permute-start(bf16[64,1024]{1,0:T(8,128)(2,1)S(1)} %collective-permute-done.10.mixed_ref), channel_id=1, source_target_pairs={{0,2},{2,0},{1,3},{3,1},{4,6},{6,4},{5,7},{7,5},{8,10},{10,8},{9,1... | collective-permute-start | bytes 393224 | tf_op jit(solution)/shard_map/ppermute | solution.py:475
  68.2 16.6 %collective-permute-start.17 = (bf16[128,1024]{1,0:T(8,128)(2,1)S(1)}, bf16[128,1024]{1,0:T(8,128)(2,1)S(1)}, u32[]{:S(2)}, u32[]{:S(2)}) collective-permute-start(bf16[128,1024]{1,0:T(8,128)(2,1)S(1)} %collective-permute-done.9), channel_id=1, source_target_pairs={{0,2},{2,0},{1,3},{3,1},{4,6},{6,4},{5,7},{7,5},{8,10},{10,8},{9,1... | collective-permute-start | bytes 786440 | tf_op jit(solution)/shard_map/ppermute | solution.py:475
  68.7 11.1 %collective-permute-start.16 = (bf16[128,1024]{1,0:T(8,128)(2,1)S(1)}, bf16[128,1024]{1,0:T(8,128)(2,1)S(1)}, u32[]{:S(2)}, u32[]{:S(2)}) collective-permute-start(bf16[128,1024]{1,0:T(8,128)(2,1)S(1)} %collective-permute-done.14), channel_id=1, source_target_pairs={{0,4},{4,0},{8,12},{12,8},{1,5},{5,1},{9,13},{13,9},{2,6},{6,2},{1... | collective-permute-start | bytes 786440 | tf_op jit(solution)/shard_map/ppermute | solution.py:510
  70.0 15.0 %collective-permute-start.18 = (bf16[64,1024]{1,0:T(8,128)(2,1)S(1)}, bf16[64,1024]{1,0:T(8,128)(2,1)S(1)}, u32[]{:S(2)}, u32[]{:S(2)}) collective-permute-start(bf16[64,1024]{1,0:T(8,128)(2,1)S(1)} %add.239), channel_id=1, source_target_pairs={{0,8},{4,12},{8,0},{12,4},{1,9},{5,13},{9,1},{13,5},{2,10},{6,14},... | collective-permute-start | bytes 393224 | tf_op jit(solution)/shard_map/ppermute | solution.py:510
  73.5 11.4 %collective-permute-start.19 = (bf16[64,1024]{1,0:T(8,128)(2,1)S(1)}, bf16[64,1024]{1,0:T(8,128)(2,1)S(1)}, u32[]{:S(2)}, u32[]{:S(2)}) collective-permute-start(bf16[64,1024]{1,0:T(8,128)(2,1)S(1)} %add.239), channel_id=1, source_target_pairs={{0,12},{4,8},{8,4},{12,0},{1,13},{5,9},{9,5},{13,1},{2,14},{6,10},... | collective-permute-start | bytes 393224 | tf_op jit(solution)/shard_map/ppermute | solution.py:510
  79.9 5.3 %collective-permute-start.20 = (bf16[64,1024]{1,0:T(8,128)(2,1)S(1)}, bf16[64,1024]{1,0:T(8,128)(2,1)S(1)}, u32[]{:S(2)}, u32[]{:S(2)}) collective-permute-start(bf16[64,1024]{1,0:T(8,128)(2,1)S(1)} %add.238), channel_id=1, source_target_pairs={{0,4},{4,0},{8,12},{12,8},{1,5},{5,1},{9,13},{13,9},{2,6},{6,2},{1... | collective-permute-start | bytes 393224 | tf_op jit(solution)/shard_map/ppermute | solution.py:510
  83.2 1.6 %collective-permute-start = (bf16[1,2,2,2,16,1024]{5,4,3,2,1,0:T(8,128)(2,1)S(1)}, bf16[1,2,2,2,16,1024]{5,4,3,2,1,0:T(8,128)(2,1)S(1)}, u32[]{:S(2)}, u32[]{:S(2)}) collective-permute-start(bf16[1,2,2,2,16,1024]{5,4,3,2,1,0:T(8,128)(2,1)S(1)} %constant_dynamic-slice_fusion), channel_id=1, source_target_pairs={{0,1},{1,0},{2,3},{3,2},{4,5},{5,4},{6,7},{7,6},{8,9},{9,8},{10,11... | collective-permute-start | bytes 786440 | tf_op jit(solution)/shard_map/cond/branch_1_fun/ppermute | solution.py:475
  85.2 6.6 %collective-permute-start.21 = (bf16[1,2,2,16,1024]{4,3,2,1,0:T(8,128)(2,1)S(1)}, bf16[1,2,2,16,1024]{4,3,2,1,0:T(8,128)(2,1)S(1)}, u32[]{:S(2)}, u32[]{:S(2)}) collective-permute-start(bf16[1,2,2,16,1024]{4,3,2,1,0:T(8,128)(2,1)S(1)} %constant_dynamic-slice_fusion.5), channel_id=1, source_target_pairs={{0,2},{2,0},{1,3},{3,1},{4,6},{6,4},{5,7},{7,5},{8,10},{10,8},{9,1... | collective-permute-start | bytes 393224 | tf_op jit(solution)/shard_map/ppermute | solution.py:475
  90.1 1.6 %collective-permute-start.1 = (bf16[1,2,2,2,16,1024]{5,4,3,2,1,0:T(8,128)(2,1)S(1)}, bf16[1,2,2,2,16,1024]{5,4,3,2,1,0:T(8,128)(2,1)S(1)}, u32[]{:S(2)}, u32[]{:S(2)}) collective-permute-start(bf16[1,2,2,2,16,1024]{5,4,3,2,1,0:T(8,128)(2,1)S(1)} %constant_dynamic-slice_fusion.1), channel_id=1, source_target_pairs={{0,1},{1,0},{2,3},{3,2},{4,5},{5,4},{6,7},{7,6},{8,9},{9,8},{10,11... | collective-permute-start | bytes 786440 | tf_op jit(solution)/shard_map/cond/branch_1_fun/ppermute | solution.py:475
  91.9 5.6 %collective-permute-start.22 = (bf16[1,2,2,16,1024]{4,3,2,1,0:T(8,128)(2,1)S(1)}, bf16[1,2,2,16,1024]{4,3,2,1,0:T(8,128)(2,1)S(1)}, u32[]{:S(2)}, u32[]{:S(2)}) collective-permute-start(bf16[1,2,2,16,1024]{4,3,2,1,0:T(8,128)(2,1)S(1)} %constant_dynamic-slice_fusion.4), channel_id=1, source_target_pairs={{0,2},{2,0},{1,3},{3,1},{4,6},{6,4},{5,7},{7,5},{8,10},{10,8},{9,1... | collective-permute-start | bytes 393224 | tf_op jit(solution)/shard_map/ppermute | solution.py:475
  97.6 7.7 %collective-permute-start.24 = (bf16[32,1024]{1,0:T(8,128)(2,1)S(1)}, bf16[32,1024]{1,0:T(8,128)(2,1)S(1)}, u32[]{:S(2)}, u32[]{:S(2)}) collective-permute-start(bf16[32,1024]{1,0:T(8,128)(2,1)S(1)} %bitcast.38), channel_id=1, source_target_pairs={{0,8},{4,12},{8,0},{12,4},{1,9},{5,13},{9,1},{13,5},{2,10},{6,14},... | collective-permute-start | bytes 196616 | tf_op jit(solution)/shard_map/ppermute | solution.py:510
  102.1 6.1 %collective-permute-start.25 = (bf16[32,1024]{1,0:T(8,128)(2,1)S(1)}, bf16[32,1024]{1,0:T(8,128)(2,1)S(1)}, u32[]{:S(2)}, u32[]{:S(2)}) collective-permute-start(bf16[32,1024]{1,0:T(8,128)(2,1)S(1)} %bitcast.37), channel_id=1, source_target_pairs={{0,12},{4,8},{8,4},{12,0},{1,13},{5,9},{9,5},{13,1},{2,14},{6,10},... | collective-permute-start | bytes 196616 | tf_op jit(solution)/shard_map/ppermute | solution.py:510
  102.1 6.1 %collective-permute-start.23 = (bf16[32,1024]{1,0:T(8,128)(2,1)S(1)}, bf16[32,1024]{1,0:T(8,128)(2,1)S(1)}, u32[]{:S(2)}, u32[]{:S(2)}) collective-permute-start(bf16[32,1024]{1,0:T(8,128)(2,1)S(1)} %bitcast.39), channel_id=1, source_target_pairs={{0,4},{4,0},{8,12},{12,8},{1,5},{5,1},{9,13},{13,9},{2,6},{6,2},{1... | collective-permute-start | bytes 196616 | tf_op jit(solution)/shard_map/ppermute | solution.py:510

commit v6 on v5

--- a/solution.py
+++ b/solution.py
@@ -619,14 +619,21 @@
 
     first, second = (across(chunk, "sub") for chunk in chunks)
     ahead = range(1, pairs)
+    cut = tokens * 3 // 4
     near_second = swap_seq(second, 1)
-    far_early = [swap_seq(second[: tokens // 2], 2 * k) for k in ahead]
-    first = across(first, "chan")
-    first, second, near_second, far_early = lax.optimization_barrier(
-        (first, second, near_second, far_early)
-    )
+    far_early = [swap_seq(second[:cut], 2 * k) for k in ahead]
     bits = bits_of("chan")
-    moving = [second[: tokens // 2], second[tokens // 2 :], *far_early]
+    halves = [first[: tokens // 2], first[tokens // 2 :]]
+    for bit in bits[:-1]:
+        halves = [add_across(value, "chan", bit, swap(value, "chan", bit)) for value in halves]
+    received = [swap(value, "chan", bits[-1]) for value in halves if bits]
+    halves, received, second, near_second, far_early = lax.optimization_barrier(
+        (halves, received, second, near_second, far_early)
+    )
+    if bits:
+        halves = [add_across(*pair[:1], "chan", bits[-1], pair[1]) for pair in zip(halves, received)]
+    first = jnp.concatenate(halves, axis=0)
+    moving = [second[:cut], second[cut:], *far_early]
     for bit in bits[:-1]:
         moving = [add_across(value, "chan", bit, swap(value, "chan", bit)) for value in moving]
     received = [swap(value, "chan", bits[-1]) for value in moving if bits]

time: 109 us -> 107 us (0.982)
  waiting for transfers between devices: 53.1 us -> 48.3 us
  starting transfers between devices: 37 us -> 39.6 us
    ppermute x13, waiting for transfers between devices: 36.1 us -> 27.4 us  [swap_seq(): return lax.ppermute(value, 'seq', [(k, k ^ distance) for k in range(count)])]
    ppermute x11 -> x12, waiting for transfers between devices: 16.9 us -> 20.9 us  [swap(): return lax.ppermute(value, axis, [(k, k ^ 1 << bit) for k in range(count)])]
    ppermute x11 -> x12, starting transfers between devices: 7.58 us -> 10.1 us  [swap(): return lax.ppermute(value, axis, [(k, k ^ 1 << bit) for k in range(count)])]
  transfers between devices with their start and end apart: 26 -> 27, of which waited for: 17 -> 13; matrix products, arithmetic and copies ran while one was open for 4% -> 4% of each run, Pallas kernels for 8% -> 8%
where the time goes in v6:
time: 107 us
  waiting for transfers between devices  48.3 us (45%)
  starting transfers between devices  39.6 us (37%)
  Pallas kernels  11.3 us (11%)
  local copies, waits for them, and re-layouts  5.1 us (5%)
  other arithmetic  2.14 us (2%)
    ppermute x13, waiting for transfers between devices, swap_seq(): return lax.ppermute(value, 'seq', [(k, k ^ distance) for k in range(count)])  27.4 us
    ppermute x13, starting transfers between devices, swap_seq(): return lax.ppermute(value, 'seq', [(k, k ^ distance) for k in range(count)])  23.7 us
    ppermute x12, waiting for transfers between devices, swap(): return lax.ppermute(value, axis, [(k, k ^ 1 << bit) for k in range(count)])  20.9 us
    pallas_call x8, Pallas kernels, call(): pl.pallas_call(kernel, out_shape=out_shape, in_specs=specs, scratch_shape...  10.1 us
    ppermute x12, starting transfers between devices, swap(): return lax.ppermute(value, axis, [(k, k ^ 1 << bit) for k in range(count)])  10.1 us
    ppermute x1, starting transfers between devices, paired_body(): lax.ppermute(straight, 'seq', [(k, k + 2 * ahead) for k in firsts])  4.5 us
    dynamic_slice x2, local copies, waits for them, and re-layouts, half_of(): return lax.dynamic_slice_in_dim(value, which * half, half, 1)  2.84 us
  transfers between devices with their start and end apart: 27, of which 13 were waited for; matrix products, arithmetic and copies ran while one was open for 4% of the time, Pallas kernels for 8%

profile of v6, /device:TPU:0, one launch (start us, length us, event | category | flops | bytes accessed | tf_op | source)
XLA Modules:
  0.0 106.9 jit_solution(8888603361911706736)
XLA Ops:
  0.0 1.3 %constant_dynamic-slice_fusion.8 = (bf16[128,1,256]{2,1,0:T(2,128)(2,1)S(1)}, bf16[128,1,256]{2,1,0:T(2,128)(2,1)S(1)}) fusion(bf16[128,2,256]{2,1,0:T(2,128)(2,1)} %param.18, s32[]{:T(128)S(6)} %select_n.150, bf16[128,2,256]{2,1,0:T(2,128)(2,1)} %param.17), kind=kLoop, calls=%fused_computation.52 | loop fusion | bytes 262148 | tf_op jit(solution)/shard_map/jit(dynamic_index_in_dim)/dynamic_slice | solution.py:537
  1.3 0.7 pad_maximum_fusion.4.steps_ref
  2.1 1.1 constant_dynamic-slice_fusion.10
  3.1 0.8 pack.1
  4.0 3.1 %collective-permute-start.5 = (bf16[128,1664]{1,0:T(8,128)(2,1)S(1)}, bf16[128,1664]{1,0:T(8,128)(2,1)S(1)}, u32[]{:S(2)}, u32[]{:S(2)}) collective-permute-start(bf16[128,1664]{1,0:T(8,128)(2,1)S(1)} %get-tuple-element.100), channel_id=1, source_target_pairs={{0,4},{4,0},{8,12},{12,8},{1,5},{5,1},{9,13},{13,9},{2,6},{6,2},{1... | collective-permute-start | bytes 1277960 | tf_op jit(solution)/shard_map/ppermute | solution.py:510
  7.1 4.5 %collective-permute-start.2 = (bf16[1296,128]{1,0:T(8,128)(2,1)S(1)}, bf16[1296,128]{1,0:T(8,128)(2,1)S(1)}, u32[]{:S(2)}, u32[]{:S(2)}) collective-permute-start(bf16[1296,128]{1,0:T(8,128)(2,1)S(1)} %get-tuple-element.97), channel_id=1, source_target_pairs={{0,8},{4,12},{1,9},{5,13},{2,10},{6,14},{3,11},{7,15},{16,24},{20,... | collective-permute-start | bytes 995336 | tf_op jit(solution)/shard_map/ppermute | solution.py:564
  11.6 1.3 %collective-permute-start.3 = (bf16[1296,128]{1,0:T(8,128)(2,1)S(1)}, bf16[1296,128]{1,0:T(8,128)(2,1)S(1)}, u32[]{:S(2)}, u32[]{:S(2)}) collective-permute-start(bf16[1296,128]{1,0:T(8,128)(2,1)S(1)} %get-tuple-element.98), channel_id=1, source_target_pairs={{0,12},{4,8},{1,13},{5,9},{2,14},{6,10},{3,15},{7,11},{16,28},{20,... | collective-permute-start | bytes 995336 | tf_op jit(solution)/shard_map/ppermute | solution.py:565
  12.9 1.8 %constant_dynamic-slice_fusion.6 = (bf16[128,1024]{1,0:T(8,128)(2,1)}, bf16[128,1024]{1,0:T(8,128)(2,1)S(1)}) fusion(bf16[128,2048]{1,0:T(8,128)(2,1)} %param.22, s32[]{:T(128)S(6)} %select_n.148, s32[]{:T(128)S(6)} %select_n.147), kind=kLoop, calls=%fused_computation.50 | loop fusion | bytes 1048584 | tf_op jit(solution)/shard_map/dynamic_slice | solution.py:547
  14.7 0.5 collective-permute-start.4
  15.2 0.7 broadcast_in_dim.67
  16.0 0.7 select_multiply_fusion
  16.7 0.5 collective-permute-done.5.msg_ref
  17.3 1.9 %pair.1 = (f32[256,1024]{1,0:T(8,128)S(1)}, f32[256,1024]{1,0:T(8,128)S(1)}, bf16[256,256]{1,0:T(8,128)(2,1)S(1)}) custom-call(s32[1]{0:T(128)} %bitcast.3.where_ref.refs_2_, bf16[128,1024]{1,0:T(8,128)(2,1)S(1)} %get-tuple-element.144.x_mine_ref.x_ref, bf16[128,640]{1,0:T(8,128)(2,1)S(1)} %get-tuple-element.99.meta_ref, ...), custom_call_target="tpu_custom_call" | custom-call | flops 1 | bytes 1 | tf_op jit(solution)/shard_map/pair/pallas_call | solution.py:497
  19.2 17.0 %collective-permute-done.4.refs_4_ = bf16[128,1024]{1,0:T(8,128)(2,1)S(1)} collective-permute-done((bf16[128,1024]{1,0:T(8,128)(2,1)}, bf16[128,1024]{1,0:T(8,128)(2,1)S(1)}, u32[]{:S(2)}, u32[]{:S(2)}) %collective-permute-start.4) | collective-permute-done | bytes 262176 | tf_op jit(solution)/shard_map/ppermute | solution.py:510
  36.2 1.1 %mix.1 = (bf16[128,1024]{1,0:T(8,128)(2,1)S(1)}, bf16[128,1024]{1,0:T(8,128)(2,1)S(1)}) custom-call(bf16[1296,128]{1,0:T(8,128)(2,1)S(1)} %collective-permute-done.2.refs_0_, bf16[1296,128]{1,0:T(8,128)(2,1)S(1)} %collective-permute-done.3.refs_1_, s32[1]{0:T(128)} %bitcast.3.where_ref.refs_2_, bf16[128,1024]{1,0:T(8,128)(2,1)S(1)} %get-tuple-element.142.refs_3_, ...), custom_call_target="tpu_custom_call" | custom-call | flops 1 | bytes 30000000 | tf_op jit(solution)/shard_map/mix/pallas_call | solution.py:598
  37.9 1.0 collective-permute-done.9
  39.0 4.1 %collective-permute-start.10 = (bf16[128,1024]{1,0:T(8,128)(2,1)S(1)}, bf16[128,1024]{1,0:T(8,128)(2,1)S(1)}, u32[]{:S(2)}, u32[]{:S(2)}) collective-permute-start(bf16[128,1024]{1,0:T(8,128)(2,1)S(1)} %add_convert_fusion.3), channel_id=1, source_target_pairs={{0,4},{4,0},{8,12},{12,8},{1,5},{5,1},{9,13},{13,9},{2,6},{6,2},{1... | collective-permute-start | bytes 786440 | tf_op jit(solution)/shard_map/ppermute | solution.py:510
  43.1 2.0 %collective-permute-start.11 = (bf16[96,1024]{1,0:T(8,128)(2,1)S(1)}, bf16[96,1024]{1,0:T(8,128)(2,1)S(1)}, u32[]{:S(2)}, u32[]{:S(2)}) collective-permute-start(bf16[96,1024]{1,0:T(8,128)(2,1)S(1)} %slice.32), channel_id=1, source_target_pairs={{0,8},{4,12},{8,0},{12,4},{1,9},{5,13},{9,1},{13,5},{2,10},{6,14},... | collective-permute-start | bytes 589832 | tf_op jit(solution)/shard_map/ppermute | solution.py:510
  45.2 1.6 %collective-permute-start.7 = (bf16[64,1024]{1,0:T(8,128)(2,1)S(1)}, bf16[64,1024]{1,0:T(8,128)(2,1)S(1)}, u32[]{:S(2)}, u32[]{:S(2)}) collective-permute-start(bf16[64,1024]{1,0:T(8,128)(2,1)S(1)} %get-tuple-element.106), channel_id=1, source_target_pairs={{0,2},{2,0},{1,3},{3,1},{4,6},{6,4},{5,7},{7,5},{8,10},{10,8},{9,1... | collective-permute-start | bytes 393224 | tf_op jit(solution)/shard_map/ppermute | solution.py:475
  46.8 0.5 collective-permute-start.8
  47.3 4.4 %collective-permute-done.7 = bf16[64,1024]{1,0:T(8,128)(2,1)S(1)} collective-permute-done((bf16[64,1024]{1,0:T(8,128)(2,1)S(1)}, bf16[64,1024]{1,0:T(8,128)(2,1)S(1)}, u32[]{:S(2)}, u32[]{:S(2)}) %collective-permute-start.7) | collective-permute-done | bytes 131104 | tf_op jit(solution)/shard_map/ppermute | solution.py:475
  51.7 1.7 %collective-permute-done.8 = bf16[64,1024]{1,0:T(8,128)(2,1)S(1)} collective-permute-done((bf16[64,1024]{1,0:T(8,128)(2,1)S(1)}, bf16[64,1024]{1,0:T(8,128)(2,1)S(1)}, u32[]{:S(2)}, u32[]{:S(2)}) %collective-permute-start.8) | collective-permute-done | bytes 131104 | tf_op jit(solution)/shard_map/ppermute | solution.py:475
  53.3 0.6 collective-permute-done.10
  54.0 2.8 %collective-permute-start.15 = (bf16[128,1024]{1,0:T(8,128)(2,1)S(1)}, bf16[128,1024]{1,0:T(8,128)(2,1)S(1)}, u32[]{:S(2)}, u32[]{:S(2)}) collective-permute-start(bf16[128,1024]{1,0:T(8,128)(2,1)S(1)} %pad_maximum_fusion), channel_id=1, source_target_pairs={{0,8},{4,12},{8,0},{12,4},{1,9},{5,13},{9,1},{13,5},{2,10},{6,14},... | collective-permute-start | bytes 786440 | tf_op jit(solution)/shard_map/ppermute | solution.py:510
  56.8 2.2 %collective-permute-start.16 = (bf16[128,1024]{1,0:T(8,128)(2,1)S(1)}, bf16[128,1024]{1,0:T(8,128)(2,1)S(1)}, u32[]{:S(2)}, u32[]{:S(2)}) collective-permute-start(bf16[128,1024]{1,0:T(8,128)(2,1)S(1)} %pad_maximum_fusion), channel_id=1, source_target_pairs={{0,4},{4,0},{8,12},{12,8},{1,5},{5,1},{9,13},{13,9},{2,6},{6,2},{1... | collective-permute-start | bytes 786440 | tf_op jit(solution)/shard_map/ppermute | solution.py:510
  59.1 1.6 %collective-permute-start.12 = (bf16[96,1024]{1,0:T(8,128)(2,1)S(1)}, bf16[96,1024]{1,0:T(8,128)(2,1)S(1)}, u32[]{:S(2)}, u32[]{:S(2)}) collective-permute-start(bf16[96,1024]{1,0:T(8,128)(2,1)S(1)} %slice.26.mixed_ref), channel_id=1, source_target_pairs={{0,2},{2,0},{1,3},{3,1},{4,6},{6,4},{5,7},{7,5},{8,10},{10,8},{9,1... | collective-permute-start | bytes 589832 | tf_op jit(solution)/shard_map/ppermute | solution.py:475
  61.2 1.5 %collective-permute-start.13 = (bf16[32,1024]{1,0:T(8,128)(2,1)S(1)}, bf16[32,1024]{1,0:T(8,128)(2,1)S(1)}, u32[]{:S(2)}, u32[]{:S(2)}) collective-permute-start(bf16[32,1024]{1,0:T(8,128)(2,1)S(1)} %slice.27.mixed_ref), channel_id=1, source_target_pairs={{0,2},{2,0},{1,3},{3,1},{4,6},{6,4},{5,7},{7,5},{8,10},{10,8},{9,1... | collective-permute-start | bytes 196616 | tf_op jit(solution)/shard_map/ppermute | solution.py:475
  62.7 6.7 %collective-permute-done.13.received_ref = bf16[32,1024]{1,0:T(8,128)(2,1)S(1)} collective-permute-done((bf16[32,1024]{1,0:T(8,128)(2,1)S(1)}, bf16[32,1024]{1,0:T(8,128)(2,1)S(1)}, u32[]{:S(2)}, u32[]{:S(2)}) %collective-permute-start.13) | collective-permute-done | bytes 65568 | tf_op jit(solution)/shard_map/ppermute | solution.py:475
  69.4 1.6 %collective-permute-start.18 = (bf16[128,1024]{1,0:T(8,128)(2,1)S(1)}, bf16[128,1024]{1,0:T(8,128)(2,1)S(1)}, u32[]{:S(2)}, u32[]{:S(2)}) collective-permute-start(bf16[128,1024]{1,0:T(8,128)(2,1)S(1)} %collective-permute-done.10), channel_id=1, source_target_pairs={{0,2},{2,0},{1,3},{3,1},{4,6},{6,4},{5,7},{7,5},{8,10},{10,8},{9,1... | collective-permute-start | bytes 786440 | tf_op jit(solution)/shard_map/ppermute | solution.py:475
  71.0 0.7 collective-permute-start.17
  71.7 3.1 %collective-permute-start.19 = (bf16[32,1024]{1,0:T(8,128)(2,1)S(1)}, bf16[32,1024]{1,0:T(8,128)(2,1)S(1)}, u32[]{:S(2)}, u32[]{:S(2)}) collective-permute-start(bf16[32,1024]{1,0:T(8,128)(2,1)S(1)} %add.245), channel_id=1, source_target_pairs={{0,8},{4,12},{8,0},{12,4},{1,9},{5,13},{9,1},{13,5},{2,10},{6,14},... | collective-permute-start | bytes 196616 | tf_op jit(solution)/shard_map/ppermute | solution.py:510
  74.9 0.6 collective-permute-start.20
  75.6 4.2 %collective-permute-done.17 = bf16[128,1024]{1,0:T(8,128)(2,1)S(1)} collective-permute-done((bf16[128,1024]{1,0:T(8,128)(2,1)S(1)}, bf16[128,1024]{1,0:T(8,128)(2,1)S(1)}, u32[]{:S(2)}, u32[]{:S(2)}) %collective-permute-start.17) | collective-permute-done | bytes 262176 | tf_op jit(solution)/shard_map/ppermute | solution.py:510
  79.8 0.7 collective-permute-start.21
  80.7 5.0 %conditional.2 = (bf16[2,2,2,16,1024]{4,3,2,1,0:T(8,128)(2,1)S(1)}) conditional(s32[]{:T(128)} %convert_element_type.102, () %tuple.22, (s32[1]{0:T(128)}, bf16[2048,1024]{1,0:T(8,128)(2,1)}, bf16[128,1024]{1,0:T(8,128)(2,1)S(1)}, bf16[128,1024]{1,0:T(8,128)(2,1)S(1)}, bf16[128,1024]{1,0:T(8,128)(2,1)S(1)}, ...), branch_computations={%region_0.1_spmd, %region_1.2_spmd} | conditional | flops 524309 | bytes 32359552 | solution.py:685
  80.7 3.3 %project.2 = bf16[2,2,2,2,16,1024]{5,4,3,2,1,0:T(8,128)(2,1)S(1)} custom-call(s32[1]{0:T(128)} %get-tuple-element.42.where_ref, bf16[2048,1024]{1,0:T(8,128)(2,1)} %get-tuple-element.44.weight_ref, bf16[128,1024]{1,0:T(8,128)(2,1)S(1)} %get-tuple-element.45.refs_0_, bf16[128,1024]{1,0:T(8,128)(2,1)S(1)} %get-tuple-element.46.refs_1_, ...), custom_call_target="tpu_custom_call" | custom-call | flops 1 | bytes 30000000 | tf_op jit(solution)/shard_map/cond/branch_1_fun/project/pallas_call | solution.py:497
  84.1 1.5 %collective-permute-done = bf16[1,2,2,2,16,1024]{5,4,3,2,1,0:T(8,128)(2,1)S(1)} collective-permute-done((bf16[1,2,2,2,16,1024]{5,4,3,2,1,0:T(8,128)(2,1)S(1)}, bf16[1,2,2,2,16,1024]{5,4,3,2,1,0:T(8,128)(2,1)S(1)}, u32[]{:S(2)}, u32[]{:S(2)}) %collective-permute-start) | collective-permute-done | bytes 262176 | tf_op jit(solution)/shard_map/cond/branch_1_fun/ppermute | solution.py:475
  85.7 0.6 collective-permute-start.22
  86.4 5.0 %conditional.3 = (bf16[2,2,2,16,1024]{4,3,2,1,0:T(8,128)(2,1)S(1)}) conditional(s32[]{:T(128)} %convert_element_type.102, () %tuple.28, (s32[1]{0:T(128)}, bf16[2048,1024]{1,0:T(8,128)(2,1)}, bf16[128,1024]{1,0:T(8,128)(2,1)S(1)}, bf16[128,1024]{1,0:T(8,128)(2,1)S(1)}, bf16[128,1024]{1,0:T(8,128)(2,1)S(1)}, ...), branch_computations={%region_2.3_spmd, %region_3.4_spmd} | conditional | flops 524309 | bytes 32359552 | solution.py:685
  86.4 3.3 %project.3 = bf16[2,2,2,2,16,1024]{5,4,3,2,1,0:T(8,128)(2,1)S(1)} custom-call(s32[1]{0:T(128)} %get-tuple-element.51.where_ref, bf16[2048,1024]{1,0:T(8,128)(2,1)} %get-tuple-element.52.weight_ref, bf16[128,1024]{1,0:T(8,128)(2,1)S(1)} %get-tuple-element.53.refs_0_, bf16[128,1024]{1,0:T(8,128)(2,1)S(1)} %get-tuple-element.54.refs_1_, ...), custom_call_target="tpu_custom_call" | custom-call | flops 1 | bytes 30000000 | tf_op jit(solution)/shard_map/cond/branch_1_fun/project/pallas_call | solution.py:497
  89.8 1.5 %collective-permute-done.1 = bf16[1,2,2,2,16,1024]{5,4,3,2,1,0:T(8,128)(2,1)S(1)} collective-permute-done((bf16[1,2,2,2,16,1024]{5,4,3,2,1,0:T(8,128)(2,1)S(1)}, bf16[1,2,2,2,16,1024]{5,4,3,2,1,0:T(8,128)(2,1)S(1)}, u32[]{:S(2)}, u32[]{:S(2)}) %collective-permute-start.1) | collective-permute-done | bytes 262176 | tf_op jit(solution)/shard_map/cond/branch_1_fun/ppermute | solution.py:475
  91.5 1.5 %collective-permute-start.23 = (bf16[1,2,2,16,1024]{4,3,2,1,0:T(8,128)(2,1)S(1)}, bf16[1,2,2,16,1024]{4,3,2,1,0:T(8,128)(2,1)S(1)}, u32[]{:S(2)}, u32[]{:S(2)}) collective-permute-start(bf16[1,2,2,16,1024]{4,3,2,1,0:T(8,128)(2,1)S(1)} %constant_dynamic-slice_fusion.4), channel_id=1, source_target_pairs={{0,2},{2,0},{1,3},{3,1},{4,6},{6,4},{5,7},{7,5},{8,10},{10,8},{9,1... | collective-permute-start | bytes 393224 | tf_op jit(solution)/shard_map/ppermute | solution.py:475
  93.0 4.1 %collective-permute-done.23 = bf16[1,2,2,16,1024]{4,3,2,1,0:T(8,128)(2,1)S(1)} collective-permute-done((bf16[1,2,2,16,1024]{4,3,2,1,0:T(8,128)(2,1)S(1)}, bf16[1,2,2,16,1024]{4,3,2,1,0:T(8,128)(2,1)S(1)}, u32[]{:S(2)}, u32[]{:S(2)}) %collective-permute-start.23) | collective-permute-done | bytes 131104 | tf_op jit(solution)/shard_map/ppermute | solution.py:475
  97.2 2.9 %collective-permute-start.25 = (bf16[32,1024]{1,0:T(8,128)(2,1)S(1)}, bf16[32,1024]{1,0:T(8,128)(2,1)S(1)}, u32[]{:S(2)}, u32[]{:S(2)}) collective-permute-start(bf16[32,1024]{1,0:T(8,128)(2,1)S(1)} %bitcast.38), channel_id=1, source_target_pairs={{0,8},{4,12},{8,0},{12,4},{1,9},{5,13},{9,1},{13,5},{2,10},{6,14},... | collective-permute-start | bytes 196616 | tf_op jit(solution)/shard_map/ppermute | solution.py:510
  100.1 0.8 collective-permute-start.26
  101.0 3.4 %collective-permute-done.25.refs_2_ = bf16[32,1024]{1,0:T(8,128)(2,1)S(1)} collective-permute-done((bf16[32,1024]{1,0:T(8,128)(2,1)S(1)}, bf16[32,1024]{1,0:T(8,128)(2,1)S(1)}, u32[]{:S(2)}, u32[]{:S(2)}) %collective-permute-start.25) | collective-permute-done | bytes 65568 | tf_op jit(solution)/shard_map/ppermute | solution.py:510
  104.5 1.7 %collective-permute-done.26.refs_3_ = bf16[32,1024]{1,0:T(8,128)(2,1)S(1)} collective-permute-done((bf16[32,1024]{1,0:T(8,128)(2,1)S(1)}, bf16[32,1024]{1,0:T(8,128)(2,1)S(1)}, u32[]{:S(2)}, u32[]{:S(2)}) %collective-permute-start.26) | collective-permute-done | bytes 65568 | tf_op jit(solution)/shard_map/ppermute | solution.py:510
  106.2 0.7 place.1
  (56 shorter events, 2.4 us)
Async XLA Ops:
  0.0 36.2 %copy-start = (bf16[256,256]{1,0:T(8,128)(2,1)S(1)}, bf16[256,256]{1,0:T(8,128)(2,1)}, u32[]{:S(2)}) copy-start(bf16[256,256]{1,0:T(8,128)(2,1)} %constant.236.clone.refs_9_) | copy-start | bytes 393220
  4.0 13.3 %collective-permute-start.5 = (bf16[128,1664]{1,0:T(8,128)(2,1)S(1)}, bf16[128,1664]{1,0:T(8,128)(2,1)S(1)}, u32[]{:S(2)}, u32[]{:S(2)}) collective-permute-start(bf16[128,1664]{1,0:T(8,128)(2,1)S(1)} %get-tuple-element.100), channel_id=1, source_target_pairs={{0,4},{4,0},{8,12},{12,8},{1,5},{5,1},{9,13},{13,9},{2,6},{6,2},{1... | collective-permute-start | bytes 1277960 | tf_op jit(solution)/shard_map/ppermute | solution.py:510
  7.1 29.1 %collective-permute-start.2 = (bf16[1296,128]{1,0:T(8,128)(2,1)S(1)}, bf16[1296,128]{1,0:T(8,128)(2,1)S(1)}, u32[]{:S(2)}, u32[]{:S(2)}) collective-permute-start(bf16[1296,128]{1,0:T(8,128)(2,1)S(1)} %get-tuple-element.97), channel_id=1, source_target_pairs={{0,8},{4,12},{1,9},{5,13},{2,10},{6,14},{3,11},{7,15},{16,24},{20,... | collective-permute-start | bytes 995336 | tf_op jit(solution)/shard_map/ppermute | solution.py:564
  11.6 24.6 %collective-permute-start.3 = (bf16[1296,128]{1,0:T(8,128)(2,1)S(1)}, bf16[1296,128]{1,0:T(8,128)(2,1)S(1)}, u32[]{:S(2)}, u32[]{:S(2)}) collective-permute-start(bf16[1296,128]{1,0:T(8,128)(2,1)S(1)} %get-tuple-element.98), channel_id=1, source_target_pairs={{0,12},{4,8},{1,13},{5,9},{2,14},{6,10},{3,15},{7,11},{16,28},{20,... | collective-permute-start | bytes 995336 | tf_op jit(solution)/shard_map/ppermute | solution.py:565
  14.7 21.5 %collective-permute-start.4 = (bf16[128,1024]{1,0:T(8,128)(2,1)}, bf16[128,1024]{1,0:T(8,128)(2,1)S(1)}, u32[]{:S(2)}, u32[]{:S(2)}) collective-permute-start(bf16[128,1024]{1,0:T(8,128)(2,1)} %get-tuple-element.141), channel_id=1, source_target_pairs={{0,4},{4,0},{8,12},{12,8},{1,5},{5,1},{9,13},{13,9},{2,6},{6,2},{1... | collective-permute-start | bytes 786440 | tf_op jit(solution)/shard_map/ppermute | solution.py:510
  19.2 43.5 %copy-start.1 = (s32[2048]{0:T(1024)S(1)}, s32[2048]{0:T(1024)}, u32[]{:S(2)}) copy-start(s32[2048]{0:T(1024)} %param.25) | copy-start | bytes 24580
  37.3 1.6 %collective-permute-start.9 = (bf16[128,1024]{1,0:T(8,128)(2,1)S(1)}, bf16[128,1024]{1,0:T(8,128)(2,1)S(1)}, u32[]{:S(2)}, u32[]{:S(2)}) collective-permute-start(bf16[128,1024]{1,0:T(8,128)(2,1)S(1)} %get-tuple-element.105), channel_id=1, source_target_pairs={{0,1},{1,0},{2,3},{3,2},{4,5},{5,4},{6,7},{7,6},{8,9},{9,8},{10,11... | collective-permute-start | bytes 786440 | tf_op jit(solution)/shard_map/ppermute | solution.py:475
  37.4 7.7 %collective-permute-start.6 = (bf16[128,1024]{1,0:T(8,128)(2,1)S(1)}, bf16[128,1024]{1,0:T(8,128)(2,1)S(1)}, u32[]{:S(2)}, u32[]{:S(2)}) collective-permute-start(bf16[128,1024]{1,0:T(8,128)(2,1)S(1)} %get-tuple-element.104), channel_id=1, source_target_pairs={{0,1},{1,0},{2,3},{3,2},{4,5},{5,4},{6,7},{7,6},{8,9},{9,8},{10,11... | collective-permute-start | bytes 786440 | tf_op jit(solution)/shard_map/ppermute | solution.py:475
  39.0 14.9 %collective-permute-start.10 = (bf16[128,1024]{1,0:T(8,128)(2,1)S(1)}, bf16[128,1024]{1,0:T(8,128)(2,1)S(1)}, u32[]{:S(2)}, u32[]{:S(2)}) collective-permute-start(bf16[128,1024]{1,0:T(8,128)(2,1)S(1)} %add_convert_fusion.3), channel_id=1, source_target_pairs={{0,4},{4,0},{8,12},{12,8},{1,5},{5,1},{9,13},{13,9},{2,6},{6,2},{1... | collective-permute-start | bytes 786440 | tf_op jit(solution)/shard_map/ppermute | solution.py:510
  43.1 10.2 %collective-permute-start.11 = (bf16[96,1024]{1,0:T(8,128)(2,1)S(1)}, bf16[96,1024]{1,0:T(8,128)(2,1)S(1)}, u32[]{:S(2)}, u32[]{:S(2)}) collective-permute-start(bf16[96,1024]{1,0:T(8,128)(2,1)S(1)} %slice.32), channel_id=1, source_target_pairs={{0,8},{4,12},{8,0},{12,4},{1,9},{5,13},{9,1},{13,5},{2,10},{6,14},... | collective-permute-start | bytes 589832 | tf_op jit(solution)/shard_map/ppermute | solution.py:510
  45.2 6.4 %collective-permute-start.7 = (bf16[64,1024]{1,0:T(8,128)(2,1)S(1)}, bf16[64,1024]{1,0:T(8,128)(2,1)S(1)}, u32[]{:S(2)}, u32[]{:S(2)}) collective-permute-start(bf16[64,1024]{1,0:T(8,128)(2,1)S(1)} %get-tuple-element.106), channel_id=1, source_target_pairs={{0,2},{2,0},{1,3},{3,1},{4,6},{6,4},{5,7},{7,5},{8,10},{10,8},{9,1... | collective-permute-start | bytes 393224 | tf_op jit(solution)/shard_map/ppermute | solution.py:475
  46.8 6.6 %collective-permute-start.8 = (bf16[64,1024]{1,0:T(8,128)(2,1)S(1)}, bf16[64,1024]{1,0:T(8,128)(2,1)S(1)}, u32[]{:S(2)}, u32[]{:S(2)}) collective-permute-start(bf16[64,1024]{1,0:T(8,128)(2,1)S(1)} %get-tuple-element.108), channel_id=1, source_target_pairs={{0,2},{2,0},{1,3},{3,1},{4,6},{6,4},{5,7},{7,5},{8,10},{10,8},{9,1... | collective-permute-start | bytes 393224 | tf_op jit(solution)/shard_map/ppermute | solution.py:475
  54.0 15.4 %collective-permute-start.15 = (bf16[128,1024]{1,0:T(8,128)(2,1)S(1)}, bf16[128,1024]{1,0:T(8,128)(2,1)S(1)}, u32[]{:S(2)}, u32[]{:S(2)}) collective-permute-start(bf16[128,1024]{1,0:T(8,128)(2,1)S(1)} %pad_maximum_fusion), channel_id=1, source_target_pairs={{0,8},{4,12},{8,0},{12,4},{1,9},{5,13},{9,1},{13,5},{2,10},{6,14},... | collective-permute-start | bytes 786440 | tf_op jit(solution)/shard_map/ppermute | solution.py:510
  56.8 12.6 %collective-permute-start.16 = (bf16[128,1024]{1,0:T(8,128)(2,1)S(1)}, bf16[128,1024]{1,0:T(8,128)(2,1)S(1)}, u32[]{:S(2)}, u32[]{:S(2)}) collective-permute-start(bf16[128,1024]{1,0:T(8,128)(2,1)S(1)} %pad_maximum_fusion), channel_id=1, source_target_pairs={{0,4},{4,0},{8,12},{12,8},{1,5},{5,1},{9,13},{13,9},{2,6},{6,2},{1... | collective-permute-start | bytes 786440 | tf_op jit(solution)/shard_map/ppermute | solution.py:510
  59.1 10.3 %collective-permute-start.12 = (bf16[96,1024]{1,0:T(8,128)(2,1)S(1)}, bf16[96,1024]{1,0:T(8,128)(2,1)S(1)}, u32[]{:S(2)}, u32[]{:S(2)}) collective-permute-start(bf16[96,1024]{1,0:T(8,128)(2,1)S(1)} %slice.26.mixed_ref), channel_id=1, source_target_pairs={{0,2},{2,0},{1,3},{3,1},{4,6},{6,4},{5,7},{7,5},{8,10},{10,8},{9,1... | collective-permute-start | bytes 589832 | tf_op jit(solution)/shard_map/ppermute | solution.py:475
  60.6 8.7 %collective-permute-start.14 = (bf16[96,1024]{1,0:T(8,128)(2,1)S(1)}, bf16[96,1024]{1,0:T(8,128)(2,1)S(1)}, u32[]{:S(2)}, u32[]{:S(2)}) collective-permute-start(bf16[96,1024]{1,0:T(8,128)(2,1)S(1)} %collective-permute-done.11.mixed_ref), channel_id=1, source_target_pairs={{0,2},{2,0},{1,3},{3,1},{4,6},{6,4},{5,7},{7,5},{8,10},{10,8},{9,1... | collective-permute-start | bytes 589832 | tf_op jit(solution)/shard_map/ppermute | solution.py:475
  61.2 8.2 %collective-permute-start.13 = (bf16[32,1024]{1,0:T(8,128)(2,1)S(1)}, bf16[32,1024]{1,0:T(8,128)(2,1)S(1)}, u32[]{:S(2)}, u32[]{:S(2)}) collective-permute-start(bf16[32,1024]{1,0:T(8,128)(2,1)S(1)} %slice.27.mixed_ref), channel_id=1, source_target_pairs={{0,2},{2,0},{1,3},{3,1},{4,6},{6,4},{5,7},{7,5},{8,10},{10,8},{9,1... | collective-permute-start | bytes 196616 | tf_op jit(solution)/shard_map/ppermute | solution.py:475
  69.4 11.2 %collective-permute-start.18 = (bf16[128,1024]{1,0:T(8,128)(2,1)S(1)}, bf16[128,1024]{1,0:T(8,128)(2,1)S(1)}, u32[]{:S(2)}, u32[]{:S(2)}) collective-permute-start(bf16[128,1024]{1,0:T(8,128)(2,1)S(1)} %collective-permute-done.10), channel_id=1, source_target_pairs={{0,2},{2,0},{1,3},{3,1},{4,6},{6,4},{5,7},{7,5},{8,10},{10,8},{9,1... | collective-permute-start | bytes 786440 | tf_op jit(solution)/shard_map/ppermute | solution.py:475
  71.0 8.9 %collective-permute-start.17 = (bf16[128,1024]{1,0:T(8,128)(2,1)S(1)}, bf16[128,1024]{1,0:T(8,128)(2,1)S(1)}, u32[]{:S(2)}, u32[]{:S(2)}) collective-permute-start(bf16[128,1024]{1,0:T(8,128)(2,1)S(1)} %collective-permute-done.15), channel_id=1, source_target_pairs={{0,4},{4,0},{8,12},{12,8},{1,5},{5,1},{9,13},{13,9},{2,6},{6,2},{1... | collective-permute-start | bytes 786440 | tf_op jit(solution)/shard_map/ppermute | solution.py:510
  71.7 13.9 %collective-permute-start.19 = (bf16[32,1024]{1,0:T(8,128)(2,1)S(1)}, bf16[32,1024]{1,0:T(8,128)(2,1)S(1)}, u32[]{:S(2)}, u32[]{:S(2)}) collective-permute-start(bf16[32,1024]{1,0:T(8,128)(2,1)S(1)} %add.245), channel_id=1, source_target_pairs={{0,8},{4,12},{8,0},{12,4},{1,9},{5,13},{9,1},{13,5},{2,10},{6,14},... | collective-permute-start | bytes 196616 | tf_op jit(solution)/shard_map/ppermute | solution.py:510
  74.9 10.8 %collective-permute-start.20 = (bf16[32,1024]{1,0:T(8,128)(2,1)S(1)}, bf16[32,1024]{1,0:T(8,128)(2,1)S(1)}, u32[]{:S(2)}, u32[]{:S(2)}) collective-permute-start(bf16[32,1024]{1,0:T(8,128)(2,1)S(1)} %add.245), channel_id=1, source_target_pairs={{0,12},{4,8},{8,4},{12,0},{1,13},{5,9},{9,5},{13,1},{2,14},{6,10},... | collective-permute-start | bytes 196616 | tf_op jit(solution)/shard_map/ppermute | solution.py:510
  79.8 5.8 %collective-permute-start.21 = (bf16[96,1024]{1,0:T(8,128)(2,1)S(1)}, bf16[96,1024]{1,0:T(8,128)(2,1)S(1)}, u32[]{:S(2)}, u32[]{:S(2)}) collective-permute-start(bf16[96,1024]{1,0:T(8,128)(2,1)S(1)} %add.244), channel_id=1, source_target_pairs={{0,4},{4,0},{8,12},{12,8},{1,5},{5,1},{9,13},{13,9},{2,6},{6,2},{1... | collective-permute-start | bytes 589832 | tf_op jit(solution)/shard_map/ppermute | solution.py:510
  84.0 1.6 %collective-permute-start = (bf16[1,2,2,2,16,1024]{5,4,3,2,1,0:T(8,128)(2,1)S(1)}, bf16[1,2,2,2,16,1024]{5,4,3,2,1,0:T(8,128)(2,1)S(1)}, u32[]{:S(2)}, u32[]{:S(2)}) collective-permute-start(bf16[1,2,2,2,16,1024]{5,4,3,2,1,0:T(8,128)(2,1)S(1)} %constant_dynamic-slice_fusion), channel_id=1, source_target_pairs={{0,1},{1,0},{2,3},{3,2},{4,5},{5,4},{6,7},{7,6},{8,9},{9,8},{10,11... | collective-permute-start | bytes 786440 | tf_op jit(solution)/shard_map/cond/branch_1_fun/ppermute | solution.py:475
  85.7 5.7 %collective-permute-start.22 = (bf16[1,2,2,16,1024]{4,3,2,1,0:T(8,128)(2,1)S(1)}, bf16[1,2,2,16,1024]{4,3,2,1,0:T(8,128)(2,1)S(1)}, u32[]{:S(2)}, u32[]{:S(2)}) collective-permute-start(bf16[1,2,2,16,1024]{4,3,2,1,0:T(8,128)(2,1)S(1)} %constant_dynamic-slice_fusion.5), channel_id=1, source_target_pairs={{0,2},{2,0},{1,3},{3,1},{4,6},{6,4},{5,7},{7,5},{8,10},{10,8},{9,1... | collective-permute-start | bytes 393224 | tf_op jit(solution)/shard_map/ppermute | solution.py:475
  89.7 1.6 %collective-permute-start.1 = (bf16[1,2,2,2,16,1024]{5,4,3,2,1,0:T(8,128)(2,1)S(1)}, bf16[1,2,2,2,16,1024]{5,4,3,2,1,0:T(8,128)(2,1)S(1)}, u32[]{:S(2)}, u32[]{:S(2)}) collective-permute-start(bf16[1,2,2,2,16,1024]{5,4,3,2,1,0:T(8,128)(2,1)S(1)} %constant_dynamic-slice_fusion.1), channel_id=1, source_target_pairs={{0,1},{1,0},{2,3},{3,2},{4,5},{5,4},{6,7},{7,6},{8,9},{9,8},{10,11... | collective-permute-start | bytes 786440 | tf_op jit(solution)/shard_map/cond/branch_1_fun/ppermute | solution.py:475
  91.5 5.6 %collective-permute-start.23 = (bf16[1,2,2,16,1024]{4,3,2,1,0:T(8,128)(2,1)S(1)}, bf16[1,2,2,16,1024]{4,3,2,1,0:T(8,128)(2,1)S(1)}, u32[]{:S(2)}, u32[]{:S(2)}) collective-permute-start(bf16[1,2,2,16,1024]{4,3,2,1,0:T(8,128)(2,1)S(1)} %constant_dynamic-slice_fusion.4), channel_id=1, source_target_pairs={{0,2},{2,0},{1,3},{3,1},{4,6},{6,4},{5,7},{7,5},{8,10},{10,8},{9,1... | collective-permute-start | bytes 393224 | tf_op jit(solution)/shard_map/ppermute | solution.py:475
  97.2 7.3 %collective-permute-start.25 = (bf16[32,1024]{1,0:T(8,128)(2,1)S(1)}, bf16[32,1024]{1,0:T(8,128)(2,1)S(1)}, u32[]{:S(2)}, u32[]{:S(2)}) collective-permute-start(bf16[32,1024]{1,0:T(8,128)(2,1)S(1)} %bitcast.38), channel_id=1, source_target_pairs={{0,8},{4,12},{8,0},{12,4},{1,9},{5,13},{9,1},{13,5},{2,10},{6,14},... | collective-permute-start | bytes 196616 | tf_op jit(solution)/shard_map/ppermute | solution.py:510
  100.1 6.1 %collective-permute-start.26 = (bf16[32,1024]{1,0:T(8,128)(2,1)S(1)}, bf16[32,1024]{1,0:T(8,128)(2,1)S(1)}, u32[]{:S(2)}, u32[]{:S(2)}) collective-permute-start(bf16[32,1024]{1,0:T(8,128)(2,1)S(1)} %bitcast.37), channel_id=1, source_target_pairs={{0,12},{4,8},{8,4},{12,0},{1,13},{5,9},{9,5},{13,1},{2,14},{6,10},... | collective-permute-start | bytes 196616 | tf_op jit(solution)/shard_map/ppermute | solution.py:510
  100.9 5.2 %collective-permute-start.24 = (bf16[32,1024]{1,0:T(8,128)(2,1)S(1)}, bf16[32,1024]{1,0:T(8,128)(2,1)S(1)}, u32[]{:S(2)}, u32[]{:S(2)}) collective-permute-start(bf16[32,1024]{1,0:T(8,128)(2,1)S(1)} %bitcast.39), channel_id=1, source_target_pairs={{0,4},{4,0},{8,12},{12,8},{1,5},{5,1},{9,13},{13,9},{2,6},{6,2},{1... | collective-permute-start | bytes 196616 | tf_op jit(solution)/shard_map/ppermute | solution.py:510

commit v7 on v6

--- a/solution.py
+++ b/solution.py
@@ -404,36 +404,35 @@
 
 def project_kernel(pairs, where_ref, weight_ref, *refs):
     pieces = refs[: 2 * pairs]
-    up_ref, down_ref, out_ref, weight_own, sums, sems = refs[2 * pairs :]
+    up_ref, down_ref, out_ref, weight_own, scaled, sums, sems = refs[2 * pairs :]
     rows, half = pieces[0].shape
     sign = (1 - 2 * where_ref[0]).astype(f32)
     sub_count, chan_count, _, blocks, size, features = out_ref.shape
-    tile = half // 2
+    bounds = [half * eighth // 4 for eighth in (0, 2, 4, 6, 7, 8)]
+    spans = [slice(*ends) for ends in zip(bounds, bounds[1:])]
     copies = start_all(
         [
-            pltpu.make_async_copy(
-                weight_ref.at[start : start + tile, :],
-                weight_own.at[start : start + tile, :],
-                sems.at[start // tile],
-            )
-            for start in range(0, 2 * half, tile)
+            pltpu.make_async_copy(weight_ref.at[at, :], weight_own.at[at, :], sems.at[index])
+            for index, at in enumerate(spans)
         ]
     )
-    for step, copy in enumerate(copies):
-        at = slice(step * tile, (step + 1) * tile)
-        inner = slice(step * tile % half, step * tile % half + tile)
-        scaled = []
+    for start in range(0, half, H_BLOCK):
+        inner = slice(start, start + H_BLOCK)
         for pair in range(pairs):
             one = pieces[2 * pair][:, inner].astype(f32)
             two = pieces[2 * pair + 1][:, inner].astype(f32)
-            mixed = (one - two) * sign if step * tile >= half else one + two
-            quant = jnp.clip(mixed * up_ref[:, at], -clip_level, clip_level).astype(bf16)
-            scaled.append((quant.astype(f32) * down_ref[:, at]).astype(bf16))
+            for side, mixed in enumerate((one + two, (one - two) * sign)):
+                at = slice(side * half + start, side * half + start + H_BLOCK)
+                quant = jnp.clip(mixed * up_ref[:, at], -clip_level, clip_level).astype(bf16)
+                scaled[pair * rows : (pair + 1) * rows, at] = (
+                    quant.astype(f32) * down_ref[:, at]
+                ).astype(bf16)
+    for index, (copy, at) in enumerate(zip(copies, spans)):
         copy.wait()
-        term = dot(jnp.concatenate(scaled, axis=0), weight_own[at, :])
-        if step == 0:
+        term = dot(scaled[:, at], weight_own[at, :])
+        if index == 0:
             sums[...] = term
-        elif step < len(copies) - 1:
+        elif index < len(spans) - 1:
             sums[...] += term
         else:
             total = (sums[...] + term).astype(bf16)
@@ -673,8 +672,9 @@
             1,
             (
                 pltpu.VMEM(out_weight.shape, bf16),
+                pltpu.VMEM((pairs * tokens, width), bf16),
                 pltpu.VMEM((pairs * tokens, features), f32),
-                pltpu.SemaphoreType.DMA((4,)),
+                pltpu.SemaphoreType.DMA((5,)),
             ),
             WIDE_PARAMS,
         )

time: 107 us -> 106 us (level)
  Pallas kernels: 11.3 us -> 10.2 us
  transfers between devices with their start and end apart: 27 -> 27, of which waited for: 13 -> 15; matrix products, arithmetic and copies ran while one was open for 4% -> 4% of each run, Pallas kernels for 8% -> 7%
where the time goes in v7:
time: 106 us
  waiting for transfers between devices  48.6 us (46%)
  starting transfers between devices  39.5 us (37%)
  Pallas kernels  10.2 us (10%)
  local copies, waits for them, and re-layouts  5.09 us (5%)
  other arithmetic  2.14 us (2%)
    ppermute x13, waiting for transfers between devices, swap_seq(): return lax.ppermute(value, 'seq', [(k, k ^ distance) for k in range(count)])  27.6 us
    ppermute x13, starting transfers between devices, swap_seq(): return lax.ppermute(value, 'seq', [(k, k ^ distance) for k in range(count)])  23.6 us
    ppermute x12, waiting for transfers between devices, swap(): return lax.ppermute(value, axis, [(k, k ^ 1 << bit) for k in range(count)])  21 us
    ppermute x12, starting transfers between devices, swap(): return lax.ppermute(value, axis, [(k, k ^ 1 << bit) for k in range(count)])  10 us
    pallas_call x8, Pallas kernels, call(): pl.pallas_call(kernel, out_shape=out_shape, in_specs=specs, scratch_shape...  9.09 us
    ppermute x1, starting transfers between devices, paired_body(): lax.ppermute(straight, 'seq', [(k, k + 2 * ahead) for k in firsts])  4.5 us
    dynamic_slice x2, local copies, waits for them, and re-layouts, half_of(): return lax.dynamic_slice_in_dim(value, which * half, half, 1)  2.84 us
  transfers between devices with their start and end apart: 27, of which 15 were waited for; matrix products, arithmetic and copies ran while one was open for 4% of the time, Pallas kernels for 7%

profile of v7, /device:TPU:0, one launch (start us, length us, event | category | flops | bytes accessed | tf_op | source)
XLA Modules:
  0.0 106.0 jit_solution(3632551780229188501)
XLA Ops:
  0.0 1.3 %constant_dynamic-slice_fusion.8 = (bf16[128,1,256]{2,1,0:T(2,128)(2,1)S(1)}, bf16[128,1,256]{2,1,0:T(2,128)(2,1)S(1)}) fusion(bf16[128,2,256]{2,1,0:T(2,128)(2,1)} %param.18, s32[]{:T(128)S(6)} %select_n.150, bf16[128,2,256]{2,1,0:T(2,128)(2,1)} %param.17), kind=kLoop, calls=%fused_computation.52 | loop fusion | bytes 262148 | tf_op jit(solution)/shard_map/jit(dynamic_index_in_dim)/dynamic_slice | solution.py:536
  1.3 0.7 pad_maximum_fusion.4.steps_ref
  2.1 1.1 %constant_dynamic-slice_fusion.10 = (bf16[128,1024]{1,0:T(8,128)(2,1)S(1)}, bf16[128,1024]{1,0:T(8,128)(2,1)S(1)}) fusion(bf16[128,2048]{1,0:T(8,128)(2,1)} %param.16, s32[]{:T(128)S(6)} %select_n.148, s32[]{:T(128)S(6)} %select_n.147), kind=kLoop, calls=%fused_computation.54 | loop fusion | bytes 1048584 | tf_op jit(solution)/shard_map/dynamic_slice | solution.py:546
  3.1 0.8 pack.1
  4.0 3.1 %collective-permute-start.5 = (bf16[128,1664]{1,0:T(8,128)(2,1)S(1)}, bf16[128,1664]{1,0:T(8,128)(2,1)S(1)}, u32[]{:S(2)}, u32[]{:S(2)}) collective-permute-start(bf16[128,1664]{1,0:T(8,128)(2,1)S(1)} %get-tuple-element.100), channel_id=1, source_target_pairs={{0,4},{4,0},{8,12},{12,8},{1,5},{5,1},{9,13},{13,9},{2,6},{6,2},{1... | collective-permute-start | bytes 1277960 | tf_op jit(solution)/shard_map/ppermute | solution.py:509
  7.1 4.5 %collective-permute-start.2 = (bf16[1296,128]{1,0:T(8,128)(2,1)S(1)}, bf16[1296,128]{1,0:T(8,128)(2,1)S(1)}, u32[]{:S(2)}, u32[]{:S(2)}) collective-permute-start(bf16[1296,128]{1,0:T(8,128)(2,1)S(1)} %get-tuple-element.97), channel_id=1, source_target_pairs={{0,8},{4,12},{1,9},{5,13},{2,10},{6,14},{3,11},{7,15},{16,24},{20,... | collective-permute-start | bytes 995336 | tf_op jit(solution)/shard_map/ppermute | solution.py:563
  11.6 1.3 %collective-permute-start.3 = (bf16[1296,128]{1,0:T(8,128)(2,1)S(1)}, bf16[1296,128]{1,0:T(8,128)(2,1)S(1)}, u32[]{:S(2)}, u32[]{:S(2)}) collective-permute-start(bf16[1296,128]{1,0:T(8,128)(2,1)S(1)} %get-tuple-element.98), channel_id=1, source_target_pairs={{0,12},{4,8},{1,13},{5,9},{2,14},{6,10},{3,15},{7,11},{16,28},{20,... | collective-permute-start | bytes 995336 | tf_op jit(solution)/shard_map/ppermute | solution.py:564
  12.9 1.8 %constant_dynamic-slice_fusion.6 = (bf16[128,1024]{1,0:T(8,128)(2,1)}, bf16[128,1024]{1,0:T(8,128)(2,1)S(1)}) fusion(bf16[128,2048]{1,0:T(8,128)(2,1)} %param.22, s32[]{:T(128)S(6)} %select_n.148, s32[]{:T(128)S(6)} %select_n.147), kind=kLoop, calls=%fused_computation.50 | loop fusion | bytes 1048584 | tf_op jit(solution)/shard_map/dynamic_slice | solution.py:546
  14.7 0.5 collective-permute-start.4
  15.2 0.7 broadcast_in_dim.67
  16.0 0.7 select_multiply_fusion
  16.7 0.5 collective-permute-done.5.msg_ref
  17.3 1.9 %pair.1 = (f32[256,1024]{1,0:T(8,128)S(1)}, f32[256,1024]{1,0:T(8,128)S(1)}, bf16[256,256]{1,0:T(8,128)(2,1)S(1)}) custom-call(s32[1]{0:T(128)} %bitcast.3.where_ref.refs_2_, bf16[128,1024]{1,0:T(8,128)(2,1)S(1)} %get-tuple-element.144.x_mine_ref.x_ref, bf16[128,640]{1,0:T(8,128)(2,1)S(1)} %get-tuple-element.99.meta_ref, ...), custom_call_target="tpu_custom_call" | custom-call | flops 1 | bytes 1 | tf_op jit(solution)/shard_map/pair/pallas_call | solution.py:496
  19.2 17.0 %collective-permute-done.4.refs_4_ = bf16[128,1024]{1,0:T(8,128)(2,1)S(1)} collective-permute-done((bf16[128,1024]{1,0:T(8,128)(2,1)}, bf16[128,1024]{1,0:T(8,128)(2,1)S(1)}, u32[]{:S(2)}, u32[]{:S(2)}) %collective-permute-start.4) | collective-permute-done | bytes 262176 | tf_op jit(solution)/shard_map/ppermute | solution.py:509
  36.2 1.1 %mix.1 = (bf16[128,1024]{1,0:T(8,128)(2,1)S(1)}, bf16[128,1024]{1,0:T(8,128)(2,1)S(1)}) custom-call(bf16[1296,128]{1,0:T(8,128)(2,1)S(1)} %collective-permute-done.2.refs_0_, bf16[1296,128]{1,0:T(8,128)(2,1)S(1)} %collective-permute-done.3.refs_1_, s32[1]{0:T(128)} %bitcast.3.where_ref.refs_2_, bf16[128,1024]{1,0:T(8,128)(2,1)S(1)} %get-tuple-element.142.refs_3_, ...), custom_call_target="tpu_custom_call" | custom-call | flops 1 | bytes 30000000 | tf_op jit(solution)/shard_map/mix/pallas_call | solution.py:597
  37.9 1.0 collective-permute-done.9
  39.0 4.1 %collective-permute-start.10 = (bf16[128,1024]{1,0:T(8,128)(2,1)S(1)}, bf16[128,1024]{1,0:T(8,128)(2,1)S(1)}, u32[]{:S(2)}, u32[]{:S(2)}) collective-permute-start(bf16[128,1024]{1,0:T(8,128)(2,1)S(1)} %add_convert_fusion.3), channel_id=1, source_target_pairs={{0,4},{4,0},{8,12},{12,8},{1,5},{5,1},{9,13},{13,9},{2,6},{6,2},{1... | collective-permute-start | bytes 786440 | tf_op jit(solution)/shard_map/ppermute | solution.py:509
  43.1 2.0 %collective-permute-start.11 = (bf16[96,1024]{1,0:T(8,128)(2,1)S(1)}, bf16[96,1024]{1,0:T(8,128)(2,1)S(1)}, u32[]{:S(2)}, u32[]{:S(2)}) collective-permute-start(bf16[96,1024]{1,0:T(8,128)(2,1)S(1)} %slice.32), channel_id=1, source_target_pairs={{0,8},{4,12},{8,0},{12,4},{1,9},{5,13},{9,1},{13,5},{2,10},{6,14},... | collective-permute-start | bytes 589832 | tf_op jit(solution)/shard_map/ppermute | solution.py:509
  45.2 1.6 %collective-permute-start.7 = (bf16[64,1024]{1,0:T(8,128)(2,1)S(1)}, bf16[64,1024]{1,0:T(8,128)(2,1)S(1)}, u32[]{:S(2)}, u32[]{:S(2)}) collective-permute-start(bf16[64,1024]{1,0:T(8,128)(2,1)S(1)} %get-tuple-element.106), channel_id=1, source_target_pairs={{0,2},{2,0},{1,3},{3,1},{4,6},{6,4},{5,7},{7,5},{8,10},{10,8},{9,1... | collective-permute-start | bytes 393224 | tf_op jit(solution)/shard_map/ppermute | solution.py:474
  46.8 0.5 collective-permute-start.8
  47.3 4.4 %collective-permute-done.7 = bf16[64,1024]{1,0:T(8,128)(2,1)S(1)} collective-permute-done((bf16[64,1024]{1,0:T(8,128)(2,1)S(1)}, bf16[64,1024]{1,0:T(8,128)(2,1)S(1)}, u32[]{:S(2)}, u32[]{:S(2)}) %collective-permute-start.7) | collective-permute-done | bytes 131104 | tf_op jit(solution)/shard_map/ppermute | solution.py:474
  51.7 1.7 %collective-permute-done.8 = bf16[64,1024]{1,0:T(8,128)(2,1)S(1)} collective-permute-done((bf16[64,1024]{1,0:T(8,128)(2,1)S(1)}, bf16[64,1024]{1,0:T(8,128)(2,1)S(1)}, u32[]{:S(2)}, u32[]{:S(2)}) %collective-permute-start.8) | collective-permute-done | bytes 131104 | tf_op jit(solution)/shard_map/ppermute | solution.py:474
  53.3 0.6 collective-permute-done.10
  54.0 2.8 %collective-permute-start.15 = (bf16[128,1024]{1,0:T(8,128)(2,1)S(1)}, bf16[128,1024]{1,0:T(8,128)(2,1)S(1)}, u32[]{:S(2)}, u32[]{:S(2)}) collective-permute-start(bf16[128,1024]{1,0:T(8,128)(2,1)S(1)} %pad_maximum_fusion), channel_id=1, source_target_pairs={{0,8},{4,12},{8,0},{12,4},{1,9},{5,13},{9,1},{13,5},{2,10},{6,14},... | collective-permute-start | bytes 786440 | tf_op jit(solution)/shard_map/ppermute | solution.py:509
  56.8 2.2 %collective-permute-start.16 = (bf16[128,1024]{1,0:T(8,128)(2,1)S(1)}, bf16[128,1024]{1,0:T(8,128)(2,1)S(1)}, u32[]{:S(2)}, u32[]{:S(2)}) collective-permute-start(bf16[128,1024]{1,0:T(8,128)(2,1)S(1)} %pad_maximum_fusion), channel_id=1, source_target_pairs={{0,4},{4,0},{8,12},{12,8},{1,5},{5,1},{9,13},{13,9},{2,6},{6,2},{1... | collective-permute-start | bytes 786440 | tf_op jit(solution)/shard_map/ppermute | solution.py:509
  59.1 1.6 %collective-permute-start.12 = (bf16[96,1024]{1,0:T(8,128)(2,1)S(1)}, bf16[96,1024]{1,0:T(8,128)(2,1)S(1)}, u32[]{:S(2)}, u32[]{:S(2)}) collective-permute-start(bf16[96,1024]{1,0:T(8,128)(2,1)S(1)} %slice.26.mixed_ref), channel_id=1, source_target_pairs={{0,2},{2,0},{1,3},{3,1},{4,6},{6,4},{5,7},{7,5},{8,10},{10,8},{9,1... | collective-permute-start | bytes 589832 | tf_op jit(solution)/shard_map/ppermute | solution.py:474
  61.2 1.5 %collective-permute-start.13 = (bf16[32,1024]{1,0:T(8,128)(2,1)S(1)}, bf16[32,1024]{1,0:T(8,128)(2,1)S(1)}, u32[]{:S(2)}, u32[]{:S(2)}) collective-permute-start(bf16[32,1024]{1,0:T(8,128)(2,1)S(1)} %slice.27.mixed_ref), channel_id=1, source_target_pairs={{0,2},{2,0},{1,3},{3,1},{4,6},{6,4},{5,7},{7,5},{8,10},{10,8},{9,1... | collective-permute-start | bytes 196616 | tf_op jit(solution)/shard_map/ppermute | solution.py:474
  62.7 6.7 %collective-permute-done.13.received_ref = bf16[32,1024]{1,0:T(8,128)(2,1)S(1)} collective-permute-done((bf16[32,1024]{1,0:T(8,128)(2,1)S(1)}, bf16[32,1024]{1,0:T(8,128)(2,1)S(1)}, u32[]{:S(2)}, u32[]{:S(2)}) %collective-permute-start.13) | collective-permute-done | bytes 65568 | tf_op jit(solution)/shard_map/ppermute | solution.py:474
  69.4 1.6 %collective-permute-start.18 = (bf16[128,1024]{1,0:T(8,128)(2,1)S(1)}, bf16[128,1024]{1,0:T(8,128)(2,1)S(1)}, u32[]{:S(2)}, u32[]{:S(2)}) collective-permute-start(bf16[128,1024]{1,0:T(8,128)(2,1)S(1)} %collective-permute-done.10), channel_id=1, source_target_pairs={{0,2},{2,0},{1,3},{3,1},{4,6},{6,4},{5,7},{7,5},{8,10},{10,8},{9,1... | collective-permute-start | bytes 786440 | tf_op jit(solution)/shard_map/ppermute | solution.py:474
  71.0 0.7 collective-permute-start.17
  71.7 3.1 %collective-permute-start.19 = (bf16[32,1024]{1,0:T(8,128)(2,1)S(1)}, bf16[32,1024]{1,0:T(8,128)(2,1)S(1)}, u32[]{:S(2)}, u32[]{:S(2)}) collective-permute-start(bf16[32,1024]{1,0:T(8,128)(2,1)S(1)} %add.245), channel_id=1, source_target_pairs={{0,8},{4,12},{8,0},{12,4},{1,9},{5,13},{9,1},{13,5},{2,10},{6,14},... | collective-permute-start | bytes 196616 | tf_op jit(solution)/shard_map/ppermute | solution.py:509
  74.9 0.6 collective-permute-start.20
  75.6 4.2 %collective-permute-done.17 = bf16[128,1024]{1,0:T(8,128)(2,1)S(1)} collective-permute-done((bf16[128,1024]{1,0:T(8,128)(2,1)S(1)}, bf16[128,1024]{1,0:T(8,128)(2,1)S(1)}, u32[]{:S(2)}, u32[]{:S(2)}) %collective-permute-start.17) | collective-permute-done | bytes 262176 | tf_op jit(solution)/shard_map/ppermute | solution.py:509
  79.8 0.7 collective-permute-start.21
  80.7 4.5 %conditional.2 = (bf16[2,2,2,16,1024]{4,3,2,1,0:T(8,128)(2,1)S(1)}) conditional(s32[]{:T(128)} %convert_element_type.102, () %tuple.22, (s32[1]{0:T(128)}, bf16[2048,1024]{1,0:T(8,128)(2,1)}, bf16[128,1024]{1,0:T(8,128)(2,1)S(1)}, bf16[128,1024]{1,0:T(8,128)(2,1)S(1)}, bf16[128,1024]{1,0:T(8,128)(2,1)S(1)}, ...), branch_computations={%region_0.1_spmd, %region_1.2_spmd} | conditional | flops 524309 | bytes 32359552 | solution.py:685
  80.7 2.7 %project.2 = bf16[2,2,2,2,16,1024]{5,4,3,2,1,0:T(8,128)(2,1)S(1)} custom-call(s32[1]{0:T(128)} %get-tuple-element.42.where_ref, bf16[2048,1024]{1,0:T(8,128)(2,1)} %get-tuple-element.44.weight_ref, bf16[128,1024]{1,0:T(8,128)(2,1)S(1)} %get-tuple-element.45.refs_0_, bf16[128,1024]{1,0:T(8,128)(2,1)S(1)} %get-tuple-element.46.refs_1_, ...), custom_call_target="tpu_custom_call" | custom-call | flops 1 | bytes 30000000 | tf_op jit(solution)/shard_map/cond/branch_1_fun/project/pallas_call | solution.py:496
  83.5 1.5 %collective-permute-done = bf16[1,2,2,2,16,1024]{5,4,3,2,1,0:T(8,128)(2,1)S(1)} collective-permute-done((bf16[1,2,2,2,16,1024]{5,4,3,2,1,0:T(8,128)(2,1)S(1)}, bf16[1,2,2,2,16,1024]{5,4,3,2,1,0:T(8,128)(2,1)S(1)}, u32[]{:S(2)}, u32[]{:S(2)}) %collective-permute-start) | collective-permute-done | bytes 262176 | tf_op jit(solution)/shard_map/cond/branch_1_fun/ppermute | solution.py:474
  85.5 0.7 collective-permute-start.22
  86.2 4.5 %conditional.3 = (bf16[2,2,2,16,1024]{4,3,2,1,0:T(8,128)(2,1)S(1)}) conditional(s32[]{:T(128)} %convert_element_type.102, () %tuple.28, (s32[1]{0:T(128)}, bf16[2048,1024]{1,0:T(8,128)(2,1)}, bf16[128,1024]{1,0:T(8,128)(2,1)S(1)}, bf16[128,1024]{1,0:T(8,128)(2,1)S(1)}, bf16[128,1024]{1,0:T(8,128)(2,1)S(1)}, ...), branch_computations={%region_2.3_spmd, %region_3.4_spmd} | conditional | flops 524309 | bytes 32359552 | solution.py:685
  86.3 2.7 %project.3 = bf16[2,2,2,2,16,1024]{5,4,3,2,1,0:T(8,128)(2,1)S(1)} custom-call(s32[1]{0:T(128)} %get-tuple-element.51.where_ref, bf16[2048,1024]{1,0:T(8,128)(2,1)} %get-tuple-element.52.weight_ref, bf16[128,1024]{1,0:T(8,128)(2,1)S(1)} %get-tuple-element.53.refs_0_, bf16[128,1024]{1,0:T(8,128)(2,1)S(1)} %get-tuple-element.54.refs_1_, ...), custom_call_target="tpu_custom_call" | custom-call | flops 1 | bytes 30000000 | tf_op jit(solution)/shard_map/cond/branch_1_fun/project/pallas_call | solution.py:496
  89.1 1.5 %collective-permute-done.1 = bf16[1,2,2,2,16,1024]{5,4,3,2,1,0:T(8,128)(2,1)S(1)} collective-permute-done((bf16[1,2,2,2,16,1024]{5,4,3,2,1,0:T(8,128)(2,1)S(1)}, bf16[1,2,2,2,16,1024]{5,4,3,2,1,0:T(8,128)(2,1)S(1)}, u32[]{:S(2)}, u32[]{:S(2)}) %collective-permute-start.1) | collective-permute-done | bytes 262176 | tf_op jit(solution)/shard_map/cond/branch_1_fun/ppermute | solution.py:474
  90.9 1.4 %collective-permute-start.23 = (bf16[1,2,2,16,1024]{4,3,2,1,0:T(8,128)(2,1)S(1)}, bf16[1,2,2,16,1024]{4,3,2,1,0:T(8,128)(2,1)S(1)}, u32[]{:S(2)}, u32[]{:S(2)}) collective-permute-start(bf16[1,2,2,16,1024]{4,3,2,1,0:T(8,128)(2,1)S(1)} %constant_dynamic-slice_fusion.4), channel_id=1, source_target_pairs={{0,2},{2,0},{1,3},{3,1},{4,6},{6,4},{5,7},{7,5},{8,10},{10,8},{9,1... | collective-permute-start | bytes 393224 | tf_op jit(solution)/shard_map/ppermute | solution.py:474
  92.3 4.1 %collective-permute-done.23 = bf16[1,2,2,16,1024]{4,3,2,1,0:T(8,128)(2,1)S(1)} collective-permute-done((bf16[1,2,2,16,1024]{4,3,2,1,0:T(8,128)(2,1)S(1)}, bf16[1,2,2,16,1024]{4,3,2,1,0:T(8,128)(2,1)S(1)}, u32[]{:S(2)}, u32[]{:S(2)}) %collective-permute-start.23) | collective-permute-done | bytes 131104 | tf_op jit(solution)/shard_map/ppermute | solution.py:474
  96.5 2.6 %collective-permute-start.25 = (bf16[32,1024]{1,0:T(8,128)(2,1)S(1)}, bf16[32,1024]{1,0:T(8,128)(2,1)S(1)}, u32[]{:S(2)}, u32[]{:S(2)}) collective-permute-start(bf16[32,1024]{1,0:T(8,128)(2,1)S(1)} %bitcast.38), channel_id=1, source_target_pairs={{0,8},{4,12},{8,0},{12,4},{1,9},{5,13},{9,1},{13,5},{2,10},{6,14},... | collective-permute-start | bytes 196616 | tf_op jit(solution)/shard_map/ppermute | solution.py:509
  99.1 0.8 collective-permute-start.26
  100.2 3.4 %collective-permute-done.25.refs_2_ = bf16[32,1024]{1,0:T(8,128)(2,1)S(1)} collective-permute-done((bf16[32,1024]{1,0:T(8,128)(2,1)S(1)}, bf16[32,1024]{1,0:T(8,128)(2,1)S(1)}, u32[]{:S(2)}, u32[]{:S(2)}) %collective-permute-start.25) | collective-permute-done | bytes 65568 | tf_op jit(solution)/shard_map/ppermute | solution.py:509
  103.6 1.6 %collective-permute-done.26.refs_3_ = bf16[32,1024]{1,0:T(8,128)(2,1)S(1)} collective-permute-done((bf16[32,1024]{1,0:T(8,128)(2,1)S(1)}, bf16[32,1024]{1,0:T(8,128)(2,1)S(1)}, u32[]{:S(2)}, u32[]{:S(2)}) %collective-permute-start.26) | collective-permute-done | bytes 65568 | tf_op jit(solution)/shard_map/ppermute | solution.py:509
  105.2 0.7 place.1
  (56 shorter events, 3.1 us)
Async XLA Ops:
  0.0 36.2 %copy-start = (bf16[256,256]{1,0:T(8,128)(2,1)S(1)}, bf16[256,256]{1,0:T(8,128)(2,1)}, u32[]{:S(2)}) copy-start(bf16[256,256]{1,0:T(8,128)(2,1)} %constant.236.clone.refs_9_) | copy-start | bytes 393220
  4.0 13.3 %collective-permute-start.5 = (bf16[128,1664]{1,0:T(8,128)(2,1)S(1)}, bf16[128,1664]{1,0:T(8,128)(2,1)S(1)}, u32[]{:S(2)}, u32[]{:S(2)}) collective-permute-start(bf16[128,1664]{1,0:T(8,128)(2,1)S(1)} %get-tuple-element.100), channel_id=1, source_target_pairs={{0,4},{4,0},{8,12},{12,8},{1,5},{5,1},{9,13},{13,9},{2,6},{6,2},{1... | collective-permute-start | bytes 1277960 | tf_op jit(solution)/shard_map/ppermute | solution.py:509
  7.1 29.1 %collective-permute-start.2 = (bf16[1296,128]{1,0:T(8,128)(2,1)S(1)}, bf16[1296,128]{1,0:T(8,128)(2,1)S(1)}, u32[]{:S(2)}, u32[]{:S(2)}) collective-permute-start(bf16[1296,128]{1,0:T(8,128)(2,1)S(1)} %get-tuple-element.97), channel_id=1, source_target_pairs={{0,8},{4,12},{1,9},{5,13},{2,10},{6,14},{3,11},{7,15},{16,24},{20,... | collective-permute-start | bytes 995336 | tf_op jit(solution)/shard_map/ppermute | solution.py:563
  11.6 24.6 %collective-permute-start.3 = (bf16[1296,128]{1,0:T(8,128)(2,1)S(1)}, bf16[1296,128]{1,0:T(8,128)(2,1)S(1)}, u32[]{:S(2)}, u32[]{:S(2)}) collective-permute-start(bf16[1296,128]{1,0:T(8,128)(2,1)S(1)} %get-tuple-element.98), channel_id=1, source_target_pairs={{0,12},{4,8},{1,13},{5,9},{2,14},{6,10},{3,15},{7,11},{16,28},{20,... | collective-permute-start | bytes 995336 | tf_op jit(solution)/shard_map/ppermute | solution.py:564
  14.7 21.5 %collective-permute-start.4 = (bf16[128,1024]{1,0:T(8,128)(2,1)}, bf16[128,1024]{1,0:T(8,128)(2,1)S(1)}, u32[]{:S(2)}, u32[]{:S(2)}) collective-permute-start(bf16[128,1024]{1,0:T(8,128)(2,1)} %get-tuple-element.141), channel_id=1, source_target_pairs={{0,4},{4,0},{8,12},{12,8},{1,5},{5,1},{9,13},{13,9},{2,6},{6,2},{1... | collective-permute-start | bytes 786440 | tf_op jit(solution)/shard_map/ppermute | solution.py:509
  19.2 43.5 %copy-start.1 = (s32[2048]{0:T(1024)S(1)}, s32[2048]{0:T(1024)}, u32[]{:S(2)}) copy-start(s32[2048]{0:T(1024)} %param.25) | copy-start | bytes 24580
  37.3 1.6 %collective-permute-start.9 = (bf16[128,1024]{1,0:T(8,128)(2,1)S(1)}, bf16[128,1024]{1,0:T(8,128)(2,1)S(1)}, u32[]{:S(2)}, u32[]{:S(2)}) collective-permute-start(bf16[128,1024]{1,0:T(8,128)(2,1)S(1)} %get-tuple-element.105), channel_id=1, source_target_pairs={{0,1},{1,0},{2,3},{3,2},{4,5},{5,4},{6,7},{7,6},{8,9},{9,8},{10,11... | collective-permute-start | bytes 786440 | tf_op jit(solution)/shard_map/ppermute | solution.py:474
  37.4 7.7 %collective-permute-start.6 = (bf16[128,1024]{1,0:T(8,128)(2,1)S(1)}, bf16[128,1024]{1,0:T(8,128)(2,1)S(1)}, u32[]{:S(2)}, u32[]{:S(2)}) collective-permute-start(bf16[128,1024]{1,0:T(8,128)(2,1)S(1)} %get-tuple-element.104), channel_id=1, source_target_pairs={{0,1},{1,0},{2,3},{3,2},{4,5},{5,4},{6,7},{7,6},{8,9},{9,8},{10,11... | collective-permute-start | bytes 786440 | tf_op jit(solution)/shard_map/ppermute | solution.py:474
  39.0 14.9 %collective-permute-start.10 = (bf16[128,1024]{1,0:T(8,128)(2,1)S(1)}, bf16[128,1024]{1,0:T(8,128)(2,1)S(1)}, u32[]{:S(2)}, u32[]{:S(2)}) collective-permute-start(bf16[128,1024]{1,0:T(8,128)(2,1)S(1)} %add_convert_fusion.3), channel_id=1, source_target_pairs={{0,4},{4,0},{8,12},{12,8},{1,5},{5,1},{9,13},{13,9},{2,6},{6,2},{1... | collective-permute-start | bytes 786440 | tf_op jit(solution)/shard_map/ppermute | solution.py:509
  43.1 10.2 %collective-permute-start.11 = (bf16[96,1024]{1,0:T(8,128)(2,1)S(1)}, bf16[96,1024]{1,0:T(8,128)(2,1)S(1)}, u32[]{:S(2)}, u32[]{:S(2)}) collective-permute-start(bf16[96,1024]{1,0:T(8,128)(2,1)S(1)} %slice.32), channel_id=1, source_target_pairs={{0,8},{4,12},{8,0},{12,4},{1,9},{5,13},{9,1},{13,5},{2,10},{6,14},... | collective-permute-start | bytes 589832 | tf_op jit(solution)/shard_map/ppermute | solution.py:509
  45.2 6.4 %collective-permute-start.7 = (bf16[64,1024]{1,0:T(8,128)(2,1)S(1)}, bf16[64,1024]{1,0:T(8,128)(2,1)S(1)}, u32[]{:S(2)}, u32[]{:S(2)}) collective-permute-start(bf16[64,1024]{1,0:T(8,128)(2,1)S(1)} %get-tuple-element.106), channel_id=1, source_target_pairs={{0,2},{2,0},{1,3},{3,1},{4,6},{6,4},{5,7},{7,5},{8,10},{10,8},{9,1... | collective-permute-start | bytes 393224 | tf_op jit(solution)/shard_map/ppermute | solution.py:474
  46.8 6.6 %collective-permute-start.8 = (bf16[64,1024]{1,0:T(8,128)(2,1)S(1)}, bf16[64,1024]{1,0:T(8,128)(2,1)S(1)}, u32[]{:S(2)}, u32[]{:S(2)}) collective-permute-start(bf16[64,1024]{1,0:T(8,128)(2,1)S(1)} %get-tuple-element.108), channel_id=1, source_target_pairs={{0,2},{2,0},{1,3},{3,1},{4,6},{6,4},{5,7},{7,5},{8,10},{10,8},{9,1... | collective-permute-start | bytes 393224 | tf_op jit(solution)/shard_map/ppermute | solution.py:474
  54.0 15.4 %collective-permute-start.15 = (bf16[128,1024]{1,0:T(8,128)(2,1)S(1)}, bf16[128,1024]{1,0:T(8,128)(2,1)S(1)}, u32[]{:S(2)}, u32[]{:S(2)}) collective-permute-start(bf16[128,1024]{1,0:T(8,128)(2,1)S(1)} %pad_maximum_fusion), channel_id=1, source_target_pairs={{0,8},{4,12},{8,0},{12,4},{1,9},{5,13},{9,1},{13,5},{2,10},{6,14},... | collective-permute-start | bytes 786440 | tf_op jit(solution)/shard_map/ppermute | solution.py:509
  56.8 12.6 %collective-permute-start.16 = (bf16[128,1024]{1,0:T(8,128)(2,1)S(1)}, bf16[128,1024]{1,0:T(8,128)(2,1)S(1)}, u32[]{:S(2)}, u32[]{:S(2)}) collective-permute-start(bf16[128,1024]{1,0:T(8,128)(2,1)S(1)} %pad_maximum_fusion), channel_id=1, source_target_pairs={{0,4},{4,0},{8,12},{12,8},{1,5},{5,1},{9,13},{13,9},{2,6},{6,2},{1... | collective-permute-start | bytes 786440 | tf_op jit(solution)/shard_map/ppermute | solution.py:509
  59.1 10.3 %collective-permute-start.12 = (bf16[96,1024]{1,0:T(8,128)(2,1)S(1)}, bf16[96,1024]{1,0:T(8,128)(2,1)S(1)}, u32[]{:S(2)}, u32[]{:S(2)}) collective-permute-start(bf16[96,1024]{1,0:T(8,128)(2,1)S(1)} %slice.26.mixed_ref), channel_id=1, source_target_pairs={{0,2},{2,0},{1,3},{3,1},{4,6},{6,4},{5,7},{7,5},{8,10},{10,8},{9,1... | collective-permute-start | bytes 589832 | tf_op jit(solution)/shard_map/ppermute | solution.py:474
  60.6 8.7 %collective-permute-start.14 = (bf16[96,1024]{1,0:T(8,128)(2,1)S(1)}, bf16[96,1024]{1,0:T(8,128)(2,1)S(1)}, u32[]{:S(2)}, u32[]{:S(2)}) collective-permute-start(bf16[96,1024]{1,0:T(8,128)(2,1)S(1)} %collective-permute-done.11.mixed_ref), channel_id=1, source_target_pairs={{0,2},{2,0},{1,3},{3,1},{4,6},{6,4},{5,7},{7,5},{8,10},{10,8},{9,1... | collective-permute-start | bytes 589832 | tf_op jit(solution)/shard_map/ppermute | solution.py:474
  61.2 8.2 %collective-permute-start.13 = (bf16[32,1024]{1,0:T(8,128)(2,1)S(1)}, bf16[32,1024]{1,0:T(8,128)(2,1)S(1)}, u32[]{:S(2)}, u32[]{:S(2)}) collective-permute-start(bf16[32,1024]{1,0:T(8,128)(2,1)S(1)} %slice.27.mixed_ref), channel_id=1, source_target_pairs={{0,2},{2,0},{1,3},{3,1},{4,6},{6,4},{5,7},{7,5},{8,10},{10,8},{9,1... | collective-permute-start | bytes 196616 | tf_op jit(solution)/shard_map/ppermute | solution.py:474
  69.4 11.2 %collective-permute-start.18 = (bf16[128,1024]{1,0:T(8,128)(2,1)S(1)}, bf16[128,1024]{1,0:T(8,128)(2,1)S(1)}, u32[]{:S(2)}, u32[]{:S(2)}) collective-permute-start(bf16[128,1024]{1,0:T(8,128)(2,1)S(1)} %collective-permute-done.10), channel_id=1, source_target_pairs={{0,2},{2,0},{1,3},{3,1},{4,6},{6,4},{5,7},{7,5},{8,10},{10,8},{9,1... | collective-permute-start | bytes 786440 | tf_op jit(solution)/shard_map/ppermute | solution.py:474
  71.0 8.9 %collective-permute-start.17 = (bf16[128,1024]{1,0:T(8,128)(2,1)S(1)}, bf16[128,1024]{1,0:T(8,128)(2,1)S(1)}, u32[]{:S(2)}, u32[]{:S(2)}) collective-permute-start(bf16[128,1024]{1,0:T(8,128)(2,1)S(1)} %collective-permute-done.15), channel_id=1, source_target_pairs={{0,4},{4,0},{8,12},{12,8},{1,5},{5,1},{9,13},{13,9},{2,6},{6,2},{1... | collective-permute-start | bytes 786440 | tf_op jit(solution)/shard_map/ppermute | solution.py:509
  71.7 13.4 %collective-permute-start.19 = (bf16[32,1024]{1,0:T(8,128)(2,1)S(1)}, bf16[32,1024]{1,0:T(8,128)(2,1)S(1)}, u32[]{:S(2)}, u32[]{:S(2)}) collective-permute-start(bf16[32,1024]{1,0:T(8,128)(2,1)S(1)} %add.245), channel_id=1, source_target_pairs={{0,8},{4,12},{8,0},{12,4},{1,9},{5,13},{9,1},{13,5},{2,10},{6,14},... | collective-permute-start | bytes 196616 | tf_op jit(solution)/shard_map/ppermute | solution.py:509
  74.9 10.3 %collective-permute-start.20 = (bf16[32,1024]{1,0:T(8,128)(2,1)S(1)}, bf16[32,1024]{1,0:T(8,128)(2,1)S(1)}, u32[]{:S(2)}, u32[]{:S(2)}) collective-permute-start(bf16[32,1024]{1,0:T(8,128)(2,1)S(1)} %add.245), channel_id=1, source_target_pairs={{0,12},{4,8},{8,4},{12,0},{1,13},{5,9},{9,5},{13,1},{2,14},{6,10},... | collective-permute-start | bytes 196616 | tf_op jit(solution)/shard_map/ppermute | solution.py:509
  79.8 5.7 %collective-permute-start.21 = (bf16[96,1024]{1,0:T(8,128)(2,1)S(1)}, bf16[96,1024]{1,0:T(8,128)(2,1)S(1)}, u32[]{:S(2)}, u32[]{:S(2)}) collective-permute-start(bf16[96,1024]{1,0:T(8,128)(2,1)S(1)} %add.244), channel_id=1, source_target_pairs={{0,4},{4,0},{8,12},{12,8},{1,5},{5,1},{9,13},{13,9},{2,6},{6,2},{1... | collective-permute-start | bytes 589832 | tf_op jit(solution)/shard_map/ppermute | solution.py:509
  83.5 1.6 %collective-permute-start = (bf16[1,2,2,2,16,1024]{5,4,3,2,1,0:T(8,128)(2,1)S(1)}, bf16[1,2,2,2,16,1024]{5,4,3,2,1,0:T(8,128)(2,1)S(1)}, u32[]{:S(2)}, u32[]{:S(2)}) collective-permute-start(bf16[1,2,2,2,16,1024]{5,4,3,2,1,0:T(8,128)(2,1)S(1)} %constant_dynamic-slice_fusion), channel_id=1, source_target_pairs={{0,1},{1,0},{2,3},{3,2},{4,5},{5,4},{6,7},{7,6},{8,9},{9,8},{10,11... | collective-permute-start | bytes 786440 | tf_op jit(solution)/shard_map/cond/branch_1_fun/ppermute | solution.py:474
  85.5 5.3 %collective-permute-start.22 = (bf16[1,2,2,16,1024]{4,3,2,1,0:T(8,128)(2,1)S(1)}, bf16[1,2,2,16,1024]{4,3,2,1,0:T(8,128)(2,1)S(1)}, u32[]{:S(2)}, u32[]{:S(2)}) collective-permute-start(bf16[1,2,2,16,1024]{4,3,2,1,0:T(8,128)(2,1)S(1)} %constant_dynamic-slice_fusion.5), channel_id=1, source_target_pairs={{0,2},{2,0},{1,3},{3,1},{4,6},{6,4},{5,7},{7,5},{8,10},{10,8},{9,1... | collective-permute-start | bytes 393224 | tf_op jit(solution)/shard_map/ppermute | solution.py:474
  89.0 1.6 %collective-permute-start.1 = (bf16[1,2,2,2,16,1024]{5,4,3,2,1,0:T(8,128)(2,1)S(1)}, bf16[1,2,2,2,16,1024]{5,4,3,2,1,0:T(8,128)(2,1)S(1)}, u32[]{:S(2)}, u32[]{:S(2)}) collective-permute-start(bf16[1,2,2,2,16,1024]{5,4,3,2,1,0:T(8,128)(2,1)S(1)} %constant_dynamic-slice_fusion.1), channel_id=1, source_target_pairs={{0,1},{1,0},{2,3},{3,2},{4,5},{5,4},{6,7},{7,6},{8,9},{9,8},{10,11... | collective-permute-start | bytes 786440 | tf_op jit(solution)/shard_map/cond/branch_1_fun/ppermute | solution.py:474
  90.9 5.5 %collective-permute-start.23 = (bf16[1,2,2,16,1024]{4,3,2,1,0:T(8,128)(2,1)S(1)}, bf16[1,2,2,16,1024]{4,3,2,1,0:T(8,128)(2,1)S(1)}, u32[]{:S(2)}, u32[]{:S(2)}) collective-permute-start(bf16[1,2,2,16,1024]{4,3,2,1,0:T(8,128)(2,1)S(1)} %constant_dynamic-slice_fusion.4), channel_id=1, source_target_pairs={{0,2},{2,0},{1,3},{3,1},{4,6},{6,4},{5,7},{7,5},{8,10},{10,8},{9,1... | collective-permute-start | bytes 393224 | tf_op jit(solution)/shard_map/ppermute | solution.py:474
  96.5 7.1 %collective-permute-start.25 = (bf16[32,1024]{1,0:T(8,128)(2,1)S(1)}, bf16[32,1024]{1,0:T(8,128)(2,1)S(1)}, u32[]{:S(2)}, u32[]{:S(2)}) collective-permute-start(bf16[32,1024]{1,0:T(8,128)(2,1)S(1)} %bitcast.38), channel_id=1, source_target_pairs={{0,8},{4,12},{8,0},{12,4},{1,9},{5,13},{9,1},{13,5},{2,10},{6,14},... | collective-permute-start | bytes 196616 | tf_op jit(solution)/shard_map/ppermute | solution.py:509
  99.1 6.2 %collective-permute-start.26 = (bf16[32,1024]{1,0:T(8,128)(2,1)S(1)}, bf16[32,1024]{1,0:T(8,128)(2,1)S(1)}, u32[]{:S(2)}, u32[]{:S(2)}) collective-permute-start(bf16[32,1024]{1,0:T(8,128)(2,1)S(1)} %bitcast.37), channel_id=1, source_target_pairs={{0,12},{4,8},{8,4},{12,0},{1,13},{5,9},{9,5},{13,1},{2,14},{6,10},... | collective-permute-start | bytes 196616 | tf_op jit(solution)/shard_map/ppermute | solution.py:509
  99.9 5.3 %collective-permute-start.24 = (bf16[32,1024]{1,0:T(8,128)(2,1)S(1)}, bf16[32,1024]{1,0:T(8,128)(2,1)S(1)}, u32[]{:S(2)}, u32[]{:S(2)}) collective-permute-start(bf16[32,1024]{1,0:T(8,128)(2,1)S(1)} %bitcast.39), channel_id=1, source_target_pairs={{0,4},{4,0},{8,12},{12,8},{1,5},{5,1},{9,13},{13,9},{2,6},{6,2},{1... | collective-permute-start | bytes 196616 | tf_op jit(solution)/shard_map/ppermute | solution.py:509

commit v8 on v7

--- a/solution.py
+++ b/solution.py
@@ -618,8 +618,8 @@
 
     first, second = (across(chunk, "sub") for chunk in chunks)
     ahead = range(1, pairs)
-    cut = tokens * 3 // 4
-    near_second = swap_seq(second, 1)
+    cut = tokens * 5 // 8
+    near_second = swap_seq(second[:cut], 1)
     far_early = [swap_seq(second[:cut], 2 * k) for k in ahead]
     bits = bits_of("chan")
     halves = [first[: tokens // 2], first[tokens // 2 :]]
@@ -644,7 +644,7 @@
     if bits:
         sign = jnp.full((1,), 1 - 2 * (lax.axis_index("chan") // 2 ** bits[-1] % 2), jnp.int32)
         moving = [
-            call(add_kernel, shape(*mixed.shape, bf16), "add", (sign, mixed, other), 1)
+            call(add_kernel, shape(*mixed.shape, bf16), "add", (sign, mixed, other), 1, cost=SMALL)
             for mixed, other in zip(moving, received)
         ]
     early, late, *far_early = moving
@@ -652,8 +652,11 @@
     all_first = [first, near_first]
     for far, passed in zip(far_first, passed_first):
         all_first += [far, passed]
-    all_first, far_early = lax.optimization_barrier((all_first, far_early))
-    passed_early = [swap_seq(value, 1) for value in far_early]
+    sending = [*far_early[:-1], jnp.concatenate([*far_early[-1:], late])]
+    all_first, sending = lax.optimization_barrier((all_first, sending))
+    passed_early = [swap_seq(value, 1) for value in sending]
+    near_late = passed_early[-1][-late.shape[0] :]
+    passed_early = [value[:cut] for value in passed_early][: len(far_early)]
     far_late = [swap_seq(late, 2 * k) for k in ahead]
     cross_late = [swap_seq(late, 2 * k + 1) for k in ahead]
     near_second = across(near_second, "chan")
@@ -690,10 +693,12 @@
         )
 
     done_first = stage(all_first)
-    done_first, near_second, far_late, cross_late, passed_early = lax.optimization_barrier(
-        (done_first, near_second, far_late, cross_late, passed_early)
-    )
-    all_second = [jnp.concatenate([early, late], axis=0), near_second]
+    done_first, near_second, near_late, far_late, cross_late, passed_early = (
+        lax.optimization_barrier(
+            (done_first, near_second, near_late, far_late, cross_late, passed_early)
+        )
+    )
+    all_second = [jnp.concatenate(parts) for parts in ([early, late], [near_second, near_late])]
     for parts in zip(far_early, far_late, passed_early, cross_late):
         all_second += [jnp.concatenate(parts[:2], axis=0), jnp.concatenate(parts[2:], axis=0)]
     done_first, done_second = lax.optimization_barrier(

time: 106 us -> 106 us (level)
  starting transfers between devices: 39.5 us -> 38.2 us
    ppermute x13, starting transfers between devices: 23.6 us -> 22.2 us  [swap_seq(): return lax.ppermute(value, 'seq', [(k, k ^ distance) for k in range(count)])]
  transfers between devices with their start and end apart: 27 -> 27, of which waited for: 15 -> 13; matrix products, arithmetic and copies ran while one was open for 4% -> 4% of each run, Pallas kernels for 7% -> 7%
where the time goes in v8:
time: 106 us
  waiting for transfers between devices  49.6 us (47%)
  starting transfers between devices  38.2 us (36%)
  Pallas kernels  10.2 us (10%)
  local copies, waits for them, and re-layouts  5.12 us (5%)
  other arithmetic  2.15 us (2%)
    ppermute x13, waiting for transfers between devices, swap_seq(): return lax.ppermute(value, 'seq', [(k, k ^ distance) for k in range(count)])  27.7 us
    ppermute x13, starting transfers between devices, swap_seq(): return lax.ppermute(value, 'seq', [(k, k ^ distance) for k in range(count)])  22.2 us
    ppermute x12, waiting for transfers between devices, swap(): return lax.ppermute(value, axis, [(k, k ^ 1 << bit) for k in range(count)])  22 us
    ppermute x12, starting transfers between devices, swap(): return lax.ppermute(value, axis, [(k, k ^ 1 << bit) for k in range(count)])  10.2 us
    pallas_call x8, Pallas kernels, call(): pl.pallas_call(kernel, out_shape=out_shape, in_specs=specs, scratch_shape...  9.08 us
    ppermute x1, starting transfers between devices, paired_body(): lax.ppermute(straight, 'seq', [(k, k + 2 * ahead) for k in firsts])  4.5 us
    dynamic_slice x2, local copies, waits for them, and re-layouts, half_of(): return lax.dynamic_slice_in_dim(value, which * half, half, 1)  2.84 us
  transfers between devices with their start and end apart: 27, of which 13 were waited for; matrix products, arithmetic and copies ran while one was open for 4% of the time, Pallas kernels for 7%

profile of v8, /device:TPU:0, one launch (start us, length us, event | category | flops | bytes accessed | tf_op | source)
XLA Modules:
  0.0 105.8 jit_solution(2763672926460486232)
XLA Ops:
  0.0 1.3 %constant_dynamic-slice_fusion.8 = (bf16[128,1,256]{2,1,0:T(2,128)(2,1)S(1)}, bf16[128,1,256]{2,1,0:T(2,128)(2,1)S(1)}) fusion(bf16[128,2,256]{2,1,0:T(2,128)(2,1)} %param.18, s32[]{:T(128)S(6)} %select_n.150, bf16[128,2,256]{2,1,0:T(2,128)(2,1)} %param.17), kind=kLoop, calls=%fused_computation.54 | loop fusion | bytes 262148 | tf_op jit(solution)/shard_map/jit(dynamic_index_in_dim)/dynamic_slice | solution.py:536
  1.3 0.7 pad_maximum_fusion.6.steps_ref
  2.1 1.1 %constant_dynamic-slice_fusion.10 = (bf16[128,1024]{1,0:T(8,128)(2,1)S(1)}, bf16[128,1024]{1,0:T(8,128)(2,1)S(1)}) fusion(bf16[128,2048]{1,0:T(8,128)(2,1)} %param.16, s32[]{:T(128)S(6)} %select_n.148, s32[]{:T(128)S(6)} %select_n.147), kind=kLoop, calls=%fused_computation.56 | loop fusion | bytes 1048584 | tf_op jit(solution)/shard_map/dynamic_slice | solution.py:546
  3.1 0.8 pack.1
  4.0 3.1 %collective-permute-start.5 = (bf16[128,1664]{1,0:T(8,128)(2,1)S(1)}, bf16[128,1664]{1,0:T(8,128)(2,1)S(1)}, u32[]{:S(2)}, u32[]{:S(2)}) collective-permute-start(bf16[128,1664]{1,0:T(8,128)(2,1)S(1)} %get-tuple-element.101), channel_id=1, source_target_pairs={{0,4},{4,0},{8,12},{12,8},{1,5},{5,1},{9,13},{13,9},{2,6},{6,2},{1... | collective-permute-start | bytes 1277960 | tf_op jit(solution)/shard_map/ppermute | solution.py:509
  7.1 4.5 %collective-permute-start.2 = (bf16[1296,128]{1,0:T(8,128)(2,1)S(1)}, bf16[1296,128]{1,0:T(8,128)(2,1)S(1)}, u32[]{:S(2)}, u32[]{:S(2)}) collective-permute-start(bf16[1296,128]{1,0:T(8,128)(2,1)S(1)} %get-tuple-element.98), channel_id=1, source_target_pairs={{0,8},{4,12},{1,9},{5,13},{2,10},{6,14},{3,11},{7,15},{16,24},{20,... | collective-permute-start | bytes 995336 | tf_op jit(solution)/shard_map/ppermute | solution.py:563
  11.6 1.3 %collective-permute-start.3 = (bf16[1296,128]{1,0:T(8,128)(2,1)S(1)}, bf16[1296,128]{1,0:T(8,128)(2,1)S(1)}, u32[]{:S(2)}, u32[]{:S(2)}) collective-permute-start(bf16[1296,128]{1,0:T(8,128)(2,1)S(1)} %get-tuple-element.99), channel_id=1, source_target_pairs={{0,12},{4,8},{1,13},{5,9},{2,14},{6,10},{3,15},{7,11},{16,28},{20,... | collective-permute-start | bytes 995336 | tf_op jit(solution)/shard_map/ppermute | solution.py:564
  12.9 1.8 %constant_dynamic-slice_fusion.6 = (bf16[128,1024]{1,0:T(8,128)(2,1)}, bf16[128,1024]{1,0:T(8,128)(2,1)S(1)}) fusion(bf16[128,2048]{1,0:T(8,128)(2,1)} %param.22, s32[]{:T(128)S(6)} %select_n.148, s32[]{:T(128)S(6)} %select_n.147), kind=kLoop, calls=%fused_computation.52 | loop fusion | bytes 1048584 | tf_op jit(solution)/shard_map/dynamic_slice | solution.py:546
  14.7 0.5 collective-permute-start.4
  15.2 0.7 broadcast_in_dim.67
  16.0 0.7 select_multiply_fusion
  16.7 0.5 collective-permute-done.5.msg_ref
  17.3 1.9 %pair.1 = (f32[256,1024]{1,0:T(8,128)S(1)}, f32[256,1024]{1,0:T(8,128)S(1)}, bf16[256,256]{1,0:T(8,128)(2,1)S(1)}) custom-call(s32[1]{0:T(128)} %bitcast.3.where_ref.refs_2_, bf16[128,1024]{1,0:T(8,128)(2,1)S(1)} %get-tuple-element.146.x_mine_ref.x_ref, bf16[128,640]{1,0:T(8,128)(2,1)S(1)} %get-tuple-element.100.meta_ref, ...), custom_call_target="tpu_custom_call" | custom-call | flops 1 | bytes 1 | tf_op jit(solution)/shard_map/pair/pallas_call | solution.py:496
  19.2 17.0 %collective-permute-done.4.refs_4_ = bf16[128,1024]{1,0:T(8,128)(2,1)S(1)} collective-permute-done((bf16[128,1024]{1,0:T(8,128)(2,1)}, bf16[128,1024]{1,0:T(8,128)(2,1)S(1)}, u32[]{:S(2)}, u32[]{:S(2)}) %collective-permute-start.4) | collective-permute-done | bytes 262176 | tf_op jit(solution)/shard_map/ppermute | solution.py:509
  36.2 1.1 %mix.1 = (bf16[128,1024]{1,0:T(8,128)(2,1)S(1)}, bf16[128,1024]{1,0:T(8,128)(2,1)S(1)}) custom-call(bf16[1296,128]{1,0:T(8,128)(2,1)S(1)} %collective-permute-done.2.refs_0_, bf16[1296,128]{1,0:T(8,128)(2,1)S(1)} %collective-permute-done.3.refs_1_, s32[1]{0:T(128)} %bitcast.3.where_ref.refs_2_, bf16[128,1024]{1,0:T(8,128)(2,1)S(1)} %get-tuple-element.144.refs_3_, ...), custom_call_target="tpu_custom_call" | custom-call | flops 1 | bytes 30000000 | tf_op jit(solution)/shard_map/mix/pallas_call | solution.py:597
  37.4 0.5 collective-permute-start.6
  37.9 1.0 collective-permute-done.9
  39.0 4.1 %collective-permute-start.10 = (bf16[80,1024]{1,0:T(8,128)(2,1)S(1)}, bf16[80,1024]{1,0:T(8,128)(2,1)S(1)}, u32[]{:S(2)}, u32[]{:S(2)}) collective-permute-start(bf16[80,1024]{1,0:T(8,128)(2,1)S(1)} %slice.41), channel_id=1, source_target_pairs={{0,4},{4,0},{8,12},{12,8},{1,5},{5,1},{9,13},{13,9},{2,6},{6,2},{1... | collective-permute-start | bytes 491528 | tf_op jit(solution)/shard_map/ppermute | solution.py:509
  43.1 2.0 %collective-permute-start.11 = (bf16[80,1024]{1,0:T(8,128)(2,1)S(1)}, bf16[80,1024]{1,0:T(8,128)(2,1)S(1)}, u32[]{:S(2)}, u32[]{:S(2)}) collective-permute-start(bf16[80,1024]{1,0:T(8,128)(2,1)S(1)} %slice.41), channel_id=1, source_target_pairs={{0,8},{4,12},{8,0},{12,4},{1,9},{5,13},{9,1},{13,5},{2,10},{6,14},... | collective-permute-start | bytes 491528 | tf_op jit(solution)/shard_map/ppermute | solution.py:509
  45.2 1.6 %collective-permute-start.7 = (bf16[64,1024]{1,0:T(8,128)(2,1)S(1)}, bf16[64,1024]{1,0:T(8,128)(2,1)S(1)}, u32[]{:S(2)}, u32[]{:S(2)}) collective-permute-start(bf16[64,1024]{1,0:T(8,128)(2,1)S(1)} %get-tuple-element.107), channel_id=1, source_target_pairs={{0,2},{2,0},{1,3},{3,1},{4,6},{6,4},{5,7},{7,5},{8,10},{10,8},{9,1... | collective-permute-start | bytes 393224 | tf_op jit(solution)/shard_map/ppermute | solution.py:474
  46.8 0.5 collective-permute-start.8
  47.3 4.4 %collective-permute-done.7 = bf16[64,1024]{1,0:T(8,128)(2,1)S(1)} collective-permute-done((bf16[64,1024]{1,0:T(8,128)(2,1)S(1)}, bf16[64,1024]{1,0:T(8,128)(2,1)S(1)}, u32[]{:S(2)}, u32[]{:S(2)}) %collective-permute-start.7) | collective-permute-done | bytes 131104 | tf_op jit(solution)/shard_map/ppermute | solution.py:474
  51.6 1.7 %collective-permute-done.8 = bf16[64,1024]{1,0:T(8,128)(2,1)S(1)} collective-permute-done((bf16[64,1024]{1,0:T(8,128)(2,1)S(1)}, bf16[64,1024]{1,0:T(8,128)(2,1)S(1)}, u32[]{:S(2)}, u32[]{:S(2)}) %collective-permute-start.8) | collective-permute-done | bytes 131104 | tf_op jit(solution)/shard_map/ppermute | solution.py:474
  53.5 0.7 collective-permute-start.15
  54.2 3.4 %collective-permute-start.16 = (bf16[128,1024]{1,0:T(8,128)(2,1)S(1)}, bf16[128,1024]{1,0:T(8,128)(2,1)S(1)}, u32[]{:S(2)}, u32[]{:S(2)}) collective-permute-start(bf16[128,1024]{1,0:T(8,128)(2,1)S(1)} %pad_maximum_fusion.3), channel_id=1, source_target_pairs={{0,4},{4,0},{8,12},{12,8},{1,5},{5,1},{9,13},{13,9},{2,6},{6,2},{1... | collective-permute-start | bytes 786440 | tf_op jit(solution)/shard_map/ppermute | solution.py:509
  57.6 1.6 %collective-permute-start.12 = (bf16[80,1024]{1,0:T(8,128)(2,1)S(1)}, bf16[80,1024]{1,0:T(8,128)(2,1)S(1)}, u32[]{:S(2)}, u32[]{:S(2)}) collective-permute-start(bf16[80,1024]{1,0:T(8,128)(2,1)S(1)} %slice.33.mixed_ref), channel_id=1, source_target_pairs={{0,2},{2,0},{1,3},{3,1},{4,6},{6,4},{5,7},{7,5},{8,10},{10,8},{9,1... | collective-permute-start | bytes 491528 | tf_op jit(solution)/shard_map/ppermute | solution.py:474
  59.2 0.5 collective-permute-start.14
  59.7 1.6 %collective-permute-start.13 = (bf16[48,1024]{1,0:T(8,128)(2,1)S(1)}, bf16[48,1024]{1,0:T(8,128)(2,1)S(1)}, u32[]{:S(2)}, u32[]{:S(2)}) collective-permute-start(bf16[48,1024]{1,0:T(8,128)(2,1)S(1)} %slice.34.mixed_ref), channel_id=1, source_target_pairs={{0,2},{2,0},{1,3},{3,1},{4,6},{6,4},{5,7},{7,5},{8,10},{10,8},{9,1... | collective-permute-start | bytes 294920 | tf_op jit(solution)/shard_map/ppermute | solution.py:474
  61.3 6.9 %collective-permute-done.13.received_ref = bf16[48,1024]{1,0:T(8,128)(2,1)S(1)} collective-permute-done((bf16[48,1024]{1,0:T(8,128)(2,1)S(1)}, bf16[48,1024]{1,0:T(8,128)(2,1)S(1)}, u32[]{:S(2)}, u32[]{:S(2)}) %collective-permute-start.13) | collective-permute-done | bytes 98336 | tf_op jit(solution)/shard_map/ppermute | solution.py:474
  68.5 1.6 %collective-permute-start.18 = (bf16[80,1024]{1,0:T(8,128)(2,1)S(1)}, bf16[80,1024]{1,0:T(8,128)(2,1)S(1)}, u32[]{:S(2)}, u32[]{:S(2)}) collective-permute-start(bf16[80,1024]{1,0:T(8,128)(2,1)S(1)} %collective-permute-done.10), channel_id=1, source_target_pairs={{0,2},{2,0},{1,3},{3,1},{4,6},{6,4},{5,7},{7,5},{8,10},{10,8},{9,1... | collective-permute-start | bytes 491528 | tf_op jit(solution)/shard_map/ppermute | solution.py:474
  70.3 4.9 %collective-permute-done.17 = bf16[128,1024]{1,0:T(8,128)(2,1)S(1)} collective-permute-done((bf16[128,1024]{1,0:T(8,128)(2,1)S(1)}, bf16[128,1024]{1,0:T(8,128)(2,1)S(1)}, u32[]{:S(2)}, u32[]{:S(2)}) %collective-permute-start.17) | collective-permute-done | bytes 262176 | tf_op jit(solution)/shard_map/ppermute | solution.py:509
  75.3 2.5 %collective-permute-start.20 = (bf16[48,1024]{1,0:T(8,128)(2,1)S(1)}, bf16[48,1024]{1,0:T(8,128)(2,1)S(1)}, u32[]{:S(2)}, u32[]{:S(2)}) collective-permute-start(bf16[48,1024]{1,0:T(8,128)(2,1)S(1)} %add.245), channel_id=1, source_target_pairs={{0,8},{4,12},{8,0},{12,4},{1,9},{5,13},{9,1},{13,5},{2,10},{6,14},... | collective-permute-start | bytes 294920 | tf_op jit(solution)/shard_map/ppermute | solution.py:509
  77.8 1.9 %collective-permute-start.21 = (bf16[48,1024]{1,0:T(8,128)(2,1)S(1)}, bf16[48,1024]{1,0:T(8,128)(2,1)S(1)}, u32[]{:S(2)}, u32[]{:S(2)}) collective-permute-start(bf16[48,1024]{1,0:T(8,128)(2,1)S(1)} %add.245), channel_id=1, source_target_pairs={{0,12},{4,8},{8,4},{12,0},{1,13},{5,9},{9,5},{13,1},{2,14},{6,10},... | collective-permute-start | bytes 294920 | tf_op jit(solution)/shard_map/ppermute | solution.py:509
  79.8 4.5 %conditional.2 = (bf16[2,2,2,16,1024]{4,3,2,1,0:T(8,128)(2,1)S(1)}) conditional(s32[]{:T(128)} %convert_element_type.102, () %tuple.22, (s32[1]{0:T(128)}, bf16[2048,1024]{1,0:T(8,128)(2,1)}, bf16[128,1024]{1,0:T(8,128)(2,1)S(1)}, bf16[128,1024]{1,0:T(8,128)(2,1)S(1)}, bf16[128,1024]{1,0:T(8,128)(2,1)S(1)}, ...), branch_computations={%region_0.1_spmd, %region_1.2_spmd} | conditional | flops 524309 | bytes 32359552 | solution.py:688
  79.8 2.7 %project.2 = bf16[2,2,2,2,16,1024]{5,4,3,2,1,0:T(8,128)(2,1)S(1)} custom-call(s32[1]{0:T(128)} %get-tuple-element.42.where_ref, bf16[2048,1024]{1,0:T(8,128)(2,1)} %get-tuple-element.44.weight_ref, bf16[128,1024]{1,0:T(8,128)(2,1)S(1)} %get-tuple-element.45.refs_0_, bf16[128,1024]{1,0:T(8,128)(2,1)S(1)} %get-tuple-element.46.refs_1_, ...), custom_call_target="tpu_custom_call" | custom-call | flops 1 | bytes 30000000 | tf_op jit(solution)/shard_map/cond/branch_1_fun/project/pallas_call | solution.py:496
  82.6 1.5 %collective-permute-done = bf16[1,2,2,2,16,1024]{5,4,3,2,1,0:T(8,128)(2,1)S(1)} collective-permute-done((bf16[1,2,2,2,16,1024]{5,4,3,2,1,0:T(8,128)(2,1)S(1)}, bf16[1,2,2,2,16,1024]{5,4,3,2,1,0:T(8,128)(2,1)S(1)}, u32[]{:S(2)}, u32[]{:S(2)}) %collective-permute-start) | collective-permute-done | bytes 262176 | tf_op jit(solution)/shard_map/cond/branch_1_fun/ppermute | solution.py:474
  84.3 1.4 %collective-permute-done.21 = bf16[48,1024]{1,0:T(8,128)(2,1)S(1)} collective-permute-done((bf16[48,1024]{1,0:T(8,128)(2,1)S(1)}, bf16[48,1024]{1,0:T(8,128)(2,1)S(1)}, u32[]{:S(2)}, u32[]{:S(2)}) %collective-permute-start.21) | collective-permute-done | bytes 98336 | tf_op jit(solution)/shard_map/ppermute | solution.py:509
  85.8 1.6 %collective-permute-start.22 = (bf16[1,2,2,16,1024]{4,3,2,1,0:T(8,128)(2,1)S(1)}, bf16[1,2,2,16,1024]{4,3,2,1,0:T(8,128)(2,1)S(1)}, u32[]{:S(2)}, u32[]{:S(2)}) collective-permute-start(bf16[1,2,2,16,1024]{4,3,2,1,0:T(8,128)(2,1)S(1)} %constant_dynamic-slice_fusion.5), channel_id=1, source_target_pairs={{0,2},{2,0},{1,3},{3,1},{4,6},{6,4},{5,7},{7,5},{8,10},{10,8},{9,1... | collective-permute-start | bytes 393224 | tf_op jit(solution)/shard_map/ppermute | solution.py:474
  87.4 4.5 %conditional.3 = (bf16[2,2,2,16,1024]{4,3,2,1,0:T(8,128)(2,1)S(1)}) conditional(s32[]{:T(128)} %convert_element_type.102, () %tuple.28, (s32[1]{0:T(128)}, bf16[2048,1024]{1,0:T(8,128)(2,1)}, bf16[128,1024]{1,0:T(8,128)(2,1)S(1)}, bf16[128,1024]{1,0:T(8,128)(2,1)S(1)}, bf16[128,1024]{1,0:T(8,128)(2,1)S(1)}, ...), branch_computations={%region_2.3_spmd, %region_3.4_spmd} | conditional | flops 524309 | bytes 32359552 | solution.py:688
  87.4 2.7 %project.3 = bf16[2,2,2,2,16,1024]{5,4,3,2,1,0:T(8,128)(2,1)S(1)} custom-call(s32[1]{0:T(128)} %get-tuple-element.51.where_ref, bf16[2048,1024]{1,0:T(8,128)(2,1)} %get-tuple-element.52.weight_ref, bf16[128,1024]{1,0:T(8,128)(2,1)S(1)} %get-tuple-element.53.refs_0_, bf16[128,1024]{1,0:T(8,128)(2,1)S(1)} %get-tuple-element.54.refs_1_, ...), custom_call_target="tpu_custom_call" | custom-call | flops 1 | bytes 30000000 | tf_op jit(solution)/shard_map/cond/branch_1_fun/project/pallas_call | solution.py:496
  90.2 1.5 %collective-permute-done.1 = bf16[1,2,2,2,16,1024]{5,4,3,2,1,0:T(8,128)(2,1)S(1)} collective-permute-done((bf16[1,2,2,2,16,1024]{5,4,3,2,1,0:T(8,128)(2,1)S(1)}, bf16[1,2,2,2,16,1024]{5,4,3,2,1,0:T(8,128)(2,1)S(1)}, u32[]{:S(2)}, u32[]{:S(2)}) %collective-permute-start.1) | collective-permute-done | bytes 262176 | tf_op jit(solution)/shard_map/cond/branch_1_fun/ppermute | solution.py:474
  91.9 0.6 collective-permute-start.23
  92.5 5.0 %collective-permute-done.23 = bf16[1,2,2,16,1024]{4,3,2,1,0:T(8,128)(2,1)S(1)} collective-permute-done((bf16[1,2,2,16,1024]{4,3,2,1,0:T(8,128)(2,1)S(1)}, bf16[1,2,2,16,1024]{4,3,2,1,0:T(8,128)(2,1)S(1)}, u32[]{:S(2)}, u32[]{:S(2)}) %collective-permute-start.23) | collective-permute-done | bytes 131104 | tf_op jit(solution)/shard_map/ppermute | solution.py:474
  97.6 0.5 collective-permute-start.25
  98.2 1.4 %collective-permute-start.26 = (bf16[32,1024]{1,0:T(8,128)(2,1)S(1)}, bf16[32,1024]{1,0:T(8,128)(2,1)S(1)}, u32[]{:S(2)}, u32[]{:S(2)}) collective-permute-start(bf16[32,1024]{1,0:T(8,128)(2,1)S(1)} %bitcast.37), channel_id=1, source_target_pairs={{0,12},{4,8},{8,4},{12,0},{1,13},{5,9},{9,5},{13,1},{2,14},{6,10},... | collective-permute-start | bytes 196616 | tf_op jit(solution)/shard_map/ppermute | solution.py:509
  99.6 1.7 %collective-permute-start.24 = (bf16[32,1024]{1,0:T(8,128)(2,1)S(1)}, bf16[32,1024]{1,0:T(8,128)(2,1)S(1)}, u32[]{:S(2)}, u32[]{:S(2)}) collective-permute-start(bf16[32,1024]{1,0:T(8,128)(2,1)S(1)} %bitcast.39), channel_id=1, source_target_pairs={{0,4},{4,0},{8,12},{12,8},{1,5},{5,1},{9,13},{13,9},{2,6},{6,2},{1... | collective-permute-start | bytes 196616 | tf_op jit(solution)/shard_map/ppermute | solution.py:509
  101.2 3.5 %collective-permute-done.25.refs_2_ = bf16[32,1024]{1,0:T(8,128)(2,1)S(1)} collective-permute-done((bf16[32,1024]{1,0:T(8,128)(2,1)S(1)}, bf16[32,1024]{1,0:T(8,128)(2,1)S(1)}, u32[]{:S(2)}, u32[]{:S(2)}) %collective-permute-start.25) | collective-permute-done | bytes 65568 | tf_op jit(solution)/shard_map/ppermute | solution.py:509
  105.0 0.7 place.1
  (59 shorter events, 2.1 us)
Async XLA Ops:
  0.0 36.2 %copy-start = (bf16[256,256]{1,0:T(8,128)(2,1)S(1)}, bf16[256,256]{1,0:T(8,128)(2,1)}, u32[]{:S(2)}) copy-start(bf16[256,256]{1,0:T(8,128)(2,1)} %constant.236.clone.refs_9_) | copy-start | bytes 393220
  4.0 13.3 %collective-permute-start.5 = (bf16[128,1664]{1,0:T(8,128)(2,1)S(1)}, bf16[128,1664]{1,0:T(8,128)(2,1)S(1)}, u32[]{:S(2)}, u32[]{:S(2)}) collective-permute-start(bf16[128,1664]{1,0:T(8,128)(2,1)S(1)} %get-tuple-element.101), channel_id=1, source_target_pairs={{0,4},{4,0},{8,12},{12,8},{1,5},{5,1},{9,13},{13,9},{2,6},{6,2},{1... | collective-permute-start | bytes 1277960 | tf_op jit(solution)/shard_map/ppermute | solution.py:509
  7.1 29.1 %collective-permute-start.2 = (bf16[1296,128]{1,0:T(8,128)(2,1)S(1)}, bf16[1296,128]{1,0:T(8,128)(2,1)S(1)}, u32[]{:S(2)}, u32[]{:S(2)}) collective-permute-start(bf16[1296,128]{1,0:T(8,128)(2,1)S(1)} %get-tuple-element.98), channel_id=1, source_target_pairs={{0,8},{4,12},{1,9},{5,13},{2,10},{6,14},{3,11},{7,15},{16,24},{20,... | collective-permute-start | bytes 995336 | tf_op jit(solution)/shard_map/ppermute | solution.py:563
  11.6 24.6 %collective-permute-start.3 = (bf16[1296,128]{1,0:T(8,128)(2,1)S(1)}, bf16[1296,128]{1,0:T(8,128)(2,1)S(1)}, u32[]{:S(2)}, u32[]{:S(2)}) collective-permute-start(bf16[1296,128]{1,0:T(8,128)(2,1)S(1)} %get-tuple-element.99), channel_id=1, source_target_pairs={{0,12},{4,8},{1,13},{5,9},{2,14},{6,10},{3,15},{7,11},{16,28},{20,... | collective-permute-start | bytes 995336 | tf_op jit(solution)/shard_map/ppermute | solution.py:564
  14.7 21.5 %collective-permute-start.4 = (bf16[128,1024]{1,0:T(8,128)(2,1)}, bf16[128,1024]{1,0:T(8,128)(2,1)S(1)}, u32[]{:S(2)}, u32[]{:S(2)}) collective-permute-start(bf16[128,1024]{1,0:T(8,128)(2,1)} %get-tuple-element.143), channel_id=1, source_target_pairs={{0,4},{4,0},{8,12},{12,8},{1,5},{5,1},{9,13},{13,9},{2,6},{6,2},{1... | collective-permute-start | bytes 786440 | tf_op jit(solution)/shard_map/ppermute | solution.py:509
  17.3 51.2 %copy-start.1 = (s32[2048]{0:T(1024)S(1)}, s32[2048]{0:T(1024)}, u32[]{:S(2)}) copy-start(s32[2048]{0:T(1024)} %param.25) | copy-start | bytes 24580
  37.3 1.6 %collective-permute-start.9 = (bf16[128,1024]{1,0:T(8,128)(2,1)S(1)}, bf16[128,1024]{1,0:T(8,128)(2,1)S(1)}, u32[]{:S(2)}, u32[]{:S(2)}) collective-permute-start(bf16[128,1024]{1,0:T(8,128)(2,1)S(1)} %get-tuple-element.106), channel_id=1, source_target_pairs={{0,1},{1,0},{2,3},{3,2},{4,5},{5,4},{6,7},{7,6},{8,9},{9,8},{10,11... | collective-permute-start | bytes 786440 | tf_op jit(solution)/shard_map/ppermute | solution.py:474
  37.4 7.7 %collective-permute-start.6 = (bf16[128,1024]{1,0:T(8,128)(2,1)S(1)}, bf16[128,1024]{1,0:T(8,128)(2,1)S(1)}, u32[]{:S(2)}, u32[]{:S(2)}) collective-permute-start(bf16[128,1024]{1,0:T(8,128)(2,1)S(1)} %get-tuple-element.105), channel_id=1, source_target_pairs={{0,1},{1,0},{2,3},{3,2},{4,5},{5,4},{6,7},{7,6},{8,9},{9,8},{10,11... | collective-permute-start | bytes 786440 | tf_op jit(solution)/shard_map/ppermute | solution.py:474
  39.0 14.3 %collective-permute-start.10 = (bf16[80,1024]{1,0:T(8,128)(2,1)S(1)}, bf16[80,1024]{1,0:T(8,128)(2,1)S(1)}, u32[]{:S(2)}, u32[]{:S(2)}) collective-permute-start(bf16[80,1024]{1,0:T(8,128)(2,1)S(1)} %slice.41), channel_id=1, source_target_pairs={{0,4},{4,0},{8,12},{12,8},{1,5},{5,1},{9,13},{13,9},{2,6},{6,2},{1... | collective-permute-start | bytes 491528 | tf_op jit(solution)/shard_map/ppermute | solution.py:509
  43.1 10.3 %collective-permute-start.11 = (bf16[80,1024]{1,0:T(8,128)(2,1)S(1)}, bf16[80,1024]{1,0:T(8,128)(2,1)S(1)}, u32[]{:S(2)}, u32[]{:S(2)}) collective-permute-start(bf16[80,1024]{1,0:T(8,128)(2,1)S(1)} %slice.41), channel_id=1, source_target_pairs={{0,8},{4,12},{8,0},{12,4},{1,9},{5,13},{9,1},{13,5},{2,10},{6,14},... | collective-permute-start | bytes 491528 | tf_op jit(solution)/shard_map/ppermute | solution.py:509
  45.2 6.4 %collective-permute-start.7 = (bf16[64,1024]{1,0:T(8,128)(2,1)S(1)}, bf16[64,1024]{1,0:T(8,128)(2,1)S(1)}, u32[]{:S(2)}, u32[]{:S(2)}) collective-permute-start(bf16[64,1024]{1,0:T(8,128)(2,1)S(1)} %get-tuple-element.107), channel_id=1, source_target_pairs={{0,2},{2,0},{1,3},{3,1},{4,6},{6,4},{5,7},{7,5},{8,10},{10,8},{9,1... | collective-permute-start | bytes 393224 | tf_op jit(solution)/shard_map/ppermute | solution.py:474
  46.8 6.6 %collective-permute-start.8 = (bf16[64,1024]{1,0:T(8,128)(2,1)S(1)}, bf16[64,1024]{1,0:T(8,128)(2,1)S(1)}, u32[]{:S(2)}, u32[]{:S(2)}) collective-permute-start(bf16[64,1024]{1,0:T(8,128)(2,1)S(1)} %get-tuple-element.109), channel_id=1, source_target_pairs={{0,2},{2,0},{1,3},{3,1},{4,6},{6,4},{5,7},{7,5},{8,10},{10,8},{9,1... | collective-permute-start | bytes 393224 | tf_op jit(solution)/shard_map/ppermute | solution.py:474
  53.5 14.7 %collective-permute-start.15 = (bf16[128,1024]{1,0:T(8,128)(2,1)S(1)}, bf16[128,1024]{1,0:T(8,128)(2,1)S(1)}, u32[]{:S(2)}, u32[]{:S(2)}) collective-permute-start(bf16[128,1024]{1,0:T(8,128)(2,1)S(1)} %pad_maximum_fusion.3), channel_id=1, source_target_pairs={{0,8},{4,12},{8,0},{12,4},{1,9},{5,13},{9,1},{13,5},{2,10},{6,14},... | collective-permute-start | bytes 786440 | tf_op jit(solution)/shard_map/ppermute | solution.py:509
  54.2 14.0 %collective-permute-start.16 = (bf16[128,1024]{1,0:T(8,128)(2,1)S(1)}, bf16[128,1024]{1,0:T(8,128)(2,1)S(1)}, u32[]{:S(2)}, u32[]{:S(2)}) collective-permute-start(bf16[128,1024]{1,0:T(8,128)(2,1)S(1)} %pad_maximum_fusion.3), channel_id=1, source_target_pairs={{0,4},{4,0},{8,12},{12,8},{1,5},{5,1},{9,13},{13,9},{2,6},{6,2},{1... | collective-permute-start | bytes 786440 | tf_op jit(solution)/shard_map/ppermute | solution.py:509
  57.6 10.5 %collective-permute-start.12 = (bf16[80,1024]{1,0:T(8,128)(2,1)S(1)}, bf16[80,1024]{1,0:T(8,128)(2,1)S(1)}, u32[]{:S(2)}, u32[]{:S(2)}) collective-permute-start(bf16[80,1024]{1,0:T(8,128)(2,1)S(1)} %slice.33.mixed_ref), channel_id=1, source_target_pairs={{0,2},{2,0},{1,3},{3,1},{4,6},{6,4},{5,7},{7,5},{8,10},{10,8},{9,1... | collective-permute-start | bytes 491528 | tf_op jit(solution)/shard_map/ppermute | solution.py:474
  59.2 9.0 %collective-permute-start.14 = (bf16[80,1024]{1,0:T(8,128)(2,1)S(1)}, bf16[80,1024]{1,0:T(8,128)(2,1)S(1)}, u32[]{:S(2)}, u32[]{:S(2)}) collective-permute-start(bf16[80,1024]{1,0:T(8,128)(2,1)S(1)} %collective-permute-done.11.mixed_ref), channel_id=1, source_target_pairs={{0,2},{2,0},{1,3},{3,1},{4,6},{6,4},{5,7},{7,5},{8,10},{10,8},{9,1... | collective-permute-start | bytes 491528 | tf_op jit(solution)/shard_map/ppermute | solution.py:474
  59.7 8.4 %collective-permute-start.13 = (bf16[48,1024]{1,0:T(8,128)(2,1)S(1)}, bf16[48,1024]{1,0:T(8,128)(2,1)S(1)}, u32[]{:S(2)}, u32[]{:S(2)}) collective-permute-start(bf16[48,1024]{1,0:T(8,128)(2,1)S(1)} %slice.34.mixed_ref), channel_id=1, source_target_pairs={{0,2},{2,0},{1,3},{3,1},{4,6},{6,4},{5,7},{7,5},{8,10},{10,8},{9,1... | collective-permute-start | bytes 294920 | tf_op jit(solution)/shard_map/ppermute | solution.py:474
  68.1 7.1 %collective-permute-start.17 = (bf16[128,1024]{1,0:T(8,128)(2,1)S(1)}, bf16[128,1024]{1,0:T(8,128)(2,1)S(1)}, u32[]{:S(2)}, u32[]{:S(2)}) collective-permute-start(bf16[128,1024]{1,0:T(8,128)(2,1)S(1)} %collective-permute-done.15), channel_id=1, source_target_pairs={{0,4},{4,0},{8,12},{12,8},{1,5},{5,1},{9,13},{13,9},{2,6},{6,2},{1... | collective-permute-start | bytes 786440 | tf_op jit(solution)/shard_map/ppermute | solution.py:509
  68.5 11.2 %collective-permute-start.18 = (bf16[80,1024]{1,0:T(8,128)(2,1)S(1)}, bf16[80,1024]{1,0:T(8,128)(2,1)S(1)}, u32[]{:S(2)}, u32[]{:S(2)}) collective-permute-start(bf16[80,1024]{1,0:T(8,128)(2,1)S(1)} %collective-permute-done.10), channel_id=1, source_target_pairs={{0,2},{2,0},{1,3},{3,1},{4,6},{6,4},{5,7},{7,5},{8,10},{10,8},{9,1... | collective-permute-start | bytes 491528 | tf_op jit(solution)/shard_map/ppermute | solution.py:474
  75.2 9.0 %collective-permute-start.19 = (bf16[128,1024]{1,0:T(8,128)(2,1)S(1)}, bf16[128,1024]{1,0:T(8,128)(2,1)S(1)}, u32[]{:S(2)}, u32[]{:S(2)}) collective-permute-start(bf16[128,1024]{1,0:T(8,128)(2,1)S(1)} %get-tuple-element.126), channel_id=1, source_target_pairs={{0,4},{4,0},{8,12},{12,8},{1,5},{5,1},{9,13},{13,9},{2,6},{6,2},{1... | collective-permute-start | bytes 786440 | tf_op jit(solution)/shard_map/ppermute | solution.py:509
  75.3 9.0 %collective-permute-start.20 = (bf16[48,1024]{1,0:T(8,128)(2,1)S(1)}, bf16[48,1024]{1,0:T(8,128)(2,1)S(1)}, u32[]{:S(2)}, u32[]{:S(2)}) collective-permute-start(bf16[48,1024]{1,0:T(8,128)(2,1)S(1)} %add.245), channel_id=1, source_target_pairs={{0,8},{4,12},{8,0},{12,4},{1,9},{5,13},{9,1},{13,5},{2,10},{6,14},... | collective-permute-start | bytes 294920 | tf_op jit(solution)/shard_map/ppermute | solution.py:509
  77.8 7.9 %collective-permute-start.21 = (bf16[48,1024]{1,0:T(8,128)(2,1)S(1)}, bf16[48,1024]{1,0:T(8,128)(2,1)S(1)}, u32[]{:S(2)}, u32[]{:S(2)}) collective-permute-start(bf16[48,1024]{1,0:T(8,128)(2,1)S(1)} %add.245), channel_id=1, source_target_pairs={{0,12},{4,8},{8,4},{12,0},{1,13},{5,9},{9,5},{13,1},{2,14},{6,10},... | collective-permute-start | bytes 294920 | tf_op jit(solution)/shard_map/ppermute | solution.py:509
  82.6 1.6 %collective-permute-start = (bf16[1,2,2,2,16,1024]{5,4,3,2,1,0:T(8,128)(2,1)S(1)}, bf16[1,2,2,2,16,1024]{5,4,3,2,1,0:T(8,128)(2,1)S(1)}, u32[]{:S(2)}, u32[]{:S(2)}) collective-permute-start(bf16[1,2,2,2,16,1024]{5,4,3,2,1,0:T(8,128)(2,1)S(1)} %constant_dynamic-slice_fusion), channel_id=1, source_target_pairs={{0,1},{1,0},{2,3},{3,2},{4,5},{5,4},{6,7},{7,6},{8,9},{9,8},{10,11... | collective-permute-start | bytes 786440 | tf_op jit(solution)/shard_map/cond/branch_1_fun/ppermute | solution.py:474
  85.8 6.1 %collective-permute-start.22 = (bf16[1,2,2,16,1024]{4,3,2,1,0:T(8,128)(2,1)S(1)}, bf16[1,2,2,16,1024]{4,3,2,1,0:T(8,128)(2,1)S(1)}, u32[]{:S(2)}, u32[]{:S(2)}) collective-permute-start(bf16[1,2,2,16,1024]{4,3,2,1,0:T(8,128)(2,1)S(1)} %constant_dynamic-slice_fusion.5), channel_id=1, source_target_pairs={{0,2},{2,0},{1,3},{3,1},{4,6},{6,4},{5,7},{7,5},{8,10},{10,8},{9,1... | collective-permute-start | bytes 393224 | tf_op jit(solution)/shard_map/ppermute | solution.py:474
  90.2 1.6 %collective-permute-start.1 = (bf16[1,2,2,2,16,1024]{5,4,3,2,1,0:T(8,128)(2,1)S(1)}, bf16[1,2,2,2,16,1024]{5,4,3,2,1,0:T(8,128)(2,1)S(1)}, u32[]{:S(2)}, u32[]{:S(2)}) collective-permute-start(bf16[1,2,2,2,16,1024]{5,4,3,2,1,0:T(8,128)(2,1)S(1)} %constant_dynamic-slice_fusion.1), channel_id=1, source_target_pairs={{0,1},{1,0},{2,3},{3,2},{4,5},{5,4},{6,7},{7,6},{8,9},{9,8},{10,11... | collective-permute-start | bytes 786440 | tf_op jit(solution)/shard_map/cond/branch_1_fun/ppermute | solution.py:474
  91.9 5.6 %collective-permute-start.23 = (bf16[1,2,2,16,1024]{4,3,2,1,0:T(8,128)(2,1)S(1)}, bf16[1,2,2,16,1024]{4,3,2,1,0:T(8,128)(2,1)S(1)}, u32[]{:S(2)}, u32[]{:S(2)}) collective-permute-start(bf16[1,2,2,16,1024]{4,3,2,1,0:T(8,128)(2,1)S(1)} %constant_dynamic-slice_fusion.4), channel_id=1, source_target_pairs={{0,2},{2,0},{1,3},{3,1},{4,6},{6,4},{5,7},{7,5},{8,10},{10,8},{9,1... | collective-permute-start | bytes 393224 | tf_op jit(solution)/shard_map/ppermute | solution.py:474
  97.6 7.1 %collective-permute-start.25 = (bf16[32,1024]{1,0:T(8,128)(2,1)S(1)}, bf16[32,1024]{1,0:T(8,128)(2,1)S(1)}, u32[]{:S(2)}, u32[]{:S(2)}) collective-permute-start(bf16[32,1024]{1,0:T(8,128)(2,1)S(1)} %bitcast.38), channel_id=1, source_target_pairs={{0,8},{4,12},{8,0},{12,4},{1,9},{5,13},{9,1},{13,5},{2,10},{6,14},... | collective-permute-start | bytes 196616 | tf_op jit(solution)/shard_map/ppermute | solution.py:509
  98.2 6.5 %collective-permute-start.26 = (bf16[32,1024]{1,0:T(8,128)(2,1)S(1)}, bf16[32,1024]{1,0:T(8,128)(2,1)S(1)}, u32[]{:S(2)}, u32[]{:S(2)}) collective-permute-start(bf16[32,1024]{1,0:T(8,128)(2,1)S(1)} %bitcast.37), channel_id=1, source_target_pairs={{0,12},{4,8},{8,4},{12,0},{1,13},{5,9},{9,5},{13,1},{2,14},{6,10},... | collective-permute-start | bytes 196616 | tf_op jit(solution)/shard_map/ppermute | solution.py:509
  99.6 5.5 %collective-permute-start.24 = (bf16[32,1024]{1,0:T(8,128)(2,1)S(1)}, bf16[32,1024]{1,0:T(8,128)(2,1)S(1)}, u32[]{:S(2)}, u32[]{:S(2)}) collective-permute-start(bf16[32,1024]{1,0:T(8,128)(2,1)S(1)} %bitcast.39), channel_id=1, source_target_pairs={{0,4},{4,0},{8,12},{12,8},{1,5},{5,1},{9,13},{13,9},{2,6},{6,2},{1... | collective-permute-start | bytes 196616 | tf_op jit(solution)/shard_map/ppermute | solution.py:509

commit v9 on v7

--- a/solution.py
+++ b/solution.py
@@ -644,7 +644,7 @@
     if bits:
         sign = jnp.full((1,), 1 - 2 * (lax.axis_index("chan") // 2 ** bits[-1] % 2), jnp.int32)
         moving = [
-            call(add_kernel, shape(*mixed.shape, bf16), "add", (sign, mixed, other), 1)
+            call(add_kernel, shape(*mixed.shape, bf16), "add", (sign, mixed, other), 1, cost=SMALL)
             for mixed, other in zip(moving, received)
         ]
     early, late, *far_early = moving

time: 106 us -> 106 us (level)
  no operation moved by 1% of the time
where the time goes in v9:
time: 106 us
  waiting for transfers between devices  48.6 us (46%)
  starting transfers between devices  39.5 us (37%)
  Pallas kernels  10.2 us (10%)
  local copies, waits for them, and re-layouts  5.09 us (5%)
  other arithmetic  2.14 us (2%)
    ppermute x13, waiting for transfers between devices, swap_seq(): return lax.ppermute(value, 'seq', [(k, k ^ distance) for k in range(count)])  27.6 us
    ppermute x13, starting transfers between devices, swap_seq(): return lax.ppermute(value, 'seq', [(k, k ^ distance) for k in range(count)])  23.6 us
    ppermute x12, waiting for transfers between devices, swap(): return lax.ppermute(value, axis, [(k, k ^ 1 << bit) for k in range(count)])  21 us
    ppermute x12, starting transfers between devices, swap(): return lax.ppermute(value, axis, [(k, k ^ 1 << bit) for k in range(count)])  10 us
    pallas_call x8, Pallas kernels, call(): pl.pallas_call(kernel, out_shape=out_shape, in_specs=specs, scratch_shape...  9.09 us
    ppermute x1, starting transfers between devices, paired_body(): lax.ppermute(straight, 'seq', [(k, k + 2 * ahead) for k in firsts])  4.5 us
    dynamic_slice x2, local copies, waits for them, and re-layouts, half_of(): return lax.dynamic_slice_in_dim(value, which * half, half, 1)  2.84 us
  transfers between devices with their start and end apart: 27, of which 15 were waited for; matrix products, arithmetic and copies ran while one was open for 4% of the time, Pallas kernels for 7%

profile of v9, /device:TPU:0, one launch (start us, length us, event | category | flops | bytes accessed | tf_op | source)
XLA Modules:
  0.0 106.0 jit_solution(3632551780229188501)
XLA Ops:
  0.0 1.3 %constant_dynamic-slice_fusion.8 = (bf16[128,1,256]{2,1,0:T(2,128)(2,1)S(1)}, bf16[128,1,256]{2,1,0:T(2,128)(2,1)S(1)}) fusion(bf16[128,2,256]{2,1,0:T(2,128)(2,1)} %param.18, s32[]{:T(128)S(6)} %select_n.150, bf16[128,2,256]{2,1,0:T(2,128)(2,1)} %param.17), kind=kLoop, calls=%fused_computation.52 | loop fusion | bytes 262148 | tf_op jit(solution)/shard_map/jit(dynamic_index_in_dim)/dynamic_slice | solution.py:536
  1.3 0.7 pad_maximum_fusion.4.steps_ref
  2.1 1.1 %constant_dynamic-slice_fusion.10 = (bf16[128,1024]{1,0:T(8,128)(2,1)S(1)}, bf16[128,1024]{1,0:T(8,128)(2,1)S(1)}) fusion(bf16[128,2048]{1,0:T(8,128)(2,1)} %param.16, s32[]{:T(128)S(6)} %select_n.148, s32[]{:T(128)S(6)} %select_n.147), kind=kLoop, calls=%fused_computation.54 | loop fusion | bytes 1048584 | tf_op jit(solution)/shard_map/dynamic_slice | solution.py:546
  3.1 0.8 pack.1
  4.0 3.1 %collective-permute-start.5 = (bf16[128,1664]{1,0:T(8,128)(2,1)S(1)}, bf16[128,1664]{1,0:T(8,128)(2,1)S(1)}, u32[]{:S(2)}, u32[]{:S(2)}) collective-permute-start(bf16[128,1664]{1,0:T(8,128)(2,1)S(1)} %get-tuple-element.100), channel_id=1, source_target_pairs={{0,4},{4,0},{8,12},{12,8},{1,5},{5,1},{9,13},{13,9},{2,6},{6,2},{1... | collective-permute-start | bytes 1277960 | tf_op jit(solution)/shard_map/ppermute | solution.py:509
  7.1 4.5 %collective-permute-start.2 = (bf16[1296,128]{1,0:T(8,128)(2,1)S(1)}, bf16[1296,128]{1,0:T(8,128)(2,1)S(1)}, u32[]{:S(2)}, u32[]{:S(2)}) collective-permute-start(bf16[1296,128]{1,0:T(8,128)(2,1)S(1)} %get-tuple-element.97), channel_id=1, source_target_pairs={{0,8},{4,12},{1,9},{5,13},{2,10},{6,14},{3,11},{7,15},{16,24},{20,... | collective-permute-start | bytes 995336 | tf_op jit(solution)/shard_map/ppermute | solution.py:563
  11.6 1.3 %collective-permute-start.3 = (bf16[1296,128]{1,0:T(8,128)(2,1)S(1)}, bf16[1296,128]{1,0:T(8,128)(2,1)S(1)}, u32[]{:S(2)}, u32[]{:S(2)}) collective-permute-start(bf16[1296,128]{1,0:T(8,128)(2,1)S(1)} %get-tuple-element.98), channel_id=1, source_target_pairs={{0,12},{4,8},{1,13},{5,9},{2,14},{6,10},{3,15},{7,11},{16,28},{20,... | collective-permute-start | bytes 995336 | tf_op jit(solution)/shard_map/ppermute | solution.py:564
  12.9 1.8 %constant_dynamic-slice_fusion.6 = (bf16[128,1024]{1,0:T(8,128)(2,1)}, bf16[128,1024]{1,0:T(8,128)(2,1)S(1)}) fusion(bf16[128,2048]{1,0:T(8,128)(2,1)} %param.22, s32[]{:T(128)S(6)} %select_n.148, s32[]{:T(128)S(6)} %select_n.147), kind=kLoop, calls=%fused_computation.50 | loop fusion | bytes 1048584 | tf_op jit(solution)/shard_map/dynamic_slice | solution.py:546
  14.7 0.5 collective-permute-start.4
  15.2 0.7 broadcast_in_dim.67
  16.0 0.7 select_multiply_fusion
  16.7 0.5 collective-permute-done.5.msg_ref
  17.3 1.9 %pair.1 = (f32[256,1024]{1,0:T(8,128)S(1)}, f32[256,1024]{1,0:T(8,128)S(1)}, bf16[256,256]{1,0:T(8,128)(2,1)S(1)}) custom-call(s32[1]{0:T(128)} %bitcast.3.where_ref.refs_2_, bf16[128,1024]{1,0:T(8,128)(2,1)S(1)} %get-tuple-element.144.x_mine_ref.x_ref, bf16[128,640]{1,0:T(8,128)(2,1)S(1)} %get-tuple-element.99.meta_ref, ...), custom_call_target="tpu_custom_call" | custom-call | flops 1 | bytes 1 | tf_op jit(solution)/shard_map/pair/pallas_call | solution.py:496
  19.2 17.0 %collective-permute-done.4.refs_4_ = bf16[128,1024]{1,0:T(8,128)(2,1)S(1)} collective-permute-done((bf16[128,1024]{1,0:T(8,128)(2,1)}, bf16[128,1024]{1,0:T(8,128)(2,1)S(1)}, u32[]{:S(2)}, u32[]{:S(2)}) %collective-permute-start.4) | collective-permute-done | bytes 262176 | tf_op jit(solution)/shard_map/ppermute | solution.py:509
  36.2 1.1 %mix.1 = (bf16[128,1024]{1,0:T(8,128)(2,1)S(1)}, bf16[128,1024]{1,0:T(8,128)(2,1)S(1)}) custom-call(bf16[1296,128]{1,0:T(8,128)(2,1)S(1)} %collective-permute-done.2.refs_0_, bf16[1296,128]{1,0:T(8,128)(2,1)S(1)} %collective-permute-done.3.refs_1_, s32[1]{0:T(128)} %bitcast.3.where_ref.refs_2_, bf16[128,1024]{1,0:T(8,128)(2,1)S(1)} %get-tuple-element.142.refs_3_, ...), custom_call_target="tpu_custom_call" | custom-call | flops 1 | bytes 30000000 | tf_op jit(solution)/shard_map/mix/pallas_call | solution.py:597
  37.9 1.0 collective-permute-done.9
  39.0 4.1 %collective-permute-start.10 = (bf16[128,1024]{1,0:T(8,128)(2,1)S(1)}, bf16[128,1024]{1,0:T(8,128)(2,1)S(1)}, u32[]{:S(2)}, u32[]{:S(2)}) collective-permute-start(bf16[128,1024]{1,0:T(8,128)(2,1)S(1)} %add_convert_fusion.3), channel_id=1, source_target_pairs={{0,4},{4,0},{8,12},{12,8},{1,5},{5,1},{9,13},{13,9},{2,6},{6,2},{1... | collective-permute-start | bytes 786440 | tf_op jit(solution)/shard_map/ppermute | solution.py:509
  43.1 2.0 %collective-permute-start.11 = (bf16[96,1024]{1,0:T(8,128)(2,1)S(1)}, bf16[96,1024]{1,0:T(8,128)(2,1)S(1)}, u32[]{:S(2)}, u32[]{:S(2)}) collective-permute-start(bf16[96,1024]{1,0:T(8,128)(2,1)S(1)} %slice.32), channel_id=1, source_target_pairs={{0,8},{4,12},{8,0},{12,4},{1,9},{5,13},{9,1},{13,5},{2,10},{6,14},... | collective-permute-start | bytes 589832 | tf_op jit(solution)/shard_map/ppermute | solution.py:509
  45.2 1.6 %collective-permute-start.7 = (bf16[64,1024]{1,0:T(8,128)(2,1)S(1)}, bf16[64,1024]{1,0:T(8,128)(2,1)S(1)}, u32[]{:S(2)}, u32[]{:S(2)}) collective-permute-start(bf16[64,1024]{1,0:T(8,128)(2,1)S(1)} %get-tuple-element.106), channel_id=1, source_target_pairs={{0,2},{2,0},{1,3},{3,1},{4,6},{6,4},{5,7},{7,5},{8,10},{10,8},{9,1... | collective-permute-start | bytes 393224 | tf_op jit(solution)/shard_map/ppermute | solution.py:474
  46.8 0.5 collective-permute-start.8
  47.3 4.4 %collective-permute-done.7 = bf16[64,1024]{1,0:T(8,128)(2,1)S(1)} collective-permute-done((bf16[64,1024]{1,0:T(8,128)(2,1)S(1)}, bf16[64,1024]{1,0:T(8,128)(2,1)S(1)}, u32[]{:S(2)}, u32[]{:S(2)}) %collective-permute-start.7) | collective-permute-done | bytes 131104 | tf_op jit(solution)/shard_map/ppermute | solution.py:474
  51.7 1.7 %collective-permute-done.8 = bf16[64,1024]{1,0:T(8,128)(2,1)S(1)} collective-permute-done((bf16[64,1024]{1,0:T(8,128)(2,1)S(1)}, bf16[64,1024]{1,0:T(8,128)(2,1)S(1)}, u32[]{:S(2)}, u32[]{:S(2)}) %collective-permute-start.8) | collective-permute-done | bytes 131104 | tf_op jit(solution)/shard_map/ppermute | solution.py:474
  53.3 0.6 collective-permute-done.10
  54.0 2.8 %collective-permute-start.15 = (bf16[128,1024]{1,0:T(8,128)(2,1)S(1)}, bf16[128,1024]{1,0:T(8,128)(2,1)S(1)}, u32[]{:S(2)}, u32[]{:S(2)}) collective-permute-start(bf16[128,1024]{1,0:T(8,128)(2,1)S(1)} %pad_maximum_fusion), channel_id=1, source_target_pairs={{0,8},{4,12},{8,0},{12,4},{1,9},{5,13},{9,1},{13,5},{2,10},{6,14},... | collective-permute-start | bytes 786440 | tf_op jit(solution)/shard_map/ppermute | solution.py:509
  56.8 2.2 %collective-permute-start.16 = (bf16[128,1024]{1,0:T(8,128)(2,1)S(1)}, bf16[128,1024]{1,0:T(8,128)(2,1)S(1)}, u32[]{:S(2)}, u32[]{:S(2)}) collective-permute-start(bf16[128,1024]{1,0:T(8,128)(2,1)S(1)} %pad_maximum_fusion), channel_id=1, source_target_pairs={{0,4},{4,0},{8,12},{12,8},{1,5},{5,1},{9,13},{13,9},{2,6},{6,2},{1... | collective-permute-start | bytes 786440 | tf_op jit(solution)/shard_map/ppermute | solution.py:509
  59.1 1.6 %collective-permute-start.12 = (bf16[96,1024]{1,0:T(8,128)(2,1)S(1)}, bf16[96,1024]{1,0:T(8,128)(2,1)S(1)}, u32[]{:S(2)}, u32[]{:S(2)}) collective-permute-start(bf16[96,1024]{1,0:T(8,128)(2,1)S(1)} %slice.26.mixed_ref), channel_id=1, source_target_pairs={{0,2},{2,0},{1,3},{3,1},{4,6},{6,4},{5,7},{7,5},{8,10},{10,8},{9,1... | collective-permute-start | bytes 589832 | tf_op jit(solution)/shard_map/ppermute | solution.py:474
  61.2 1.5 %collective-permute-start.13 = (bf16[32,1024]{1,0:T(8,128)(2,1)S(1)}, bf16[32,1024]{1,0:T(8,128)(2,1)S(1)}, u32[]{:S(2)}, u32[]{:S(2)}) collective-permute-start(bf16[32,1024]{1,0:T(8,128)(2,1)S(1)} %slice.27.mixed_ref), channel_id=1, source_target_pairs={{0,2},{2,0},{1,3},{3,1},{4,6},{6,4},{5,7},{7,5},{8,10},{10,8},{9,1... | collective-permute-start | bytes 196616 | tf_op jit(solution)/shard_map/ppermute | solution.py:474
  62.7 6.7 %collective-permute-done.13.received_ref = bf16[32,1024]{1,0:T(8,128)(2,1)S(1)} collective-permute-done((bf16[32,1024]{1,0:T(8,128)(2,1)S(1)}, bf16[32,1024]{1,0:T(8,128)(2,1)S(1)}, u32[]{:S(2)}, u32[]{:S(2)}) %collective-permute-start.13) | collective-permute-done | bytes 65568 | tf_op jit(solution)/shard_map/ppermute | solution.py:474
  69.4 1.6 %collective-permute-start.18 = (bf16[128,1024]{1,0:T(8,128)(2,1)S(1)}, bf16[128,1024]{1,0:T(8,128)(2,1)S(1)}, u32[]{:S(2)}, u32[]{:S(2)}) collective-permute-start(bf16[128,1024]{1,0:T(8,128)(2,1)S(1)} %collective-permute-done.10), channel_id=1, source_target_pairs={{0,2},{2,0},{1,3},{3,1},{4,6},{6,4},{5,7},{7,5},{8,10},{10,8},{9,1... | collective-permute-start | bytes 786440 | tf_op jit(solution)/shard_map/ppermute | solution.py:474
  71.0 0.7 collective-permute-start.17
  71.7 3.1 %collective-permute-start.19 = (bf16[32,1024]{1,0:T(8,128)(2,1)S(1)}, bf16[32,1024]{1,0:T(8,128)(2,1)S(1)}, u32[]{:S(2)}, u32[]{:S(2)}) collective-permute-start(bf16[32,1024]{1,0:T(8,128)(2,1)S(1)} %add.245), channel_id=1, source_target_pairs={{0,8},{4,12},{8,0},{12,4},{1,9},{5,13},{9,1},{13,5},{2,10},{6,14},... | collective-permute-start | bytes 196616 | tf_op jit(solution)/shard_map/ppermute | solution.py:509
  74.9 0.6 collective-permute-start.20
  75.6 4.2 %collective-permute-done.17 = bf16[128,1024]{1,0:T(8,128)(2,1)S(1)} collective-permute-done((bf16[128,1024]{1,0:T(8,128)(2,1)S(1)}, bf16[128,1024]{1,0:T(8,128)(2,1)S(1)}, u32[]{:S(2)}, u32[]{:S(2)}) %collective-permute-start.17) | collective-permute-done | bytes 262176 | tf_op jit(solution)/shard_map/ppermute | solution.py:509
  79.8 0.7 collective-permute-start.21
  80.7 4.5 %conditional.2 = (bf16[2,2,2,16,1024]{4,3,2,1,0:T(8,128)(2,1)S(1)}) conditional(s32[]{:T(128)} %convert_element_type.102, () %tuple.22, (s32[1]{0:T(128)}, bf16[2048,1024]{1,0:T(8,128)(2,1)}, bf16[128,1024]{1,0:T(8,128)(2,1)S(1)}, bf16[128,1024]{1,0:T(8,128)(2,1)S(1)}, bf16[128,1024]{1,0:T(8,128)(2,1)S(1)}, ...), branch_computations={%region_0.1_spmd, %region_1.2_spmd} | conditional | flops 524309 | bytes 32359552 | solution.py:685
  80.7 2.7 %project.2 = bf16[2,2,2,2,16,1024]{5,4,3,2,1,0:T(8,128)(2,1)S(1)} custom-call(s32[1]{0:T(128)} %get-tuple-element.42.where_ref, bf16[2048,1024]{1,0:T(8,128)(2,1)} %get-tuple-element.44.weight_ref, bf16[128,1024]{1,0:T(8,128)(2,1)S(1)} %get-tuple-element.45.refs_0_, bf16[128,1024]{1,0:T(8,128)(2,1)S(1)} %get-tuple-element.46.refs_1_, ...), custom_call_target="tpu_custom_call" | custom-call | flops 1 | bytes 30000000 | tf_op jit(solution)/shard_map/cond/branch_1_fun/project/pallas_call | solution.py:496
  83.5 1.5 %collective-permute-done = bf16[1,2,2,2,16,1024]{5,4,3,2,1,0:T(8,128)(2,1)S(1)} collective-permute-done((bf16[1,2,2,2,16,1024]{5,4,3,2,1,0:T(8,128)(2,1)S(1)}, bf16[1,2,2,2,16,1024]{5,4,3,2,1,0:T(8,128)(2,1)S(1)}, u32[]{:S(2)}, u32[]{:S(2)}) %collective-permute-start) | collective-permute-done | bytes 262176 | tf_op jit(solution)/shard_map/cond/branch_1_fun/ppermute | solution.py:474
  85.5 0.7 collective-permute-start.22
  86.2 4.5 %conditional.3 = (bf16[2,2,2,16,1024]{4,3,2,1,0:T(8,128)(2,1)S(1)}) conditional(s32[]{:T(128)} %convert_element_type.102, () %tuple.28, (s32[1]{0:T(128)}, bf16[2048,1024]{1,0:T(8,128)(2,1)}, bf16[128,1024]{1,0:T(8,128)(2,1)S(1)}, bf16[128,1024]{1,0:T(8,128)(2,1)S(1)}, bf16[128,1024]{1,0:T(8,128)(2,1)S(1)}, ...), branch_computations={%region_2.3_spmd, %region_3.4_spmd} | conditional | flops 524309 | bytes 32359552 | solution.py:685
  86.3 2.7 %project.3 = bf16[2,2,2,2,16,1024]{5,4,3,2,1,0:T(8,128)(2,1)S(1)} custom-call(s32[1]{0:T(128)} %get-tuple-element.51.where_ref, bf16[2048,1024]{1,0:T(8,128)(2,1)} %get-tuple-element.52.weight_ref, bf16[128,1024]{1,0:T(8,128)(2,1)S(1)} %get-tuple-element.53.refs_0_, bf16[128,1024]{1,0:T(8,128)(2,1)S(1)} %get-tuple-element.54.refs_1_, ...), custom_call_target="tpu_custom_call" | custom-call | flops 1 | bytes 30000000 | tf_op jit(solution)/shard_map/cond/branch_1_fun/project/pallas_call | solution.py:496
  89.1 1.5 %collective-permute-done.1 = bf16[1,2,2,2,16,1024]{5,4,3,2,1,0:T(8,128)(2,1)S(1)} collective-permute-done((bf16[1,2,2,2,16,1024]{5,4,3,2,1,0:T(8,128)(2,1)S(1)}, bf16[1,2,2,2,16,1024]{5,4,3,2,1,0:T(8,128)(2,1)S(1)}, u32[]{:S(2)}, u32[]{:S(2)}) %collective-permute-start.1) | collective-permute-done | bytes 262176 | tf_op jit(solution)/shard_map/cond/branch_1_fun/ppermute | solution.py:474
  90.9 1.4 %collective-permute-start.23 = (bf16[1,2,2,16,1024]{4,3,2,1,0:T(8,128)(2,1)S(1)}, bf16[1,2,2,16,1024]{4,3,2,1,0:T(8,128)(2,1)S(1)}, u32[]{:S(2)}, u32[]{:S(2)}) collective-permute-start(bf16[1,2,2,16,1024]{4,3,2,1,0:T(8,128)(2,1)S(1)} %constant_dynamic-slice_fusion.4), channel_id=1, source_target_pairs={{0,2},{2,0},{1,3},{3,1},{4,6},{6,4},{5,7},{7,5},{8,10},{10,8},{9,1... | collective-permute-start | bytes 393224 | tf_op jit(solution)/shard_map/ppermute | solution.py:474
  92.3 4.1 %collective-permute-done.23 = bf16[1,2,2,16,1024]{4,3,2,1,0:T(8,128)(2,1)S(1)} collective-permute-done((bf16[1,2,2,16,1024]{4,3,2,1,0:T(8,128)(2,1)S(1)}, bf16[1,2,2,16,1024]{4,3,2,1,0:T(8,128)(2,1)S(1)}, u32[]{:S(2)}, u32[]{:S(2)}) %collective-permute-start.23) | collective-permute-done | bytes 131104 | tf_op jit(solution)/shard_map/ppermute | solution.py:474
  96.5 2.6 %collective-permute-start.25 = (bf16[32,1024]{1,0:T(8,128)(2,1)S(1)}, bf16[32,1024]{1,0:T(8,128)(2,1)S(1)}, u32[]{:S(2)}, u32[]{:S(2)}) collective-permute-start(bf16[32,1024]{1,0:T(8,128)(2,1)S(1)} %bitcast.38), channel_id=1, source_target_pairs={{0,8},{4,12},{8,0},{12,4},{1,9},{5,13},{9,1},{13,5},{2,10},{6,14},... | collective-permute-start | bytes 196616 | tf_op jit(solution)/shard_map/ppermute | solution.py:509
  99.1 0.8 collective-permute-start.26
  100.2 3.4 %collective-permute-done.25.refs_2_ = bf16[32,1024]{1,0:T(8,128)(2,1)S(1)} collective-permute-done((bf16[32,1024]{1,0:T(8,128)(2,1)S(1)}, bf16[32,1024]{1,0:T(8,128)(2,1)S(1)}, u32[]{:S(2)}, u32[]{:S(2)}) %collective-permute-start.25) | collective-permute-done | bytes 65568 | tf_op jit(solution)/shard_map/ppermute | solution.py:509
  103.6 1.6 %collective-permute-done.26.refs_3_ = bf16[32,1024]{1,0:T(8,128)(2,1)S(1)} collective-permute-done((bf16[32,1024]{1,0:T(8,128)(2,1)S(1)}, bf16[32,1024]{1,0:T(8,128)(2,1)S(1)}, u32[]{:S(2)}, u32[]{:S(2)}) %collective-permute-start.26) | collective-permute-done | bytes 65568 | tf_op jit(solution)/shard_map/ppermute | solution.py:509
  105.2 0.7 place.1
  (56 shorter events, 3.1 us)
Async XLA Ops:
  0.0 36.2 %copy-start = (bf16[256,256]{1,0:T(8,128)(2,1)S(1)}, bf16[256,256]{1,0:T(8,128)(2,1)}, u32[]{:S(2)}) copy-start(bf16[256,256]{1,0:T(8,128)(2,1)} %constant.236.clone.refs_9_) | copy-start | bytes 393220
  4.0 13.3 %collective-permute-start.5 = (bf16[128,1664]{1,0:T(8,128)(2,1)S(1)}, bf16[128,1664]{1,0:T(8,128)(2,1)S(1)}, u32[]{:S(2)}, u32[]{:S(2)}) collective-permute-start(bf16[128,1664]{1,0:T(8,128)(2,1)S(1)} %get-tuple-element.100), channel_id=1, source_target_pairs={{0,4},{4,0},{8,12},{12,8},{1,5},{5,1},{9,13},{13,9},{2,6},{6,2},{1... | collective-permute-start | bytes 1277960 | tf_op jit(solution)/shard_map/ppermute | solution.py:509
  7.1 29.1 %collective-permute-start.2 = (bf16[1296,128]{1,0:T(8,128)(2,1)S(1)}, bf16[1296,128]{1,0:T(8,128)(2,1)S(1)}, u32[]{:S(2)}, u32[]{:S(2)}) collective-permute-start(bf16[1296,128]{1,0:T(8,128)(2,1)S(1)} %get-tuple-element.97), channel_id=1, source_target_pairs={{0,8},{4,12},{1,9},{5,13},{2,10},{6,14},{3,11},{7,15},{16,24},{20,... | collective-permute-start | bytes 995336 | tf_op jit(solution)/shard_map/ppermute | solution.py:563
  11.6 24.6 %collective-permute-start.3 = (bf16[1296,128]{1,0:T(8,128)(2,1)S(1)}, bf16[1296,128]{1,0:T(8,128)(2,1)S(1)}, u32[]{:S(2)}, u32[]{:S(2)}) collective-permute-start(bf16[1296,128]{1,0:T(8,128)(2,1)S(1)} %get-tuple-element.98), channel_id=1, source_target_pairs={{0,12},{4,8},{1,13},{5,9},{2,14},{6,10},{3,15},{7,11},{16,28},{20,... | collective-permute-start | bytes 995336 | tf_op jit(solution)/shard_map/ppermute | solution.py:564
  14.7 21.5 %collective-permute-start.4 = (bf16[128,1024]{1,0:T(8,128)(2,1)}, bf16[128,1024]{1,0:T(8,128)(2,1)S(1)}, u32[]{:S(2)}, u32[]{:S(2)}) collective-permute-start(bf16[128,1024]{1,0:T(8,128)(2,1)} %get-tuple-element.141), channel_id=1, source_target_pairs={{0,4},{4,0},{8,12},{12,8},{1,5},{5,1},{9,13},{13,9},{2,6},{6,2},{1... | collective-permute-start | bytes 786440 | tf_op jit(solution)/shard_map/ppermute | solution.py:509
  19.2 43.5 %copy-start.1 = (s32[2048]{0:T(1024)S(1)}, s32[2048]{0:T(1024)}, u32[]{:S(2)}) copy-start(s32[2048]{0:T(1024)} %param.25) | copy-start | bytes 24580
  37.3 1.6 %collective-permute-start.9 = (bf16[128,1024]{1,0:T(8,128)(2,1)S(1)}, bf16[128,1024]{1,0:T(8,128)(2,1)S(1)}, u32[]{:S(2)}, u32[]{:S(2)}) collective-permute-start(bf16[128,1024]{1,0:T(8,128)(2,1)S(1)} %get-tuple-element.105), channel_id=1, source_target_pairs={{0,1},{1,0},{2,3},{3,2},{4,5},{5,4},{6,7},{7,6},{8,9},{9,8},{10,11... | collective-permute-start | bytes 786440 | tf_op jit(solution)/shard_map/ppermute | solution.py:474
  37.4 7.7 %collective-permute-start.6 = (bf16[128,1024]{1,0:T(8,128)(2,1)S(1)}, bf16[128,1024]{1,0:T(8,128)(2,1)S(1)}, u32[]{:S(2)}, u32[]{:S(2)}) collective-permute-start(bf16[128,1024]{1,0:T(8,128)(2,1)S(1)} %get-tuple-element.104), channel_id=1, source_target_pairs={{0,1},{1,0},{2,3},{3,2},{4,5},{5,4},{6,7},{7,6},{8,9},{9,8},{10,11... | collective-permute-start | bytes 786440 | tf_op jit(solution)/shard_map/ppermute | solution.py:474
  39.0 14.9 %collective-permute-start.10 = (bf16[128,1024]{1,0:T(8,128)(2,1)S(1)}, bf16[128,1024]{1,0:T(8,128)(2,1)S(1)}, u32[]{:S(2)}, u32[]{:S(2)}) collective-permute-start(bf16[128,1024]{1,0:T(8,128)(2,1)S(1)} %add_convert_fusion.3), channel_id=1, source_target_pairs={{0,4},{4,0},{8,12},{12,8},{1,5},{5,1},{9,13},{13,9},{2,6},{6,2},{1... | collective-permute-start | bytes 786440 | tf_op jit(solution)/shard_map/ppermute | solution.py:509
  43.1 10.2 %collective-permute-start.11 = (bf16[96,1024]{1,0:T(8,128)(2,1)S(1)}, bf16[96,1024]{1,0:T(8,128)(2,1)S(1)}, u32[]{:S(2)}, u32[]{:S(2)}) collective-permute-start(bf16[96,1024]{1,0:T(8,128)(2,1)S(1)} %slice.32), channel_id=1, source_target_pairs={{0,8},{4,12},{8,0},{12,4},{1,9},{5,13},{9,1},{13,5},{2,10},{6,14},... | collective-permute-start | bytes 589832 | tf_op jit(solution)/shard_map/ppermute | solution.py:509
  45.2 6.4 %collective-permute-start.7 = (bf16[64,1024]{1,0:T(8,128)(2,1)S(1)}, bf16[64,1024]{1,0:T(8,128)(2,1)S(1)}, u32[]{:S(2)}, u32[]{:S(2)}) collective-permute-start(bf16[64,1024]{1,0:T(8,128)(2,1)S(1)} %get-tuple-element.106), channel_id=1, source_target_pairs={{0,2},{2,0},{1,3},{3,1},{4,6},{6,4},{5,7},{7,5},{8,10},{10,8},{9,1... | collective-permute-start | bytes 393224 | tf_op jit(solution)/shard_map/ppermute | solution.py:474
  46.8 6.6 %collective-permute-start.8 = (bf16[64,1024]{1,0:T(8,128)(2,1)S(1)}, bf16[64,1024]{1,0:T(8,128)(2,1)S(1)}, u32[]{:S(2)}, u32[]{:S(2)}) collective-permute-start(bf16[64,1024]{1,0:T(8,128)(2,1)S(1)} %get-tuple-element.108), channel_id=1, source_target_pairs={{0,2},{2,0},{1,3},{3,1},{4,6},{6,4},{5,7},{7,5},{8,10},{10,8},{9,1... | collective-permute-start | bytes 393224 | tf_op jit(solution)/shard_map/ppermute | solution.py:474
  54.0 15.4 %collective-permute-start.15 = (bf16[128,1024]{1,0:T(8,128)(2,1)S(1)}, bf16[128,1024]{1,0:T(8,128)(2,1)S(1)}, u32[]{:S(2)}, u32[]{:S(2)}) collective-permute-start(bf16[128,1024]{1,0:T(8,128)(2,1)S(1)} %pad_maximum_fusion), channel_id=1, source_target_pairs={{0,8},{4,12},{8,0},{12,4},{1,9},{5,13},{9,1},{13,5},{2,10},{6,14},... | collective-permute-start | bytes 786440 | tf_op jit(solution)/shard_map/ppermute | solution.py:509
  56.8 12.6 %collective-permute-start.16 = (bf16[128,1024]{1,0:T(8,128)(2,1)S(1)}, bf16[128,1024]{1,0:T(8,128)(2,1)S(1)}, u32[]{:S(2)}, u32[]{:S(2)}) collective-permute-start(bf16[128,1024]{1,0:T(8,128)(2,1)S(1)} %pad_maximum_fusion), channel_id=1, source_target_pairs={{0,4},{4,0},{8,12},{12,8},{1,5},{5,1},{9,13},{13,9},{2,6},{6,2},{1... | collective-permute-start | bytes 786440 | tf_op jit(solution)/shard_map/ppermute | solution.py:509
  59.1 10.3 %collective-permute-start.12 = (bf16[96,1024]{1,0:T(8,128)(2,1)S(1)}, bf16[96,1024]{1,0:T(8,128)(2,1)S(1)}, u32[]{:S(2)}, u32[]{:S(2)}) collective-permute-start(bf16[96,1024]{1,0:T(8,128)(2,1)S(1)} %slice.26.mixed_ref), channel_id=1, source_target_pairs={{0,2},{2,0},{1,3},{3,1},{4,6},{6,4},{5,7},{7,5},{8,10},{10,8},{9,1... | collective-permute-start | bytes 589832 | tf_op jit(solution)/shard_map/ppermute | solution.py:474
  60.6 8.7 %collective-permute-start.14 = (bf16[96,1024]{1,0:T(8,128)(2,1)S(1)}, bf16[96,1024]{1,0:T(8,128)(2,1)S(1)}, u32[]{:S(2)}, u32[]{:S(2)}) collective-permute-start(bf16[96,1024]{1,0:T(8,128)(2,1)S(1)} %collective-permute-done.11.mixed_ref), channel_id=1, source_target_pairs={{0,2},{2,0},{1,3},{3,1},{4,6},{6,4},{5,7},{7,5},{8,10},{10,8},{9,1... | collective-permute-start | bytes 589832 | tf_op jit(solution)/shard_map/ppermute | solution.py:474
  61.2 8.2 %collective-permute-start.13 = (bf16[32,1024]{1,0:T(8,128)(2,1)S(1)}, bf16[32,1024]{1,0:T(8,128)(2,1)S(1)}, u32[]{:S(2)}, u32[]{:S(2)}) collective-permute-start(bf16[32,1024]{1,0:T(8,128)(2,1)S(1)} %slice.27.mixed_ref), channel_id=1, source_target_pairs={{0,2},{2,0},{1,3},{3,1},{4,6},{6,4},{5,7},{7,5},{8,10},{10,8},{9,1... | collective-permute-start | bytes 196616 | tf_op jit(solution)/shard_map/ppermute | solution.py:474
  69.4 11.2 %collective-permute-start.18 = (bf16[128,1024]{1,0:T(8,128)(2,1)S(1)}, bf16[128,1024]{1,0:T(8,128)(2,1)S(1)}, u32[]{:S(2)}, u32[]{:S(2)}) collective-permute-start(bf16[128,1024]{1,0:T(8,128)(2,1)S(1)} %collective-permute-done.10), channel_id=1, source_target_pairs={{0,2},{2,0},{1,3},{3,1},{4,6},{6,4},{5,7},{7,5},{8,10},{10,8},{9,1... | collective-permute-start | bytes 786440 | tf_op jit(solution)/shard_map/ppermute | solution.py:474
  71.0 8.9 %collective-permute-start.17 = (bf16[128,1024]{1,0:T(8,128)(2,1)S(1)}, bf16[128,1024]{1,0:T(8,128)(2,1)S(1)}, u32[]{:S(2)}, u32[]{:S(2)}) collective-permute-start(bf16[128,1024]{1,0:T(8,128)(2,1)S(1)} %collective-permute-done.15), channel_id=1, source_target_pairs={{0,4},{4,0},{8,12},{12,8},{1,5},{5,1},{9,13},{13,9},{2,6},{6,2},{1... | collective-permute-start | bytes 786440 | tf_op jit(solution)/shard_map/ppermute | solution.py:509
  71.7 13.4 %collective-permute-start.19 = (bf16[32,1024]{1,0:T(8,128)(2,1)S(1)}, bf16[32,1024]{1,0:T(8,128)(2,1)S(1)}, u32[]{:S(2)}, u32[]{:S(2)}) collective-permute-start(bf16[32,1024]{1,0:T(8,128)(2,1)S(1)} %add.245), channel_id=1, source_target_pairs={{0,8},{4,12},{8,0},{12,4},{1,9},{5,13},{9,1},{13,5},{2,10},{6,14},... | collective-permute-start | bytes 196616 | tf_op jit(solution)/shard_map/ppermute | solution.py:509
  74.9 10.3 %collective-permute-start.20 = (bf16[32,1024]{1,0:T(8,128)(2,1)S(1)}, bf16[32,1024]{1,0:T(8,128)(2,1)S(1)}, u32[]{:S(2)}, u32[]{:S(2)}) collective-permute-start(bf16[32,1024]{1,0:T(8,128)(2,1)S(1)} %add.245), channel_id=1, source_target_pairs={{0,12},{4,8},{8,4},{12,0},{1,13},{5,9},{9,5},{13,1},{2,14},{6,10},... | collective-permute-start | bytes 196616 | tf_op jit(solution)/shard_map/ppermute | solution.py:509
  79.8 5.7 %collective-permute-start.21 = (bf16[96,1024]{1,0:T(8,128)(2,1)S(1)}, bf16[96,1024]{1,0:T(8,128)(2,1)S(1)}, u32[]{:S(2)}, u32[]{:S(2)}) collective-permute-start(bf16[96,1024]{1,0:T(8,128)(2,1)S(1)} %add.244), channel_id=1, source_target_pairs={{0,4},{4,0},{8,12},{12,8},{1,5},{5,1},{9,13},{13,9},{2,6},{6,2},{1... | collective-permute-start | bytes 589832 | tf_op jit(solution)/shard_map/ppermute | solution.py:509
  83.5 1.6 %collective-permute-start = (bf16[1,2,2,2,16,1024]{5,4,3,2,1,0:T(8,128)(2,1)S(1)}, bf16[1,2,2,2,16,1024]{5,4,3,2,1,0:T(8,128)(2,1)S(1)}, u32[]{:S(2)}, u32[]{:S(2)}) collective-permute-start(bf16[1,2,2,2,16,1024]{5,4,3,2,1,0:T(8,128)(2,1)S(1)} %constant_dynamic-slice_fusion), channel_id=1, source_target_pairs={{0,1},{1,0},{2,3},{3,2},{4,5},{5,4},{6,7},{7,6},{8,9},{9,8},{10,11... | collective-permute-start | bytes 786440 | tf_op jit(solution)/shard_map/cond/branch_1_fun/ppermute | solution.py:474
  85.5 5.3 %collective-permute-start.22 = (bf16[1,2,2,16,1024]{4,3,2,1,0:T(8,128)(2,1)S(1)}, bf16[1,2,2,16,1024]{4,3,2,1,0:T(8,128)(2,1)S(1)}, u32[]{:S(2)}, u32[]{:S(2)}) collective-permute-start(bf16[1,2,2,16,1024]{4,3,2,1,0:T(8,128)(2,1)S(1)} %constant_dynamic-slice_fusion.5), channel_id=1, source_target_pairs={{0,2},{2,0},{1,3},{3,1},{4,6},{6,4},{5,7},{7,5},{8,10},{10,8},{9,1... | collective-permute-start | bytes 393224 | tf_op jit(solution)/shard_map/ppermute | solution.py:474
  89.0 1.6 %collective-permute-start.1 = (bf16[1,2,2,2,16,1024]{5,4,3,2,1,0:T(8,128)(2,1)S(1)}, bf16[1,2,2,2,16,1024]{5,4,3,2,1,0:T(8,128)(2,1)S(1)}, u32[]{:S(2)}, u32[]{:S(2)}) collective-permute-start(bf16[1,2,2,2,16,1024]{5,4,3,2,1,0:T(8,128)(2,1)S(1)} %constant_dynamic-slice_fusion.1), channel_id=1, source_target_pairs={{0,1},{1,0},{2,3},{3,2},{4,5},{5,4},{6,7},{7,6},{8,9},{9,8},{10,11... | collective-permute-start | bytes 786440 | tf_op jit(solution)/shard_map/cond/branch_1_fun/ppermute | solution.py:474
  90.9 5.5 %collective-permute-start.23 = (bf16[1,2,2,16,1024]{4,3,2,1,0:T(8,128)(2,1)S(1)}, bf16[1,2,2,16,1024]{4,3,2,1,0:T(8,128)(2,1)S(1)}, u32[]{:S(2)}, u32[]{:S(2)}) collective-permute-start(bf16[1,2,2,16,1024]{4,3,2,1,0:T(8,128)(2,1)S(1)} %constant_dynamic-slice_fusion.4), channel_id=1, source_target_pairs={{0,2},{2,0},{1,3},{3,1},{4,6},{6,4},{5,7},{7,5},{8,10},{10,8},{9,1... | collective-permute-start | bytes 393224 | tf_op jit(solution)/shard_map/ppermute | solution.py:474
  96.5 7.1 %collective-permute-start.25 = (bf16[32,1024]{1,0:T(8,128)(2,1)S(1)}, bf16[32,1024]{1,0:T(8,128)(2,1)S(1)}, u32[]{:S(2)}, u32[]{:S(2)}) collective-permute-start(bf16[32,1024]{1,0:T(8,128)(2,1)S(1)} %bitcast.38), channel_id=1, source_target_pairs={{0,8},{4,12},{8,0},{12,4},{1,9},{5,13},{9,1},{13,5},{2,10},{6,14},... | collective-permute-start | bytes 196616 | tf_op jit(solution)/shard_map/ppermute | solution.py:509
  99.1 6.2 %collective-permute-start.26 = (bf16[32,1024]{1,0:T(8,128)(2,1)S(1)}, bf16[32,1024]{1,0:T(8,128)(2,1)S(1)}, u32[]{:S(2)}, u32[]{:S(2)}) collective-permute-start(bf16[32,1024]{1,0:T(8,128)(2,1)S(1)} %bitcast.37), channel_id=1, source_target_pairs={{0,12},{4,8},{8,4},{12,0},{1,13},{5,9},{9,5},{13,1},{2,14},{6,10},... | collective-permute-start | bytes 196616 | tf_op jit(solution)/shard_map/ppermute | solution.py:509
  99.9 5.3 %collective-permute-start.24 = (bf16[32,1024]{1,0:T(8,128)(2,1)S(1)}, bf16[32,1024]{1,0:T(8,128)(2,1)S(1)}, u32[]{:S(2)}, u32[]{:S(2)}) collective-permute-start(bf16[32,1024]{1,0:T(8,128)(2,1)S(1)} %bitcast.39), channel_id=1, source_target_pairs={{0,4},{4,0},{8,12},{12,8},{1,5},{5,1},{9,13},{13,9},{2,6},{6,2},{1... | collective-permute-start | bytes 196616 | tf_op jit(solution)/shard_map/ppermute | solution.py:509
